TPU v7x, 32 devices: a whole 2x2x4 slice. The times are simulated.
32 devices in a mesh: blk: 16 (over z, x, core), req: 2 (over y).
Axes of the slice: x: 2, y: 2, z: 4, core: 2. Of those that a mesh axis runs over, the one named last changes fastest.
Arguments:
- prefill_queries: bfloat16 [2, 512, 1024], P('req', 'blk'), may hold values from -6 to 6
- decode_queries: bfloat16 [32, 1024], P('req'), may hold values from -6 to 6
- new_prefill: bfloat16 [2, 512, 512], P('req', 'blk'), may hold values from -6 to 6
- new_decode: bfloat16 [32, 512], P('req'), may hold values from -6 to 6
- prefill_cache: bfloat16 [2, 2048, 512], P('req', 'blk'), may hold values from -5 to 5
- decode_cache: bfloat16 [32, 2048, 512], P('req', 'blk'), may hold values from -5 to 5
- prefill_offsets: int32 [2], P('req'), may hold values from 2 to 1536, as said below
- decode_lengths: int32 [32], P('req'), may hold values from 2 to 2047, as said below
- dealing: int32 [34], replicated, may hold values from 0 to 31, as said below
Outputs:
- prefill_out: bfloat16 [2, 512, 1024], P('req', 'blk')
- decode_out: bfloat16 [32, 1024], P('req')
- prefill_cache_out: bfloat16 [2, 2048, 512], P('req', 'blk')
- decode_cache_out: bfloat16 [32, 2048, 512], P('req', 'blk')
Inputs may be any that keep to these rules, and one draw needn't show every extreme that they name: The block of prefill slot i fills positions prefill_offsets[i] to prefill_offsets[i] + 511; some slot has offset 2048 - 512. The new token of decode slot j goes to position decode_lengths[j]; some slot has length 2047. `dealing`: the first 2 entries are a permutation of 0 to 1, the other 32 a permutation of 0 to 31.
All inputs are finite; a program needn't handle non-finite values.
Results may differ from a plain program's by a relative error of at most 0.0085.
Values may be sent and summed in bfloat16 or wider, within the bound.
No kernel may reach another device: no remote copies, remote signals or barrier semaphores. Data moves between devices by JAX's collectives and lax.ppermute only.
A program may use at most 64 MiB of HBM per device.

v0:
```python
import jax
import jax.numpy as jnp
from jax import lax
from jax.sharding import PartitionSpec as P

QUERY_HEADS = 8
KEY_VALUE_HEADS = 2
HEAD_SIZE = 128


masked_fill = -1e30


def merged(part, axis, combine):
    gathered = jax.tree.map(lambda a: lax.all_gather(a, axis), part)

    def take(source):
        return jax.tree.map(lambda a: lax.dynamic_index_in_dim(a, source, 0, False), gathered)

    return lax.fori_loop(
        1, lax.axis_size(axis), lambda source, state: combine(state, take(source)), take(0)
    )


def write_block(cache_table, block_rows, offsets, positions):
    piece_len = block_rows.shape[1]
    relative = positions[None, :] - offsets[:, None]
    picked = jax.vmap(lambda source_rows, row_index: source_rows[row_index])(
        block_rows, jnp.clip(relative, 0, piece_len - 1)
    )
    inside = (relative >= 0) & (relative < piece_len)
    return jnp.where(inside[:, :, None], picked, cache_table)


def scores_of(query_rows, cache_table, limits, key_pos):
    slot_total, row_total = (query_rows.shape[0], query_rows.shape[1])
    column_total = cache_table.shape[1]
    grouped_queries = query_rows.reshape(
        slot_total, row_total, KEY_VALUE_HEADS, QUERY_HEADS // KEY_VALUE_HEADS, HEAD_SIZE
    )
    key_portion = cache_table[:, :, : KEY_VALUE_HEADS * HEAD_SIZE].reshape(
        slot_total, column_total, KEY_VALUE_HEADS, HEAD_SIZE
    )
    scores = jnp.einsum(
        "nrgqd,ncgd->ngqrc", grouped_queries, key_portion, preferred_element_type=jnp.float32
    ) * HEAD_SIZE ** (-0.5)
    visible = (key_pos[None, None, :] <= limits[:, :, None])[:, None, None]
    return (jnp.where(visible, scores, masked_fill), visible)


def weigh_values(scores, visible, maxima, cache_table):
    slot_total, column_total = (cache_table.shape[0], cache_table.shape[1])
    exponent = jnp.where(visible, jnp.exp(scores - maxima[..., None]), 0.0)
    value_portion = cache_table[:, :, KEY_VALUE_HEADS * HEAD_SIZE :].reshape(
        slot_total, column_total, KEY_VALUE_HEADS, HEAD_SIZE
    )
    weighted = jnp.einsum(
        "ngqrc,ncgd->ngqrd",
        exponent.astype(jnp.bfloat16),
        value_portion,
        preferred_element_type=jnp.float32,
    )
    return (jnp.sum(exponent, axis=-1), weighted)


def finish_rows(totals, weighted):
    normed = weighted / totals[..., None]
    slot_total, row_total = (normed.shape[0], normed.shape[3])
    return (
        jnp.transpose(normed, (0, 3, 1, 2, 4))
        .reshape(slot_total, row_total, QUERY_HEADS * HEAD_SIZE)
        .astype(jnp.bfloat16)
    )


def combine(first, second):
    first_max, first_total, first_sum = first
    second_max, second_total, second_sum = second
    joined = jnp.maximum(first_max, second_max)
    first_scale = jnp.exp(first_max - joined)
    second_scale = jnp.exp(second_max - joined)
    return (
        joined,
        first_total * first_scale + second_total * second_scale,
        first_sum * first_scale[..., None] + second_sum * second_scale[..., None],
    )


def per_device(
    prefill_queries,
    decode_queries,
    new_prefill,
    new_decode,
    prefill_cache,
    decode_cache,
    prefill_offsets,
    decode_lengths,
    dealing,
):
    ctx_dev = prefill_cache.shape[1]
    blk_index = lax.axis_index("blk")
    positions = blk_index * ctx_dev + jnp.arange(ctx_dev, dtype=jnp.int32)
    written = positions[None, :] == decode_lengths[:, None]
    decode_cache_out = jnp.where(written[:, :, None], new_decode[:, None, :], decode_cache)
    dec_scores, dec_visible = scores_of(
        decode_queries[:, None, :], decode_cache_out, decode_lengths[:, None], positions
    )
    dec_max = jnp.max(dec_scores, axis=-1)
    dec_total, dec_sum = weigh_values(dec_scores, dec_visible, dec_max, decode_cache_out)
    dec_max, dec_total, dec_sum = merged((dec_max, dec_total, dec_sum), "blk", combine)
    decode_attn = finish_rows(dec_total, dec_sum)[:, 0, :]
    block_rows, whole_queries = (
        lax.all_gather(new_prefill, "blk", axis=1, tiled=True),
        lax.all_gather(prefill_queries, "blk", axis=1, tiled=True),
    )
    prefill_cache_out = write_block(prefill_cache, block_rows, prefill_offsets, positions)
    limits = prefill_offsets[:, None] + jnp.arange(whole_queries.shape[1], dtype=jnp.int32)[None, :]
    scores, visible = scores_of(whole_queries, prefill_cache_out, limits, positions)
    maxima = jnp.max(scores, axis=-1)
    totals, weighted = weigh_values(scores, visible, maxima, prefill_cache_out)
    peer_max, peer_total, peer_sum = (
        lax.all_to_all(maxima[None], "blk", split_axis=4, concat_axis=0, tiled=True),
        lax.all_to_all(totals[None], "blk", split_axis=4, concat_axis=0, tiled=True),
        lax.all_to_all(weighted[None], "blk", split_axis=4, concat_axis=0, tiled=True),
    )
    joined = jnp.max(peer_max, axis=0)
    peer_scale = jnp.exp(peer_max - joined[None])
    totals = jnp.sum(peer_total * peer_scale, axis=0)
    weighted = jnp.sum(peer_sum * peer_scale[..., None], axis=0)
    prefill_attn = finish_rows(totals, weighted)
    gathered_pre, gathered_dec = (
        lax.all_gather(prefill_attn, "req", axis=0, tiled=True),
        lax.all_gather(decode_attn, "req", axis=0, tiled=True),
    )
    group_index = lax.axis_index("req")
    pre_count = prefill_attn.shape[0]
    dec_count = decode_attn.shape[0]
    total_pre = gathered_pre.shape[0]
    own_pre = group_index * pre_count + jnp.arange(pre_count, dtype=jnp.int32)
    own_dec = group_index * dec_count + jnp.arange(dec_count, dtype=jnp.int32)
    pre_selector = (dealing[:total_pre][None, :] == own_pre[:, None]).astype(jnp.bfloat16)
    dec_selector = (dealing[total_pre:][None, :] == own_dec[:, None]).astype(jnp.bfloat16)
    prefill_out = jnp.einsum(
        "rs,sbf->rbf", pre_selector, gathered_pre, preferred_element_type=jnp.float32
    ).astype(jnp.bfloat16)
    decode_out = jnp.dot(dec_selector, gathered_dec, preferred_element_type=jnp.float32).astype(
        jnp.bfloat16
    )
    return (prefill_out, decode_out, prefill_cache_out, decode_cache_out)


def solution(mesh):
    in_specs = (
        P("req", "blk", None),
        P("req", None),
        P("req", "blk", None),
        P("req", None),
        P("req", "blk", None),
        P("req", "blk", None),
        P("req"),
        P("req"),
        P(),
    )
    out_specs = (
        P("req", "blk", None),
        P("req", None),
        P("req", "blk", None),
        P("req", "blk", None),
    )
    return jax.shard_map(
        per_device, mesh=mesh, in_specs=in_specs, out_specs=out_specs, check_vma=False
    )
```

profile of v0, /device:TPU:0, one launch (start us, length us, event | category | flops | bytes accessed | tf_op | source)
XLA Modules:
  0.0 180.2 jit_solution(12204312932083461674)
XLA Ops:
  8.0 3.9 %copy.83 = bf16[16,128,512]{1,2,0:T(8,128)(2,1)} copy(bf16[16,128,512]{2,1,0:T(8,128)(2,1)} %param.16) | data formatting | bytes 4194304 | tf_op args[5]
  12.0 2.5 %broadcast_select_fusion = bf16[16,128,512]{1,2,0:T(8,128)(2,1)S(1)} fusion(bf16[16,128,512]{1,2,0:T(8,128)(2,1)} %copy.83, pred[16,128]{1,0:T(8,128)(4,1)S(1)} %get-tuple-element.246, bf16[16,512]{1,0:T(8,128)(2,1)S(1)} %copy-done.4), kind=kLoop, calls=%fused_computation.15 | loop fusion | flops 1048576 | bytes 4212736 | tf_op jit(solution)/shard_map/jit(_where)/select_n | solution.py:104
  15.1 1.3 fusion.30
  16.5 2.6 %copy.95 = bf16[16,128,512]{2,1,0:T(8,128)(2,1)} copy(bf16[16,128,512]{1,2,0:T(8,128)(2,1)S(1)} %broadcast_select_fusion) | data formatting | bytes 4194304
  19.8 24.9 %all_gather.30 = bf16[1,512,512]{2,1,0:T(8,128)(2,1)S(1)} all-gather(bf16[1,32,512]{2,1,0:T(8,128)(2,1)S(1)} %copy-done.2), channel_id=1, replica_groups=mesh['blk'=16,'req'=2] {'blk'}, dimensions={1}, use_global_device_ids=true | all-gather | bytes 557056 | tf_op jit(solution)/shard_map/all_gather | solution.py:113
  44.7 1.2 gather_fusion
  46.3 18.3 %all-gather = f32[256,2,4]{2,1,0:T(2,128)S(1)} all-gather(f32[16,2,4]{2,1,0:T(2,128)S(1)} %get-tuple-element.249), channel_id=2, replica_groups=mesh['blk'=16,'req'=2] {'blk'}, dimensions={0}, use_global_device_ids=true | all-gather | bytes 8704 | tf_op jit(solution)/shard_map/all_gather | solution.py:15
  64.9 19.4 %all-gather.1 = f32[256,2,4]{2,1,0:T(2,128)S(1)} all-gather(f32[16,2,4]{2,1,0:T(2,128)S(1)} %fusion.28), channel_id=3, replica_groups=mesh['blk'=16,'req'=2] {'blk'}, dimensions={0}, use_global_device_ids=true | all-gather | bytes 8704 | tf_op jit(solution)/shard_map/all_gather | solution.py:15
  84.4 0.9 copy.91
  85.2 0.9 copy.92
  86.4 1.5 copy.70
  88.7 1.4 reshape.386
  90.1 3.5 %all-to-all-start.1 = ((f32[16,1,256]{2,1,0:T(1,128)}), f32[16,1,256]{2,1,0:T(1,128)S(1)}, u32[]{:S(2)}, u32[]{:S(2)}) async-start(f32[16,1,256]{2,1,0:T(1,128)} %reshape.386), calls=%async_computation.1 | async-start | bytes 32768 | tf_op jit(solution)/shard_map/all_to_all | solution.py:122
  94.4 1.3 reshape.388
  95.7 4.3 %all-to-all-done.1 = f32[16,1,256]{2,1,0:T(1,128)S(1)} async-done(((f32[16,1,256]{2,1,0:T(1,128)}), f32[16,1,256]{2,1,0:T(1,128)S(1)}, u32[]{:S(2)}, u32[]{:S(2)}) %all-to-all-start.1) | async-done | bytes 16416 | tf_op jit(solution)/shard_map/all_to_all | solution.py:122
  100.0 3.4 %all-to-all-start.2 = ((f32[16,1,256]{2,1,0:T(1,128)}), f32[16,1,256]{2,1,0:T(1,128)S(1)}, u32[]{:S(2)}, u32[]{:S(2)}) async-start(f32[16,1,256]{2,1,0:T(1,128)} %reshape.388), calls=%async_computation.2 | async-start | bytes 32768 | tf_op jit(solution)/shard_map/all_to_all | solution.py:123
  104.2 2.7 %copy.76 = f32[1,1,2,4,512,128]{5,3,2,1,0,4:T(4,128)} copy(f32[1,1,2,4,512,128]{5,4,3,2,1,0:T(8,128)S(1)} %convolution_bitcast_fusion) | data formatting | bytes 4194304 | tf_op jit(solution)/shard_map/broadcast_in_dim | solution.py:124
  107.8 2.1 %all-to-all-done.2 = f32[16,1,256]{2,1,0:T(1,128)S(1)} async-done(((f32[16,1,256]{2,1,0:T(1,128)}), f32[16,1,256]{2,1,0:T(1,128)S(1)}, u32[]{:S(2)}, u32[]{:S(2)}) %all-to-all-start.2) | async-done | bytes 16416 | tf_op jit(solution)/shard_map/all_to_all | solution.py:123
  109.9 3.9 %all-to-all-start = ((f32[1,1,2,4,512,128]{5,3,2,1,0,4:T(4,128)}), f32[1,1,2,4,512,128]{5,3,2,1,0,4:T(4,128)S(1)}, u32[]{:S(2)}, u32[]{:S(2)}) async-start(f32[1,1,2,4,512,128]{5,3,2,1,0,4:T(4,128)} %copy.76), calls=%async_computation | async-start | bytes 4194304 | tf_op jit(solution)/shard_map/all_to_all | solution.py:124
  113.8 42.7 %while.19 = (s32[]{:T(128)}, f32[16,2,4,1]{0,2,3,1:T(4,128)S(1)}, f32[16,2,4,1]{0,2,3,1:T(4,128)S(1)}, f32[16,2,4,1,128]{4,3,2,1,0:T(1,128)S(1)}, f32[16,16,2,4,...) while((s32[]{:T(128)}, f32[16,2,4,1]{0,2,3,1:T(4,128)S(1)}, ...), condition=%wide.region_8.9_spmd, body=%wide.region_7.8_spmd.sunk | while | flops 50053 | bytes 337563 | solution.py:20
  115.2 0.9 constant_dynamic-slice_fusion.2
  118.0 0.9 constant_dynamic-slice_fusion.2
  123.7 0.9 constant_dynamic-slice_fusion.2
  126.5 0.9 constant_dynamic-slice_fusion.2
  129.4 0.9 constant_dynamic-slice_fusion.2
  135.1 0.9 constant_dynamic-slice_fusion.2
  138.0 0.9 constant_dynamic-slice_fusion.2
  140.8 0.9 constant_dynamic-slice_fusion.2
  146.5 0.9 constant_dynamic-slice_fusion.2
  149.3 0.9 constant_dynamic-slice_fusion.2
  156.9 4.6 %all_gather.39 = bf16[32,1024]{1,0:T(8,128)(2,1)S(1)} all-gather(bf16[16,1024]{1,0:T(8,128)(2,1)S(1)} %convert_element_type.51), channel_id=1, replica_groups=mesh['blk'=16,'req'=2] {'req'}, dimensions={0}, use_global_device_ids=true | all-gather | bytes 98304 | tf_op jit(solution)/shard_map/all_gather | solution.py:133
  167.5 4.9 %all_gather.32 = bf16[2,32,1024]{2,1,0:T(8,128)(2,1)S(1)} all-gather(bf16[1,32,1024]{2,1,0:T(8,128)(2,1)S(1)} %convert_element_type.46), channel_id=1, replica_groups=mesh['blk'=16,'req'=2] {'req'}, dimensions={0}, use_global_device_ids=true | all-gather | bytes 196608 | tf_op jit(solution)/shard_map/all_gather | solution.py:132
  (164 shorter events, 46.8 us)
Async XLA Ops:
  7.2 79.2 %all-gather.6.cloned.1.call-start = ((), (), s32[]{:S(2)}) async-start(), calls=%async_computation.3 | async-start | bytes 1114112 | tf_op jit(solution)/shard_map/all_gather | solution.py:114
  7.9 99.1 %all-gather.8.cloned.1.call-start = ((), (), s32[]{:S(2)}) async-start(), calls=%async_computation.4 | async-start | bytes 1114112 | tf_op jit(solution)/shard_map/all_gather | solution.py:15
  8.0 4.0 %copy-start.3 = (bf16[16,1024]{1,0:T(8,128)(2,1)S(1)}, bf16[16,1024]{1,0:T(8,128)(2,1)}, u32[]{:S(2)}) copy-start(bf16[16,1024]{1,0:T(8,128)(2,1)} %param.12) | copy-start | bytes 98308
  8.0 4.0 %copy-start.5 = (s32[16]{0:T(128)S(1)}, s32[16]{0:T(128)}, u32[]{:S(2)}) copy-start(s32[16]{0:T(128)} %param.18) | copy-start | bytes 196
  8.0 4.1 %copy-start.4 = (bf16[16,512]{1,0:T(8,128)(2,1)S(1)}, bf16[16,512]{1,0:T(8,128)(2,1)}, u32[]{:S(2)}) copy-start(bf16[16,512]{1,0:T(8,128)(2,1)} %param.14) | copy-start | bytes 49156
  16.5 3.3 %copy-start.2 = (bf16[1,32,512]{2,1,0:T(8,128)(2,1)S(1)}, bf16[1,32,512]{2,1,0:T(8,128)(2,1)}, u32[]{:S(2)}) copy-start(bf16[1,32,512]{2,1,0:T(8,128)(2,1)} %param.13) | copy-start | bytes 98308
  16.5 29.4 %copy-start.1 = (bf16[1,128,512]{2,1,0:T(8,128)(2,1)S(1)}, bf16[1,128,512]{2,1,0:T(8,128)(2,1)}, u32[]{:S(2)}) copy-start(bf16[1,128,512]{2,1,0:T(8,128)(2,1)} %param.15) | copy-start | bytes 393220
  19.1 67.0 %copy-start.6 = (s32[34]{0:T(128)S(1)}, s32[34]{0:T(128)}, u32[]{:S(2)}) copy-start(s32[34]{0:T(128)} %param.19) | copy-start | bytes 412
  46.0 42.4 %copy-start = (bf16[1,128,512]{2,1,0:T(8,128)(2,1)}, bf16[1,128,512]{2,1,0:T(8,128)(2,1)S(1)}, u32[]{:S(2)}) copy-start(bf16[1,128,512]{2,1,0:T(8,128)(2,1)S(1)} %bitcast_select_fusion.1) | copy-start | bytes 393220
  90.1 10.0 %all-to-all-start.1 = ((f32[16,1,256]{2,1,0:T(1,128)}), f32[16,1,256]{2,1,0:T(1,128)S(1)}, u32[]{:S(2)}, u32[]{:S(2)}) async-start(f32[16,1,256]{2,1,0:T(1,128)} %reshape.386), calls=%async_computation.1 | async-start | bytes 32768 | tf_op jit(solution)/shard_map/all_to_all | solution.py:122
  100.0 9.9 %all-to-all-start.2 = ((f32[16,1,256]{2,1,0:T(1,128)}), f32[16,1,256]{2,1,0:T(1,128)S(1)}, u32[]{:S(2)}, u32[]{:S(2)}) async-start(f32[16,1,256]{2,1,0:T(1,128)} %reshape.388), calls=%async_computation.2 | async-start | bytes 32768 | tf_op jit(solution)/shard_map/all_to_all | solution.py:123
  109.9 56.6 %all-to-all-start = ((f32[1,1,2,4,512,128]{5,3,2,1,0,4:T(4,128)}), f32[1,1,2,4,512,128]{5,3,2,1,0,4:T(4,128)S(1)}, u32[]{:S(2)}, u32[]{:S(2)}) async-start(f32[1,1,2,4,512,128]{5,3,2,1,0,4:T(4,128)} %copy.76), calls=%async_computation | async-start | bytes 4194304 | tf_op jit(solution)/shard_map/all_to_all | solution.py:124
Sparse Core Ops, SparseCore 0:
  10.2 40.8 all-gather.5
  53.8 36.8 all-gather.7
where the time goes:
time: 182 us; the launch traced here: 180 us
  blocking collectives  72.1 us (40%)
  local copies, waits for them, and re-layouts  37.6 us (21%)
  other arithmetic  32.8 us (18%)
  between operations  15.1 us (8%)
  starting transfers between devices  10.9 us (6%)
  waiting for transfers between devices  7.15 us (4%)
  matrix products  4.24 us (2%)
    all_gather x2, blocking collectives, merged(): gathered = jax.tree.map(lambda a: lax.all_gather(a, axis), part)  37.6 us
    all_gather x1, blocking collectives, per_device(): lax.all_gather(new_prefill, 'blk', axis=1, tiled=True)  24.9 us
    dynamic_slice x20, local copies, waits for them, and re-layouts, take(): lax.dynamic_index_in_dim(a, source, 0, False)  13.8 us
    unnamed x20, local copies, waits for them, and re-layouts  10.9 us
    mul x15, other arithmetic, combine(): second_sum * second_scale[..., None]  10.5 us
    mul x15, other arithmetic, combine(): first_sum * first_scale[..., None] + second_sum * second_scale[..., None]  10.4 us
    add x15, other arithmetic, combine(): first_sum * first_scale[..., None] + second_sum * second_scale[..., None]  5.83 us
    all_gather x1, blocking collectives, per_device(): lax.all_gather(prefill_attn, 'req', axis=0, tiled=True)  4.94 us
  transfers between devices with their start and end apart: 5, of which 2 were waited for; matrix products, arithmetic and copies ran while one was open for 40% of the time, Pallas kernels for 0%

commit v1 on v0

v1 whole, which is shorter than its diff:
```python
import functools

import jax
import jax.numpy as jnp
from jax import lax
from jax.experimental import pallas as pl
from jax.experimental.pallas import tpu as pltpu
from jax.sharding import PartitionSpec as P

QUERY_HEADS = 8
KEY_VALUE_HEADS = 2
HEAD_SIZE = 128
GROUP = QUERY_HEADS // KEY_VALUE_HEADS
QW = QUERY_HEADS * HEAD_SIZE
KW = KEY_VALUE_HEADS * HEAD_SIZE
GW = GROUP * HEAD_SIZE
STATS = 128
QUAD = 4
SCALE = HEAD_SIZE**-0.5
MASKED = -1e30
FLOOR = -1e20
F32 = jnp.float32
BF16 = jnp.bfloat16

VMEM = pl.BlockSpec(memory_space=pltpu.VMEM)
SMEM = pl.BlockSpec(memory_space=pltpu.SMEM)


def dot_t(a, b):
    return lax.dot_general(a, b, (((1,), (1,)), ((), ())), preferred_element_type=F32)


def dot(a, b):
    return lax.dot_general(a, b, (((1,), (0,)), ((), ())), preferred_element_type=F32)


def split3(value):
    high = value.astype(BF16).astype(F32)
    rest = value - high
    middle = rest.astype(BF16).astype(F32)
    return high, middle, rest - middle


def stats_block(columns, rows):
    lane = lax.broadcasted_iota(jnp.int32, (rows, STATS), 1)
    count = len(columns)
    out = jnp.zeros((rows, STATS), F32)
    for head, column in enumerate(columns):
        for term, part in enumerate(split3(column)):
            out = jnp.where(lane == term * count + head, part, out)
    return out.astype(BF16)


def spread_matrix(heads):
    lane = lax.broadcasted_iota(jnp.int32, (STATS, heads * HEAD_SIZE), 0)
    head = lax.broadcasted_iota(jnp.int32, (STATS, heads * HEAD_SIZE), 1) // HEAD_SIZE
    hit = (lane == head) | (lane == head + heads) | (lane == head + 2 * heads)
    return jnp.where(hit, 1.0, 0.0).astype(BF16)


def join(parts, heads):
    width = heads * HEAD_SIZE
    spread = spread_matrix(heads)
    logs = [dot(part[:, width:], spread) for part in parts]
    top = functools.reduce(jnp.maximum, logs)
    scales = [jnp.exp(log - top) for log in logs]
    total = functools.reduce(jnp.add, scales)
    summed = functools.reduce(
        jnp.add, [scale * part[:, :width].astype(F32) for scale, part in zip(scales, parts)]
    )
    return (summed / total).astype(BF16)


def decode_kernel(step_slots, len_ref, q_ref, new_ref, cache_ref, out_ref, part_ref, acc, top, tot):
    step = pl.program_id(0)
    slots = q_ref.shape[0]
    ctx = cache_ref.shape[1]
    rows = GROUP * slots
    base = lax.axis_index("blk") * ctx
    row_slot = lax.broadcasted_iota(jnp.int32, (rows, ctx), 0) % slots
    column = lax.broadcasted_iota(jnp.int32, (rows, ctx), 1)
    cache_row = lax.broadcasted_iota(jnp.int32, (ctx, cache_ref.shape[2]), 0)

    @pl.when(step == 0)
    def _():
        acc[...] = jnp.zeros_like(acc)
        top[...] = jnp.zeros_like(top)
        tot[...] = jnp.zeros_like(tot)

    limit = jnp.full((rows, ctx), -1, jnp.int32)
    for s in range(step_slots):
        slot = step * step_slots + s
        relative = len_ref[slot] - base
        new_row = new_ref[slot]
        out_ref[s] = jnp.where(cache_row == relative, new_row, cache_ref[s])
        limit = jnp.where(row_slot == slot, relative, limit)
    visible = column <= limit
    inside = (row_slot >= step * step_slots) & (row_slot < (step + 1) * step_slots)
    for g in range(KEY_VALUE_HEADS):
        query = jnp.concatenate(
            [q_ref[:, pl.ds((g * GROUP + h) * HEAD_SIZE, HEAD_SIZE)] for h in range(GROUP)], axis=0
        )
        scores = jnp.full((rows, ctx), MASKED, F32)
        for s in range(step_slots):
            key = out_ref[s, :, pl.ds(g * HEAD_SIZE, HEAD_SIZE)]
            scores = jnp.where(row_slot == step * step_slots + s, dot_t(query, key), scores)
        scores = jnp.where(visible, scores * SCALE, MASKED)
        maxima = jnp.maximum(jnp.max(scores, axis=1, keepdims=True), FLOOR)
        weights = jnp.exp(scores - maxima)
        totals = jnp.sum(weights, axis=1, keepdims=True)
        rounded = weights.astype(BF16)
        total_sum = acc[g]
        for s in range(step_slots):
            value = out_ref[s, :, pl.ds(KW + g * HEAD_SIZE, HEAD_SIZE)]
            picked = jnp.where(row_slot == step * step_slots + s, rounded, jnp.zeros_like(rounded))
            total_sum += dot(picked, value)
        acc[g] = total_sum
        top[g] = jnp.where(inside, maxima, top[g])
        tot[g] = jnp.where(inside, totals, tot[g])

    @pl.when(step == pl.num_programs(0) - 1)
    def _():
        for g in range(KEY_VALUE_HEADS):
            totals = tot[g]
            seen = totals > 0.0
            normed = acc[g] / jnp.where(seen, totals, 1.0)
            logs = jnp.where(seen, top[g] + jnp.log(jnp.where(seen, totals, 1.0)), MASKED)
            columns = []
            for h in range(GROUP):
                part = pl.ds(h * HEAD_SIZE, HEAD_SIZE)
                part_ref[g, :, part] = normed[h * slots : (h + 1) * slots].astype(BF16)
                columns.append(logs[h * slots : (h + 1) * slots, :1])
            part_ref[g, :, pl.ds(GW, STATS)] = stats_block(columns, slots)


def decode_partials(lengths, queries, new_rows, cache):
    slots, ctx, width = cache.shape
    step_slots = 4
    rows = GROUP * slots
    whole = lambda *shape: pl.BlockSpec(shape, lambda i: (0,) * len(shape))
    block = pl.BlockSpec((step_slots, ctx, width), lambda i: (i, 0, 0))
    return pl.pallas_call(
        functools.partial(decode_kernel, step_slots),
        grid=(slots // step_slots,),
        in_specs=[SMEM, whole(slots, QW), whole(slots, 1, width), block],
        out_specs=[block, whole(KEY_VALUE_HEADS, slots, GW + STATS)],
        out_shape=[
            jax.ShapeDtypeStruct(cache.shape, BF16),
            jax.ShapeDtypeStruct((KEY_VALUE_HEADS, slots, GW + STATS), BF16),
        ],
        scratch_shapes=[pltpu.VMEM((KEY_VALUE_HEADS, rows, HEAD_SIZE), F32)] * 3,
        compiler_params=pltpu.CompilerParams(vmem_limit_bytes=16 << 20),
        cost_estimate=pl.CostEstimate(
            flops=4 * slots * ctx * QW, bytes_accessed=2 * cache.size * 2, transcendentals=slots * ctx * 8
        ),
        name="decode_partials",
    )(lengths, queries, new_rows[:, None, :], cache)


def prefill_kernel(hi_count, ctx, off_ref, *refs):
    packs, tables, outs = refs[:hi_count], refs[hi_count : hi_count + QUAD], refs[hi_count + QUAD :]
    tokens = packs[0].shape[0]
    span = tables[0].shape[0]
    me = lax.axis_index("blk")
    hi, quad = me // QUAD, me % QUAD
    offset = off_ref[0]
    pieces = []
    for k in range(QUAD):
        holder = hi * QUAD + (quad ^ k)
        index = lax.broadcasted_iota(jnp.int32, (1, span), 1)
        old = jnp.where(holder * ctx + index < offset, -1, 1 << 30)
        pieces.append(jnp.where(index < ctx, old, holder * tokens + index - ctx))
    key_mark = jnp.concatenate(pieces, axis=1)
    in_block = lax.broadcasted_iota(jnp.int32, (GROUP * tokens, 1), 0) % tokens
    for g in range(KEY_VALUE_HEADS):
        keys = jnp.concatenate([t[:, pl.ds(g * HEAD_SIZE, HEAD_SIZE)] for t in tables], axis=0)
        values = jnp.concatenate([t[:, pl.ds(KW + g * HEAD_SIZE, HEAD_SIZE)] for t in tables], axis=0)
        for k in range(hi_count):
            token = ((hi ^ k) * QUAD + quad) * tokens + in_block
            query = jnp.concatenate(
                [packs[k][:, pl.ds((g * GROUP + h) * HEAD_SIZE, HEAD_SIZE)] for h in range(GROUP)], axis=0
            )
            scores = jnp.where(key_mark <= token, dot_t(query, keys) * SCALE, MASKED)
            maxima = jnp.maximum(jnp.max(scores, axis=1, keepdims=True), FLOOR)
            weights = jnp.exp(scores - maxima)
            totals = jnp.sum(weights, axis=1, keepdims=True)
            summed = dot(weights.astype(BF16), values)
            seen = totals > 0.0
            safe = jnp.where(seen, totals, 1.0)
            normed = (summed / safe).astype(BF16)
            logs = jnp.where(seen, maxima + jnp.log(safe), MASKED)
            for h in range(GROUP):
                part = slice(h * tokens, (h + 1) * tokens)
                outs[k][:, pl.ds((g * GROUP + h) * HEAD_SIZE, HEAD_SIZE)] = normed[part]
            lane = lax.broadcasted_iota(jnp.int32, (tokens, STATS), 1)
            block = jnp.zeros((tokens, STATS), F32) if g == 0 else outs[k][:, pl.ds(QW, STATS)].astype(F32)
            for h in range(GROUP):
                for term, value in enumerate(split3(logs[h * tokens : (h + 1) * tokens])):
                    block = jnp.where(lane == term * QUERY_HEADS + g * GROUP + h, value, block)
            outs[k][:, pl.ds(QW, STATS)] = block.astype(BF16)


def prefill_partials(offset, packs, tables, ctx):
    tokens = packs[0].shape[0]
    span = tables[0].shape[0]
    pairs = len(packs) * tokens * QUAD * span
    return pl.pallas_call(
        functools.partial(prefill_kernel, len(packs), ctx),
        in_specs=[SMEM] + [VMEM] * (len(packs) + len(tables)),
        out_specs=[VMEM] * len(packs),
        out_shape=[jax.ShapeDtypeStruct((tokens, QW + STATS), BF16)] * len(packs),
        compiler_params=pltpu.CompilerParams(vmem_limit_bytes=32 << 20),
        cost_estimate=pl.CostEstimate(
            flops=4 * pairs * QW, bytes_accessed=4 << 20, transcendentals=pairs * QUERY_HEADS
        ),
        name="prefill_partials",
    )(offset, *packs, *tables)


def join_prefill_kernel(*refs):
    refs[-1][...] = join([ref[...] for ref in refs[:-1]], QUERY_HEADS)


def join_prefill(parts):
    return pl.pallas_call(
        join_prefill_kernel,
        in_specs=[VMEM] * len(parts),
        out_specs=VMEM,
        out_shape=jax.ShapeDtypeStruct((parts[0].shape[0], QW), BF16),
        compiler_params=pltpu.CompilerParams(vmem_limit_bytes=16 << 20),
        name="join_prefill",
    )(*parts)


def join_decode_kernel(part_ref, out_ref):
    out_ref[...] = join([part_ref[i] for i in range(part_ref.shape[0])], GROUP)


def join_decode(parts):
    return pl.pallas_call(
        join_decode_kernel,
        in_specs=[VMEM],
        out_specs=VMEM,
        out_shape=jax.ShapeDtypeStruct((parts.shape[1], GW), BF16),
        compiler_params=pltpu.CompilerParams(vmem_limit_bytes=16 << 20),
        name="join_decode",
    )(parts)


def update_kernel(hi_count, off_ref, cache_ref, *refs):
    packs, tables, others, out_ref = (
        refs[:hi_count],
        refs[hi_count : hi_count + QUAD],
        refs[hi_count + QUAD : -1],
        refs[-1],
    )
    ctx = cache_ref.shape[0]
    tokens = packs[0].shape[0]
    me = lax.axis_index("blk")
    hi, quad = me // QUAD, me % QUAD
    blocks = []
    for k in range(hi_count):
        for j in range(QUAD):
            if j == 0:
                blocks.append(packs[k][:, pl.ds(QW, 2 * KW)])
            elif k == 0:
                blocks.append(tables[j][pl.ds(ctx, tokens), :])
            else:
                blocks.append(others[j - 1][pl.ds((k - 1) * tokens, tokens), :])
    rows = jnp.concatenate(blocks, axis=0)
    count = rows.shape[0]
    index = lax.broadcasted_iota(jnp.int32, (1, count), 1)
    block = index // tokens
    token = ((hi ^ (block // QUAD)) * QUAD + (quad ^ (block % QUAD))) * tokens + index % tokens
    wanted = me * ctx + lax.broadcasted_iota(jnp.int32, (ctx, 1), 0) - off_ref[0]
    picked = dot(jnp.where(wanted == token, 1.0, 0.0).astype(BF16), rows).astype(BF16)
    inside = jnp.broadcast_to((wanted >= 0) & (wanted < count), out_ref.shape)
    out_ref[...] = jnp.where(inside, picked, cache_ref[...])


def update_cache(offset, cache, packs, tables, others):
    return pl.pallas_call(
        functools.partial(update_kernel, len(packs)),
        in_specs=[SMEM] + [VMEM] * (1 + len(packs) + len(tables) + len(others)),
        out_specs=VMEM,
        out_shape=jax.ShapeDtypeStruct(cache.shape, BF16),
        compiler_params=pltpu.CompilerParams(vmem_limit_bytes=16 << 20),
        name="update_cache",
    )(offset, cache, *packs, *tables, *others)


def per_device(
    prefill_queries,
    decode_queries,
    new_prefill,
    new_decode,
    prefill_cache,
    decode_cache,
    prefill_offsets,
    decode_lengths,
    dealing,
):
    blk = lax.axis_size("blk")
    req = lax.axis_size("req")
    hi_count = blk // QUAD
    ctx = prefill_cache.shape[1]
    slots = decode_cache.shape[0]
    group = lax.axis_index("req")

    def over_quad(array, k):
        return lax.ppermute(array, "blk", [(i, i ^ k) for i in range(blk)])

    def over_hi(array, k):
        return lax.ppermute(array, "blk", [(i, i ^ (k * QUAD)) for i in range(blk)])

    table = jnp.concatenate([prefill_cache[0], new_prefill[0]], axis=0)
    pack = jnp.concatenate([prefill_queries[0], new_prefill[0]], axis=1)
    packs = [pack] + [over_hi(pack, k) for k in range(1, hi_count)]
    tables = [table] + [over_quad(table, k) for k in range(1, QUAD)]

    decode_cache_out, decode_part = decode_partials(decode_lengths, decode_queries, new_decode, decode_cache)
    pieces = KEY_VALUE_HEADS * slots // blk
    decode_part = decode_part.reshape(blk, pieces, GW + STATS)
    decode_parts = lax.all_to_all(decode_part, "blk", split_axis=0, concat_axis=0, tiled=True)

    parts = prefill_partials(prefill_offsets, packs, tables, ctx)
    arrived = [over_hi(parts[k], k) for k in range(1, hi_count)]

    decode_piece = join_decode(decode_parts)
    everywhere = jnp.broadcast_to(decode_piece[None], (req * blk, pieces, GW))
    gathered = lax.all_to_all(everywhere, ("req", "blk"), split_axis=0, concat_axis=0, tiled=True)

    new_rows = jnp.concatenate([p[:, QW:] for p in packs[1:]], axis=0)
    others = [over_quad(new_rows, k) for k in range(1, QUAD)]
    prefill_cache_out = update_cache(prefill_offsets, prefill_cache[0], packs, tables, others)[None]

    attended = join_prefill([parts[0]] + arrived)
    if req == 2:
        other = lax.ppermute(attended, "req", [(0, 1), (1, 0)])
        prefill_out = jnp.where(dealing[group] == group, attended, other)[None]
    else:
        spread = lax.all_gather(attended, "req", axis=0)
        source = jnp.argmax(dealing[:req] == group)
        prefill_out = lax.dynamic_index_in_dim(spread, source, 0, True)

    gathered = gathered.reshape(req, KEY_VALUE_HEADS, slots, GW)
    own = group * slots + jnp.arange(slots, dtype=jnp.int32)
    chosen = (dealing[req:][None, :] == own[:, None]).astype(BF16)
    decode_out = jnp.einsum(
        "ors,rgsf->ogf", chosen.reshape(slots, req, slots), gathered, preferred_element_type=F32
    )
    decode_out = decode_out.reshape(slots, QW).astype(BF16)
    return (prefill_out, decode_out, prefill_cache_out, decode_cache_out)


def solution(mesh):
    in_specs = (
        P("req", "blk", None),
        P("req", None),
        P("req", "blk", None),
        P("req", None),
        P("req", "blk", None),
        P("req", "blk", None),
        P("req"),
        P("req"),
        P(),
    )
    out_specs = (
        P("req", "blk", None),
        P("req", None),
        P("req", "blk", None),
        P("req", "blk", None),
    )
    return jax.shard_map(
        per_device, mesh=mesh, in_specs=in_specs, out_specs=out_specs, check_vma=False
    )
```

time: 182 us -> 55.3 us (0.30)
  blocking collectives: 72.1 us -> 0 us
  local copies, waits for them, and re-layouts: 37.6 us -> 5.84 us
  other arithmetic: 32.8 us -> 2.46 us
  starting transfers between devices: 10.9 us -> 24.9 us
  between operations: 15.1 us -> 2.11 us
  Pallas kernels: 0 us -> 9.07 us
  matrix products: 4.24 us -> 0.87 us
  waiting for transfers between devices: 7.15 us -> 9.56 us
    all_gather x5 -> x0, blocking collectives: 72.1 us -> none  [the longest x2 37.6 us: merged(): gathered = jax.tree.map(lambda a: lax.all_gather(a, axis), part)]
    mul x30 -> x0, other arithmetic: 20.9 us -> none  [the longest x15 10.5 us: combine(): second_sum * second_scale[..., None]]
    ppermute x0 -> x13, starting transfers between devices: none -> 17.4 us  [the longest x6 10.1 us: over_hi(): return lax.ppermute(array, 'blk', [(i, i ^ k * QUAD) for i in range(blk)])]
    dynamic_slice x20 -> x1, local copies, waits for them, and re-layouts: 13.8 us -> 0.58 us  [per_device(): prefill_out = jnp.where(dealing[group] == group, attended, other)[None]]
    pallas_call x0 -> x5, Pallas kernels: none -> 9.07 us  [the longest x1 4.73 us: decode_partials(): pl.pallas_call(functools.partial(decode_kernel, step_slots), grid=(slots...]
    unnamed x20 -> x10, local copies, waits for them, and re-layouts: 10.9 us -> 3.01 us
    ppermute x0 -> x13, waiting for transfers between devices: none -> 7.14 us  [the longest x6 5.23 us: over_hi(): return lax.ppermute(array, 'blk', [(i, i ^ k * QUAD) for i in range(blk)])]
    add x18 -> x1, other arithmetic: 5.84 us -> 0.01 us  [per_device(): own = group * slots + jnp.arange(slots, dtype=jnp.int32)]
  transfers between devices with their start and end apart: 5 -> 15, of which waited for: 2 -> 3; matrix products, arithmetic and copies ran while one was open for 40% -> 8% of each run, Pallas kernels for 0% -> 16%
where the time goes in v1:
time: 55.3 us; the launch traced here: 54.8 us
  starting transfers between devices  24.9 us (45%)
  waiting for transfers between devices  9.56 us (17%)
  Pallas kernels  9.07 us (16%)
  local copies, waits for them, and re-layouts  5.84 us (11%)
  other arithmetic  2.46 us (4%)
  between operations  2.11 us (4%)
  matrix products  0.87 us (2%)
    ppermute x6, starting transfers between devices, over_hi(): return lax.ppermute(array, 'blk', [(i, i ^ k * QUAD) for i in range(blk)])  10.1 us
    ppermute x6, starting transfers between devices, over_quad(): return lax.ppermute(array, 'blk', [(i, i ^ k) for i in range(blk)])  5.72 us
    ppermute x6, waiting for transfers between devices, over_hi(): return lax.ppermute(array, 'blk', [(i, i ^ k * QUAD) for i in range(blk)])  5.23 us
    all_to_all x1, starting transfers between devices, per_device(): lax.all_to_all(decode_part, 'blk', split_axis=0, concat_axis=0, tiled=True)  4.98 us
    pallas_call x1, Pallas kernels, decode_partials(): pl.pallas_call(functools.partial(decode_kernel, step_slots), grid=(slots...  4.73 us
    unnamed x10, local copies, waits for them, and re-layouts  3.01 us
    pallas_call x1, Pallas kernels, prefill_partials(): pl.pallas_call(functools.partial(prefill_kernel, len(packs), ctx), in_spe...  2.74 us
    all_to_all x1, starting transfers between devices, per_device(): lax.all_to_all(everywhere, ('req', 'blk'), split_axis=0, concat_axis=0, t...  2.57 us
  transfers between devices with their start and end apart: 15, of which 3 were waited for; matrix products, arithmetic and copies ran while one was open for 8% of the time, Pallas kernels for 16%

profile of v1, /device:TPU:0, one launch (start us, length us, event | category | flops | bytes accessed | tf_op | source)
XLA Modules:
  0.0 54.8 jit_solution(15662860905227728709)
XLA Ops:
  0.6 0.9 %pad_maximum_fusion.1.refs_0_ = bf16[32,1536]{1,0:T(8,128)(2,1)S(1)} fusion(bf16[32,512]{1,0:T(8,128)(2,1)} %bitcast.21, bf16[32,1024]{1,0:T(8,128)(2,1)} %bitcast.23), kind=kLoop, calls=%fused_computation.3 | loop fusion | flops 196608 | bytes 196608 | tf_op jit(solution)/shard_map/concatenate | solution.py:317
  1.5 3.0 %collective-permute-start = (bf16[32,1536]{1,0:T(8,128)(2,1)S(1)}, bf16[32,1536]{1,0:T(8,128)(2,1)S(1)}, u32[]{:S(2)}, u32[]{:S(2)}) collective-permute-start(bf16[32,1536]{1,0:T(8,128)(2,1)S(1)} %pad_maximum_fusion.1.refs_0_), channel_id=1, source_target_pairs={{0,8},{2,10},{4,12},{6,14},{8,0},{10,2},{12,4},{14,6},{16,24},{18,... | collective-permute-start | bytes 294920 | tf_op jit(solution)/shard_map/ppermute | solution.py:314
  4.5 2.6 %collective-permute-start.1 = (bf16[32,1536]{1,0:T(8,128)(2,1)S(1)}, bf16[32,1536]{1,0:T(8,128)(2,1)S(1)}, u32[]{:S(2)}, u32[]{:S(2)}) collective-permute-start(bf16[32,1536]{1,0:T(8,128)(2,1)S(1)} %pad_maximum_fusion.1.refs_0_), channel_id=1, source_target_pairs={{0,16},{2,18},{4,20},{6,22},{8,24},{10,26},{12,28},{14,30},{16,0},... | collective-permute-start | bytes 294920 | tf_op jit(solution)/shard_map/ppermute | solution.py:314
  7.1 0.9 %pad_maximum_fusion.refs_4_ = bf16[160,512]{1,0:T(8,128)(2,1)S(1)} fusion(bf16[32,512]{1,0:T(8,128)(2,1)} %bitcast.22, bf16[128,512]{1,0:T(8,128)(2,1)} %bitcast.16), kind=kLoop, calls=%fused_computation.2 | loop fusion | flops 327680 | bytes 327680 | tf_op jit(solution)/shard_map/concatenate | solution.py:316
  8.2 1.8 %collective-permute-start.4 = (bf16[160,512]{1,0:T(8,128)(2,1)S(1)}, bf16[160,512]{1,0:T(8,128)(2,1)S(1)}, u32[]{:S(2)}, u32[]{:S(2)}) collective-permute-start(bf16[160,512]{1,0:T(8,128)(2,1)S(1)} %pad_maximum_fusion.refs_4_), channel_id=1, source_target_pairs={{0,4},{2,6},{4,0},{6,2},{8,12},{10,14},{12,8},{14,10},{16,20},{18,... | collective-permute-start | bytes 491528 | tf_op jit(solution)/shard_map/ppermute | solution.py:311
  9.9 0.7 %copy.13.new_ref = bf16[16,1,512]{2,1,0:T(2,128)(2,1)S(1)} copy(bf16[16,1,512]{2,0,1:T(8,128)(2,1)} %bitcast.24) | data formatting | bytes 32768 | tf_op jit(solution)/shard_map/broadcast_in_dim | solution.py:157
  10.7 1.6 %copy-done = bf16[16,128,512]{2,1,0:T(8,128)(2,1)S(1)} copy-done((bf16[16,128,512]{2,1,0:T(8,128)(2,1)S(1)}, bf16[16,128,512]{2,1,0:T(8,128)(2,1)}, u32[]{:S(2)}) %copy-start) | copy-done | bytes 2097176
  12.3 0.8 %copy-done.2 = bf16[16,1024]{1,0:T(8,128)(2,1)S(1)} copy-done((bf16[16,1024]{1,0:T(8,128)(2,1)S(1)}, bf16[16,1024]{1,0:T(8,128)(2,1)}, u32[]{:S(2)}) %copy-start.2) | copy-done | bytes 32792
  13.0 0.7 %copy-done.3 = s32[16]{0:T(128)S(1)} copy-done((s32[16]{0:T(128)S(1)}, s32[16]{0:T(128)}, u32[]{:S(2)}) %copy-start.3) | copy-done | bytes 88
  13.7 4.7 %decode_partials.1 = (bf16[16,128,512]{2,1,0:T(8,128)(2,1)}, bf16[2,16,640]{2,1,0:T(8,128)(2,1)S(1)}) custom-call(s32[16]{0:T(128)S(1)} %copy-done.3, bf16[16,1024]{1,0:T(8,128)(2,1)S(1)} %copy-done.2, bf16[16,1,512]{2,1,0:T(2,128)(2,1)S(1)} %copy.13.new_ref, bf16[16,128,512]{2,1,0:T(8,128)(2,1)S(1)} %copy-done), custom_call_target="tpu_custom_call" | custom-call | flops 8388608 | bytes 4194304 | tf_op jit(solution)/shard_map/decode_partials/pallas_call | solution.py:142
  18.4 0.6 %reshape.36 = bf16[16,2,640]{2,1,0:T(2,128)(2,1)} reshape(bf16[2,16,640]{2,1,0:T(8,128)(2,1)S(1)} %get-tuple-element.14) | data formatting | bytes 81920 | tf_op jit(solution)/shard_map/reshape | solution.py:323
  19.1 5.0 %all-to-all-start = ((bf16[16,2,640]{2,1,0:T(2,128)(2,1)}), bf16[16,2,640]{2,1,0:T(2,128)(2,1)S(1)}, u32[]{:S(2)}, u32[]{:S(2)}) async-start(bf16[16,2,640]{2,1,0:T(2,128)(2,1)} %reshape.36), calls=%async_computation | async-start | bytes 81920 | tf_op jit(solution)/shard_map/all_to_all | solution.py:324
  24.1 1.7 %collective-permute-start.5 = (bf16[160,512]{1,0:T(8,128)(2,1)S(1)}, bf16[160,512]{1,0:T(8,128)(2,1)S(1)}, u32[]{:S(2)}, u32[]{:S(2)}) collective-permute-start(bf16[160,512]{1,0:T(8,128)(2,1)S(1)} %pad_maximum_fusion.refs_4_), channel_id=1, source_target_pairs={{0,6},{2,4},{4,2},{6,0},{8,14},{10,12},{12,10},{14,8},{16,22},{18,... | collective-permute-start | bytes 491528 | tf_op jit(solution)/shard_map/ppermute | solution.py:311
  25.8 0.4 collective-permute-start.10
  27.0 0.6 %dynamic_slice.3 = s32[1]{0:T(128)} dynamic-slice(s32[34]{0:T(128)S(1)} %copy-done.4, s32[]{:T(128)S(6)} %select_n.11), dynamic_slice_sizes={1} | dynamic-slice | bytes 12 | tf_op jit(solution)/shard_map/dynamic_slice | solution.py:340
  28.2 0.1 eq.24
  28.3 2.4 %all-to-all-done.part_ref = bf16[16,2,640]{2,1,0:T(2,128)(2,1)S(1)} async-done(((bf16[16,2,640]{2,1,0:T(2,128)(2,1)}), bf16[16,2,640]{2,1,0:T(2,128)(2,1)S(1)}, u32[]{:S(2)}, u32[]{:S(2)}) %all-to-all-start) | async-done | bytes 40992 | tf_op jit(solution)/shard_map/all_to_all | solution.py:324
  30.7 0.4 join_decode.1
  31.1 0.7 %broadcast_in_dim.19 = bf16[32,2,512]{2,1,0:T(2,128)(2,1)} broadcast(bf16[2,512]{1,0:T(2,128)(2,1)S(1)} %join_decode.1), dimensions={1,2} | broadcast | bytes 67584 | tf_op jit(solution)/shard_map/broadcast_in_dim | solution.py:330
  31.8 2.6 %all-to-all-start.1 = ((bf16[32,2,512]{2,1,0:T(2,128)(2,1)}), bf16[32,2,512]{2,1,0:T(2,128)(2,1)S(1)}, u32[]{:S(2)}, u32[]{:S(2)}) async-start(bf16[32,2,512]{2,1,0:T(2,128)(2,1)} %broadcast_in_dim.19), calls=%async_computation.1 | async-start | bytes 131072 | tf_op jit(solution)/shard_map/all_to_all | solution.py:331
  34.4 1.7 %collective-permute-start.11 = (bf16[96,512]{1,0:T(8,128)(2,1)S(1)}, bf16[96,512]{1,0:T(8,128)(2,1)S(1)}, u32[]{:S(2)}, u32[]{:S(2)}) collective-permute-start(bf16[96,512]{1,0:T(8,128)(2,1)S(1)} %pad_maximum_fusion.2), channel_id=1, source_target_pairs={{0,4},{2,6},{4,0},{6,2},{8,12},{10,14},{12,8},{14,10},{16,20},{18,... | collective-permute-start | bytes 294920 | tf_op jit(solution)/shard_map/ppermute | solution.py:311
  36.1 2.7 %prefill_partials.1 = (bf16[32,1152]{1,0:T(8,128)(2,1)S(1)}, bf16[32,1152]{1,0:T(8,128)(2,1)S(1)}, bf16[32,1152]{1,0:T(8,128)(2,1)S(1)}, bf16[32,1152]{1,0:T(8,128)(2,1)S(1)}) custom-call(s32[1]{0:T(128)S(6)} %copy.16.off_ref, bf16[32,1536]{1,0:T(8,128)(2,1)S(1)} %pad_maximum_fusion.1.refs_0_, bf16[32,1536]{1,0:T(8,128)(2,1)S(1)} %collective-permute-done.refs_1_, ...), custom_call_target="tpu_custom_call" | custom-call | flops 335544320 | bytes 4194304 | tf_op jit(solution)/shard_map/prefill_partials/pallas_call | solution.py:207
  38.8 1.6 %collective-permute-start.6 = (bf16[32,1152]{1,0:T(8,128)(2,1)S(1)}, bf16[32,1152]{1,0:T(8,128)(2,1)S(1)}, u32[]{:S(2)}, u32[]{:S(2)}) collective-permute-start(bf16[32,1152]{1,0:T(8,128)(2,1)S(1)} %get-tuple-element.11), channel_id=1, source_target_pairs={{0,8},{2,10},{4,12},{6,14},{8,0},{10,2},{12,4},{14,6},{16,24},{18,... | collective-permute-start | bytes 221192 | tf_op jit(solution)/shard_map/ppermute | solution.py:314
  40.5 2.5 %collective-permute-start.7 = (bf16[32,1152]{1,0:T(8,128)(2,1)S(1)}, bf16[32,1152]{1,0:T(8,128)(2,1)S(1)}, u32[]{:S(2)}, u32[]{:S(2)}) collective-permute-start(bf16[32,1152]{1,0:T(8,128)(2,1)S(1)} %get-tuple-element.12), channel_id=1, source_target_pairs={{0,16},{2,18},{4,20},{6,22},{8,24},{10,26},{12,28},{14,30},{16,0},... | collective-permute-start | bytes 221192 | tf_op jit(solution)/shard_map/ppermute | solution.py:314
  43.0 0.3 collective-permute-start.8
  43.3 0.9 %update_cache.1 = bf16[128,512]{1,0:T(8,128)(2,1)} custom-call(s32[1]{0:T(128)S(6)} %copy.16.off_ref, bf16[128,512]{1,0:T(8,128)(2,1)S(1)} %bitcast.17, bf16[32,1536]{1,0:T(8,128)(2,1)S(1)} %pad_maximum_fusion.1.refs_0_, bf16[32,1536]{1,0:T(8,128)(2,1)S(1)} %collective-permute-done.refs_1_, bf16[32,1536]{1,0:T(8,128)(2,1)S(1)} %collective-permute-done.1.refs_2_, ...), custom_call_target="tpu_custom_call" | custom-call | tf_op jit(solution)/shard_map/update_cache/pallas_call | solution.py:282
  44.3 5.2 %collective-permute-done.7.refs_2_ = bf16[32,1152]{1,0:T(8,128)(2,1)S(1)} collective-permute-done((bf16[32,1152]{1,0:T(8,128)(2,1)S(1)}, bf16[32,1152]{1,0:T(8,128)(2,1)S(1)}, u32[]{:S(2)}, u32[]{:S(2)}) %collective-permute-start.7) | collective-permute-done | bytes 73760 | tf_op jit(solution)/shard_map/ppermute | solution.py:314
  49.5 0.3 join_prefill.1
  49.8 1.6 %collective-permute-start.9 = (bf16[32,1024]{1,0:T(8,128)(2,1)S(1)}, bf16[32,1024]{1,0:T(8,128)(2,1)S(1)}, u32[]{:S(2)}, u32[]{:S(2)}) collective-permute-start(bf16[32,1024]{1,0:T(8,128)(2,1)S(1)} %join_prefill.1), channel_id=1, source_target_pairs={{0,1},{1,0},{2,3},{3,2},{4,5},{5,4},{6,7},{7,6},{8,9},{9,8},{10,11... | collective-permute-start | bytes 196616 | tf_op jit(solution)/shard_map/ppermute | solution.py:339
  51.4 0.9 %fusion = bf16[16,1024]{1,0:T(8,128)(2,1)} fusion(bf16[1024,2,16]{0,2,1:T(8,128)(2,1)S(1)} %bitcast.18, s32[2,16]{1,0:T(2,128)S(1)} %eq.24, s32[16]{0:T(128)S(1)} %iota_add_fusion), kind=kOutput, calls=%fused_computation.1 | convolution fusion | flops 1065472 | bytes 98496 | tf_op jit(solution)/shard_map/ors,rgsf->ogf/dot_general | solution.py:349
  52.3 1.9 %collective-permute-done.9 = bf16[32,1024]{1,0:T(8,128)(2,1)S(1)} collective-permute-done((bf16[32,1024]{1,0:T(8,128)(2,1)S(1)}, bf16[32,1024]{1,0:T(8,128)(2,1)S(1)}, u32[]{:S(2)}, u32[]{:S(2)}) %collective-permute-start.9) | collective-permute-done | bytes 65568 | tf_op jit(solution)/shard_map/ppermute | solution.py:339
  54.2 0.6 %select_bitcast_fusion = bf16[1,32,1024]{2,1,0:T(8,128)(2,1)} fusion(bf16[32,1024]{1,0:T(8,128)(2,1)S(1)} %join_prefill.1, bf16[32,1024]{1,0:T(8,128)(2,1)S(1)} %collective-permute-done.9, pred[]{:T(512)S(6)} %eq.23), kind=kLoop, calls=%fused_computation.5 | loop fusion | flops 32768 | bytes 196609 | tf_op jit(solution)/shard_map/broadcast_in_dim | solution.py:340
  (30 shorter events, 0.3 us)
Async XLA Ops:
  0.6 26.3 %copy-start.4 = (s32[34]{0:T(128)S(1)}, s32[34]{0:T(128)}, u32[]{:S(2)}) copy-start(s32[34]{0:T(128)} %param.17) | copy-start | bytes 412
  1.5 22.5 %collective-permute-start = (bf16[32,1536]{1,0:T(8,128)(2,1)S(1)}, bf16[32,1536]{1,0:T(8,128)(2,1)S(1)}, u32[]{:S(2)}, u32[]{:S(2)}) collective-permute-start(bf16[32,1536]{1,0:T(8,128)(2,1)S(1)} %pad_maximum_fusion.1.refs_0_), channel_id=1, source_target_pairs={{0,8},{2,10},{4,12},{6,14},{8,0},{10,2},{12,4},{14,6},{16,24},{18,... | collective-permute-start | bytes 294920 | tf_op jit(solution)/shard_map/ppermute | solution.py:314
  4.5 21.3 %collective-permute-start.1 = (bf16[32,1536]{1,0:T(8,128)(2,1)S(1)}, bf16[32,1536]{1,0:T(8,128)(2,1)S(1)}, u32[]{:S(2)}, u32[]{:S(2)}) collective-permute-start(bf16[32,1536]{1,0:T(8,128)(2,1)S(1)} %pad_maximum_fusion.1.refs_0_), channel_id=1, source_target_pairs={{0,16},{2,18},{4,20},{6,22},{8,24},{10,26},{12,28},{14,30},{16,0},... | collective-permute-start | bytes 294920 | tf_op jit(solution)/shard_map/ppermute | solution.py:314
  7.1 18.7 %collective-permute-start.2 = (bf16[32,1536]{1,0:T(8,128)(2,1)S(1)}, bf16[32,1536]{1,0:T(8,128)(2,1)S(1)}, u32[]{:S(2)}, u32[]{:S(2)}) collective-permute-start(bf16[32,1536]{1,0:T(8,128)(2,1)S(1)} %pad_maximum_fusion.1.refs_0_), channel_id=1, source_target_pairs={{0,24},{2,26},{4,28},{6,30},{8,16},{10,18},{12,20},{14,22},{16,8},... | collective-permute-start | bytes 294920 | tf_op jit(solution)/shard_map/ppermute | solution.py:314
  8.1 28.0 %collective-permute-start.3 = (bf16[160,512]{1,0:T(8,128)(2,1)S(1)}, bf16[160,512]{1,0:T(8,128)(2,1)S(1)}, u32[]{:S(2)}, u32[]{:S(2)}) collective-permute-start(bf16[160,512]{1,0:T(8,128)(2,1)S(1)} %pad_maximum_fusion.refs_4_), channel_id=1, source_target_pairs={{0,2},{2,0},{4,6},{6,4},{8,10},{10,8},{12,14},{14,12},{16,18},{18,... | collective-permute-start | bytes 491528 | tf_op jit(solution)/shard_map/ppermute | solution.py:311
  8.2 27.9 %collective-permute-start.4 = (bf16[160,512]{1,0:T(8,128)(2,1)S(1)}, bf16[160,512]{1,0:T(8,128)(2,1)S(1)}, u32[]{:S(2)}, u32[]{:S(2)}) collective-permute-start(bf16[160,512]{1,0:T(8,128)(2,1)S(1)} %pad_maximum_fusion.refs_4_), channel_id=1, source_target_pairs={{0,4},{2,6},{4,0},{6,2},{8,12},{10,14},{12,8},{14,10},{16,20},{18,... | collective-permute-start | bytes 491528 | tf_op jit(solution)/shard_map/ppermute | solution.py:311
  10.7 1.6 %copy-start = (bf16[16,128,512]{2,1,0:T(8,128)(2,1)S(1)}, bf16[16,128,512]{2,1,0:T(8,128)(2,1)}, u32[]{:S(2)}) copy-start(bf16[16,128,512]{2,1,0:T(8,128)(2,1)} %cache_ref.1) | copy-start | bytes 6291460
  12.3 0.8 %copy-start.2 = (bf16[16,1024]{1,0:T(8,128)(2,1)S(1)}, bf16[16,1024]{1,0:T(8,128)(2,1)}, u32[]{:S(2)}) copy-start(bf16[16,1024]{1,0:T(8,128)(2,1)} %q_ref.1) | copy-start | bytes 98308
  13.0 0.7 %copy-start.3 = (s32[16]{0:T(128)S(1)}, s32[16]{0:T(128)}, u32[]{:S(2)}) copy-start(s32[16]{0:T(128)} %len_ref.1) | copy-start | bytes 196
  13.7 29.6 %copy-start.1 = (bf16[1,128,512]{2,1,0:T(8,128)(2,1)S(1)}, bf16[1,128,512]{2,1,0:T(8,128)(2,1)}, u32[]{:S(2)}) copy-start(bf16[1,128,512]{2,1,0:T(8,128)(2,1)} %param.13) | copy-start | bytes 393220
  19.1 11.7 %all-to-all-start = ((bf16[16,2,640]{2,1,0:T(2,128)(2,1)}), bf16[16,2,640]{2,1,0:T(2,128)(2,1)S(1)}, u32[]{:S(2)}, u32[]{:S(2)}) async-start(bf16[16,2,640]{2,1,0:T(2,128)(2,1)} %reshape.36), calls=%async_computation | async-start | bytes 81920 | tf_op jit(solution)/shard_map/all_to_all | solution.py:324
  24.1 12.0 %collective-permute-start.5 = (bf16[160,512]{1,0:T(8,128)(2,1)S(1)}, bf16[160,512]{1,0:T(8,128)(2,1)S(1)}, u32[]{:S(2)}, u32[]{:S(2)}) collective-permute-start(bf16[160,512]{1,0:T(8,128)(2,1)S(1)} %pad_maximum_fusion.refs_4_), channel_id=1, source_target_pairs={{0,6},{2,4},{4,2},{6,0},{8,14},{10,12},{12,10},{14,8},{16,22},{18,... | collective-permute-start | bytes 491528 | tf_op jit(solution)/shard_map/ppermute | solution.py:311
  25.8 17.1 %collective-permute-start.10 = (bf16[96,512]{1,0:T(8,128)(2,1)S(1)}, bf16[96,512]{1,0:T(8,128)(2,1)S(1)}, u32[]{:S(2)}, u32[]{:S(2)}) collective-permute-start(bf16[96,512]{1,0:T(8,128)(2,1)S(1)} %pad_maximum_fusion.2), channel_id=1, source_target_pairs={{0,2},{2,0},{4,6},{6,4},{8,10},{10,8},{12,14},{14,12},{16,18},{18,... | collective-permute-start | bytes 294920 | tf_op jit(solution)/shard_map/ppermute | solution.py:311
  31.8 12.4 %all-to-all-start.1 = ((bf16[32,2,512]{2,1,0:T(2,128)(2,1)}), bf16[32,2,512]{2,1,0:T(2,128)(2,1)S(1)}, u32[]{:S(2)}, u32[]{:S(2)}) async-start(bf16[32,2,512]{2,1,0:T(2,128)(2,1)} %broadcast_in_dim.19), calls=%async_computation.1 | async-start | bytes 131072 | tf_op jit(solution)/shard_map/all_to_all | solution.py:331
  34.4 8.9 %collective-permute-start.11 = (bf16[96,512]{1,0:T(8,128)(2,1)S(1)}, bf16[96,512]{1,0:T(8,128)(2,1)S(1)}, u32[]{:S(2)}, u32[]{:S(2)}) collective-permute-start(bf16[96,512]{1,0:T(8,128)(2,1)S(1)} %pad_maximum_fusion.2), channel_id=1, source_target_pairs={{0,4},{2,6},{4,0},{6,2},{8,12},{10,14},{12,8},{14,10},{16,20},{18,... | collective-permute-start | bytes 294920 | tf_op jit(solution)/shard_map/ppermute | solution.py:311
  36.1 7.2 %collective-permute-start.12 = (bf16[96,512]{1,0:T(8,128)(2,1)S(1)}, bf16[96,512]{1,0:T(8,128)(2,1)S(1)}, u32[]{:S(2)}, u32[]{:S(2)}) collective-permute-start(bf16[96,512]{1,0:T(8,128)(2,1)S(1)} %pad_maximum_fusion.2), channel_id=1, source_target_pairs={{0,6},{2,4},{4,2},{6,0},{8,14},{10,12},{12,10},{14,8},{16,22},{18,... | collective-permute-start | bytes 294920 | tf_op jit(solution)/shard_map/ppermute | solution.py:311
  38.8 5.4 %collective-permute-start.6 = (bf16[32,1152]{1,0:T(8,128)(2,1)S(1)}, bf16[32,1152]{1,0:T(8,128)(2,1)S(1)}, u32[]{:S(2)}, u32[]{:S(2)}) collective-permute-start(bf16[32,1152]{1,0:T(8,128)(2,1)S(1)} %get-tuple-element.11), channel_id=1, source_target_pairs={{0,8},{2,10},{4,12},{6,14},{8,0},{10,2},{12,4},{14,6},{16,24},{18,... | collective-permute-start | bytes 221192 | tf_op jit(solution)/shard_map/ppermute | solution.py:314
  40.5 9.0 %collective-permute-start.7 = (bf16[32,1152]{1,0:T(8,128)(2,1)S(1)}, bf16[32,1152]{1,0:T(8,128)(2,1)S(1)}, u32[]{:S(2)}, u32[]{:S(2)}) collective-permute-start(bf16[32,1152]{1,0:T(8,128)(2,1)S(1)} %get-tuple-element.12), channel_id=1, source_target_pairs={{0,16},{2,18},{4,20},{6,22},{8,24},{10,26},{12,28},{14,30},{16,0},... | collective-permute-start | bytes 221192 | tf_op jit(solution)/shard_map/ppermute | solution.py:314
  43.0 6.5 %collective-permute-start.8 = (bf16[32,1152]{1,0:T(8,128)(2,1)S(1)}, bf16[32,1152]{1,0:T(8,128)(2,1)S(1)}, u32[]{:S(2)}, u32[]{:S(2)}) collective-permute-start(bf16[32,1152]{1,0:T(8,128)(2,1)S(1)} %get-tuple-element.13), channel_id=1, source_target_pairs={{0,24},{2,26},{4,28},{6,30},{8,16},{10,18},{12,20},{14,22},{16,8},... | collective-permute-start | bytes 221192 | tf_op jit(solution)/shard_map/ppermute | solution.py:314
  49.8 4.3 %collective-permute-start.9 = (bf16[32,1024]{1,0:T(8,128)(2,1)S(1)}, bf16[32,1024]{1,0:T(8,128)(2,1)S(1)}, u32[]{:S(2)}, u32[]{:S(2)}) collective-permute-start(bf16[32,1024]{1,0:T(8,128)(2,1)S(1)} %join_prefill.1), channel_id=1, source_target_pairs={{0,1},{1,0},{2,3},{3,2},{4,5},{5,4},{6,7},{7,6},{8,9},{9,8},{10,11... | collective-permute-start | bytes 196616 | tf_op jit(solution)/shard_map/ppermute | solution.py:339

commit v2 on v1

v2 whole, which is shorter than its diff:
```python
import functools

import jax
import jax.numpy as jnp
from jax import lax
from jax.experimental import pallas as pl
from jax.experimental.pallas import tpu as pltpu
from jax.sharding import PartitionSpec as P

QUERY_HEADS = 8
KEY_VALUE_HEADS = 2
HEAD_SIZE = 128
GROUP = QUERY_HEADS // KEY_VALUE_HEADS
QW = QUERY_HEADS * HEAD_SIZE
KW = KEY_VALUE_HEADS * HEAD_SIZE
GW = GROUP * HEAD_SIZE
STATS = 128
QUAD = 4
SCALE = HEAD_SIZE**-0.5
MASKED = -1e30
FLOOR = -1e20
F32 = jnp.float32
BF16 = jnp.bfloat16

BLK = ("hi", "quad")
KVW = 2 * KW
CHUNKS = 4
TILE = 16

ANY = pl.BlockSpec(memory_space=pl.ANY)
HBM = pl.BlockSpec(memory_space=pltpu.HBM)
VMEM = pl.BlockSpec(memory_space=pltpu.VMEM)
SMEM = pl.BlockSpec(memory_space=pltpu.SMEM)


def dot_t(a, b):
    return lax.dot_general(a, b, (((1,), (1,)), ((), ())), preferred_element_type=F32)


def dot(a, b):
    return lax.dot_general(a, b, (((1,), (0,)), ((), ())), preferred_element_type=F32)


def split3(value):
    high = value.astype(BF16).astype(F32)
    rest = value - high
    middle = rest.astype(BF16).astype(F32)
    return high, middle, rest - middle


def stats_block(columns, rows):
    lane = lax.broadcasted_iota(jnp.int32, (rows, STATS), 1)
    count = len(columns)
    out = jnp.zeros((rows, STATS), F32)
    for head, column in enumerate(columns):
        for term, part in enumerate(split3(column)):
            out = jnp.where(lane == term * count + head, part, out)
    return out.astype(BF16)


def spread_matrix(heads):
    lane = lax.broadcasted_iota(jnp.int32, (STATS, heads * HEAD_SIZE), 0)
    head = lax.broadcasted_iota(jnp.int32, (STATS, heads * HEAD_SIZE), 1) // HEAD_SIZE
    hit = (lane == head) | (lane == head + heads) | (lane == head + 2 * heads)
    return jnp.where(hit, 1.0, 0.0).astype(BF16)


def join(parts, heads):
    width = heads * HEAD_SIZE
    spread = spread_matrix(heads)
    logs = [dot(part[:, width:], spread) for part in parts]
    top = functools.reduce(jnp.maximum, logs)
    scales = [jnp.exp(log - top) for log in logs]
    total = functools.reduce(jnp.add, scales)
    summed = functools.reduce(
        jnp.add, [scale * part[:, :width].astype(F32) for scale, part in zip(scales, parts)]
    )
    return (summed / total).astype(BF16)


def decode_kernel(
    len_hbm, q_hbm, new_hbm, cache_hbm, out_hbm, part_ref, lens, query_ref, new_ref, table, sems
):
    slots, ctx, _ = table.shape
    rows = GROUP * slots
    chunk = slots // CHUNKS
    base = lax.axis_index(BLK) * ctx
    small = [
        pltpu.make_async_copy(len_hbm, lens, sems.at[0]),
        pltpu.make_async_copy(q_hbm, query_ref, sems.at[1]),
        pltpu.make_async_copy(new_hbm, new_ref, sems.at[2]),
    ]
    loads, stores = [], []
    for c in range(CHUNKS):
        part = pl.ds(c * chunk, chunk)
        loads.append(pltpu.make_async_copy(cache_hbm.at[part], table.at[part], sems.at[3 + c]))
        stores.append(pltpu.make_async_copy(table.at[part], out_hbm.at[part], sems.at[3 + CHUNKS + c]))
    for copy in small + loads:
        copy.start()
    for copy in small:
        copy.wait()
    row_slot = lax.broadcasted_iota(jnp.int32, (rows, ctx), 0) % slots
    column = lax.broadcasted_iota(jnp.int32, (rows, ctx), 1)
    in_tile = lax.broadcasted_iota(jnp.int32, (TILE, KVW), 0)
    limit = jnp.full((rows, ctx), -1, jnp.int32)
    queries = [
        jnp.concatenate(
            [query_ref[:, pl.ds((g * GROUP + h) * HEAD_SIZE, HEAD_SIZE)] for h in range(GROUP)], axis=0
        )
        for g in range(KEY_VALUE_HEADS)
    ]
    scores = [jnp.zeros((rows, ctx), F32) for _ in range(KEY_VALUE_HEADS)]
    for c in range(CHUNKS):
        loads[c].wait()
        for s in range(c * chunk, (c + 1) * chunk):
            relative = lens[s] - base
            limit = jnp.where(row_slot == s, relative, limit)

            @pl.when((relative >= 0) & (relative < ctx))
            def _():
                start = pl.multiple_of(relative // TILE * TILE, TILE)
                tile = table[s, pl.ds(start, TILE), :]
                table[s, pl.ds(start, TILE), :] = jnp.where(
                    in_tile == relative - start, new_ref[s : s + 1, :], tile
                )

        stores[c].start()
        for s in range(c * chunk, (c + 1) * chunk):
            for g in range(KEY_VALUE_HEADS):
                key = table[s, :, pl.ds(g * HEAD_SIZE, HEAD_SIZE)]
                scores[g] = jnp.where(row_slot == s, dot_t(queries[g], key), scores[g])
    visible = column <= limit
    for g in range(KEY_VALUE_HEADS):
        masked = jnp.where(visible, scores[g] * SCALE, MASKED)
        maxima = jnp.maximum(jnp.max(masked, axis=1, keepdims=True), FLOOR)
        weights = jnp.exp(masked - maxima)
        totals = jnp.sum(weights, axis=1, keepdims=True)
        summed = jnp.zeros((rows, HEAD_SIZE), F32)
        for s in range(slots):
            value = table[s, :, pl.ds(KW + g * HEAD_SIZE, HEAD_SIZE)]
            picked = jnp.where(row_slot == s, weights, 0.0).astype(BF16)
            summed += dot(picked, value)
        seen = totals > 0.0
        safe = jnp.where(seen, totals, 1.0)
        normed = (summed / safe).astype(BF16)
        logs = jnp.where(seen, maxima + jnp.log(safe), MASKED)
        columns = []
        for h in range(GROUP):
            part = slice(h * slots, (h + 1) * slots)
            part_ref[g, :, pl.ds(h * HEAD_SIZE, HEAD_SIZE)] = normed[part]
            columns.append(logs[part])
        part_ref[g, :, pl.ds(GW, STATS)] = stats_block(columns, slots)
    for copy in stores:
        copy.wait()


def decode_partials(lengths, queries, new_rows, cache):
    slots, ctx, width = cache.shape
    return pl.pallas_call(
        decode_kernel,
        in_specs=[HBM] * 4,
        out_specs=[HBM, VMEM],
        out_shape=[
            jax.ShapeDtypeStruct(cache.shape, BF16),
            jax.ShapeDtypeStruct((KEY_VALUE_HEADS, slots, GW + STATS), BF16),
        ],
        scratch_shapes=[
            pltpu.SMEM(lengths.shape, jnp.int32),
            pltpu.VMEM(queries.shape, BF16),
            pltpu.VMEM(new_rows.shape, BF16),
            pltpu.VMEM(cache.shape, BF16),
            pltpu.SemaphoreType.DMA((3 + 2 * CHUNKS,)),
        ],
        compiler_params=pltpu.CompilerParams(vmem_limit_bytes=16 << 20),
        cost_estimate=pl.CostEstimate(
            flops=4 * slots * ctx * QW, bytes_accessed=2 * cache.size * 2, transcendentals=slots * ctx * 8
        ),
        name="decode_partials",
    )(lengths, queries, new_rows, cache)


def prepare_kernel(q_hbm, new_hbm, cache_hbm, pack_ref, table_ref, sems):
    ctx, tokens = cache_hbm.shape[1], new_hbm.shape[1]
    copies = []
    for k in range(pack_ref.shape[0]):
        copies.append((q_hbm.at[0], pack_ref.at[k, :, pl.ds(0, QW)]))
        copies.append((new_hbm.at[0], pack_ref.at[k, :, pl.ds(QW, KVW)]))
    for k in range(QUAD):
        copies.append((cache_hbm.at[0], table_ref.at[k, pl.ds(0, ctx), :]))
        copies.append((new_hbm.at[0], table_ref.at[k, pl.ds(ctx, tokens), :]))
    copies = [pltpu.make_async_copy(a, b, sems.at[i]) for i, (a, b) in enumerate(copies)]
    for copy in copies:
        copy.start()
    for copy in copies:
        copy.wait()


def prepare(queries, new_rows, cache, hi_count):
    tokens, ctx = queries.shape[1], cache.shape[1]
    return pl.pallas_call(
        prepare_kernel,
        in_specs=[HBM] * 3,
        out_specs=[ANY] * 2,
        out_shape=[
            jax.ShapeDtypeStruct((hi_count, tokens, QW + KVW), BF16),
            jax.ShapeDtypeStruct((QUAD, ctx + tokens, KVW), BF16),
        ],
        scratch_shapes=[pltpu.SemaphoreType.DMA((2 * hi_count + 2 * QUAD,))],
        name="prepare",
    )(queries, new_rows, cache)


def prefill_kernel(ctx, off_ref, packs, tables, outs, news):
    hi_count, tokens, _ = packs.shape
    span = tables.shape[1]
    quad = lax.axis_index("quad")
    offset = off_ref[0]
    hi = lax.axis_index("hi")
    pieces = []
    for k in range(QUAD):
        holder = hi * QUAD + k
        index = lax.broadcasted_iota(jnp.int32, (1, span), 1)
        old = jnp.where(holder * ctx + index < offset, -1, 1 << 30)
        pieces.append(jnp.where(index < ctx, old, holder * tokens + index - ctx))
    key_mark = jnp.concatenate(pieces, axis=1)
    in_block = lax.broadcasted_iota(jnp.int32, (GROUP * tokens, 1), 0) % tokens
    for k in range(hi_count):
        for j in range(QUAD):
            news[j, pl.ds(k * tokens, tokens), :] = packs[k, :, pl.ds(QW, KVW)]
    for g in range(KEY_VALUE_HEADS):
        keys = jnp.concatenate([tables[k, :, pl.ds(g * HEAD_SIZE, HEAD_SIZE)] for k in range(QUAD)], axis=0)
        values = jnp.concatenate(
            [tables[k, :, pl.ds(KW + g * HEAD_SIZE, HEAD_SIZE)] for k in range(QUAD)], axis=0
        )
        for k in range(hi_count):
            token = (k * QUAD + quad) * tokens + in_block
            query = jnp.concatenate(
                [packs[k, :, pl.ds((g * GROUP + h) * HEAD_SIZE, HEAD_SIZE)] for h in range(GROUP)], axis=0
            )
            scores = jnp.where(key_mark <= token, dot_t(query, keys) * SCALE, MASKED)
            maxima = jnp.maximum(jnp.max(scores, axis=1, keepdims=True), FLOOR)
            weights = jnp.exp(scores - maxima)
            totals = jnp.sum(weights, axis=1, keepdims=True)
            summed = dot(weights.astype(BF16), values)
            seen = totals > 0.0
            safe = jnp.where(seen, totals, 1.0)
            normed = (summed / safe).astype(BF16)
            logs = jnp.where(seen, maxima + jnp.log(safe), MASKED)
            for h in range(GROUP):
                part = slice(h * tokens, (h + 1) * tokens)
                outs[k, :, pl.ds((g * GROUP + h) * HEAD_SIZE, HEAD_SIZE)] = normed[part]
            lane = lax.broadcasted_iota(jnp.int32, (tokens, STATS), 1)
            block = jnp.zeros((tokens, STATS), F32) if g == 0 else outs[k, :, pl.ds(QW, STATS)].astype(F32)
            for h in range(GROUP):
                for term, value in enumerate(split3(logs[h * tokens : (h + 1) * tokens])):
                    block = jnp.where(lane == term * QUERY_HEADS + g * GROUP + h, value, block)
            outs[k, :, pl.ds(QW, STATS)] = block.astype(BF16)


def prefill_partials(offset, packs, tables, ctx):
    hi_count, tokens, _ = packs.shape
    span = tables.shape[1]
    pairs = hi_count * tokens * QUAD * span
    return pl.pallas_call(
        functools.partial(prefill_kernel, ctx),
        in_specs=[SMEM, VMEM, VMEM],
        out_specs=[VMEM, VMEM],
        out_shape=[
            jax.ShapeDtypeStruct((hi_count, tokens, QW + STATS), BF16),
            jax.ShapeDtypeStruct((QUAD, hi_count * tokens, KVW), BF16),
        ],
        compiler_params=pltpu.CompilerParams(vmem_limit_bytes=32 << 20),
        cost_estimate=pl.CostEstimate(
            flops=4 * pairs * QW, bytes_accessed=4 << 20, transcendentals=pairs * QUERY_HEADS
        ),
        name="prefill_partials",
    )(offset, packs, tables)


def join_kernel(heads, part_ref, out_ref):
    out_ref[...] = join([part_ref[i] for i in range(part_ref.shape[0])], heads)


def join_parts(parts, heads, name):
    return pl.pallas_call(
        functools.partial(join_kernel, heads),
        in_specs=[VMEM],
        out_specs=VMEM,
        out_shape=jax.ShapeDtypeStruct((parts.shape[1], heads * HEAD_SIZE), BF16),
        compiler_params=pltpu.CompilerParams(vmem_limit_bytes=16 << 20),
        name=name,
    )(parts)


def update_kernel(tokens, off_ref, cache_ref, news, out_ref):
    ctx = cache_ref.shape[0]
    rows = jnp.concatenate([news[j] for j in range(QUAD)], axis=0)
    count = rows.shape[0]
    index = lax.broadcasted_iota(jnp.int32, (1, count), 1)
    block = index // tokens
    hi_count = count // (QUAD * tokens)
    token = ((block % hi_count) * QUAD + block // hi_count) * tokens + index % tokens
    wanted = lax.axis_index(BLK) * ctx + lax.broadcasted_iota(jnp.int32, (ctx, 1), 0) - off_ref[0]
    picked = dot(jnp.where(wanted == token, 1.0, 0.0).astype(BF16), rows).astype(BF16)
    inside = jnp.broadcast_to((wanted >= 0) & (wanted < count), out_ref.shape)
    out_ref[...] = jnp.where(inside, picked, cache_ref[...])


def update_cache(offset, cache, news, tokens):
    return pl.pallas_call(
        functools.partial(update_kernel, tokens),
        in_specs=[SMEM, VMEM, VMEM],
        out_specs=VMEM,
        out_shape=jax.ShapeDtypeStruct(cache.shape, BF16),
        compiler_params=pltpu.CompilerParams(vmem_limit_bytes=16 << 20),
        name="update_cache",
    )(offset, cache, news)


def exchange(array, axis):
    return lax.all_to_all(array, axis, split_axis=0, concat_axis=0, tiled=True)


def per_device(
    prefill_queries,
    decode_queries,
    new_prefill,
    new_decode,
    prefill_cache,
    decode_cache,
    prefill_offsets,
    decode_lengths,
    dealing,
):
    hi_count = lax.axis_size("hi")
    blk = hi_count * QUAD
    req = lax.axis_size("req")
    ctx = prefill_cache.shape[1]
    tokens = prefill_queries.shape[1]
    slots = decode_cache.shape[0]
    group = lax.axis_index("req")

    pack, table = prepare(prefill_queries, new_prefill, prefill_cache, hi_count)
    packs = exchange(pack, "hi")
    tables = exchange(table, "quad")

    decode_cache_out, decode_part = decode_partials(decode_lengths, decode_queries, new_decode, decode_cache)
    pieces = KEY_VALUE_HEADS * slots // blk
    decode_parts = exchange(decode_part.reshape(blk, pieces, GW + STATS), BLK)

    parts, news = prefill_partials(prefill_offsets, packs, tables, ctx)
    arrived = exchange(parts, "hi")

    decode_parts, news, parts = lax.optimization_barrier((decode_parts, news, parts))
    decode_piece = join_parts(decode_parts, GROUP, "join_decode")
    everywhere = jnp.broadcast_to(decode_piece[None], (req * blk, pieces, GW))
    gathered = exchange(everywhere, ("req",) + BLK)

    prefill_cache_out = update_cache(prefill_offsets, prefill_cache[0], exchange(news, "quad"), tokens)[None]

    attended = join_parts(arrived, QUERY_HEADS, "join_prefill")
    if req == 2:
        other = lax.ppermute(attended, "req", [(0, 1), (1, 0)])
        prefill_out = jnp.where(dealing[group] == group, attended, other)[None]
    else:
        spread = lax.all_gather(attended, "req", axis=0)
        source = jnp.argmax(dealing[:req] == group)
        prefill_out = lax.dynamic_index_in_dim(spread, source, 0, True)

    gathered = gathered.reshape(req, KEY_VALUE_HEADS, slots, GW)
    own = group * slots + jnp.arange(slots, dtype=jnp.int32)
    chosen = (dealing[req:][None, :] == own[:, None]).astype(BF16)
    decode_out = jnp.einsum(
        "ors,rgsf->ogf", chosen.reshape(slots, req, slots), gathered, preferred_element_type=F32
    )
    decode_out = decode_out.reshape(slots, QW).astype(BF16)
    return (prefill_out, decode_out, prefill_cache_out, decode_cache_out)


def solution(mesh):
    blk, req = mesh.shape["blk"], mesh.shape["req"]
    mesh = jax.sharding.Mesh(mesh.devices.reshape(blk // QUAD, QUAD, req), ("hi", "quad", "req"))
    in_specs = (
        P("req", BLK, None),
        P("req", None),
        P("req", BLK, None),
        P("req", None),
        P("req", BLK, None),
        P("req", BLK, None),
        P("req"),
        P("req"),
        P(),
    )
    out_specs = (
        P("req", BLK, None),
        P("req", None),
        P("req", BLK, None),
        P("req", BLK, None),
    )
    return jax.shard_map(
        per_device, mesh=mesh, in_specs=in_specs, out_specs=out_specs, check_vma=False
    )
```

time: 55.3 us -> 113 us (2.04)
  blocking collectives: 0 us -> 37.6 us
  Pallas kernels: 9.07 us -> 40.5 us
  starting transfers between devices: 24.9 us -> 13.1 us
  waiting for transfers between devices: 9.56 us -> 16.3 us
  local copies, waits for them, and re-layouts: 5.84 us -> 1.48 us
  other arithmetic: 2.46 us -> 0.64 us
    all_to_all x0 -> x3, blocking collectives: none -> 37.6 us  [exchange(): return lax.all_to_all(array, axis, split_axis=0, concat_axis=0, tiled=True)]
    pallas_call x5 -> x6, Pallas kernels: 9.07 us -> 40.5 us  [the longest x1 33 us: prepare(): pl.pallas_call(prepare_kernel, in_specs=[HBM] * 3, out_specs=[ANY] * 2, o...]
    ppermute x12 -> x0, starting transfers between devices: 15.8 us -> none  [the longest x6 10.1 us: over_hi(): return lax.ppermute(array, 'blk', [(i, i ^ k * QUAD) for i in range(blk)])]
    all_to_all x2 -> x3, waiting for transfers between devices: 2.42 us -> 16.3 us  [exchange(): return lax.all_to_all(array, axis, split_axis=0, concat_axis=0, tiled=True)]
    ppermute x12 -> x0, waiting for transfers between devices: 5.24 us -> none  [the longest x6 5.23 us: over_hi(): return lax.ppermute(array, 'blk', [(i, i ^ k * QUAD) for i in range(blk)])]
    all_to_all x2 -> x3, starting transfers between devices: 7.55 us -> 12.5 us  [exchange(): return lax.all_to_all(array, axis, split_axis=0, concat_axis=0, tiled=True)]
    unnamed x10 -> x12, local copies, waits for them, and re-layouts: 3.01 us -> 0.03 us
    ppermute x1, waiting for transfers between devices: 1.9 us -> 0.01 us  [per_device(): other = lax.ppermute(attended, 'req', [(0, 1), (1, 0)])]
  transfers between devices with their start and end apart: 15 -> 4, of which waited for: 3 -> 3; matrix products, arithmetic and copies ran while one was open for 8% -> 2% of each run, Pallas kernels for 16% -> 6%
where the time goes in v2:
time: 113 us
  Pallas kernels  40.5 us (36%)
  blocking collectives  37.6 us (33%)
  waiting for transfers between devices  16.3 us (14%)
  starting transfers between devices  13.1 us (12%)
  between operations  2.08 us (2%)
  local copies, waits for them, and re-layouts  1.48 us (1%)
    all_to_all x3, blocking collectives, exchange(): return lax.all_to_all(array, axis, split_axis=0, concat_axis=0, tiled=True)  37.6 us
    pallas_call x1, Pallas kernels, prepare(): pl.pallas_call(prepare_kernel, in_specs=[HBM] * 3, out_specs=[ANY] * 2, o...  33 us
    all_to_all x3, waiting for transfers between devices, exchange(): return lax.all_to_all(array, axis, split_axis=0, concat_axis=0, tiled=True)  16.3 us
    all_to_all x3, starting transfers between devices, exchange(): return lax.all_to_all(array, axis, split_axis=0, concat_axis=0, tiled=True)  12.5 us
    pallas_call x1, Pallas kernels, prefill_partials(): pl.pallas_call(functools.partial(prefill_kernel, ctx), in_specs=[SMEM, VM...  3.5 us
    pallas_call x1, Pallas kernels, decode_partials(): pl.pallas_call(decode_kernel, in_specs=[HBM] * 4, out_specs=[HBM, VMEM],...  2.41 us
  transfers between devices with their start and end apart: 4, of which 3 were waited for; matrix products, arithmetic and copies ran while one was open for 2% of the time, Pallas kernels for 6%

profile of v2, /device:TPU:0, one launch (start us, length us, event | category | flops | bytes accessed | tf_op | source)
XLA Modules:
  0.0 112.6 jit_solution(11476835356981039455)
XLA Ops:
  0.6 0.0 copy-start.4
  0.6 0.0 copy-start
  0.7 0.0 copy-start.3
  0.7 0.0 copy-start.2
  0.7 33.0 %prepare.1 = (bf16[4,32,1536]{2,1,0:T(8,128)(2,1)}, bf16[4,160,512]{2,1,0:T(8,128)(2,1)}) custom-call(bf16[1,32,1024]{2,1,0:T(8,128)(2,1)} %q_hbm.2, bf16[1,32,512]{2,1,0:T(8,128)(2,1)} %new_hbm.2, bf16[1,128,512]{2,1,0:T(8,128)(2,1)} %cache_hbm.2), custom_call_target="tpu_custom_call" | custom-call | tf_op jit(solution)/shard_map/prepare/pallas_call | solution.py:200
  33.7 14.5 %all_to_all.30.tables = bf16[4,160,512]{2,1,0:T(8,128)(2,1)S(1)} all-to-all(bf16[4,160,512]{2,1,0:T(8,128)(2,1)} %get-tuple-element.13), channel_id=1, replica_groups=mesh['hi'=4,'quad'=4,'req'=2] {'quad'}, dimensions={0} | all-to-all | bytes 1310720 | tf_op jit(solution)/shard_map/all_to_all | solution.py:321
  48.2 5.6 %all-to-all-start = ((bf16[4,32,1536]{2,1,0:T(8,128)(2,1)}), bf16[4,32,1536]{2,1,0:T(8,128)(2,1)S(1)}, u32[]{:S(2)}, u32[]{:S(2)}) async-start(bf16[4,32,1536]{2,1,0:T(8,128)(2,1)} %get-tuple-element.12), calls=%async_computation | async-start | bytes 786432 | tf_op jit(solution)/shard_map/all_to_all | solution.py:321
  53.7 0.0 copy-done.4
  53.7 0.0 copy-done
  53.7 0.0 copy-done.3
  53.7 2.4 %decode_partials.1 = (bf16[16,128,512]{2,1,0:T(8,128)(2,1)}, bf16[2,16,640]{2,1,0:T(8,128)(2,1)S(1)}) custom-call(s32[16]{0:T(128)S(1)} %copy-done.4, bf16[16,1024]{1,0:T(8,128)(2,1)S(1)} %copy-done.2, bf16[16,512]{1,0:T(8,128)(2,1)S(1)} %copy-done.3, bf16[16,128,512]{2,1,0:T(8,128)(2,1)S(1)} %copy-done), custom_call_target="tpu_custom_call" | custom-call | flops 8388608 | bytes 4194304 | tf_op jit(solution)/shard_map/decode_partials/pallas_call | solution.py:159
  56.2 0.0 copy-start.5
  56.2 0.0 copy-start.1
  56.2 0.6 reshape.36
  56.8 8.2 %all-to-all-done.packs = bf16[4,32,1536]{2,1,0:T(8,128)(2,1)S(1)} async-done(((bf16[4,32,1536]{2,1,0:T(8,128)(2,1)}), bf16[4,32,1536]{2,1,0:T(8,128)(2,1)S(1)}, u32[]{:S(2)}, u32[]{:S(2)}) %all-to-all-start) | async-done | bytes 393248 | tf_op jit(solution)/shard_map/all_to_all | solution.py:321
  65.0 3.5 %all-to-all-start.3 = ((bf16[16,2,640]{2,1,0:T(2,128)(2,1)}), bf16[16,2,640]{2,1,0:T(2,128)(2,1)S(1)}, u32[]{:S(2)}, u32[]{:S(2)}) async-start(bf16[16,2,640]{2,1,0:T(2,128)(2,1)} %reshape.36), calls=%async_computation.3 | async-start | bytes 81920 | tf_op jit(solution)/shard_map/all_to_all | solution.py:321
  69.2 3.5 %prefill_partials.1 = (bf16[4,32,1152]{2,1,0:T(8,128)(2,1)S(1)}, bf16[4,128,512]{2,1,0:T(8,128)(2,1)}) custom-call(s32[1]{0:T(128)S(6)} %copy.15.off_ref, bf16[4,32,1536]{2,1,0:T(8,128)(2,1)S(1)} %all-to-all-done.packs, bf16[4,160,512]{2,1,0:T(8,128)(2,1)S(1)} %all_to_all.30.tables), custom_call_target="tpu_custom_call" | custom-call | flops 335544320 | bytes 4194304 | tf_op jit(solution)/shard_map/prefill_partials/pallas_call | solution.py:264
  72.7 2.5 %all-to-all-done.3.part_ref = bf16[16,2,640]{2,1,0:T(2,128)(2,1)S(1)} async-done(((bf16[16,2,640]{2,1,0:T(2,128)(2,1)}), bf16[16,2,640]{2,1,0:T(2,128)(2,1)S(1)}, u32[]{:S(2)}, u32[]{:S(2)}) %all-to-all-start.3) | async-done | bytes 40992 | tf_op jit(solution)/shard_map/all_to_all | solution.py:321
  75.2 0.4 join_decode.1
  75.6 10.6 %all_to_all.31 = bf16[32,2,512]{2,1,0:T(2,128)(2,1)S(1)} all-to-all(bf16[32,2,512]{2,1,0:T(2,128)(2,1)S(1)} %broadcast_in_dim.7), channel_id=1, replica_groups=mesh['hi'=4,'quad'=4,'req'=2] {'req','hi','quad'}, dimensions={0} | all-to-all | bytes 131072 | tf_op jit(solution)/shard_map/all_to_all | solution.py:321
  86.2 12.5 %all_to_all.32.part_ref = bf16[4,32,1152]{2,1,0:T(8,128)(2,1)S(1)} all-to-all(bf16[4,32,1152]{2,1,0:T(8,128)(2,1)S(1)} %get-tuple-element.14), channel_id=1, replica_groups=mesh['hi'=4,'quad'=4,'req'=2] {'hi'}, dimensions={0} | all-to-all | bytes 589824 | tf_op jit(solution)/shard_map/all_to_all | solution.py:321
  98.7 3.5 %all-to-all-start.5 = ((bf16[4,128,512]{2,1,0:T(8,128)(2,1)}), bf16[4,128,512]{2,1,0:T(8,128)(2,1)S(1)}, u32[]{:S(2)}, u32[]{:S(2)}) async-start(bf16[4,128,512]{2,1,0:T(8,128)(2,1)} %get-tuple-element.18), calls=%async_computation.5 | async-start | bytes 1048576 | tf_op jit(solution)/shard_map/all_to_all | solution.py:321
  102.2 0.1 slice.3
  102.3 0.6 dynamic_slice.3
  103.5 0.1 eq.24
  103.7 0.3 join_prefill.1
  104.0 0.6 collective-permute-start
  104.6 0.9 fusion
  105.5 5.5 %all-to-all-done.5.news = bf16[4,128,512]{2,1,0:T(8,128)(2,1)S(1)} async-done(((bf16[4,128,512]{2,1,0:T(8,128)(2,1)}), bf16[4,128,512]{2,1,0:T(8,128)(2,1)S(1)}, u32[]{:S(2)}, u32[]{:S(2)}) %all-to-all-start.5) | async-done | bytes 524320 | tf_op jit(solution)/shard_map/all_to_all | solution.py:321
  111.0 0.9 update_cache.1
  111.9 0.0 collective-permute-done
  111.9 0.6 select_bitcast_fusion
  (7 shorter events, 0.1 us)
Async XLA Ops:
  0.6 53.1 %copy-start.4 = (s32[16]{0:T(128)S(1)}, s32[16]{0:T(128)}, u32[]{:S(2)}) copy-start(s32[16]{0:T(128)} %len_hbm.1) | copy-start | bytes 196
  0.6 53.1 %copy-start = (bf16[16,128,512]{2,1,0:T(8,128)(2,1)S(1)}, bf16[16,128,512]{2,1,0:T(8,128)(2,1)}, u32[]{:S(2)}) copy-start(bf16[16,128,512]{2,1,0:T(8,128)(2,1)} %cache_hbm.3) | copy-start | bytes 6291460
  0.7 53.1 %copy-start.3 = (bf16[16,512]{1,0:T(8,128)(2,1)S(1)}, bf16[16,512]{1,0:T(8,128)(2,1)}, u32[]{:S(2)}) copy-start(bf16[16,512]{1,0:T(8,128)(2,1)} %new_hbm.3) | copy-start | bytes 49156
  0.7 53.1 %copy-start.2 = (bf16[16,1024]{1,0:T(8,128)(2,1)S(1)}, bf16[16,1024]{1,0:T(8,128)(2,1)}, u32[]{:S(2)}) copy-start(bf16[16,1024]{1,0:T(8,128)(2,1)} %q_hbm.3) | copy-start | bytes 98308
  48.2 16.9 %all-to-all-start = ((bf16[4,32,1536]{2,1,0:T(8,128)(2,1)}), bf16[4,32,1536]{2,1,0:T(8,128)(2,1)S(1)}, u32[]{:S(2)}, u32[]{:S(2)}) async-start(bf16[4,32,1536]{2,1,0:T(8,128)(2,1)} %get-tuple-element.12), calls=%async_computation | async-start | bytes 786432 | tf_op jit(solution)/shard_map/all_to_all | solution.py:321
  56.2 46.0 %copy-start.5 = (s32[34]{0:T(128)S(1)}, s32[34]{0:T(128)}, u32[]{:S(2)}) copy-start(s32[34]{0:T(128)} %param.17) | copy-start | bytes 412
  56.2 54.8 %copy-start.1 = (bf16[1,128,512]{2,1,0:T(8,128)(2,1)S(1)}, bf16[1,128,512]{2,1,0:T(8,128)(2,1)}, u32[]{:S(2)}) copy-start(bf16[1,128,512]{2,1,0:T(8,128)(2,1)} %cache_hbm.2) | copy-start | bytes 393220
  65.0 10.2 %all-to-all-start.3 = ((bf16[16,2,640]{2,1,0:T(2,128)(2,1)}), bf16[16,2,640]{2,1,0:T(2,128)(2,1)S(1)}, u32[]{:S(2)}, u32[]{:S(2)}) async-start(bf16[16,2,640]{2,1,0:T(2,128)(2,1)} %reshape.36), calls=%async_computation.3 | async-start | bytes 81920 | tf_op jit(solution)/shard_map/all_to_all | solution.py:321
  98.7 12.3 %all-to-all-start.5 = ((bf16[4,128,512]{2,1,0:T(8,128)(2,1)}), bf16[4,128,512]{2,1,0:T(8,128)(2,1)S(1)}, u32[]{:S(2)}, u32[]{:S(2)}) async-start(bf16[4,128,512]{2,1,0:T(8,128)(2,1)} %get-tuple-element.18), calls=%async_computation.5 | async-start | bytes 1048576 | tf_op jit(solution)/shard_map/all_to_all | solution.py:321
  104.0 7.9 %collective-permute-start = (bf16[32,1024]{1,0:T(8,128)(2,1)S(1)}, bf16[32,1024]{1,0:T(8,128)(2,1)S(1)}, u32[]{:S(2)}, u32[]{:S(2)}) collective-permute-start(bf16[32,1024]{1,0:T(8,128)(2,1)S(1)} %join_prefill.1), channel_id=1, source_target_pairs={{0,1},{1,0},{2,3},{3,2},{4,5},{5,4},{6,7},{7,6},{8,9},{9,8},{10,11... | collective-permute-start | bytes 196616 | tf_op jit(solution)/shard_map/ppermute | solution.py:363

commit v3 on v2

v3 whole, which is shorter than its diff:
```python
import functools

import jax
import jax.numpy as jnp
from jax import lax
from jax.experimental import pallas as pl
from jax.experimental.pallas import tpu as pltpu
from jax.sharding import PartitionSpec as P

QUERY_HEADS = 8
KEY_VALUE_HEADS = 2
HEAD_SIZE = 128
GROUP = QUERY_HEADS // KEY_VALUE_HEADS
QW = QUERY_HEADS * HEAD_SIZE
KW = KEY_VALUE_HEADS * HEAD_SIZE
STATS = 128
QUAD = 4
SCALE = HEAD_SIZE**-0.5
MASKED = -1e30
FLOOR = -1e20
F32 = jnp.float32
BF16 = jnp.bfloat16

KVW = 2 * KW
CHUNKS = 4
TILE = 16

HBM = pl.BlockSpec(memory_space=pltpu.HBM)
VMEM = pl.BlockSpec(memory_space=pltpu.VMEM)


def dot_t(a, b):
    return lax.dot_general(a, b, (((1,), (1,)), ((), ())), preferred_element_type=F32)


def dot(a, b):
    return lax.dot_general(a, b, (((1,), (0,)), ((), ())), preferred_element_type=F32)


def split3(value):
    high = value.astype(BF16).astype(F32)
    rest = value - high
    middle = rest.astype(BF16).astype(F32)
    return high, middle, rest - middle


def stats_block(columns, rows):
    lane = lax.broadcasted_iota(jnp.int32, (rows, STATS), 1)
    count = len(columns)
    out = jnp.zeros((rows, STATS), F32)
    for head, column in enumerate(columns):
        for term, part in enumerate(split3(column)):
            out = jnp.where(lane == term * count + head, part, out)
    return out.astype(BF16)


def spread_matrix(heads):
    lane = lax.broadcasted_iota(jnp.int32, (STATS, heads * HEAD_SIZE), 0)
    head = lax.broadcasted_iota(jnp.int32, (STATS, heads * HEAD_SIZE), 1) // HEAD_SIZE
    hit = (lane == head) | (lane == head + heads) | (lane == head + 2 * heads)
    return jnp.where(hit, 1.0, 0.0).astype(BF16)


def join(parts):
    spread = spread_matrix(QUERY_HEADS)
    logs = [dot(part[:, QW:], spread) for part in parts]
    top = functools.reduce(jnp.maximum, logs)
    scales = [jnp.exp(log - top) for log in logs]
    total = functools.reduce(jnp.add, scales)
    summed = functools.reduce(
        jnp.add, [scale * part[:, :QW].astype(F32) for scale, part in zip(scales, parts)]
    )
    return (summed / total).astype(BF16), top + jnp.log(total)


def source_group(j):
    return lax.axis_index("req") ^ j if lax.axis_size("req") == 2 else j


def decode_kernel(
    len_hbm,
    off_hbm,
    deal_hbm,
    q_hbm,
    new_hbm,
    cache_hbm,
    out_hbm,
    part_ref,
    off_ref,
    route_ref,
    lens,
    off,
    deal,
    query_ref,
    new_ref,
    table,
    sems,
):
    slots, ctx, _ = table.shape
    rows = GROUP * slots
    chunk = slots // CHUNKS
    base = lax.axis_index("blk") * ctx
    small = [(len_hbm, lens), (off_hbm, off), (deal_hbm, deal), (q_hbm, query_ref), (new_hbm, new_ref)]
    small = [pltpu.make_async_copy(a, b, sems.at[i]) for i, (a, b) in enumerate(small)]
    loads, stores = [], []
    for c in range(CHUNKS):
        part = pl.ds(c * chunk, chunk)
        loads.append(pltpu.make_async_copy(cache_hbm.at[part], table.at[part], sems.at[5 + c]))
        stores.append(pltpu.make_async_copy(table.at[part], out_hbm.at[part], sems.at[5 + CHUNKS + c]))
    for copy in small + loads:
        copy.start()
    for copy in small:
        copy.wait()
    off_ref[...] = jnp.full(off_ref.shape, off[0], jnp.int32)
    group = lax.axis_index("req")
    req = route_ref.shape[0]
    out_row = lax.broadcasted_iota(jnp.int32, (slots, HEAD_SIZE), 0)
    out_lane = lax.broadcasted_iota(jnp.int32, (slots, HEAD_SIZE), 1)
    for j in range(req):
        source = source_group(j)
        chosen = jnp.zeros((slots, HEAD_SIZE), F32)
        for s in range(slots):
            place = deal[req + source * slots + s] - group * slots
            chosen = jnp.where((out_lane == s) & (out_row == place), 1.0, chosen)
        route_ref[j, pl.ds(0, slots), :] = chosen
        mine = (deal[source] == group).astype(F32)
        route_ref[j, pl.ds(slots, 8), :] = jnp.full((8, HEAD_SIZE), mine, F32)
    row_slot = lax.broadcasted_iota(jnp.int32, (rows, ctx), 0) % slots
    column = lax.broadcasted_iota(jnp.int32, (rows, ctx), 1)
    in_tile = lax.broadcasted_iota(jnp.int32, (TILE, KVW), 0)
    limit = jnp.full((rows, ctx), -1, jnp.int32)
    queries = [
        jnp.concatenate(
            [query_ref[:, pl.ds((g * GROUP + h) * HEAD_SIZE, HEAD_SIZE)] for h in range(GROUP)], axis=0
        )
        for g in range(KEY_VALUE_HEADS)
    ]
    scores = [jnp.zeros((rows, ctx), F32) for _ in range(KEY_VALUE_HEADS)]
    for c in range(CHUNKS):
        loads[c].wait()
        for s in range(c * chunk, (c + 1) * chunk):
            relative = lens[s] - base
            limit = jnp.where(row_slot == s, relative, limit)

            @pl.when((relative >= 0) & (relative < ctx))
            def _():
                start = pl.multiple_of(relative // TILE * TILE, TILE)
                tile = table[s, pl.ds(start, TILE), :]
                table[s, pl.ds(start, TILE), :] = jnp.where(
                    in_tile == relative - start, new_ref[s : s + 1, :], tile
                )

        stores[c].start()
        for s in range(c * chunk, (c + 1) * chunk):
            for g in range(KEY_VALUE_HEADS):
                key = table[s, :, pl.ds(g * HEAD_SIZE, HEAD_SIZE)]
                scores[g] = jnp.where(row_slot == s, dot_t(queries[g], key), scores[g])
    visible = column <= limit
    columns = []
    for g in range(KEY_VALUE_HEADS):
        masked = jnp.where(visible, scores[g] * SCALE, MASKED)
        maxima = jnp.maximum(jnp.max(masked, axis=1, keepdims=True), FLOOR)
        weights = jnp.exp(masked - maxima)
        totals = jnp.sum(weights, axis=1, keepdims=True)
        summed = jnp.zeros((rows, HEAD_SIZE), F32)
        for s in range(slots):
            value = table[s, :, pl.ds(KW + g * HEAD_SIZE, HEAD_SIZE)]
            picked = jnp.where(row_slot == s, weights, 0.0).astype(BF16)
            summed += dot(picked, value)
        seen = totals > 0.0
        safe = jnp.where(seen, totals, 1.0)
        normed = (summed / safe).astype(BF16)
        logs = jnp.where(seen, maxima + jnp.log(safe), MASKED)
        for h in range(GROUP):
            part = slice(h * slots, (h + 1) * slots)
            part_ref[:, pl.ds((g * GROUP + h) * HEAD_SIZE, HEAD_SIZE)] = normed[part]
            columns.append(logs[part])
    part_ref[:, pl.ds(QW, STATS)] = stats_block(columns, slots)
    for copy in stores:
        copy.wait()


def decode_partials(lengths, offset, dealing, queries, new_rows, cache, req):
    slots, ctx, width = cache.shape
    return pl.pallas_call(
        decode_kernel,
        in_specs=[HBM] * 6,
        out_specs=[HBM, VMEM, VMEM, VMEM],
        out_shape=[
            jax.ShapeDtypeStruct(cache.shape, BF16),
            jax.ShapeDtypeStruct((slots, QW + STATS), BF16),
            jax.ShapeDtypeStruct((8, HEAD_SIZE), jnp.int32),
            jax.ShapeDtypeStruct((req, slots + 8, HEAD_SIZE), F32),
        ],
        scratch_shapes=[
            pltpu.SMEM(lengths.shape, jnp.int32),
            pltpu.SMEM(offset.shape, jnp.int32),
            pltpu.SMEM(dealing.shape, jnp.int32),
            pltpu.VMEM(queries.shape, BF16),
            pltpu.VMEM(new_rows.shape, BF16),
            pltpu.VMEM(cache.shape, BF16),
            pltpu.SemaphoreType.DMA((5 + 2 * CHUNKS,)),
        ],
        compiler_params=pltpu.CompilerParams(vmem_limit_bytes=16 << 20),
        cost_estimate=pl.CostEstimate(
            flops=4 * slots * ctx * QW, bytes_accessed=2 * cache.size * 2, transcendentals=slots * ctx * 8
        ),
        name="decode_partials",
    )(lengths, offset, dealing, queries, new_rows, cache)


def prepare_kernel(q_hbm, new_hbm, cache_hbm, pack_ref, table_ref, sems):
    ctx, tokens = cache_hbm.shape[1], new_hbm.shape[1]
    copies = [
        (q_hbm.at[0], pack_ref.at[:, pl.ds(0, QW)]),
        (new_hbm.at[0], pack_ref.at[:, pl.ds(QW, KVW)]),
        (cache_hbm.at[0], table_ref.at[pl.ds(0, ctx), :]),
        (new_hbm.at[0], table_ref.at[pl.ds(ctx, tokens), :]),
    ]
    copies = [pltpu.make_async_copy(a, b, sems.at[i]) for i, (a, b) in enumerate(copies)]
    for copy in copies:
        copy.start()
    for copy in copies:
        copy.wait()


def prepare(queries, new_rows, cache):
    tokens, ctx = queries.shape[1], cache.shape[1]
    return pl.pallas_call(
        prepare_kernel,
        in_specs=[HBM] * 3,
        out_specs=[VMEM] * 2,
        out_shape=[
            jax.ShapeDtypeStruct((tokens, QW + KVW), BF16),
            jax.ShapeDtypeStruct((ctx + tokens, KVW), BF16),
        ],
        scratch_shapes=[pltpu.SemaphoreType.DMA((4,))],
        name="prepare",
    )(queries, new_rows, cache)


def prefill_kernel(hi_count, ctx, off_ref, *refs):
    packs, tables, decodes = refs[:hi_count], refs[hi_count : hi_count + QUAD], refs[hi_count + QUAD : -hi_count - 1]
    outs, news = refs[-hi_count - 1 : -1], refs[-1]
    tokens = packs[0].shape[0]
    slots = decodes[0].shape[0]
    span = tables[0].shape[0]
    me = lax.axis_index("blk")
    hi, quad = me // QUAD, me % QUAD
    offset = off_ref[:1, :1]
    pieces = []
    for k in range(QUAD):
        holder = hi * QUAD + (quad ^ k)
        index = lax.broadcasted_iota(jnp.int32, (1, span), 1)
        old = jnp.where(holder * ctx + index < offset, -1, 1 << 30)
        pieces.append(jnp.where(index < ctx, old, holder * tokens + index - ctx))
    key_mark = jnp.concatenate(pieces, axis=1)
    in_block = lax.broadcasted_iota(jnp.int32, (GROUP * tokens, 1), 0) % tokens
    for k in range(1, hi_count):
        news[pl.ds((k - 1) * tokens, tokens), :] = packs[k][:, pl.ds(QW, KVW)]
    lane = lax.broadcasted_iota(jnp.int32, (tokens, STATS), 1)
    stats = [jnp.zeros((tokens, STATS), F32) for _ in range(hi_count)]
    for g in range(KEY_VALUE_HEADS):
        keys = jnp.concatenate([t[:, pl.ds(g * HEAD_SIZE, HEAD_SIZE)] for t in tables], axis=0)
        values = jnp.concatenate([t[:, pl.ds(KW + g * HEAD_SIZE, HEAD_SIZE)] for t in tables], axis=0)
        for k in range(hi_count):
            token = ((hi ^ k) * QUAD + quad) * tokens + in_block
            query = jnp.concatenate(
                [packs[k][:, pl.ds((g * GROUP + h) * HEAD_SIZE, HEAD_SIZE)] for h in range(GROUP)], axis=0
            )
            scores = jnp.where(key_mark <= token, dot_t(query, keys) * SCALE, MASKED)
            maxima = jnp.maximum(jnp.max(scores, axis=1, keepdims=True), FLOOR)
            weights = jnp.exp(scores - maxima)
            totals = jnp.sum(weights, axis=1, keepdims=True)
            summed = dot(weights.astype(BF16), values)
            seen = totals > 0.0
            safe = jnp.where(seen, totals, 1.0)
            normed = (summed / safe).astype(BF16)
            logs = jnp.where(seen, maxima + jnp.log(safe), MASKED)
            for h in range(GROUP):
                part = slice(h * tokens, (h + 1) * tokens)
                outs[k][pl.ds(0, tokens), pl.ds((g * GROUP + h) * HEAD_SIZE, HEAD_SIZE)] = normed[part]
                for term, value in enumerate(split3(logs[part])):
                    stats[k] = jnp.where(lane == term * QUERY_HEADS + g * GROUP + h, value, stats[k])
    joined, logs = join([d[...] for d in decodes])
    joined_stats = stats_block([logs[:, h * HEAD_SIZE : h * HEAD_SIZE + 1] for h in range(QUERY_HEADS)], slots)
    for k in range(hi_count):
        outs[k][pl.ds(0, tokens), pl.ds(QW, STATS)] = stats[k].astype(BF16)
        outs[k][pl.ds(tokens, slots), pl.ds(0, QW)] = joined
        outs[k][pl.ds(tokens, slots), pl.ds(QW, STATS)] = joined_stats


def prefill_partials(offset, packs, tables, decodes, ctx):
    tokens = packs[0].shape[0]
    slots = decodes[0].shape[0]
    pairs = len(packs) * tokens * QUAD * tables[0].shape[0]
    return pl.pallas_call(
        functools.partial(prefill_kernel, len(packs), ctx),
        in_specs=[VMEM] * (1 + len(packs) + len(tables) + len(decodes)),
        out_specs=[VMEM] * (len(packs) + 1),
        out_shape=[jax.ShapeDtypeStruct((tokens + slots, QW + STATS), BF16)] * len(packs)
        + [jax.ShapeDtypeStruct(((len(packs) - 1) * tokens, KVW), BF16)],
        compiler_params=pltpu.CompilerParams(vmem_limit_bytes=32 << 20),
        cost_estimate=pl.CostEstimate(
            flops=4 * pairs * QW, bytes_accessed=4 << 20, transcendentals=pairs * QUERY_HEADS
        ),
        name="prefill_partials",
    )(offset, *packs, *tables, *decodes)


def join_kernel(*refs):
    refs[-1][...] = join([ref[...] for ref in refs[:-1]])[0]


def join_parts(parts):
    return pl.pallas_call(
        join_kernel,
        in_specs=[VMEM] * len(parts),
        out_specs=VMEM,
        out_shape=jax.ShapeDtypeStruct((parts[0].shape[0], QW), BF16),
        compiler_params=pltpu.CompilerParams(vmem_limit_bytes=16 << 20),
        name="join_parts",
    )(*parts)


def update_kernel(hi_count, off_ref, cache_hbm, *refs):
    packs, tables, others = refs[:hi_count], refs[hi_count : hi_count + QUAD], refs[hi_count + QUAD : -3]
    out_ref, cache_ref, sem = refs[-3:]
    load = pltpu.make_async_copy(cache_hbm.at[0], cache_ref, sem)
    load.start()
    ctx = cache_ref.shape[0]
    tokens = packs[0].shape[0]
    me = lax.axis_index("blk")
    hi, quad = me // QUAD, me % QUAD
    blocks = []
    for k in range(hi_count):
        for j in range(QUAD):
            if j == 0:
                blocks.append(packs[k][:, pl.ds(QW, KVW)])
            elif k == 0:
                blocks.append(tables[j][pl.ds(ctx, tokens), :])
            else:
                blocks.append(others[j - 1][pl.ds((k - 1) * tokens, tokens), :])
    rows = jnp.concatenate(blocks, axis=0)
    count = rows.shape[0]
    index = lax.broadcasted_iota(jnp.int32, (1, count), 1)
    block = index // tokens
    token = ((hi ^ (block // QUAD)) * QUAD + (quad ^ (block % QUAD))) * tokens + index % tokens
    wanted = me * ctx + lax.broadcasted_iota(jnp.int32, (ctx, 1), 0) - off_ref[:1, :1]
    picked = dot(jnp.where(wanted == token, 1.0, 0.0).astype(BF16), rows).astype(BF16)
    inside = jnp.broadcast_to((wanted >= 0) & (wanted < count), cache_ref.shape)
    load.wait()
    out_ref[0] = jnp.where(inside, picked, cache_ref[...])


def update_cache(offset, cache, packs, tables, others):
    return pl.pallas_call(
        functools.partial(update_kernel, len(packs)),
        in_specs=[VMEM, HBM] + [VMEM] * (len(packs) + len(tables) + len(others)),
        out_specs=VMEM,
        out_shape=jax.ShapeDtypeStruct(cache.shape, BF16),
        scratch_shapes=[pltpu.VMEM(cache.shape[1:], BF16), pltpu.SemaphoreType.DMA],
        compiler_params=pltpu.CompilerParams(vmem_limit_bytes=16 << 20),
        name="update_cache",
    )(offset, cache, *packs, *tables, *others)


def route_kernel(count, route_ref, *refs):
    held, (pre_ref, dec_ref) = refs[:-2], refs[-2:]
    if len(held) < count:
        held = [held[0].at[j] for j in range(count)]
    tokens, slots = pre_ref.shape[1], dec_ref.shape[0]
    prefill = jnp.zeros(pre_ref.shape[1:], F32)
    decode = jnp.zeros(dec_ref.shape, F32)
    for j in range(count):
        flag = route_ref[j, pl.ds(slots, 1), pl.ds(0, 1)]
        prefill += flag * held[j][pl.ds(0, tokens), :].astype(F32)
        chosen = route_ref[j, pl.ds(0, slots), pl.ds(0, slots)].astype(BF16)
        decode += dot(chosen, held[j][pl.ds(tokens, slots), :])
    pre_ref[0] = prefill.astype(BF16)
    dec_ref[...] = decode.astype(BF16)


def route_outputs(route, held, tokens, slots):
    return pl.pallas_call(
        functools.partial(route_kernel, route.shape[0]),
        in_specs=[VMEM] * (1 + len(held)),
        out_specs=[VMEM] * 2,
        out_shape=[
            jax.ShapeDtypeStruct((1, tokens, QW), BF16),
            jax.ShapeDtypeStruct((slots, QW), BF16),
        ],
        compiler_params=pltpu.CompilerParams(vmem_limit_bytes=16 << 20),
        name="route_outputs",
    )(route, *held)


def per_device(
    prefill_queries,
    decode_queries,
    new_prefill,
    new_decode,
    prefill_cache,
    decode_cache,
    prefill_offsets,
    decode_lengths,
    dealing,
):
    blk = lax.axis_size("blk")
    req = lax.axis_size("req")
    hi_count = blk // QUAD
    ctx = prefill_cache.shape[1]
    tokens = prefill_queries.shape[1]
    slots = decode_cache.shape[0]

    def swap(array, distance):
        return lax.ppermute(array, "blk", [(i, i ^ distance) for i in range(blk)])

    def over_quad(array):
        beside, across = swap(array, 1), swap(array, 2)
        return [beside, across, swap(across, 1)]

    pack, table = prepare(prefill_queries, new_prefill, prefill_cache)
    packs = [pack] + [swap(pack, k * QUAD) for k in range(1, hi_count)]
    tables = [table] + over_quad(table)

    decode_cache_out, decode_part, offset, route = decode_partials(
        decode_lengths, prefill_offsets, dealing, decode_queries, new_decode, decode_cache, req
    )
    decodes = [decode_part] + [swap(decode_part, k) for k in range(1, QUAD)]

    *parts, news = prefill_partials(offset, packs, tables, decodes, ctx)
    arrived = [parts[0]] + [swap(parts[k], k * QUAD) for k in range(1, hi_count)]
    attended = join_parts(arrived)

    prefill_cache_out = update_cache(offset, prefill_cache, packs, tables, over_quad(news))

    if req == 2:
        held = [attended, lax.ppermute(attended, "req", [(0, 1), (1, 0)])]
    else:
        held = [lax.all_gather(attended, "req", axis=0)]
    prefill_out, decode_out = route_outputs(route, held, tokens, slots)
    return (prefill_out, decode_out, prefill_cache_out, decode_cache_out)


def solution(mesh):
    in_specs = (
        P("req", "blk", None),
        P("req", None),
        P("req", "blk", None),
        P("req", None),
        P("req", "blk", None),
        P("req", "blk", None),
        P("req"),
        P("req"),
        P(),
    )
    out_specs = (
        P("req", "blk", None),
        P("req", None),
        P("req", "blk", None),
        P("req", "blk", None),
    )
    return jax.shard_map(
        per_device, mesh=mesh, in_specs=in_specs, out_specs=out_specs, check_vma=False
    )
```

time: 113 us -> 54.5 us (0.48)
  blocking collectives: 37.6 us -> 0 us
  Pallas kernels: 40.5 us -> 9.57 us
  starting transfers between devices: 13.1 us -> 20.3 us
  local copies, waits for them, and re-layouts: 1.48 us -> 4.38 us
  waiting for transfers between devices: 16.3 us -> 18.6 us
    all_to_all x3 -> x0, blocking collectives: 37.6 us -> none  [exchange(): return lax.all_to_all(array, axis, split_axis=0, concat_axis=0, tiled=True)]
    pallas_call x6, Pallas kernels: 40.5 us -> 9.57 us  [the longest x1 3 us: prefill_partials(): pl.pallas_call(functools.partial(prefill_kernel, len(packs), ctx), in_spe...]
    ppermute x1 -> x16, starting transfers between devices: 0.6 us -> 20.3 us  [the longest x15 18.7 us: swap(): return lax.ppermute(array, 'blk', [(i, i ^ distance) for i in range(blk)])]
    ppermute x1 -> x16, waiting for transfers between devices: 0.01 us -> 18.6 us  [the longest x15 16.7 us: swap(): return lax.ppermute(array, 'blk', [(i, i ^ distance) for i in range(blk)])]
    all_to_all x3 -> x0, waiting for transfers between devices: 16.3 us -> none  [exchange(): return lax.all_to_all(array, axis, split_axis=0, concat_axis=0, tiled=True)]
    all_to_all x3 -> x0, starting transfers between devices: 12.5 us -> none  [exchange(): return lax.all_to_all(array, axis, split_axis=0, concat_axis=0, tiled=True)]
    unnamed x12 -> x16, local copies, waits for them, and re-layouts: 0.03 us -> 4.38 us
  transfers between devices with their start and end apart: 4 -> 16, of which waited for: 3 -> 6; matrix products, arithmetic and copies ran while one was open for 2% -> 0% of each run, Pallas kernels for 6% -> 8%
where the time goes in v3:
time: 54.5 us; the launch traced here: 54.2 us
  starting transfers between devices  20.3 us (37%)
  waiting for transfers between devices  18.6 us (34%)
  Pallas kernels  9.57 us (18%)
  local copies, waits for them, and re-layouts  4.38 us (8%)
  between operations  1.38 us (3%)
    ppermute x15, starting transfers between devices, swap(): return lax.ppermute(array, 'blk', [(i, i ^ distance) for i in range(blk)])  18.7 us
    ppermute x15, waiting for transfers between devices, swap(): return lax.ppermute(array, 'blk', [(i, i ^ distance) for i in range(blk)])  16.7 us
    unnamed x16, local copies, waits for them, and re-layouts  4.38 us
    pallas_call x1, Pallas kernels, prefill_partials(): pl.pallas_call(functools.partial(prefill_kernel, len(packs), ctx), in_spe...  3 us
    pallas_call x1, Pallas kernels, decode_partials(): pl.pallas_call(decode_kernel, in_specs=[HBM] * 6, out_specs=[HBM, VMEM, V...  2.49 us
    ppermute x1, waiting for transfers between devices, per_device(): held = [attended, lax.ppermute(attended, 'req', [(0, 1), (1, 0)])]  1.9 us
    pallas_call x1, Pallas kernels, prepare(): pl.pallas_call(prepare_kernel, in_specs=[HBM] * 3, out_specs=[VMEM] * 2,...  1.73 us
    ppermute x1, starting transfers between devices, per_device(): held = [attended, lax.ppermute(attended, 'req', [(0, 1), (1, 0)])]  1.61 us
  transfers between devices with their start and end apart: 16, of which 6 were waited for; matrix products, arithmetic and copies ran while one was open for 0% of the time, Pallas kernels for 8%

profile of v3, /device:TPU:0, one launch (start us, length us, event | category | flops | bytes accessed | tf_op | source)
XLA Modules:
  0.0 54.2 jit_solution(1910438047040344575)
XLA Ops:
  0.6 1.7 %prepare.1 = (bf16[32,1536]{1,0:T(8,128)(2,1)}, bf16[160,512]{1,0:T(8,128)(2,1)}) custom-call(bf16[1,32,1024]{2,1,0:T(8,128)(2,1)} %q_hbm.3, bf16[1,32,512]{2,1,0:T(8,128)(2,1)} %new_hbm.3, bf16[1,128,512]{2,1,0:T(8,128)(2,1)} %cache_hbm.5), custom_call_target="tpu_custom_call" | custom-call | tf_op jit(solution)/shard_map/prepare/pallas_call | solution.py:229
  2.4 3.0 %collective-permute-start.4 = (bf16[160,512]{1,0:T(8,128)(2,1)}, bf16[160,512]{1,0:T(8,128)(2,1)S(1)}, u32[]{:S(2)}, u32[]{:S(2)}) collective-permute-start(bf16[160,512]{1,0:T(8,128)(2,1)} %get-tuple-element.20.refs_4_), channel_id=1, source_target_pairs={{0,4},{2,6},{4,0},{6,2},{8,12},{10,14},{12,8},{14,10},{16,20},{18,... | collective-permute-start | bytes 491528 | tf_op jit(solution)/shard_map/ppermute | solution.py:417
  5.4 4.4 %collective-permute-done.4.refs_6_ = bf16[160,512]{1,0:T(8,128)(2,1)S(1)} collective-permute-done((bf16[160,512]{1,0:T(8,128)(2,1)}, bf16[160,512]{1,0:T(8,128)(2,1)S(1)}, u32[]{:S(2)}, u32[]{:S(2)}) %collective-permute-start.4) | collective-permute-done | bytes 163872 | tf_op jit(solution)/shard_map/ppermute | solution.py:417
  9.8 0.0 collective-permute-start.5
  10.4 0.0 copy-start
  10.5 1.6 %copy-done = bf16[16,128,512]{2,1,0:T(8,128)(2,1)S(1)} copy-done((bf16[16,128,512]{2,1,0:T(8,128)(2,1)S(1)}, bf16[16,128,512]{2,1,0:T(8,128)(2,1)}, u32[]{:S(2)}) %copy-start) | copy-done | bytes 2097176
  12.0 0.8 %copy-done.4 = bf16[16,1024]{1,0:T(8,128)(2,1)S(1)} copy-done((bf16[16,1024]{1,0:T(8,128)(2,1)S(1)}, bf16[16,1024]{1,0:T(8,128)(2,1)}, u32[]{:S(2)}) %copy-start.4) | copy-done | bytes 32792
  12.8 0.7 %copy-done.5 = bf16[16,512]{1,0:T(8,128)(2,1)S(1)} copy-done((bf16[16,512]{1,0:T(8,128)(2,1)S(1)}, bf16[16,512]{1,0:T(8,128)(2,1)}, u32[]{:S(2)}) %copy-start.5) | copy-done | bytes 16408
  13.5 0.7 %copy-done.6 = s32[16]{0:T(128)S(1)} copy-done((s32[16]{0:T(128)S(1)}, s32[16]{0:T(128)}, u32[]{:S(2)}) %copy-start.6) | copy-done | bytes 88
  14.2 0.7 %copy-done.7 = s32[34]{0:T(128)S(1)} copy-done((s32[34]{0:T(128)S(1)}, s32[34]{0:T(128)}, u32[]{:S(2)}) %copy-start.7) | copy-done | bytes 160
  14.8 2.5 %decode_partials.1 = (bf16[16,128,512]{2,1,0:T(8,128)(2,1)}, bf16[16,1152]{1,0:T(8,128)(2,1)S(1)}, s32[8,128]{1,0:T(8,128)S(1)}, f32[2,24,128]{2,1,0:T(8,128)S(1)}) custom-call(s32[16]{0:T(128)S(1)} %copy-done.6, s32[1]{0:T(128)S(6)} %copy.13.off_hbm, s32[34]{0:T(128)S(1)} %copy-done.7, bf16[16,1024]{1,0:T(8,128)(2,1)S(1)} %copy-done.4, ...), custom_call_target="tpu_custom_call" | custom-call | flops 8388608 | bytes 4194304 | tf_op jit(solution)/shard_map/decode_partials/pallas_call | solution.py:185
  17.3 0.5 collective-permute-start.6
  17.8 1.8 %collective-permute-start.7 = (bf16[16,1152]{1,0:T(8,128)(2,1)S(1)}, bf16[16,1152]{1,0:T(8,128)(2,1)S(1)}, u32[]{:S(2)}, u32[]{:S(2)}) collective-permute-start(bf16[16,1152]{1,0:T(8,128)(2,1)S(1)} %get-tuple-element.21.refs_8_), channel_id=1, source_target_pairs={{0,4},{2,6},{4,0},{6,2},{8,12},{10,14},{12,8},{14,10},{16,20},{18,... | collective-permute-start | bytes 110600 | tf_op jit(solution)/shard_map/ppermute | solution.py:417
  19.6 0.0 collective-permute-start.8
  19.6 0.0 collective-permute-done.6.refs_9_
  19.6 1.6 %collective-permute-start = (bf16[32,1536]{1,0:T(8,128)(2,1)S(1)}, bf16[32,1536]{1,0:T(8,128)(2,1)S(1)}, u32[]{:S(2)}, u32[]{:S(2)}) collective-permute-start(bf16[32,1536]{1,0:T(8,128)(2,1)S(1)} %copy-done.3), channel_id=1, source_target_pairs={{0,8},{2,10},{4,12},{6,14},{8,0},{10,2},{12,4},{14,6},{16,24},{18,... | collective-permute-start | bytes 294920 | tf_op jit(solution)/shard_map/ppermute | solution.py:417
  21.2 0.6 %collective-permute-done.7.refs_10_ = bf16[16,1152]{1,0:T(8,128)(2,1)S(1)} collective-permute-done((bf16[16,1152]{1,0:T(8,128)(2,1)S(1)}, bf16[16,1152]{1,0:T(8,128)(2,1)S(1)}, u32[]{:S(2)}, u32[]{:S(2)}) %collective-permute-start.7) | collective-permute-done | bytes 36896 | tf_op jit(solution)/shard_map/ppermute | solution.py:417
  21.8 2.8 %collective-permute-start.1 = (bf16[32,1536]{1,0:T(8,128)(2,1)S(1)}, bf16[32,1536]{1,0:T(8,128)(2,1)S(1)}, u32[]{:S(2)}, u32[]{:S(2)}) collective-permute-start(bf16[32,1536]{1,0:T(8,128)(2,1)S(1)} %copy-done.3), channel_id=1, source_target_pairs={{0,16},{2,18},{4,20},{6,22},{8,24},{10,26},{12,28},{14,30},{16,0},... | collective-permute-start | bytes 294920 | tf_op jit(solution)/shard_map/ppermute | solution.py:417
  24.6 2.3 %collective-permute-start.2 = (bf16[32,1536]{1,0:T(8,128)(2,1)S(1)}, bf16[32,1536]{1,0:T(8,128)(2,1)S(1)}, u32[]{:S(2)}, u32[]{:S(2)}) collective-permute-start(bf16[32,1536]{1,0:T(8,128)(2,1)S(1)} %copy-done.3), channel_id=1, source_target_pairs={{0,24},{2,26},{4,28},{6,30},{8,16},{10,18},{12,20},{14,22},{16,8},... | collective-permute-start | bytes 294920 | tf_op jit(solution)/shard_map/ppermute | solution.py:417
  26.9 5.1 %collective-permute-done.1.refs_2_ = bf16[32,1536]{1,0:T(8,128)(2,1)S(1)} collective-permute-done((bf16[32,1536]{1,0:T(8,128)(2,1)S(1)}, bf16[32,1536]{1,0:T(8,128)(2,1)S(1)}, u32[]{:S(2)}, u32[]{:S(2)}) %collective-permute-start.1) | collective-permute-done | bytes 98336 | tf_op jit(solution)/shard_map/ppermute | solution.py:417
  32.1 3.0 %prefill_partials.1 = (bf16[48,1152]{1,0:T(8,128)(2,1)S(1)}, bf16[48,1152]{1,0:T(8,128)(2,1)S(1)}, bf16[48,1152]{1,0:T(8,128)(2,1)S(1)}, bf16[48,1152]{1,0:T(8,128)(2,1)S(1)}, bf16[96,512]{1,0:T(8,128)(2,1)S(1)}) custom-call(s32[8,128]{1,0:T(8,128)S(1)} %get-tuple-element.18.off_ref, bf16[32,1536]{1,0:T(8,128)(2,1)S(1)} %copy-done.3, ...), custom_call_target="tpu_custom_call" | custom-call | flops 335544320 | bytes 4194304 | tf_op jit(solution)/shard_map/prefill_partials/pallas_call | solution.py:297
  35.1 2.2 %collective-permute-start.9 = (bf16[48,1152]{1,0:T(8,128)(2,1)S(1)}, bf16[48,1152]{1,0:T(8,128)(2,1)S(1)}, u32[]{:S(2)}, u32[]{:S(2)}) collective-permute-start(bf16[48,1152]{1,0:T(8,128)(2,1)S(1)} %get-tuple-element.23), channel_id=1, source_target_pairs={{0,8},{2,10},{4,12},{6,14},{8,0},{10,2},{12,4},{14,6},{16,24},{18,... | collective-permute-start | bytes 331784 | tf_op jit(solution)/shard_map/ppermute | solution.py:417
  37.3 1.7 %collective-permute-start.10 = (bf16[48,1152]{1,0:T(8,128)(2,1)S(1)}, bf16[48,1152]{1,0:T(8,128)(2,1)S(1)}, u32[]{:S(2)}, u32[]{:S(2)}) collective-permute-start(bf16[48,1152]{1,0:T(8,128)(2,1)S(1)} %get-tuple-element.24), channel_id=1, source_target_pairs={{0,16},{2,18},{4,20},{6,22},{8,24},{10,26},{12,28},{14,30},{16,0},... | collective-permute-start | bytes 331784 | tf_op jit(solution)/shard_map/ppermute | solution.py:417
  39.0 1.2 %collective-permute-start.11 = (bf16[48,1152]{1,0:T(8,128)(2,1)S(1)}, bf16[48,1152]{1,0:T(8,128)(2,1)S(1)}, u32[]{:S(2)}, u32[]{:S(2)}) collective-permute-start(bf16[48,1152]{1,0:T(8,128)(2,1)S(1)} %get-tuple-element.25), channel_id=1, source_target_pairs={{0,24},{2,26},{4,28},{6,30},{8,16},{10,18},{12,20},{14,22},{16,8},... | collective-permute-start | bytes 331784 | tf_op jit(solution)/shard_map/ppermute | solution.py:417
  40.1 1.6 %collective-permute-start.14 = (bf16[96,512]{1,0:T(8,128)(2,1)S(1)}, bf16[96,512]{1,0:T(8,128)(2,1)S(1)}, u32[]{:S(2)}, u32[]{:S(2)}) collective-permute-start(bf16[96,512]{1,0:T(8,128)(2,1)S(1)} %get-tuple-element.28), channel_id=1, source_target_pairs={{0,4},{2,6},{4,0},{6,2},{8,12},{10,14},{12,8},{14,10},{16,20},{18,... | collective-permute-start | bytes 294920 | tf_op jit(solution)/shard_map/ppermute | solution.py:417
  41.7 3.0 %collective-permute-done.14.refs_9_ = bf16[96,512]{1,0:T(8,128)(2,1)S(1)} collective-permute-done((bf16[96,512]{1,0:T(8,128)(2,1)S(1)}, bf16[96,512]{1,0:T(8,128)(2,1)S(1)}, u32[]{:S(2)}, u32[]{:S(2)}) %collective-permute-start.14) | collective-permute-done | bytes 98336 | tf_op jit(solution)/shard_map/ppermute | solution.py:417
  44.8 3.6 %collective-permute-done.10.refs_2_ = bf16[48,1152]{1,0:T(8,128)(2,1)S(1)} collective-permute-done((bf16[48,1152]{1,0:T(8,128)(2,1)S(1)}, bf16[48,1152]{1,0:T(8,128)(2,1)S(1)}, u32[]{:S(2)}, u32[]{:S(2)}) %collective-permute-start.10) | collective-permute-done | bytes 110624 | tf_op jit(solution)/shard_map/ppermute | solution.py:417
  48.3 0.4 join_parts.1.refs_0_
  48.8 1.6 %collective-permute-start.12 = (bf16[48,1024]{1,0:T(8,128)(2,1)S(1)}, bf16[48,1024]{1,0:T(8,128)(2,1)S(1)}, u32[]{:S(2)}, u32[]{:S(2)}) collective-permute-start(bf16[48,1024]{1,0:T(8,128)(2,1)S(1)} %join_parts.1.refs_0_), channel_id=1, source_target_pairs={{0,1},{1,0},{2,3},{3,2},{4,5},{5,4},{6,7},{7,6},{8,9},{9,8},{10,11... | collective-permute-start | bytes 294920 | tf_op jit(solution)/shard_map/ppermute | solution.py:439
  50.4 1.2 %update_cache.1 = bf16[1,128,512]{2,1,0:T(8,128)(2,1)} custom-call(s32[8,128]{1,0:T(8,128)S(1)} %get-tuple-element.18.off_ref, bf16[1,128,512]{2,1,0:T(8,128)(2,1)S(1)} %copy-done.1, bf16[32,1536]{1,0:T(8,128)(2,1)S(1)} %copy-done.3, bf16[32,1536]{1,0:T(8,128)(2,1)S(1)} %collective-permute-done.refs_1_, bf16[32,1536]{1,0:T(8,128)(2,1)S(1)} %collective-permute-done.1.refs_2_, ...), custom_call_target="tpu_custom_call" | custom-call | tf_op jit(solution)/shard_map/update_cache/pallas_call | solution.py:357
  51.6 1.9 %collective-permute-done.12.refs_1_ = bf16[48,1024]{1,0:T(8,128)(2,1)S(1)} collective-permute-done((bf16[48,1024]{1,0:T(8,128)(2,1)S(1)}, bf16[48,1024]{1,0:T(8,128)(2,1)S(1)}, u32[]{:S(2)}, u32[]{:S(2)}) %collective-permute-start.12) | collective-permute-done | bytes 98336 | tf_op jit(solution)/shard_map/ppermute | solution.py:439
  53.5 0.8 %route_outputs.1 = (bf16[1,32,1024]{2,1,0:T(8,128)(2,1)}, bf16[16,1024]{1,0:T(8,128)(2,1)}) custom-call(f32[2,24,128]{2,1,0:T(8,128)S(1)} %get-tuple-element.17.route_ref, bf16[48,1024]{1,0:T(8,128)(2,1)S(1)} %join_parts.1.refs_0_, bf16[48,1024]{1,0:T(8,128)(2,1)S(1)} %collective-permute-done.12.refs_1_), custom_call_target="tpu_custom_call" | custom-call | tf_op jit(solution)/shard_map/route_outputs/pallas_call | solution.py:385
  (22 shorter events, 0.0 us)
Async XLA Ops:
  0.6 49.8 %copy-start.1 = (bf16[1,128,512]{2,1,0:T(8,128)(2,1)S(1)}, bf16[1,128,512]{2,1,0:T(8,128)(2,1)}, u32[]{:S(2)}) copy-start(bf16[1,128,512]{2,1,0:T(8,128)(2,1)} %cache_hbm.5) | copy-start | bytes 393220
  2.4 7.4 %collective-permute-start.4 = (bf16[160,512]{1,0:T(8,128)(2,1)}, bf16[160,512]{1,0:T(8,128)(2,1)S(1)}, u32[]{:S(2)}, u32[]{:S(2)}) collective-permute-start(bf16[160,512]{1,0:T(8,128)(2,1)} %get-tuple-element.20.refs_4_), channel_id=1, source_target_pairs={{0,4},{2,6},{4,0},{6,2},{8,12},{10,14},{12,8},{14,10},{16,20},{18,... | collective-permute-start | bytes 491528 | tf_op jit(solution)/shard_map/ppermute | solution.py:417
  5.4 26.7 %collective-permute-start.3 = (bf16[160,512]{1,0:T(8,128)(2,1)}, bf16[160,512]{1,0:T(8,128)(2,1)S(1)}, u32[]{:S(2)}, u32[]{:S(2)}) collective-permute-start(bf16[160,512]{1,0:T(8,128)(2,1)} %get-tuple-element.20.refs_4_), channel_id=1, source_target_pairs={{0,2},{2,0},{4,6},{6,4},{8,10},{10,8},{12,14},{14,12},{16,18},{18,... | collective-permute-start | bytes 491528 | tf_op jit(solution)/shard_map/ppermute | solution.py:417
  9.8 22.3 %collective-permute-start.5 = (bf16[160,512]{1,0:T(8,128)(2,1)S(1)}, bf16[160,512]{1,0:T(8,128)(2,1)S(1)}, u32[]{:S(2)}, u32[]{:S(2)}) collective-permute-start(bf16[160,512]{1,0:T(8,128)(2,1)S(1)} %collective-permute-done.4.refs_6_), channel_id=1, source_target_pairs={{0,2},{2,0},{4,6},{6,4},{8,10},{10,8},{12,14},{14,12},{16,18},{18,... | collective-permute-start | bytes 491528 | tf_op jit(solution)/shard_map/ppermute | solution.py:417
  10.4 1.6 %copy-start = (bf16[16,128,512]{2,1,0:T(8,128)(2,1)S(1)}, bf16[16,128,512]{2,1,0:T(8,128)(2,1)}, u32[]{:S(2)}) copy-start(bf16[16,128,512]{2,1,0:T(8,128)(2,1)} %cache_hbm.3) | copy-start | bytes 6291460
  12.0 0.8 %copy-start.4 = (bf16[16,1024]{1,0:T(8,128)(2,1)S(1)}, bf16[16,1024]{1,0:T(8,128)(2,1)}, u32[]{:S(2)}) copy-start(bf16[16,1024]{1,0:T(8,128)(2,1)} %q_hbm.2) | copy-start | bytes 98308
  12.8 0.7 %copy-start.5 = (bf16[16,512]{1,0:T(8,128)(2,1)S(1)}, bf16[16,512]{1,0:T(8,128)(2,1)}, u32[]{:S(2)}) copy-start(bf16[16,512]{1,0:T(8,128)(2,1)} %new_hbm.2) | copy-start | bytes 49156
  13.5 0.7 %copy-start.6 = (s32[16]{0:T(128)S(1)}, s32[16]{0:T(128)}, u32[]{:S(2)}) copy-start(s32[16]{0:T(128)} %len_hbm.1) | copy-start | bytes 196
  14.2 0.7 %copy-start.7 = (s32[34]{0:T(128)S(1)}, s32[34]{0:T(128)}, u32[]{:S(2)}) copy-start(s32[34]{0:T(128)} %deal_hbm.1) | copy-start | bytes 412
  14.8 4.8 %copy-start.3 = (bf16[32,1536]{1,0:T(8,128)(2,1)S(1)}, bf16[32,1536]{1,0:T(8,128)(2,1)}, u32[]{:S(2)}) copy-start(bf16[32,1536]{1,0:T(8,128)(2,1)} %get-tuple-element.19.refs_0_) | copy-start | bytes 294916
  14.8 17.2 %copy-start.2 = (bf16[160,512]{1,0:T(8,128)(2,1)S(1)}, bf16[160,512]{1,0:T(8,128)(2,1)}, u32[]{:S(2)}) copy-start(bf16[160,512]{1,0:T(8,128)(2,1)} %get-tuple-element.20.refs_4_) | copy-start | bytes 491524
  17.3 2.3 %collective-permute-start.6 = (bf16[16,1152]{1,0:T(8,128)(2,1)S(1)}, bf16[16,1152]{1,0:T(8,128)(2,1)S(1)}, u32[]{:S(2)}, u32[]{:S(2)}) collective-permute-start(bf16[16,1152]{1,0:T(8,128)(2,1)S(1)} %get-tuple-element.21.refs_8_), channel_id=1, source_target_pairs={{0,2},{2,0},{4,6},{6,4},{8,10},{10,8},{12,14},{14,12},{16,18},{18,... | collective-permute-start | bytes 110600 | tf_op jit(solution)/shard_map/ppermute | solution.py:417
  17.8 4.0 %collective-permute-start.7 = (bf16[16,1152]{1,0:T(8,128)(2,1)S(1)}, bf16[16,1152]{1,0:T(8,128)(2,1)S(1)}, u32[]{:S(2)}, u32[]{:S(2)}) collective-permute-start(bf16[16,1152]{1,0:T(8,128)(2,1)S(1)} %get-tuple-element.21.refs_8_), channel_id=1, source_target_pairs={{0,4},{2,6},{4,0},{6,2},{8,12},{10,14},{12,8},{14,10},{16,20},{18,... | collective-permute-start | bytes 110600 | tf_op jit(solution)/shard_map/ppermute | solution.py:417
  19.6 5.0 %collective-permute-start.8 = (bf16[16,1152]{1,0:T(8,128)(2,1)S(1)}, bf16[16,1152]{1,0:T(8,128)(2,1)S(1)}, u32[]{:S(2)}, u32[]{:S(2)}) collective-permute-start(bf16[16,1152]{1,0:T(8,128)(2,1)S(1)} %get-tuple-element.21.refs_8_), channel_id=1, source_target_pairs={{0,6},{2,4},{4,2},{6,0},{8,14},{10,12},{12,10},{14,8},{16,22},{18,... | collective-permute-start | bytes 110600 | tf_op jit(solution)/shard_map/ppermute | solution.py:417
  19.6 7.3 %collective-permute-start = (bf16[32,1536]{1,0:T(8,128)(2,1)S(1)}, bf16[32,1536]{1,0:T(8,128)(2,1)S(1)}, u32[]{:S(2)}, u32[]{:S(2)}) collective-permute-start(bf16[32,1536]{1,0:T(8,128)(2,1)S(1)} %copy-done.3), channel_id=1, source_target_pairs={{0,8},{2,10},{4,12},{6,14},{8,0},{10,2},{12,4},{14,6},{16,24},{18,... | collective-permute-start | bytes 294920 | tf_op jit(solution)/shard_map/ppermute | solution.py:417
  21.8 10.2 %collective-permute-start.1 = (bf16[32,1536]{1,0:T(8,128)(2,1)S(1)}, bf16[32,1536]{1,0:T(8,128)(2,1)S(1)}, u32[]{:S(2)}, u32[]{:S(2)}) collective-permute-start(bf16[32,1536]{1,0:T(8,128)(2,1)S(1)} %copy-done.3), channel_id=1, source_target_pairs={{0,16},{2,18},{4,20},{6,22},{8,24},{10,26},{12,28},{14,30},{16,0},... | collective-permute-start | bytes 294920 | tf_op jit(solution)/shard_map/ppermute | solution.py:417
  24.6 7.4 %collective-permute-start.2 = (bf16[32,1536]{1,0:T(8,128)(2,1)S(1)}, bf16[32,1536]{1,0:T(8,128)(2,1)S(1)}, u32[]{:S(2)}, u32[]{:S(2)}) collective-permute-start(bf16[32,1536]{1,0:T(8,128)(2,1)S(1)} %copy-done.3), channel_id=1, source_target_pairs={{0,24},{2,26},{4,28},{6,30},{8,16},{10,18},{12,20},{14,22},{16,8},... | collective-permute-start | bytes 294920 | tf_op jit(solution)/shard_map/ppermute | solution.py:417
  35.1 9.7 %collective-permute-start.9 = (bf16[48,1152]{1,0:T(8,128)(2,1)S(1)}, bf16[48,1152]{1,0:T(8,128)(2,1)S(1)}, u32[]{:S(2)}, u32[]{:S(2)}) collective-permute-start(bf16[48,1152]{1,0:T(8,128)(2,1)S(1)} %get-tuple-element.23), channel_id=1, source_target_pairs={{0,8},{2,10},{4,12},{6,14},{8,0},{10,2},{12,4},{14,6},{16,24},{18,... | collective-permute-start | bytes 331784 | tf_op jit(solution)/shard_map/ppermute | solution.py:417
  37.3 11.0 %collective-permute-start.10 = (bf16[48,1152]{1,0:T(8,128)(2,1)S(1)}, bf16[48,1152]{1,0:T(8,128)(2,1)S(1)}, u32[]{:S(2)}, u32[]{:S(2)}) collective-permute-start(bf16[48,1152]{1,0:T(8,128)(2,1)S(1)} %get-tuple-element.24), channel_id=1, source_target_pairs={{0,16},{2,18},{4,20},{6,22},{8,24},{10,26},{12,28},{14,30},{16,0},... | collective-permute-start | bytes 331784 | tf_op jit(solution)/shard_map/ppermute | solution.py:417
  39.0 9.4 %collective-permute-start.11 = (bf16[48,1152]{1,0:T(8,128)(2,1)S(1)}, bf16[48,1152]{1,0:T(8,128)(2,1)S(1)}, u32[]{:S(2)}, u32[]{:S(2)}) collective-permute-start(bf16[48,1152]{1,0:T(8,128)(2,1)S(1)} %get-tuple-element.25), channel_id=1, source_target_pairs={{0,24},{2,26},{4,28},{6,30},{8,16},{10,18},{12,20},{14,22},{16,8},... | collective-permute-start | bytes 331784 | tf_op jit(solution)/shard_map/ppermute | solution.py:417
  40.1 4.6 %collective-permute-start.14 = (bf16[96,512]{1,0:T(8,128)(2,1)S(1)}, bf16[96,512]{1,0:T(8,128)(2,1)S(1)}, u32[]{:S(2)}, u32[]{:S(2)}) collective-permute-start(bf16[96,512]{1,0:T(8,128)(2,1)S(1)} %get-tuple-element.28), channel_id=1, source_target_pairs={{0,4},{2,6},{4,0},{6,2},{8,12},{10,14},{12,8},{14,10},{16,20},{18,... | collective-permute-start | bytes 294920 | tf_op jit(solution)/shard_map/ppermute | solution.py:417
  41.7 8.6 %collective-permute-start.13 = (bf16[96,512]{1,0:T(8,128)(2,1)S(1)}, bf16[96,512]{1,0:T(8,128)(2,1)S(1)}, u32[]{:S(2)}, u32[]{:S(2)}) collective-permute-start(bf16[96,512]{1,0:T(8,128)(2,1)S(1)} %get-tuple-element.28), channel_id=1, source_target_pairs={{0,2},{2,0},{4,6},{6,4},{8,10},{10,8},{12,14},{14,12},{16,18},{18,... | collective-permute-start | bytes 294920 | tf_op jit(solution)/shard_map/ppermute | solution.py:417
  44.8 5.6 %collective-permute-start.15 = (bf16[96,512]{1,0:T(8,128)(2,1)S(1)}, bf16[96,512]{1,0:T(8,128)(2,1)S(1)}, u32[]{:S(2)}, u32[]{:S(2)}) collective-permute-start(bf16[96,512]{1,0:T(8,128)(2,1)S(1)} %collective-permute-done.14.refs_9_), channel_id=1, source_target_pairs={{0,2},{2,0},{4,6},{6,4},{8,10},{10,8},{12,14},{14,12},{16,18},{18,... | collective-permute-start | bytes 294920 | tf_op jit(solution)/shard_map/ppermute | solution.py:417
  48.8 4.7 %collective-permute-start.12 = (bf16[48,1024]{1,0:T(8,128)(2,1)S(1)}, bf16[48,1024]{1,0:T(8,128)(2,1)S(1)}, u32[]{:S(2)}, u32[]{:S(2)}) collective-permute-start(bf16[48,1024]{1,0:T(8,128)(2,1)S(1)} %join_parts.1.refs_0_), channel_id=1, source_target_pairs={{0,1},{1,0},{2,3},{3,2},{4,5},{5,4},{6,7},{7,6},{8,9},{9,8},{10,11... | collective-permute-start | bytes 294920 | tf_op jit(solution)/shard_map/ppermute | solution.py:439

commit v4 on v3

--- a/solution.py
+++ b/solution.py
@@ -15,6 +15,7 @@
 KW = KEY_VALUE_HEADS * HEAD_SIZE
 STATS = 128
 QUAD = 4
+KEY_SET = 8
 SCALE = HEAD_SIZE**-0.5
 MASKED = -1e30
 FLOOR = -1e20
@@ -22,6 +23,7 @@
 BF16 = jnp.bfloat16
 
 KVW = 2 * KW
+BLK = ("hi", "quad")
 CHUNKS = 4
 TILE = 16
 
@@ -84,8 +86,10 @@
     q_hbm,
     new_hbm,
     cache_hbm,
+    pre_new_hbm,
+    pre_cache_hbm,
     out_hbm,
-    part_ref,
+    shared_ref,
     off_ref,
     route_ref,
     lens,
@@ -99,14 +103,24 @@
     slots, ctx, _ = table.shape
     rows = GROUP * slots
     chunk = slots // CHUNKS
-    base = lax.axis_index("blk") * ctx
-    small = [(len_hbm, lens), (off_hbm, off), (deal_hbm, deal), (q_hbm, query_ref), (new_hbm, new_ref)]
+    base = lax.axis_index(BLK) * ctx
+    tokens = pre_new_hbm.shape[1]
+    first = ctx + tokens
+    small = [
+        (len_hbm, lens),
+        (off_hbm, off),
+        (deal_hbm, deal),
+        (q_hbm, query_ref),
+        (new_hbm, new_ref),
+        (pre_cache_hbm.at[0], shared_ref.at[pl.ds(0, ctx), :]),
+        (pre_new_hbm.at[0], shared_ref.at[pl.ds(ctx, tokens), :]),
+    ]
     small = [pltpu.make_async_copy(a, b, sems.at[i]) for i, (a, b) in enumerate(small)]
     loads, stores = [], []
     for c in range(CHUNKS):
         part = pl.ds(c * chunk, chunk)
-        loads.append(pltpu.make_async_copy(cache_hbm.at[part], table.at[part], sems.at[5 + c]))
-        stores.append(pltpu.make_async_copy(table.at[part], out_hbm.at[part], sems.at[5 + CHUNKS + c]))
+        loads.append(pltpu.make_async_copy(cache_hbm.at[part], table.at[part], sems.at[7 + c]))
+        stores.append(pltpu.make_async_copy(table.at[part], out_hbm.at[part], sems.at[7 + CHUNKS + c]))
     for copy in small + loads:
         copy.start()
     for copy in small:
@@ -173,22 +187,25 @@
         logs = jnp.where(seen, maxima + jnp.log(safe), MASKED)
         for h in range(GROUP):
             part = slice(h * slots, (h + 1) * slots)
-            part_ref[:, pl.ds((g * GROUP + h) * HEAD_SIZE, HEAD_SIZE)] = normed[part]
+            shared_ref[pl.ds(first + g * slots, slots), pl.ds(h * HEAD_SIZE, HEAD_SIZE)] = normed[part]
             columns.append(logs[part])
-    part_ref[:, pl.ds(QW, STATS)] = stats_block(columns, slots)
+    last = pl.ds(first + KEY_VALUE_HEADS * slots, slots)
+    shared_ref[last, pl.ds(0, STATS)] = stats_block(columns, slots)
+    shared_ref[last, pl.ds(STATS, KVW - STATS)] = jnp.zeros((slots, KVW - STATS), BF16)
     for copy in stores:
         copy.wait()
 
 
-def decode_partials(lengths, offset, dealing, queries, new_rows, cache, req):
+def decode_partials(lengths, offset, dealing, queries, new_rows, cache, pre_new, pre_cache, req):
     slots, ctx, width = cache.shape
+    rows = ctx + pre_new.shape[1] + (KEY_VALUE_HEADS + 1) * slots
     return pl.pallas_call(
         decode_kernel,
-        in_specs=[HBM] * 6,
+        in_specs=[HBM] * 8,
         out_specs=[HBM, VMEM, VMEM, VMEM],
         out_shape=[
             jax.ShapeDtypeStruct(cache.shape, BF16),
-            jax.ShapeDtypeStruct((slots, QW + STATS), BF16),
+            jax.ShapeDtypeStruct((rows, KVW), BF16),
             jax.ShapeDtypeStruct((8, HEAD_SIZE), jnp.int32),
             jax.ShapeDtypeStruct((req, slots + 8, HEAD_SIZE), F32),
         ],
@@ -199,72 +216,37 @@
             pltpu.VMEM(queries.shape, BF16),
             pltpu.VMEM(new_rows.shape, BF16),
             pltpu.VMEM(cache.shape, BF16),
-            pltpu.SemaphoreType.DMA((5 + 2 * CHUNKS,)),
+            pltpu.SemaphoreType.DMA((7 + 2 * CHUNKS,)),
         ],
-        compiler_params=pltpu.CompilerParams(vmem_limit_bytes=16 << 20),
         cost_estimate=pl.CostEstimate(
             flops=4 * slots * ctx * QW, bytes_accessed=2 * cache.size * 2, transcendentals=slots * ctx * 8
         ),
         name="decode_partials",
-    )(lengths, offset, dealing, queries, new_rows, cache)
-
-
-def prepare_kernel(q_hbm, new_hbm, cache_hbm, pack_ref, table_ref, sems):
-    ctx, tokens = cache_hbm.shape[1], new_hbm.shape[1]
-    copies = [
-        (q_hbm.at[0], pack_ref.at[:, pl.ds(0, QW)]),
-        (new_hbm.at[0], pack_ref.at[:, pl.ds(QW, KVW)]),
-        (cache_hbm.at[0], table_ref.at[pl.ds(0, ctx), :]),
-        (new_hbm.at[0], table_ref.at[pl.ds(ctx, tokens), :]),
-    ]
-    copies = [pltpu.make_async_copy(a, b, sems.at[i]) for i, (a, b) in enumerate(copies)]
-    for copy in copies:
-        copy.start()
-    for copy in copies:
-        copy.wait()
-
-
-def prepare(queries, new_rows, cache):
-    tokens, ctx = queries.shape[1], cache.shape[1]
-    return pl.pallas_call(
-        prepare_kernel,
-        in_specs=[HBM] * 3,
-        out_specs=[VMEM] * 2,
-        out_shape=[
-            jax.ShapeDtypeStruct((tokens, QW + KVW), BF16),
-            jax.ShapeDtypeStruct((ctx + tokens, KVW), BF16),
-        ],
-        scratch_shapes=[pltpu.SemaphoreType.DMA((4,))],
-        name="prepare",
-    )(queries, new_rows, cache)
-
-
-def prefill_kernel(hi_count, ctx, off_ref, *refs):
-    packs, tables, decodes = refs[:hi_count], refs[hi_count : hi_count + QUAD], refs[hi_count + QUAD : -hi_count - 1]
-    outs, news = refs[-hi_count - 1 : -1], refs[-1]
+    )(lengths, offset, dealing, queries, new_rows, cache, pre_new, pre_cache)
+
+
+def prefill_kernel(query_count, ctx, slots, off_ref, *refs):
+    packs, tables, outs = refs[:query_count], refs[query_count:-query_count], refs[-query_count:]
+    packs = [packs[0].at[0]] + list(packs[1:])
     tokens = packs[0].shape[0]
-    slots = decodes[0].shape[0]
-    span = tables[0].shape[0]
-    me = lax.axis_index("blk")
-    hi, quad = me // QUAD, me % QUAD
+    span = ctx + tokens
+    me = lax.axis_index(BLK)
     offset = off_ref[:1, :1]
     pieces = []
-    for k in range(QUAD):
-        holder = hi * QUAD + (quad ^ k)
+    for k in range(KEY_SET):
+        holder = me ^ k
         index = lax.broadcasted_iota(jnp.int32, (1, span), 1)
         old = jnp.where(holder * ctx + index < offset, -1, 1 << 30)
         pieces.append(jnp.where(index < ctx, old, holder * tokens + index - ctx))
     key_mark = jnp.concatenate(pieces, axis=1)
     in_block = lax.broadcasted_iota(jnp.int32, (GROUP * tokens, 1), 0) % tokens
-    for k in range(1, hi_count):
-        news[pl.ds((k - 1) * tokens, tokens), :] = packs[k][:, pl.ds(QW, KVW)]
     lane = lax.broadcasted_iota(jnp.int32, (tokens, STATS), 1)
-    stats = [jnp.zeros((tokens, STATS), F32) for _ in range(hi_count)]
+    stats = [jnp.zeros((tokens, STATS), F32) for _ in range(query_count)]
     for g in range(KEY_VALUE_HEADS):
-        keys = jnp.concatenate([t[:, pl.ds(g * HEAD_SIZE, HEAD_SIZE)] for t in tables], axis=0)
-        values = jnp.concatenate([t[:, pl.ds(KW + g * HEAD_SIZE, HEAD_SIZE)] for t in tables], axis=0)
-        for k in range(hi_count):
-            token = ((hi ^ k) * QUAD + quad) * tokens + in_block
+        keys = jnp.concatenate([t[pl.ds(0, span), pl.ds(g * HEAD_SIZE, HEAD_SIZE)] for t in tables], axis=0)
+        values = jnp.concatenate([t[pl.ds(0, span), pl.ds(KW + g * HEAD_SIZE, HEAD_SIZE)] for t in tables], axis=0)
+        for k in range(query_count):
+            token = (me ^ (k * KEY_SET)) * tokens + in_block
             query = jnp.concatenate(
                 [packs[k][:, pl.ds((g * GROUP + h) * HEAD_SIZE, HEAD_SIZE)] for h in range(GROUP)], axis=0
             )
@@ -282,30 +264,36 @@
                 outs[k][pl.ds(0, tokens), pl.ds((g * GROUP + h) * HEAD_SIZE, HEAD_SIZE)] = normed[part]
                 for term, value in enumerate(split3(logs[part])):
                     stats[k] = jnp.where(lane == term * QUERY_HEADS + g * GROUP + h, value, stats[k])
-    joined, logs = join([d[...] for d in decodes])
+    decodes = [
+        jnp.concatenate(
+            [t[pl.ds(span + g * slots, slots), :] for g in range(KEY_VALUE_HEADS)]
+            + [t[pl.ds(span + KEY_VALUE_HEADS * slots, slots), pl.ds(0, STATS)]],
+            axis=1,
+        )
+        for t in tables
+    ]
+    joined, logs = join(decodes)
     joined_stats = stats_block([logs[:, h * HEAD_SIZE : h * HEAD_SIZE + 1] for h in range(QUERY_HEADS)], slots)
-    for k in range(hi_count):
+    for k in range(query_count):
         outs[k][pl.ds(0, tokens), pl.ds(QW, STATS)] = stats[k].astype(BF16)
         outs[k][pl.ds(tokens, slots), pl.ds(0, QW)] = joined
         outs[k][pl.ds(tokens, slots), pl.ds(QW, STATS)] = joined_stats
 
 
-def prefill_partials(offset, packs, tables, decodes, ctx):
-    tokens = packs[0].shape[0]
-    slots = decodes[0].shape[0]
-    pairs = len(packs) * tokens * QUAD * tables[0].shape[0]
+def prefill_partials(offset, packs, tables, ctx, slots):
+    tokens = packs[0].shape[1]
+    pairs = len(packs) * tokens * KEY_SET * (ctx + tokens)
     return pl.pallas_call(
-        functools.partial(prefill_kernel, len(packs), ctx),
-        in_specs=[VMEM] * (1 + len(packs) + len(tables) + len(decodes)),
-        out_specs=[VMEM] * (len(packs) + 1),
-        out_shape=[jax.ShapeDtypeStruct((tokens + slots, QW + STATS), BF16)] * len(packs)
-        + [jax.ShapeDtypeStruct(((len(packs) - 1) * tokens, KVW), BF16)],
+        functools.partial(prefill_kernel, len(packs), ctx, slots),
+        in_specs=[VMEM] * (1 + len(packs) + len(tables)),
+        out_specs=[VMEM] * len(packs),
+        out_shape=[jax.ShapeDtypeStruct((tokens + slots, QW + STATS), BF16)] * len(packs),
         compiler_params=pltpu.CompilerParams(vmem_limit_bytes=32 << 20),
         cost_estimate=pl.CostEstimate(
             flops=4 * pairs * QW, bytes_accessed=4 << 20, transcendentals=pairs * QUERY_HEADS
         ),
         name="prefill_partials",
-    )(offset, *packs, *tables, *decodes)
+    )(offset, *packs, *tables)
 
 
 def join_kernel(*refs):
@@ -323,46 +311,32 @@
     )(*parts)
 
 
-def update_kernel(hi_count, off_ref, cache_hbm, *refs):
-    packs, tables, others = refs[:hi_count], refs[hi_count : hi_count + QUAD], refs[hi_count + QUAD : -3]
-    out_ref, cache_ref, sem = refs[-3:]
+def update_kernel(tokens, off_ref, cache_hbm, news, out_ref, cache_ref, sem):
     load = pltpu.make_async_copy(cache_hbm.at[0], cache_ref, sem)
     load.start()
     ctx = cache_ref.shape[0]
-    tokens = packs[0].shape[0]
-    me = lax.axis_index("blk")
-    hi, quad = me // QUAD, me % QUAD
-    blocks = []
-    for k in range(hi_count):
-        for j in range(QUAD):
-            if j == 0:
-                blocks.append(packs[k][:, pl.ds(QW, KVW)])
-            elif k == 0:
-                blocks.append(tables[j][pl.ds(ctx, tokens), :])
-            else:
-                blocks.append(others[j - 1][pl.ds((k - 1) * tokens, tokens), :])
-    rows = jnp.concatenate(blocks, axis=0)
-    count = rows.shape[0]
+    count = news.shape[0]
+    hi_count = count // (QUAD * tokens)
     index = lax.broadcasted_iota(jnp.int32, (1, count), 1)
     block = index // tokens
-    token = ((hi ^ (block // QUAD)) * QUAD + (quad ^ (block % QUAD))) * tokens + index % tokens
-    wanted = me * ctx + lax.broadcasted_iota(jnp.int32, (ctx, 1), 0) - off_ref[:1, :1]
-    picked = dot(jnp.where(wanted == token, 1.0, 0.0).astype(BF16), rows).astype(BF16)
+    token = ((block % hi_count) * QUAD + block // hi_count) * tokens + index % tokens
+    wanted = lax.axis_index(BLK) * ctx + lax.broadcasted_iota(jnp.int32, (ctx, 1), 0) - off_ref[:1, :1]
+    picked = dot(jnp.where(wanted == token, 1.0, 0.0).astype(BF16), news[...]).astype(BF16)
     inside = jnp.broadcast_to((wanted >= 0) & (wanted < count), cache_ref.shape)
     load.wait()
     out_ref[0] = jnp.where(inside, picked, cache_ref[...])
 
 
-def update_cache(offset, cache, packs, tables, others):
+def update_cache(offset, cache, news, tokens):
     return pl.pallas_call(
-        functools.partial(update_kernel, len(packs)),
-        in_specs=[VMEM, HBM] + [VMEM] * (len(packs) + len(tables) + len(others)),
+        functools.partial(update_kernel, tokens),
+        in_specs=[VMEM, HBM, VMEM],
         out_specs=VMEM,
         out_shape=jax.ShapeDtypeStruct(cache.shape, BF16),
         scratch_shapes=[pltpu.VMEM(cache.shape[1:], BF16), pltpu.SemaphoreType.DMA],
         compiler_params=pltpu.CompilerParams(vmem_limit_bytes=16 << 20),
         name="update_cache",
-    )(offset, cache, *packs, *tables, *others)
+    )(offset, cache, news)
 
 
 def route_kernel(count, route_ref, *refs):
@@ -406,34 +380,37 @@
     decode_lengths,
     dealing,
 ):
-    blk = lax.axis_size("blk")
+    blk = lax.axis_size(BLK)
     req = lax.axis_size("req")
-    hi_count = blk // QUAD
     ctx = prefill_cache.shape[1]
     tokens = prefill_queries.shape[1]
     slots = decode_cache.shape[0]
 
     def swap(array, distance):
-        return lax.ppermute(array, "blk", [(i, i ^ distance) for i in range(blk)])
-
-    def over_quad(array):
-        beside, across = swap(array, 1), swap(array, 2)
-        return [beside, across, swap(across, 1)]
-
-    pack, table = prepare(prefill_queries, new_prefill, prefill_cache)
-    packs = [pack] + [swap(pack, k * QUAD) for k in range(1, hi_count)]
-    tables = [table] + over_quad(table)
-
-    decode_cache_out, decode_part, offset, route = decode_partials(
-        decode_lengths, prefill_offsets, dealing, decode_queries, new_decode, decode_cache, req
+        return lax.ppermute(array, BLK, [(i, i ^ distance) for i in range(blk)])
+
+    packs = [prefill_queries] + [swap(prefill_queries[0], k) for k in range(KEY_SET, blk, KEY_SET)]
+    news = lax.all_gather(new_prefill[0], "hi", axis=0, tiled=True)
+    news = lax.all_gather(news, "quad", axis=0, tiled=True)
+
+    decode_cache_out, table, offset, route = decode_partials(
+        decode_lengths,
+        prefill_offsets,
+        dealing,
+        decode_queries,
+        new_decode,
+        decode_cache,
+        new_prefill,
+        prefill_cache,
+        req,
     )
-    decodes = [decode_part] + [swap(decode_part, k) for k in range(1, QUAD)]
-
-    *parts, news = prefill_partials(offset, packs, tables, decodes, ctx)
-    arrived = [parts[0]] + [swap(parts[k], k * QUAD) for k in range(1, hi_count)]
-    attended = join_parts(arrived)
-
-    prefill_cache_out = update_cache(offset, prefill_cache, packs, tables, over_quad(news))
+    lanes = [table] + [swap(table, k) for k in range(2, KEY_SET, 2)]
+    tables = [t for lane in lanes for t in (lane, swap(lane, 1))]
+
+    parts = prefill_partials(offset, packs, tables, ctx, slots)
+    attended = join_parts([parts[0]] + [swap(part, k * KEY_SET) for k, part in enumerate(parts) if k])
+
+    prefill_cache_out = update_cache(offset, prefill_cache, news, tokens)
 
     if req == 2:
         held = [attended, lax.ppermute(attended, "req", [(0, 1), (1, 0)])]
@@ -444,22 +421,24 @@
 
 
 def solution(mesh):
+    blk, req = mesh.shape["blk"], mesh.shape["req"]
+    mesh = jax.sharding.Mesh(mesh.devices.reshape(blk // QUAD, QUAD, req), ("hi", "quad", "req"))
     in_specs = (
-        P("req", "blk", None),
+        P("req", BLK, None),
         P("req", None),
-        P("req", "blk", None),
+        P("req", BLK, None),
         P("req", None),
-        P("req", "blk", None),
-        P("req", "blk", None),
+        P("req", BLK, None),
+        P("req", BLK, None),
         P("req"),
         P("req"),
         P(),
     )
     out_specs = (
-        P("req", "blk", None),
+        P("req", BLK, None),
         P("req", None),
-        P("req", "blk", None),
-        P("req", "blk", None),
+        P("req", BLK, None),
+        P("req", BLK, None),
     )
     return jax.shard_map(
         per_device, mesh=mesh, in_specs=in_specs, out_specs=out_specs, check_vma=False

time: 54.5 us -> 56.3 us (1.033)
  blocking collectives: 0 us -> 20.7 us
  starting transfers between devices: 20.3 us -> 10.2 us
  waiting for transfers between devices: 18.6 us -> 13.9 us
  local copies, waits for them, and re-layouts: 4.38 us -> 1.63 us
  Pallas kernels: 9.57 us -> 8.19 us
    all_gather x0 -> x2, blocking collectives: none -> 20.7 us  [the longest x1 13.5 us: per_device(): news = lax.all_gather(new_prefill[0], 'hi', axis=0, tiled=True)]
    ppermute x15 -> x9, starting transfers between devices: 18.7 us -> 8.61 us  [swap(): return lax.ppermute(array, BLK, [(i, i ^ distance) for i in range(blk)])]
    unnamed x16 -> x12, local copies, waits for them, and re-layouts: 4.38 us -> 1.63 us
    ppermute x15 -> x9, waiting for transfers between devices: 16.7 us -> 13.9 us  [swap(): return lax.ppermute(array, BLK, [(i, i ^ distance) for i in range(blk)])]
    ppermute x1, waiting for transfers between devices: 1.9 us -> 0.01 us  [per_device(): held = [attended, lax.ppermute(attended, 'req', [(0, 1), (1, 0)])]]
    pallas_call x4 -> x3, Pallas kernels: 8.38 us -> 7.16 us  [the longest x1 3.77 us: decode_partials(): pl.pallas_call(decode_kernel, in_specs=[HBM] * 8, out_specs=[HBM, VMEM, V...]
  transfers between devices with their start and end apart: 16 -> 10, of which waited for: 6 -> 4; matrix products, arithmetic and copies ran while one was open for 0% -> 0% of each run, Pallas kernels for 8% -> 2%
where the time goes in v4:
time: 56.3 us; the launch traced here: 56.1 us
  blocking collectives  20.7 us (37%)
  waiting for transfers between devices  13.9 us (25%)
  starting transfers between devices  10.2 us (18%)
  Pallas kernels  8.19 us (15%)
  local copies, waits for them, and re-layouts  1.63 us (3%)
  between operations  1.41 us (3%)
    ppermute x9, waiting for transfers between devices, swap(): return lax.ppermute(array, BLK, [(i, i ^ distance) for i in range(blk)])  13.9 us
    all_gather x1, blocking collectives, per_device(): news = lax.all_gather(new_prefill[0], 'hi', axis=0, tiled=True)  13.5 us
    ppermute x9, starting transfers between devices, swap(): return lax.ppermute(array, BLK, [(i, i ^ distance) for i in range(blk)])  8.61 us
    all_gather x1, blocking collectives, per_device(): news = lax.all_gather(news, 'quad', axis=0, tiled=True)  7.19 us
    pallas_call x1, Pallas kernels, decode_partials(): pl.pallas_call(decode_kernel, in_specs=[HBM] * 8, out_specs=[HBM, VMEM, V...  3.77 us
    pallas_call x1, Pallas kernels, prefill_partials(): pl.pallas_call(functools.partial(prefill_kernel, len(packs), ctx, slots),...  2.26 us
    unnamed x12, local copies, waits for them, and re-layouts  1.63 us
    ppermute x1, starting transfers between devices, per_device(): held = [attended, lax.ppermute(attended, 'req', [(0, 1), (1, 0)])]  1.59 us
  transfers between devices with their start and end apart: 10, of which 4 were waited for; matrix products, arithmetic and copies ran while one was open for 0% of the time, Pallas kernels for 2%

profile of v4, /device:TPU:0, one launch (start us, length us, event | category | flops | bytes accessed | tf_op | source)
XLA Modules:
  0.0 56.1 jit_solution(11421257048362747560)
XLA Ops:
  0.6 0.0 copy-start.5
  0.6 0.0 copy-start.2
  1.3 3.8 %decode_partials.1 = (bf16[16,128,512]{2,1,0:T(8,128)(2,1)}, bf16[208,512]{1,0:T(8,128)(2,1)}, s32[8,128]{1,0:T(8,128)}, f32[2,24,128]{2,1,0:T(8,128)}) custom-call(s32[16]{0:T(128)} %len_hbm.1, s32[1]{0:T(128)S(6)} %copy.13.off_hbm, s32[34]{0:T(128)} %deal_hbm.1, bf16[16,1024]{1,0:T(8,128)(2,1)} %q_hbm.1, bf16[16,512]{1,0:T(8,128)(2,1)} %new_hbm.1, ...), custom_call_target="tpu_custom_call" | custom-call | flops 8388608 | bytes 4194304 | tf_op jit(solution)/shard_map/decode_partials/pallas_call | solution.py:202
  5.1 2.9 %collective-permute-start.2 = (bf16[208,512]{1,0:T(8,128)(2,1)}, bf16[208,512]{1,0:T(8,128)(2,1)S(1)}, u32[]{:S(2)}, u32[]{:S(2)}) collective-permute-start(bf16[208,512]{1,0:T(8,128)(2,1)} %get-tuple-element.14.refs_2_), channel_id=1, source_target_pairs={{0,4},{2,6},{4,0},{6,2},{8,12},{10,14},{12,8},{14,10},{16,20},{18,... | collective-permute-start | bytes 638984 | tf_op jit(solution)/shard_map/ppermute | solution.py:390
  8.1 1.6 %collective-permute-start.4 = (bf16[208,512]{1,0:T(8,128)(2,1)}, bf16[208,512]{1,0:T(8,128)(2,1)S(1)}, u32[]{:S(2)}, u32[]{:S(2)}) collective-permute-start(bf16[208,512]{1,0:T(8,128)(2,1)} %get-tuple-element.14.refs_2_), channel_id=1, source_target_pairs={{0,8},{2,10},{4,12},{6,14},{8,0},{10,2},{12,4},{14,6},{16,24},{18,... | collective-permute-start | bytes 638984 | tf_op jit(solution)/shard_map/ppermute | solution.py:390
  9.6 0.0 collective-permute-start.6
  9.6 0.0 collective-permute-start.1
  9.6 3.9 %collective-permute-done.2.refs_4_ = bf16[208,512]{1,0:T(8,128)(2,1)S(1)} collective-permute-done((bf16[208,512]{1,0:T(8,128)(2,1)}, bf16[208,512]{1,0:T(8,128)(2,1)S(1)}, u32[]{:S(2)}, u32[]{:S(2)}) %collective-permute-start.2) | collective-permute-done | bytes 213024 | tf_op jit(solution)/shard_map/ppermute | solution.py:390
  13.6 0.0 collective-permute-start.3
  13.6 2.9 %collective-permute-done.4.refs_6_ = bf16[208,512]{1,0:T(8,128)(2,1)S(1)} collective-permute-done((bf16[208,512]{1,0:T(8,128)(2,1)}, bf16[208,512]{1,0:T(8,128)(2,1)S(1)}, u32[]{:S(2)}, u32[]{:S(2)}) %collective-permute-start.4) | collective-permute-done | bytes 213024 | tf_op jit(solution)/shard_map/ppermute | solution.py:390
  16.4 0.0 collective-permute-start.5
  16.4 3.0 %collective-permute-done.6.refs_8_ = bf16[208,512]{1,0:T(8,128)(2,1)S(1)} collective-permute-done((bf16[208,512]{1,0:T(8,128)(2,1)}, bf16[208,512]{1,0:T(8,128)(2,1)S(1)}, u32[]{:S(2)}, u32[]{:S(2)}) %collective-permute-start.6) | collective-permute-done | bytes 213024 | tf_op jit(solution)/shard_map/ppermute | solution.py:390
  19.4 0.0 collective-permute-start.7
  19.4 2.7 %collective-permute-start = (bf16[32,1024]{1,0:T(8,128)(2,1)S(1)}, bf16[32,1024]{1,0:T(8,128)(2,1)S(1)}, u32[]{:S(2)}, u32[]{:S(2)}) collective-permute-start(bf16[32,1024]{1,0:T(8,128)(2,1)S(1)} %bitcast.3), channel_id=1, source_target_pairs={{0,16},{2,18},{4,20},{6,22},{8,24},{10,26},{12,28},{14,30},{16,0},... | collective-permute-start | bytes 196616 | tf_op jit(solution)/shard_map/ppermute | solution.py:390
  22.1 4.2 %collective-permute-done.refs_1_ = bf16[32,1024]{1,0:T(8,128)(2,1)S(1)} collective-permute-done((bf16[32,1024]{1,0:T(8,128)(2,1)S(1)}, bf16[32,1024]{1,0:T(8,128)(2,1)S(1)}, u32[]{:S(2)}, u32[]{:S(2)}) %collective-permute-start) | collective-permute-done | bytes 65568 | tf_op jit(solution)/shard_map/ppermute | solution.py:390
  26.3 0.0 collective-permute-done.1.refs_3_
  26.3 0.0 collective-permute-done.3.refs_5_
  26.3 0.0 collective-permute-done.5.refs_7_
  26.3 0.0 collective-permute-done.7.refs_9_
  26.3 0.9 %copy-done.1 = bf16[208,512]{1,0:T(8,128)(2,1)S(1)} copy-done((bf16[208,512]{1,0:T(8,128)(2,1)S(1)}, bf16[208,512]{1,0:T(8,128)(2,1)}, u32[]{:S(2)}) %copy-start.1) | copy-done | bytes 213016
  27.2 0.7 %copy-done.4 = s32[8,128]{1,0:T(8,128)S(1)} copy-done((s32[8,128]{1,0:T(8,128)S(1)}, s32[8,128]{1,0:T(8,128)}, u32[]{:S(2)}) %copy-start.4) | copy-done | bytes 4120
  27.9 2.3 %prefill_partials.1 = (bf16[48,1152]{1,0:T(8,128)(2,1)S(1)}, bf16[48,1152]{1,0:T(8,128)(2,1)S(1)}) custom-call(s32[8,128]{1,0:T(8,128)S(1)} %copy-done.4, bf16[1,32,1024]{2,1,0:T(8,128)(2,1)S(1)} %copy-done.2, bf16[32,1024]{1,0:T(8,128)(2,1)S(1)} %collective-permute-done.refs_1_, bf16[208,512]{1,0:T(8,128)(2,1)S(1)} %copy-done.1, ...), custom_call_target="tpu_custom_call" | custom-call | flops 335544320 | bytes 4194304 | tf_op jit(solution)/shard_map/prefill_partials/pallas_call | solution.py:286
  30.2 1.4 %collective-permute-start.8 = (bf16[48,1152]{1,0:T(8,128)(2,1)S(1)}, bf16[48,1152]{1,0:T(8,128)(2,1)S(1)}, u32[]{:S(2)}, u32[]{:S(2)}) collective-permute-start(bf16[48,1152]{1,0:T(8,128)(2,1)S(1)} %get-tuple-element.16), channel_id=1, source_target_pairs={{0,16},{2,18},{4,20},{6,22},{8,24},{10,26},{12,28},{14,30},{16,0},... | collective-permute-start | bytes 331784 | tf_op jit(solution)/shard_map/ppermute | solution.py:390
  31.6 0.0 copy-done.5
  31.6 13.5 %all-gather = bf16[1,128,512]{2,1,0:T(8,128)(2,1)S(1)} all-gather(bf16[1,32,512]{2,1,0:T(8,128)(2,1)S(1)} %copy-done.5), channel_id=2, replica_groups=mesh['hi'=4,'quad'=4,'req'=2] {'hi'}, dimensions={1}, use_global_device_ids=true | all-gather | bytes 163840 | tf_op jit(solution)/shard_map/all_gather | solution.py:393
  45.1 0.0 collective-permute-done.8.refs_1_
  45.1 0.3 join_parts.1.refs_0_
  45.4 1.6 %collective-permute-start.9 = (bf16[48,1024]{1,0:T(8,128)(2,1)S(1)}, bf16[48,1024]{1,0:T(8,128)(2,1)S(1)}, u32[]{:S(2)}, u32[]{:S(2)}) collective-permute-start(bf16[48,1024]{1,0:T(8,128)(2,1)S(1)} %join_parts.1.refs_0_), channel_id=1, source_target_pairs={{0,1},{1,0},{2,3},{3,2},{4,5},{5,4},{6,7},{7,6},{8,9},{9,8},{10,11... | collective-permute-start | bytes 294920 | tf_op jit(solution)/shard_map/ppermute | solution.py:416
  47.0 7.2 %all-gather.1 = bf16[1,512,512]{2,1,0:T(8,128)(2,1)S(1)} all-gather(bf16[1,128,512]{2,1,0:T(8,128)(2,1)S(1)} %all-gather), channel_id=3, replica_groups=mesh['hi'=4,'quad'=4,'req'=2] {'quad'}, dimensions={1}, use_global_device_ids=true | all-gather | bytes 655360 | tf_op jit(solution)/shard_map/all_gather | solution.py:394
  54.2 1.1 %update_cache.1 = bf16[1,128,512]{2,1,0:T(8,128)(2,1)} custom-call(s32[8,128]{1,0:T(8,128)S(1)} %copy-done.4, bf16[1,128,512]{2,1,0:T(8,128)(2,1)S(1)} %copy-done, bf16[512,512]{1,0:T(8,128)(2,1)S(1)} %bitcast.2), custom_call_target="tpu_custom_call" | custom-call | tf_op jit(solution)/shard_map/update_cache/pallas_call | solution.py:331
  55.3 0.0 collective-permute-done.9.refs_1_
  55.3 0.8 %route_outputs.1 = (bf16[1,32,1024]{2,1,0:T(8,128)(2,1)}, bf16[16,1024]{1,0:T(8,128)(2,1)}) custom-call(f32[2,24,128]{2,1,0:T(8,128)S(1)} %copy-done.3, bf16[48,1024]{1,0:T(8,128)(2,1)S(1)} %join_parts.1.refs_0_, bf16[48,1024]{1,0:T(8,128)(2,1)S(1)} %collective-permute-done.9.refs_1_), custom_call_target="tpu_custom_call" | custom-call | tf_op jit(solution)/shard_map/route_outputs/pallas_call | solution.py:359
  (7 shorter events, 0.0 us)
Async XLA Ops:
  0.6 31.0 %copy-start.5 = (bf16[1,32,512]{2,1,0:T(8,128)(2,1)S(1)}, bf16[1,32,512]{2,1,0:T(8,128)(2,1)}, u32[]{:S(2)}) copy-start(bf16[1,32,512]{2,1,0:T(8,128)(2,1)} %pre_new_hbm.1) | copy-start | bytes 98308
  0.6 18.8 %copy-start.2 = (bf16[1,32,1024]{2,1,0:T(8,128)(2,1)S(1)}, bf16[1,32,1024]{2,1,0:T(8,128)(2,1)}, u32[]{:S(2)}) copy-start(bf16[1,32,1024]{2,1,0:T(8,128)(2,1)} %refs_0_.1) | copy-start | bytes 196612
  1.3 52.8 %copy-start = (bf16[1,128,512]{2,1,0:T(8,128)(2,1)S(1)}, bf16[1,128,512]{2,1,0:T(8,128)(2,1)}, u32[]{:S(2)}) copy-start(bf16[1,128,512]{2,1,0:T(8,128)(2,1)} %cache_hbm.3) | copy-start | bytes 393220
  5.1 8.5 %collective-permute-start.2 = (bf16[208,512]{1,0:T(8,128)(2,1)}, bf16[208,512]{1,0:T(8,128)(2,1)S(1)}, u32[]{:S(2)}, u32[]{:S(2)}) collective-permute-start(bf16[208,512]{1,0:T(8,128)(2,1)} %get-tuple-element.14.refs_2_), channel_id=1, source_target_pairs={{0,4},{2,6},{4,0},{6,2},{8,12},{10,14},{12,8},{14,10},{16,20},{18,... | collective-permute-start | bytes 638984 | tf_op jit(solution)/shard_map/ppermute | solution.py:390
  8.1 8.4 %collective-permute-start.4 = (bf16[208,512]{1,0:T(8,128)(2,1)}, bf16[208,512]{1,0:T(8,128)(2,1)S(1)}, u32[]{:S(2)}, u32[]{:S(2)}) collective-permute-start(bf16[208,512]{1,0:T(8,128)(2,1)} %get-tuple-element.14.refs_2_), channel_id=1, source_target_pairs={{0,8},{2,10},{4,12},{6,14},{8,0},{10,2},{12,4},{14,6},{16,24},{18,... | collective-permute-start | bytes 638984 | tf_op jit(solution)/shard_map/ppermute | solution.py:390
  9.6 9.8 %collective-permute-start.6 = (bf16[208,512]{1,0:T(8,128)(2,1)}, bf16[208,512]{1,0:T(8,128)(2,1)S(1)}, u32[]{:S(2)}, u32[]{:S(2)}) collective-permute-start(bf16[208,512]{1,0:T(8,128)(2,1)} %get-tuple-element.14.refs_2_), channel_id=1, source_target_pairs={{0,12},{2,14},{4,8},{6,10},{8,4},{10,6},{12,0},{14,2},{16,28},{18,... | collective-permute-start | bytes 638984 | tf_op jit(solution)/shard_map/ppermute | solution.py:390
  9.6 16.6 %collective-permute-start.1 = (bf16[208,512]{1,0:T(8,128)(2,1)}, bf16[208,512]{1,0:T(8,128)(2,1)S(1)}, u32[]{:S(2)}, u32[]{:S(2)}) collective-permute-start(bf16[208,512]{1,0:T(8,128)(2,1)} %get-tuple-element.14.refs_2_), channel_id=1, source_target_pairs={{0,2},{2,0},{4,6},{6,4},{8,10},{10,8},{12,14},{14,12},{16,18},{18,... | collective-permute-start | bytes 638984 | tf_op jit(solution)/shard_map/ppermute | solution.py:390
  13.6 12.7 %collective-permute-start.3 = (bf16[208,512]{1,0:T(8,128)(2,1)S(1)}, bf16[208,512]{1,0:T(8,128)(2,1)S(1)}, u32[]{:S(2)}, u32[]{:S(2)}) collective-permute-start(bf16[208,512]{1,0:T(8,128)(2,1)S(1)} %collective-permute-done.2.refs_4_), channel_id=1, source_target_pairs={{0,2},{2,0},{4,6},{6,4},{8,10},{10,8},{12,14},{14,12},{16,18},{18,... | collective-permute-start | bytes 638984 | tf_op jit(solution)/shard_map/ppermute | solution.py:390
  16.4 9.8 %collective-permute-start.5 = (bf16[208,512]{1,0:T(8,128)(2,1)S(1)}, bf16[208,512]{1,0:T(8,128)(2,1)S(1)}, u32[]{:S(2)}, u32[]{:S(2)}) collective-permute-start(bf16[208,512]{1,0:T(8,128)(2,1)S(1)} %collective-permute-done.4.refs_6_), channel_id=1, source_target_pairs={{0,2},{2,0},{4,6},{6,4},{8,10},{10,8},{12,14},{14,12},{16,18},{18,... | collective-permute-start | bytes 638984 | tf_op jit(solution)/shard_map/ppermute | solution.py:390
  19.4 6.9 %collective-permute-start.7 = (bf16[208,512]{1,0:T(8,128)(2,1)S(1)}, bf16[208,512]{1,0:T(8,128)(2,1)S(1)}, u32[]{:S(2)}, u32[]{:S(2)}) collective-permute-start(bf16[208,512]{1,0:T(8,128)(2,1)S(1)} %collective-permute-done.6.refs_8_), channel_id=1, source_target_pairs={{0,2},{2,0},{4,6},{6,4},{8,10},{10,8},{12,14},{14,12},{16,18},{18,... | collective-permute-start | bytes 638984 | tf_op jit(solution)/shard_map/ppermute | solution.py:390
  19.4 6.9 %collective-permute-start = (bf16[32,1024]{1,0:T(8,128)(2,1)S(1)}, bf16[32,1024]{1,0:T(8,128)(2,1)S(1)}, u32[]{:S(2)}, u32[]{:S(2)}) collective-permute-start(bf16[32,1024]{1,0:T(8,128)(2,1)S(1)} %bitcast.3), channel_id=1, source_target_pairs={{0,16},{2,18},{4,20},{6,22},{8,24},{10,26},{12,28},{14,30},{16,0},... | collective-permute-start | bytes 196616 | tf_op jit(solution)/shard_map/ppermute | solution.py:390
  26.3 0.9 %copy-start.1 = (bf16[208,512]{1,0:T(8,128)(2,1)S(1)}, bf16[208,512]{1,0:T(8,128)(2,1)}, u32[]{:S(2)}) copy-start(bf16[208,512]{1,0:T(8,128)(2,1)} %get-tuple-element.14.refs_2_) | copy-start | bytes 638980
  27.2 0.7 %copy-start.4 = (s32[8,128]{1,0:T(8,128)S(1)}, s32[8,128]{1,0:T(8,128)}, u32[]{:S(2)}) copy-start(s32[8,128]{1,0:T(8,128)} %get-tuple-element.13.off_ref) | copy-start | bytes 12292
  27.9 27.4 %copy-start.3 = (f32[2,24,128]{2,1,0:T(8,128)S(1)}, f32[2,24,128]{2,1,0:T(8,128)}, u32[]{:S(2)}) copy-start(f32[2,24,128]{2,1,0:T(8,128)} %get-tuple-element.12.route_ref) | copy-start | bytes 73732
  30.2 14.9 %collective-permute-start.8 = (bf16[48,1152]{1,0:T(8,128)(2,1)S(1)}, bf16[48,1152]{1,0:T(8,128)(2,1)S(1)}, u32[]{:S(2)}, u32[]{:S(2)}) collective-permute-start(bf16[48,1152]{1,0:T(8,128)(2,1)S(1)} %get-tuple-element.16), channel_id=1, source_target_pairs={{0,16},{2,18},{4,20},{6,22},{8,24},{10,26},{12,28},{14,30},{16,0},... | collective-permute-start | bytes 331784 | tf_op jit(solution)/shard_map/ppermute | solution.py:390
  45.4 9.9 %collective-permute-start.9 = (bf16[48,1024]{1,0:T(8,128)(2,1)S(1)}, bf16[48,1024]{1,0:T(8,128)(2,1)S(1)}, u32[]{:S(2)}, u32[]{:S(2)}) collective-permute-start(bf16[48,1024]{1,0:T(8,128)(2,1)S(1)} %join_parts.1.refs_0_), channel_id=1, source_target_pairs={{0,1},{1,0},{2,3},{3,2},{4,5},{5,4},{6,7},{7,6},{8,9},{9,8},{10,11... | collective-permute-start | bytes 294920 | tf_op jit(solution)/shard_map/ppermute | solution.py:416

commit v5 on v4

--- a/solution.py
+++ b/solution.py
@@ -28,6 +28,7 @@
 TILE = 16
 
 HBM = pl.BlockSpec(memory_space=pltpu.HBM)
+SMEM = pl.BlockSpec(memory_space=pltpu.SMEM)
 VMEM = pl.BlockSpec(memory_space=pltpu.VMEM)
 
 
@@ -81,19 +82,18 @@
 
 def decode_kernel(
     len_hbm,
-    off_hbm,
     deal_hbm,
     q_hbm,
     new_hbm,
     cache_hbm,
+    pre_q_hbm,
     pre_new_hbm,
     pre_cache_hbm,
     out_hbm,
     shared_ref,
-    off_ref,
+    pre_q_ref,
     route_ref,
     lens,
-    off,
     deal,
     query_ref,
     new_ref,
@@ -108,10 +108,10 @@
     first = ctx + tokens
     small = [
         (len_hbm, lens),
-        (off_hbm, off),
         (deal_hbm, deal),
         (q_hbm, query_ref),
         (new_hbm, new_ref),
+        (pre_q_hbm.at[0], pre_q_ref),
         (pre_cache_hbm.at[0], shared_ref.at[pl.ds(0, ctx), :]),
         (pre_new_hbm.at[0], shared_ref.at[pl.ds(ctx, tokens), :]),
     ]
@@ -125,7 +125,6 @@
         copy.start()
     for copy in small:
         copy.wait()
-    off_ref[...] = jnp.full(off_ref.shape, off[0], jnp.int32)
     group = lax.axis_index("req")
     req = route_ref.shape[0]
     out_row = lax.broadcasted_iota(jnp.int32, (slots, HEAD_SIZE), 0)
@@ -196,42 +195,42 @@
         copy.wait()
 
 
-def decode_partials(lengths, offset, dealing, queries, new_rows, cache, pre_new, pre_cache, req):
+def decode_partials(lengths, dealing, queries, new_rows, cache, pre_queries, pre_new, pre_cache, req):
     slots, ctx, width = cache.shape
     rows = ctx + pre_new.shape[1] + (KEY_VALUE_HEADS + 1) * slots
+    inputs = (lengths, dealing, queries, new_rows, cache, pre_queries, pre_new, pre_cache)
     return pl.pallas_call(
         decode_kernel,
-        in_specs=[HBM] * 8,
+        in_specs=[HBM] * len(inputs),
         out_specs=[HBM, VMEM, VMEM, VMEM],
         out_shape=[
-            jax.ShapeDtypeStruct(cache.shape, BF16),
-            jax.ShapeDtypeStruct((rows, KVW), BF16),
-            jax.ShapeDtypeStruct((8, HEAD_SIZE), jnp.int32),
-            jax.ShapeDtypeStruct((req, slots + 8, HEAD_SIZE), F32),
+            pltpu.HBM(cache.shape, BF16),
+            pltpu.VMEM((rows, KVW), BF16),
+            pltpu.VMEM(pre_queries.shape[1:], BF16),
+            pltpu.VMEM((req, slots + 8, HEAD_SIZE), F32),
         ],
         scratch_shapes=[
             pltpu.SMEM(lengths.shape, jnp.int32),
-            pltpu.SMEM(offset.shape, jnp.int32),
             pltpu.SMEM(dealing.shape, jnp.int32),
             pltpu.VMEM(queries.shape, BF16),
             pltpu.VMEM(new_rows.shape, BF16),
             pltpu.VMEM(cache.shape, BF16),
             pltpu.SemaphoreType.DMA((7 + 2 * CHUNKS,)),
         ],
+        compiler_params=pltpu.CompilerParams(vmem_limit_bytes=16 << 20),
         cost_estimate=pl.CostEstimate(
             flops=4 * slots * ctx * QW, bytes_accessed=2 * cache.size * 2, transcendentals=slots * ctx * 8
         ),
         name="decode_partials",
-    )(lengths, offset, dealing, queries, new_rows, cache, pre_new, pre_cache)
+    )(*[pltpu.with_memory_space_constraint(x, pltpu.HBM) for x in inputs])
 
 
 def prefill_kernel(query_count, ctx, slots, off_ref, *refs):
     packs, tables, outs = refs[:query_count], refs[query_count:-query_count], refs[-query_count:]
-    packs = [packs[0].at[0]] + list(packs[1:])
     tokens = packs[0].shape[0]
     span = ctx + tokens
     me = lax.axis_index(BLK)
-    offset = off_ref[:1, :1]
+    offset = off_ref[0]
     pieces = []
     for k in range(KEY_SET):
         holder = me ^ k
@@ -281,11 +280,11 @@
 
 
 def prefill_partials(offset, packs, tables, ctx, slots):
-    tokens = packs[0].shape[1]
+    tokens = packs[0].shape[0]
     pairs = len(packs) * tokens * KEY_SET * (ctx + tokens)
     return pl.pallas_call(
         functools.partial(prefill_kernel, len(packs), ctx, slots),
-        in_specs=[VMEM] * (1 + len(packs) + len(tables)),
+        in_specs=[SMEM] + [VMEM] * (len(packs) + len(tables)),
         out_specs=[VMEM] * len(packs),
         out_shape=[jax.ShapeDtypeStruct((tokens + slots, QW + STATS), BF16)] * len(packs),
         compiler_params=pltpu.CompilerParams(vmem_limit_bytes=32 << 20),
@@ -311,32 +310,38 @@
     )(*parts)
 
 
-def update_kernel(tokens, off_ref, cache_hbm, news, out_ref, cache_ref, sem):
+def update_kernel(off_ref, cache_hbm, *refs):
+    tables, news, (out_ref, cache_ref, sem) = refs[:KEY_SET], refs[KEY_SET:-3], refs[-3:]
     load = pltpu.make_async_copy(cache_hbm.at[0], cache_ref, sem)
     load.start()
     ctx = cache_ref.shape[0]
-    count = news.shape[0]
-    hi_count = count // (QUAD * tokens)
+    tokens = news[0].shape[0] // (KEY_SET // 2)
+    me = lax.axis_index(BLK)
+    rows = jnp.concatenate([t[pl.ds(ctx, tokens), :] for t in tables] + [n[...] for n in news], axis=0)
+    count = rows.shape[0]
     index = lax.broadcasted_iota(jnp.int32, (1, count), 1)
     block = index // tokens
-    token = ((block % hi_count) * QUAD + block // hi_count) * tokens + index % tokens
-    wanted = lax.axis_index(BLK) * ctx + lax.broadcasted_iota(jnp.int32, (ctx, 1), 0) - off_ref[:1, :1]
-    picked = dot(jnp.where(wanted == token, 1.0, 0.0).astype(BF16), news[...]).astype(BF16)
+    inner = block % KEY_SET
+    turned = inner % (KEY_SET // 2) * 2 + inner // (KEY_SET // 2)
+    distance = jnp.where(block < KEY_SET, block, block // KEY_SET * KEY_SET + turned)
+    token = (me ^ distance) * tokens + index % tokens
+    wanted = me * ctx + lax.broadcasted_iota(jnp.int32, (ctx, 1), 0) - off_ref[0]
+    picked = dot(jnp.where(wanted == token, 1.0, 0.0).astype(BF16), rows).astype(BF16)
     inside = jnp.broadcast_to((wanted >= 0) & (wanted < count), cache_ref.shape)
     load.wait()
     out_ref[0] = jnp.where(inside, picked, cache_ref[...])
 
 
-def update_cache(offset, cache, news, tokens):
+def update_cache(offset, cache, tables, news):
     return pl.pallas_call(
-        functools.partial(update_kernel, tokens),
-        in_specs=[VMEM, HBM, VMEM],
+        update_kernel,
+        in_specs=[SMEM, HBM] + [VMEM] * (len(tables) + len(news)),
         out_specs=VMEM,
         out_shape=jax.ShapeDtypeStruct(cache.shape, BF16),
         scratch_shapes=[pltpu.VMEM(cache.shape[1:], BF16), pltpu.SemaphoreType.DMA],
         compiler_params=pltpu.CompilerParams(vmem_limit_bytes=16 << 20),
         name="update_cache",
-    )(offset, cache, news)
+    )(offset, pltpu.with_memory_space_constraint(cache, pltpu.HBM), *tables, *news)
 
 
 def route_kernel(count, route_ref, *refs):
@@ -389,28 +394,32 @@
     def swap(array, distance):
         return lax.ppermute(array, BLK, [(i, i ^ distance) for i in range(blk)])
 
-    packs = [prefill_queries] + [swap(prefill_queries[0], k) for k in range(KEY_SET, blk, KEY_SET)]
-    news = lax.all_gather(new_prefill[0], "hi", axis=0, tiled=True)
-    news = lax.all_gather(news, "quad", axis=0, tiled=True)
-
-    decode_cache_out, table, offset, route = decode_partials(
+    others = range(KEY_SET, blk, KEY_SET)
+    packs = [swap(prefill_queries[0], k) for k in others]
+    decode_cache_out, table, queries, route = decode_partials(
         decode_lengths,
-        prefill_offsets,
         dealing,
         decode_queries,
         new_decode,
         decode_cache,
+        prefill_queries,
         new_prefill,
         prefill_cache,
         req,
     )
     lanes = [table] + [swap(table, k) for k in range(2, KEY_SET, 2)]
+    lanes[1], *packs = lax.optimization_barrier((lanes[1], *packs))
     tables = [t for lane in lanes for t in (lane, swap(lane, 1))]
 
-    parts = prefill_partials(offset, packs, tables, ctx, slots)
+    news = jnp.concatenate([lane[ctx : ctx + tokens] for lane in lanes], axis=0)
+    news = [swap(news, k) for k in others]
+
+    parts = prefill_partials(prefill_offsets, [queries] + packs, tables, ctx, slots)
     attended = join_parts([parts[0]] + [swap(part, k * KEY_SET) for k, part in enumerate(parts) if k])
 
-    prefill_cache_out = update_cache(offset, prefill_cache, news, tokens)
+    news, _ = lax.optimization_barrier((news, parts[0]))
+    news = [n for near in news for n in (near, swap(near, 1))]
+    prefill_cache_out = update_cache(prefill_offsets, prefill_cache, tables, news)
 
     if req == 2:
         held = [attended, lax.ppermute(attended, "req", [(0, 1), (1, 0)])]

time: 56.3 us -> 40.1 us (0.71)
  blocking collectives: 20.7 us -> 0 us
  starting transfers between devices: 10.2 us -> 13.7 us
  waiting for transfers between devices: 13.9 us -> 16.8 us
  local copies, waits for them, and re-layouts: 1.63 us -> 0.02 us
    all_gather x2 -> x0, blocking collectives: 20.7 us -> none  [the longest x1 13.5 us: per_device(): news = lax.all_gather(new_prefill[0], 'hi', axis=0, tiled=True)]
    ppermute x9 -> x11, starting transfers between devices: 8.61 us -> 12.1 us  [swap(): return lax.ppermute(array, BLK, [(i, i ^ distance) for i in range(blk)])]
    unnamed x12 -> x2, local copies, waits for them, and re-layouts: 1.63 us -> 0.01 us
    ppermute x9 -> x11, waiting for transfers between devices: 13.9 us -> 15.4 us  [swap(): return lax.ppermute(array, BLK, [(i, i ^ distance) for i in range(blk)])]
    ppermute x1, waiting for transfers between devices: 0.01 us -> 1.43 us  [per_device(): held = [attended, lax.ppermute(attended, 'req', [(0, 1), (1, 0)])]]
  transfers between devices with their start and end apart: 10 -> 12, of which waited for: 4 -> 5; matrix products, arithmetic and copies ran while one was open for 0% -> 0% of each run, Pallas kernels for 2% -> 10%
where the time goes in v5:
time: 40.1 us; the launch traced here: 39.9 us
  waiting for transfers between devices  16.8 us (42%)
  starting transfers between devices  13.7 us (34%)
  Pallas kernels  8 us (20%)
  between operations  1.39 us (3%)
    ppermute x11, waiting for transfers between devices, swap(): return lax.ppermute(array, BLK, [(i, i ^ distance) for i in range(blk)])  15.4 us
    ppermute x11, starting transfers between devices, swap(): return lax.ppermute(array, BLK, [(i, i ^ distance) for i in range(blk)])  12.1 us
    pallas_call x1, Pallas kernels, decode_partials(): pl.pallas_call(decode_kernel, in_specs=[HBM] * len(inputs), out_specs=[HB...  3.07 us
    pallas_call x1, Pallas kernels, prefill_partials(): pl.pallas_call(functools.partial(prefill_kernel, len(packs), ctx, slots),...  2.23 us
    pallas_call x1, Pallas kernels, update_cache(): pl.pallas_call(update_kernel, in_specs=[SMEM, HBM] + [VMEM] * (len(tables...  1.66 us
    ppermute x1, starting transfers between devices, per_device(): held = [attended, lax.ppermute(attended, 'req', [(0, 1), (1, 0)])]  1.58 us
    ppermute x1, waiting for transfers between devices, per_device(): held = [attended, lax.ppermute(attended, 'req', [(0, 1), (1, 0)])]  1.43 us
  transfers between devices with their start and end apart: 12, of which 5 were waited for; matrix products, arithmetic and copies ran while one was open for 0% of the time, Pallas kernels for 10%

profile of v5, /device:TPU:0, one launch (start us, length us, event | category | flops | bytes accessed | tf_op | source)
XLA Modules:
  0.0 39.9 jit_solution(3153176347634312086)
XLA Ops:
  0.6 0.0 copy-start
  0.6 3.1 %decode_partials.1 = (bf16[16,128,512]{2,1,0:T(8,128)(2,1)}, bf16[208,512]{1,0:T(8,128)(2,1)S(1)}, bf16[32,1024]{1,0:T(8,128)(2,1)S(1)}, f32[2,24,128]{2,1,0:T(8,128)S(1)}) custom-call(s32[16]{0:T(128)} %len_hbm.1, s32[34]{0:T(128)} %deal_hbm.1, bf16[16,1024]{1,0:T(8,128)(2,1)} %q_hbm.1, bf16[16,512]{1,0:T(8,128)(2,1)} %new_hbm.1, ...), custom_call_target="tpu_custom_call" | custom-call | flops 8388608 | bytes 4194304 | tf_op jit(solution)/shard_map/decode_partials/pallas_call | solution.py:202
  3.7 3.0 %collective-permute-start = (bf16[208,512]{1,0:T(8,128)(2,1)S(1)}, bf16[208,512]{1,0:T(8,128)(2,1)S(1)}, u32[]{:S(2)}, u32[]{:S(2)}) collective-permute-start(bf16[208,512]{1,0:T(8,128)(2,1)S(1)} %get-tuple-element.17.refs_2_.refs_0_), channel_id=1, source_target_pairs={{0,4},{2,6},{4,0},{6,2},{8,12},{10,14},{12,8},{14,10},{16,20},{18,... | collective-permute-start | bytes 638984 | tf_op jit(solution)/shard_map/ppermute | solution.py:395
  6.7 1.6 %collective-permute-start.4 = (bf16[208,512]{1,0:T(8,128)(2,1)S(1)}, bf16[208,512]{1,0:T(8,128)(2,1)S(1)}, u32[]{:S(2)}, u32[]{:S(2)}) collective-permute-start(bf16[208,512]{1,0:T(8,128)(2,1)S(1)} %get-tuple-element.17.refs_2_.refs_0_), channel_id=1, source_target_pairs={{0,8},{2,10},{4,12},{6,14},{8,0},{10,2},{12,4},{14,6},{16,24},{18,... | collective-permute-start | bytes 638984 | tf_op jit(solution)/shard_map/ppermute | solution.py:395
  8.3 0.0 collective-permute-start.6
  8.3 0.0 copy-done
  8.3 3.0 %collective-permute-start.1 = (bf16[32,1024]{1,0:T(8,128)(2,1)S(1)}, bf16[32,1024]{1,0:T(8,128)(2,1)S(1)}, u32[]{:S(2)}, u32[]{:S(2)}) collective-permute-start(bf16[32,1024]{1,0:T(8,128)(2,1)S(1)} %bitcast.1), channel_id=1, source_target_pairs={{0,16},{2,18},{4,20},{6,22},{8,24},{10,26},{12,28},{14,30},{16,0},... | collective-permute-start | bytes 196616 | tf_op jit(solution)/shard_map/ppermute | solution.py:395
  11.3 0.0 collective-permute-start.2
  11.3 7.2 %collective-permute-done.1.refs_1_ = bf16[32,1024]{1,0:T(8,128)(2,1)S(1)} collective-permute-done((bf16[32,1024]{1,0:T(8,128)(2,1)S(1)}, bf16[32,1024]{1,0:T(8,128)(2,1)S(1)}, u32[]{:S(2)}, u32[]{:S(2)}) %collective-permute-start.1) | collective-permute-done | bytes 65568 | tf_op jit(solution)/shard_map/ppermute | solution.py:395
  18.5 0.0 collective-permute-done.refs_4_.refs_2_
  18.5 0.0 collective-permute-start.3
  18.5 0.0 collective-permute-done.4.refs_6_.refs_4_
  18.5 0.5 %collective-permute-start.5 = (bf16[208,512]{1,0:T(8,128)(2,1)S(1)}, bf16[208,512]{1,0:T(8,128)(2,1)S(1)}, u32[]{:S(2)}, u32[]{:S(2)}) collective-permute-start(bf16[208,512]{1,0:T(8,128)(2,1)S(1)} %collective-permute-done.4.refs_6_.refs_4_), channel_id=1, source_target_pairs={{0,2},{2,0},{4,6},{6,4},{8,10},{10,8},{12,14},{14,12},{16,18},{18,... | collective-permute-start | bytes 638984 | tf_op jit(solution)/shard_map/ppermute | solution.py:395
  19.0 0.2 collective-permute-done.6.refs_8_.refs_6_
  19.2 0.0 collective-permute-start.7
  19.3 3.3 %collective-permute-start.10 = (bf16[128,512]{1,0:T(8,128)(2,1)S(1)}, bf16[128,512]{1,0:T(8,128)(2,1)S(1)}, u32[]{:S(2)}, u32[]{:S(2)}) collective-permute-start(bf16[128,512]{1,0:T(8,128)(2,1)S(1)} %pad_maximum_fusion), channel_id=1, source_target_pairs={{0,16},{2,18},{4,20},{6,22},{8,24},{10,26},{12,28},{14,30},{16,0},... | collective-permute-start | bytes 393224 | tf_op jit(solution)/shard_map/ppermute | solution.py:395
  23.2 0.0 collective-permute-done.2.refs_3_.refs_1_
  23.2 0.0 collective-permute-done.3.refs_5_.refs_3_
  23.2 0.0 collective-permute-done.5.refs_7_.refs_5_
  23.3 0.0 collective-permute-done.7.refs_9_.refs_7_
  23.3 2.2 %prefill_partials.1 = (bf16[48,1152]{1,0:T(8,128)(2,1)S(1)}, bf16[48,1152]{1,0:T(8,128)(2,1)S(1)}) custom-call(s32[1]{0:T(128)S(6)} %copy.13.off_ref, bf16[32,1024]{1,0:T(8,128)(2,1)S(1)} %get-tuple-element.16.refs_0_, bf16[32,1024]{1,0:T(8,128)(2,1)S(1)} %collective-permute-done.1.refs_1_, bf16[208,512]{1,0:T(8,128)(2,1)S(1)} %get-tuple-element.17.refs_2_.refs_0_, ...), custom_call_target="tpu_custom_call" | custom-call | flops 335544320 | bytes 4194304 | tf_op jit(solution)/shard_map/prefill_partials/pallas_call | solution.py:285
  25.5 0.7 %collective-permute-start.8 = (bf16[48,1152]{1,0:T(8,128)(2,1)S(1)}, bf16[48,1152]{1,0:T(8,128)(2,1)S(1)}, u32[]{:S(2)}, u32[]{:S(2)}) collective-permute-start(bf16[48,1152]{1,0:T(8,128)(2,1)S(1)} %get-tuple-element.21), channel_id=1, source_target_pairs={{0,16},{2,18},{4,20},{6,22},{8,24},{10,26},{12,28},{14,30},{16,0},... | collective-permute-start | bytes 331784 | tf_op jit(solution)/shard_map/ppermute | solution.py:395
  26.2 3.5 %collective-permute-done.10.refs_8_ = bf16[128,512]{1,0:T(8,128)(2,1)S(1)} collective-permute-done((bf16[128,512]{1,0:T(8,128)(2,1)S(1)}, bf16[128,512]{1,0:T(8,128)(2,1)S(1)}, u32[]{:S(2)}, u32[]{:S(2)}) %collective-permute-start.10) | collective-permute-done | bytes 131104 | tf_op jit(solution)/shard_map/ppermute | solution.py:395
  29.7 0.0 collective-permute-start.11
  29.7 4.5 %collective-permute-done.8.refs_1_ = bf16[48,1152]{1,0:T(8,128)(2,1)S(1)} collective-permute-done((bf16[48,1152]{1,0:T(8,128)(2,1)S(1)}, bf16[48,1152]{1,0:T(8,128)(2,1)S(1)}, u32[]{:S(2)}, u32[]{:S(2)}) %collective-permute-start.8) | collective-permute-done | bytes 110624 | tf_op jit(solution)/shard_map/ppermute | solution.py:395
  34.2 0.3 join_parts.1.refs_0_
  34.5 1.6 %collective-permute-start.9 = (bf16[48,1024]{1,0:T(8,128)(2,1)S(1)}, bf16[48,1024]{1,0:T(8,128)(2,1)S(1)}, u32[]{:S(2)}, u32[]{:S(2)}) collective-permute-start(bf16[48,1024]{1,0:T(8,128)(2,1)S(1)} %join_parts.1.refs_0_), channel_id=1, source_target_pairs={{0,1},{1,0},{2,3},{3,2},{4,5},{5,4},{6,7},{7,6},{8,9},{9,8},{10,11... | collective-permute-start | bytes 294920 | tf_op jit(solution)/shard_map/ppermute | solution.py:425
  36.1 0.0 collective-permute-done.11.refs_9_
  36.1 1.7 %update_cache.1 = bf16[1,128,512]{2,1,0:T(8,128)(2,1)} custom-call(s32[1]{0:T(128)S(6)} %copy.13.off_ref, bf16[1,128,512]{2,1,0:T(8,128)(2,1)} %cache_hbm.3, bf16[208,512]{1,0:T(8,128)(2,1)S(1)} %get-tuple-element.17.refs_2_.refs_0_, bf16[208,512]{1,0:T(8,128)(2,1)S(1)} %collective-permute-done.2.refs_3_.refs_1_, ...), custom_call_target="tpu_custom_call" | custom-call | tf_op jit(solution)/shard_map/update_cache/pallas_call | solution.py:336
  37.7 1.4 %collective-permute-done.9.refs_1_ = bf16[48,1024]{1,0:T(8,128)(2,1)S(1)} collective-permute-done((bf16[48,1024]{1,0:T(8,128)(2,1)S(1)}, bf16[48,1024]{1,0:T(8,128)(2,1)S(1)}, u32[]{:S(2)}, u32[]{:S(2)}) %collective-permute-start.9) | collective-permute-done | bytes 98336 | tf_op jit(solution)/shard_map/ppermute | solution.py:425
  39.2 0.8 %route_outputs.1 = (bf16[1,32,1024]{2,1,0:T(8,128)(2,1)}, bf16[16,1024]{1,0:T(8,128)(2,1)}) custom-call(f32[2,24,128]{2,1,0:T(8,128)S(1)} %get-tuple-element.15.route_ref, bf16[48,1024]{1,0:T(8,128)(2,1)S(1)} %join_parts.1.refs_0_, bf16[48,1024]{1,0:T(8,128)(2,1)S(1)} %collective-permute-done.9.refs_1_), custom_call_target="tpu_custom_call" | custom-call | tf_op jit(solution)/shard_map/route_outputs/pallas_call | solution.py:364
  (5 shorter events, 0.0 us)
Async XLA Ops:
  0.6 7.7 %copy-start = (bf16[1,32,1024]{2,1,0:T(8,128)(2,1)S(1)}, bf16[1,32,1024]{2,1,0:T(8,128)(2,1)}, u32[]{:S(2)}) copy-start(bf16[1,32,1024]{2,1,0:T(8,128)(2,1)} %pre_q_hbm.1) | copy-start | bytes 196612
  3.7 14.8 %collective-permute-start = (bf16[208,512]{1,0:T(8,128)(2,1)S(1)}, bf16[208,512]{1,0:T(8,128)(2,1)S(1)}, u32[]{:S(2)}, u32[]{:S(2)}) collective-permute-start(bf16[208,512]{1,0:T(8,128)(2,1)S(1)} %get-tuple-element.17.refs_2_.refs_0_), channel_id=1, source_target_pairs={{0,4},{2,6},{4,0},{6,2},{8,12},{10,14},{12,8},{14,10},{16,20},{18,... | collective-permute-start | bytes 638984 | tf_op jit(solution)/shard_map/ppermute | solution.py:395
  6.7 11.8 %collective-permute-start.4 = (bf16[208,512]{1,0:T(8,128)(2,1)S(1)}, bf16[208,512]{1,0:T(8,128)(2,1)S(1)}, u32[]{:S(2)}, u32[]{:S(2)}) collective-permute-start(bf16[208,512]{1,0:T(8,128)(2,1)S(1)} %get-tuple-element.17.refs_2_.refs_0_), channel_id=1, source_target_pairs={{0,8},{2,10},{4,12},{6,14},{8,0},{10,2},{12,4},{14,6},{16,24},{18,... | collective-permute-start | bytes 638984 | tf_op jit(solution)/shard_map/ppermute | solution.py:395
  8.3 10.9 %collective-permute-start.6 = (bf16[208,512]{1,0:T(8,128)(2,1)S(1)}, bf16[208,512]{1,0:T(8,128)(2,1)S(1)}, u32[]{:S(2)}, u32[]{:S(2)}) collective-permute-start(bf16[208,512]{1,0:T(8,128)(2,1)S(1)} %get-tuple-element.17.refs_2_.refs_0_), channel_id=1, source_target_pairs={{0,12},{2,14},{4,8},{6,10},{8,4},{10,6},{12,0},{14,2},{16,28},{18,... | collective-permute-start | bytes 638984 | tf_op jit(solution)/shard_map/ppermute | solution.py:395
  8.3 10.2 %collective-permute-start.1 = (bf16[32,1024]{1,0:T(8,128)(2,1)S(1)}, bf16[32,1024]{1,0:T(8,128)(2,1)S(1)}, u32[]{:S(2)}, u32[]{:S(2)}) collective-permute-start(bf16[32,1024]{1,0:T(8,128)(2,1)S(1)} %bitcast.1), channel_id=1, source_target_pairs={{0,16},{2,18},{4,20},{6,22},{8,24},{10,26},{12,28},{14,30},{16,0},... | collective-permute-start | bytes 196616 | tf_op jit(solution)/shard_map/ppermute | solution.py:395
  11.3 11.9 %collective-permute-start.2 = (bf16[208,512]{1,0:T(8,128)(2,1)S(1)}, bf16[208,512]{1,0:T(8,128)(2,1)S(1)}, u32[]{:S(2)}, u32[]{:S(2)}) collective-permute-start(bf16[208,512]{1,0:T(8,128)(2,1)S(1)} %get-tuple-element.17.refs_2_.refs_0_), channel_id=1, source_target_pairs={{0,2},{2,0},{4,6},{6,4},{8,10},{10,8},{12,14},{14,12},{16,18},{18,... | collective-permute-start | bytes 638984 | tf_op jit(solution)/shard_map/ppermute | solution.py:395
  18.5 4.7 %collective-permute-start.3 = (bf16[208,512]{1,0:T(8,128)(2,1)S(1)}, bf16[208,512]{1,0:T(8,128)(2,1)S(1)}, u32[]{:S(2)}, u32[]{:S(2)}) collective-permute-start(bf16[208,512]{1,0:T(8,128)(2,1)S(1)} %collective-permute-done.refs_4_.refs_2_), channel_id=1, source_target_pairs={{0,2},{2,0},{4,6},{6,4},{8,10},{10,8},{12,14},{14,12},{16,18},{18,... | collective-permute-start | bytes 638984 | tf_op jit(solution)/shard_map/ppermute | solution.py:395
  18.5 4.7 %collective-permute-start.5 = (bf16[208,512]{1,0:T(8,128)(2,1)S(1)}, bf16[208,512]{1,0:T(8,128)(2,1)S(1)}, u32[]{:S(2)}, u32[]{:S(2)}) collective-permute-start(bf16[208,512]{1,0:T(8,128)(2,1)S(1)} %collective-permute-done.4.refs_6_.refs_4_), channel_id=1, source_target_pairs={{0,2},{2,0},{4,6},{6,4},{8,10},{10,8},{12,14},{14,12},{16,18},{18,... | collective-permute-start | bytes 638984 | tf_op jit(solution)/shard_map/ppermute | solution.py:395
  19.2 4.1 %collective-permute-start.7 = (bf16[208,512]{1,0:T(8,128)(2,1)S(1)}, bf16[208,512]{1,0:T(8,128)(2,1)S(1)}, u32[]{:S(2)}, u32[]{:S(2)}) collective-permute-start(bf16[208,512]{1,0:T(8,128)(2,1)S(1)} %collective-permute-done.6.refs_8_.refs_6_), channel_id=1, source_target_pairs={{0,2},{2,0},{4,6},{6,4},{8,10},{10,8},{12,14},{14,12},{16,18},{18,... | collective-permute-start | bytes 638984 | tf_op jit(solution)/shard_map/ppermute | solution.py:395
  19.3 10.5 %collective-permute-start.10 = (bf16[128,512]{1,0:T(8,128)(2,1)S(1)}, bf16[128,512]{1,0:T(8,128)(2,1)S(1)}, u32[]{:S(2)}, u32[]{:S(2)}) collective-permute-start(bf16[128,512]{1,0:T(8,128)(2,1)S(1)} %pad_maximum_fusion), channel_id=1, source_target_pairs={{0,16},{2,18},{4,20},{6,22},{8,24},{10,26},{12,28},{14,30},{16,0},... | collective-permute-start | bytes 393224 | tf_op jit(solution)/shard_map/ppermute | solution.py:395
  25.5 8.7 %collective-permute-start.8 = (bf16[48,1152]{1,0:T(8,128)(2,1)S(1)}, bf16[48,1152]{1,0:T(8,128)(2,1)S(1)}, u32[]{:S(2)}, u32[]{:S(2)}) collective-permute-start(bf16[48,1152]{1,0:T(8,128)(2,1)S(1)} %get-tuple-element.21), channel_id=1, source_target_pairs={{0,16},{2,18},{4,20},{6,22},{8,24},{10,26},{12,28},{14,30},{16,0},... | collective-permute-start | bytes 331784 | tf_op jit(solution)/shard_map/ppermute | solution.py:395
  29.7 6.3 %collective-permute-start.11 = (bf16[128,512]{1,0:T(8,128)(2,1)S(1)}, bf16[128,512]{1,0:T(8,128)(2,1)S(1)}, u32[]{:S(2)}, u32[]{:S(2)}) collective-permute-start(bf16[128,512]{1,0:T(8,128)(2,1)S(1)} %collective-permute-done.10.refs_8_), channel_id=1, source_target_pairs={{0,2},{2,0},{4,6},{6,4},{8,10},{10,8},{12,14},{14,12},{16,18},{18,... | collective-permute-start | bytes 393224 | tf_op jit(solution)/shard_map/ppermute | solution.py:395
  34.5 4.7 %collective-permute-start.9 = (bf16[48,1024]{1,0:T(8,128)(2,1)S(1)}, bf16[48,1024]{1,0:T(8,128)(2,1)S(1)}, u32[]{:S(2)}, u32[]{:S(2)}) collective-permute-start(bf16[48,1024]{1,0:T(8,128)(2,1)S(1)} %join_parts.1.refs_0_), channel_id=1, source_target_pairs={{0,1},{1,0},{2,3},{3,2},{4,5},{5,4},{6,7},{7,6},{8,9},{9,8},{10,11... | collective-permute-start | bytes 294920 | tf_op jit(solution)/shard_map/ppermute | solution.py:425

commit v6 on v5

--- a/solution.py
+++ b/solution.py
@@ -28,7 +28,6 @@
 TILE = 16
 
 HBM = pl.BlockSpec(memory_space=pltpu.HBM)
-SMEM = pl.BlockSpec(memory_space=pltpu.SMEM)
 VMEM = pl.BlockSpec(memory_space=pltpu.VMEM)
 
 
@@ -164,10 +163,12 @@
                 )
 
         stores[c].start()
-        for s in range(c * chunk, (c + 1) * chunk):
-            for g in range(KEY_VALUE_HEADS):
-                key = table[s, :, pl.ds(g * HEAD_SIZE, HEAD_SIZE)]
-                scores[g] = jnp.where(row_slot == s, dot_t(queries[g], key), scores[g])
+        for g in range(KEY_VALUE_HEADS):
+            key = table[pl.ds(c * chunk, chunk), :, pl.ds(g * HEAD_SIZE, HEAD_SIZE)]
+            wide = dot_t(queries[g], key.reshape(chunk * ctx, HEAD_SIZE))
+            for s in range(chunk):
+                part = wide[:, s * ctx : (s + 1) * ctx]
+                scores[g] = jnp.where(row_slot == c * chunk + s, part, scores[g])
     visible = column <= limit
     columns = []
     for g in range(KEY_VALUE_HEADS):
@@ -176,10 +177,11 @@
         weights = jnp.exp(masked - maxima)
         totals = jnp.sum(weights, axis=1, keepdims=True)
         summed = jnp.zeros((rows, HEAD_SIZE), F32)
-        for s in range(slots):
-            value = table[s, :, pl.ds(KW + g * HEAD_SIZE, HEAD_SIZE)]
-            picked = jnp.where(row_slot == s, weights, 0.0).astype(BF16)
-            summed += dot(picked, value)
+        for c in range(CHUNKS):
+            value = table[pl.ds(c * chunk, chunk), :, pl.ds(KW + g * HEAD_SIZE, HEAD_SIZE)]
+            picked = [jnp.where(row_slot == c * chunk + s, weights, 0.0) for s in range(chunk)]
+            picked = jnp.concatenate(picked, axis=1).astype(BF16)
+            summed += dot(picked, value.reshape(chunk * ctx, HEAD_SIZE))
         seen = totals > 0.0
         safe = jnp.where(seen, totals, 1.0)
         normed = (summed / safe).astype(BF16)
@@ -195,9 +197,9 @@
         copy.wait()
 
 
-def decode_partials(lengths, dealing, queries, new_rows, cache, pre_queries, pre_new, pre_cache, req):
+def decode_partials(lengths, dealing, queries, new_rows, cache, pre_queries, pre_new, pre_cache, req, extra):
     slots, ctx, width = cache.shape
-    rows = ctx + pre_new.shape[1] + (KEY_VALUE_HEADS + 1) * slots
+    rows = ctx + pre_new.shape[1] + (KEY_VALUE_HEADS + 1) * slots + extra
     inputs = (lengths, dealing, queries, new_rows, cache, pre_queries, pre_new, pre_cache)
     return pl.pallas_call(
         decode_kernel,
@@ -230,7 +232,7 @@
     tokens = packs[0].shape[0]
     span = ctx + tokens
     me = lax.axis_index(BLK)
-    offset = off_ref[0]
+    offset = off_ref[:1, :1]
     pieces = []
     for k in range(KEY_SET):
         holder = me ^ k
@@ -284,7 +286,7 @@
     pairs = len(packs) * tokens * KEY_SET * (ctx + tokens)
     return pl.pallas_call(
         functools.partial(prefill_kernel, len(packs), ctx, slots),
-        in_specs=[SMEM] + [VMEM] * (len(packs) + len(tables)),
+        in_specs=[VMEM] * (1 + len(packs) + len(tables)),
         out_specs=[VMEM] * len(packs),
         out_shape=[jax.ShapeDtypeStruct((tokens + slots, QW + STATS), BF16)] * len(packs),
         compiler_params=pltpu.CompilerParams(vmem_limit_bytes=32 << 20),
@@ -310,38 +312,34 @@
     )(*parts)
 
 
-def update_kernel(off_ref, cache_hbm, *refs):
-    tables, news, (out_ref, cache_ref, sem) = refs[:KEY_SET], refs[KEY_SET:-3], refs[-3:]
+def update_kernel(tokens, extra, off_ref, cache_hbm, *refs):
+    tables, (out_ref, cache_ref, sem) = refs[:KEY_SET], refs[-3:]
     load = pltpu.make_async_copy(cache_hbm.at[0], cache_ref, sem)
     load.start()
-    ctx = cache_ref.shape[0]
-    tokens = news[0].shape[0] // (KEY_SET // 2)
+    ctx, total = cache_ref.shape[0], tables[0].shape[0]
     me = lax.axis_index(BLK)
-    rows = jnp.concatenate([t[pl.ds(ctx, tokens), :] for t in tables] + [n[...] for n in news], axis=0)
+    starts = [ctx] + list(range(total - extra, total, tokens))
+    rows = jnp.concatenate([t[pl.ds(start, tokens), :] for start in starts for t in tables], axis=0)
     count = rows.shape[0]
     index = lax.broadcasted_iota(jnp.int32, (1, count), 1)
-    block = index // tokens
-    inner = block % KEY_SET
-    turned = inner % (KEY_SET // 2) * 2 + inner // (KEY_SET // 2)
-    distance = jnp.where(block < KEY_SET, block, block // KEY_SET * KEY_SET + turned)
-    token = (me ^ distance) * tokens + index % tokens
-    wanted = me * ctx + lax.broadcasted_iota(jnp.int32, (ctx, 1), 0) - off_ref[0]
+    token = (me ^ (index // tokens)) * tokens + index % tokens
+    wanted = me * ctx + lax.broadcasted_iota(jnp.int32, (ctx, 1), 0) - off_ref[:1, :1]
     picked = dot(jnp.where(wanted == token, 1.0, 0.0).astype(BF16), rows).astype(BF16)
     inside = jnp.broadcast_to((wanted >= 0) & (wanted < count), cache_ref.shape)
     load.wait()
     out_ref[0] = jnp.where(inside, picked, cache_ref[...])
 
 
-def update_cache(offset, cache, tables, news):
+def update_cache(offset, cache, tables, tokens, extra):
     return pl.pallas_call(
-        update_kernel,
-        in_specs=[SMEM, HBM] + [VMEM] * (len(tables) + len(news)),
+        functools.partial(update_kernel, tokens, extra),
+        in_specs=[VMEM, HBM] + [VMEM] * len(tables),
         out_specs=VMEM,
         out_shape=jax.ShapeDtypeStruct(cache.shape, BF16),
         scratch_shapes=[pltpu.VMEM(cache.shape[1:], BF16), pltpu.SemaphoreType.DMA],
         compiler_params=pltpu.CompilerParams(vmem_limit_bytes=16 << 20),
         name="update_cache",
-    )(offset, pltpu.with_memory_space_constraint(cache, pltpu.HBM), *tables, *news)
+    )(offset, pltpu.with_memory_space_constraint(cache, pltpu.HBM), *tables)
 
 
 def route_kernel(count, route_ref, *refs):
@@ -395,6 +393,8 @@
         return lax.ppermute(array, BLK, [(i, i ^ distance) for i in range(blk)])
 
     others = range(KEY_SET, blk, KEY_SET)
+    extra = len(others) * tokens
+    far_rows = [swap(new_prefill[0], k) for k in others]
     packs = [swap(prefill_queries[0], k) for k in others]
     decode_cache_out, table, queries, route = decode_partials(
         decode_lengths,
@@ -406,20 +406,22 @@
         new_prefill,
         prefill_cache,
         req,
+        extra,
     )
+    far_rows, packs, table = lax.optimization_barrier((far_rows, packs, table))
+    for i, rows in enumerate(far_rows):
+        table = lax.dynamic_update_slice(table, rows, (table.shape[0] - extra + i * tokens, 0))
     lanes = [table] + [swap(table, k) for k in range(2, KEY_SET, 2)]
-    lanes[1], *packs = lax.optimization_barrier((lanes[1], *packs))
+    offset = jnp.full((8, HEAD_SIZE), prefill_offsets[0], jnp.int32)
+    lanes[1], offset = lax.optimization_barrier((lanes[1], offset))
+    for i in range(2, len(lanes)):
+        lanes[i], _ = lax.optimization_barrier((lanes[i], lanes[i - 1]))
     tables = [t for lane in lanes for t in (lane, swap(lane, 1))]
 
-    news = jnp.concatenate([lane[ctx : ctx + tokens] for lane in lanes], axis=0)
-    news = [swap(news, k) for k in others]
-
-    parts = prefill_partials(prefill_offsets, [queries] + packs, tables, ctx, slots)
+    parts = prefill_partials(offset, [queries] + packs, tables, ctx, slots)
     attended = join_parts([parts[0]] + [swap(part, k * KEY_SET) for k, part in enumerate(parts) if k])
 
-    news, _ = lax.optimization_barrier((news, parts[0]))
-    news = [n for near in news for n in (near, swap(near, 1))]
-    prefill_cache_out = update_cache(prefill_offsets, prefill_cache, tables, news)
+    prefill_cache_out = update_cache(offset, prefill_cache, tables, tokens, extra)
 
     if req == 2:
         held = [attended, lax.ppermute(attended, "req", [(0, 1), (1, 0)])]

time: 40.1 us -> 42.7 us (1.065)
  waiting for transfers between devices: 16.8 us -> 20.6 us
  starting transfers between devices: 13.7 us -> 12.7 us
    ppermute x11 -> x10, waiting for transfers between devices: 15.4 us -> 19.3 us  [swap(): return lax.ppermute(array, BLK, [(i, i ^ distance) for i in range(blk)])]
    ppermute x11 -> x10, starting transfers between devices: 12.1 us -> 11.1 us  [swap(): return lax.ppermute(array, BLK, [(i, i ^ distance) for i in range(blk)])]
  transfers between devices with their start and end apart: 12 -> 11, of which waited for: 5 -> 9; matrix products, arithmetic and copies ran while one was open for 0% -> 0% of each run, Pallas kernels for 10% -> 11%
where the time goes in v6:
time: 42.7 us; the launch traced here: 42.6 us
  waiting for transfers between devices  20.6 us (48%)
  starting transfers between devices  12.7 us (30%)
  Pallas kernels  7.9 us (19%)
  between operations  1.33 us (3%)
    ppermute x10, waiting for transfers between devices, swap(): return lax.ppermute(array, BLK, [(i, i ^ distance) for i in range(blk)])  19.3 us
    ppermute x10, starting transfers between devices, swap(): return lax.ppermute(array, BLK, [(i, i ^ distance) for i in range(blk)])  11.1 us
    pallas_call x1, Pallas kernels, decode_partials(): pl.pallas_call(decode_kernel, in_specs=[HBM] * len(inputs), out_specs=[HB...  2.9 us
    pallas_call x1, Pallas kernels, prefill_partials(): pl.pallas_call(functools.partial(prefill_kernel, len(packs), ctx, slots),...  2.27 us
    pallas_call x1, Pallas kernels, update_cache(): pl.pallas_call(functools.partial(update_kernel, tokens, extra), in_specs=...  1.71 us
    ppermute x1, starting transfers between devices, per_device(): held = [attended, lax.ppermute(attended, 'req', [(0, 1), (1, 0)])]  1.67 us
    ppermute x1, waiting for transfers between devices, per_device(): held = [attended, lax.ppermute(attended, 'req', [(0, 1), (1, 0)])]  1.29 us
  transfers between devices with their start and end apart: 11, of which 9 were waited for; matrix products, arithmetic and copies ran while one was open for 0% of the time, Pallas kernels for 11%

profile of v6, /device:TPU:0, one launch (start us, length us, event | category | flops | bytes accessed | tf_op | source)
XLA Modules:
  0.0 42.6 jit_solution(17051617770193151944)
XLA Ops:
  0.6 4.1 %collective-permute-start.1 = (bf16[32,1024]{1,0:T(8,128)(2,1)}, bf16[32,1024]{1,0:T(8,128)(2,1)S(1)}, u32[]{:S(2)}, u32[]{:S(2)}) collective-permute-start(bf16[32,1024]{1,0:T(8,128)(2,1)} %bitcast.4), channel_id=1, source_target_pairs={{0,16},{2,18},{4,20},{6,22},{8,24},{10,26},{12,28},{14,30},{16,0},... | collective-permute-start | bytes 196616 | tf_op jit(solution)/shard_map/ppermute | solution.py:393
  4.7 0.1 collective-permute-start
  4.8 2.9 %decode_partials.1 = (bf16[16,128,512]{2,1,0:T(8,128)(2,1)}, bf16[240,512]{1,0:T(8,128)(2,1)S(1)}, bf16[32,1024]{1,0:T(8,128)(2,1)S(1)}, f32[2,24,128]{2,1,0:T(8,128)S(1)}) custom-call(s32[16]{0:T(128)} %len_hbm.1, s32[34]{0:T(128)} %deal_hbm.1, bf16[16,1024]{1,0:T(8,128)(2,1)} %q_hbm.1, bf16[16,512]{1,0:T(8,128)(2,1)} %new_hbm.1, ...), custom_call_target="tpu_custom_call" | custom-call | flops 8388608 | bytes 4194304 | tf_op jit(solution)/shard_map/decode_partials/pallas_call | solution.py:204
  7.7 2.0 %collective-permute-done = bf16[32,512]{1,0:T(8,128)(2,1)S(1)} collective-permute-done((bf16[32,512]{1,0:T(8,128)(2,1)}, bf16[32,512]{1,0:T(8,128)(2,1)S(1)}, u32[]{:S(2)}, u32[]{:S(2)}) %collective-permute-start) | collective-permute-done | bytes 32800 | tf_op jit(solution)/shard_map/ppermute | solution.py:393
  9.8 0.0 collective-permute-done.1.refs_1_
  9.8 1.6 %collective-permute-start.2 = (bf16[240,512]{1,0:T(8,128)(2,1)S(1)}, bf16[240,512]{1,0:T(8,128)(2,1)S(1)}, u32[]{:S(2)}, u32[]{:S(2)}) collective-permute-start(bf16[240,512]{1,0:T(8,128)(2,1)S(1)} %constant_dynamic-update-slice_fusion.refs_2_.refs_0_), channel_id=1, source_target_pairs={{0,4},{2,6},{4,0},{6,2},{8,12},{10,14},{12,8},{14,10},{16,20},{18,... | collective-permute-start | bytes 737288 | tf_op jit(solution)/shard_map/ppermute | solution.py:393
  11.4 1.5 %collective-permute-start.5 = (bf16[240,512]{1,0:T(8,128)(2,1)S(1)}, bf16[240,512]{1,0:T(8,128)(2,1)S(1)}, u32[]{:S(2)}, u32[]{:S(2)}) collective-permute-start(bf16[240,512]{1,0:T(8,128)(2,1)S(1)} %constant_dynamic-update-slice_fusion.refs_2_.refs_0_), channel_id=1, source_target_pairs={{0,8},{2,10},{4,12},{6,14},{8,0},{10,2},{12,4},{14,6},{16,24},{18,... | collective-permute-start | bytes 737288 | tf_op jit(solution)/shard_map/ppermute | solution.py:393
  12.8 0.4 collective-permute-start.7
  13.9 0.1 collective-permute-start.3
  14.0 3.6 %collective-permute-done.2.refs_4_.refs_2_ = bf16[240,512]{1,0:T(8,128)(2,1)S(1)} collective-permute-done((bf16[240,512]{1,0:T(8,128)(2,1)S(1)}, bf16[240,512]{1,0:T(8,128)(2,1)S(1)}, u32[]{:S(2)}, u32[]{:S(2)}) %collective-permute-start.2) | collective-permute-done | bytes 245792 | tf_op jit(solution)/shard_map/ppermute | solution.py:393
  17.6 2.6 %collective-permute-done.5.refs_6_.refs_4_ = bf16[240,512]{1,0:T(8,128)(2,1)S(1)} collective-permute-done((bf16[240,512]{1,0:T(8,128)(2,1)S(1)}, bf16[240,512]{1,0:T(8,128)(2,1)S(1)}, u32[]{:S(2)}, u32[]{:S(2)}) %collective-permute-start.5) | collective-permute-done | bytes 245792 | tf_op jit(solution)/shard_map/ppermute | solution.py:393
  20.2 3.6 %collective-permute-done.7.refs_8_.refs_6_ = bf16[240,512]{1,0:T(8,128)(2,1)S(1)} collective-permute-done((bf16[240,512]{1,0:T(8,128)(2,1)S(1)}, bf16[240,512]{1,0:T(8,128)(2,1)S(1)}, u32[]{:S(2)}, u32[]{:S(2)}) %collective-permute-start.7) | collective-permute-done | bytes 245792 | tf_op jit(solution)/shard_map/ppermute | solution.py:393
  23.8 0.0 collective-permute-start.8
  23.8 0.5 %collective-permute-start.6 = (bf16[240,512]{1,0:T(8,128)(2,1)S(1)}, bf16[240,512]{1,0:T(8,128)(2,1)S(1)}, u32[]{:S(2)}, u32[]{:S(2)}) collective-permute-start(bf16[240,512]{1,0:T(8,128)(2,1)S(1)} %collective-permute-done.5.refs_6_.refs_4_), channel_id=1, source_target_pairs={{0,2},{2,0},{4,6},{6,4},{8,10},{10,8},{12,14},{14,12},{16,18},{18,... | collective-permute-start | bytes 737288 | tf_op jit(solution)/shard_map/ppermute | solution.py:393
  24.3 0.0 collective-permute-start.4
  24.3 0.0 collective-permute-done.3.refs_3_.refs_1_
  24.3 1.0 %collective-permute-done.8.refs_9_.refs_7_ = bf16[240,512]{1,0:T(8,128)(2,1)S(1)} collective-permute-done((bf16[240,512]{1,0:T(8,128)(2,1)S(1)}, bf16[240,512]{1,0:T(8,128)(2,1)S(1)}, u32[]{:S(2)}, u32[]{:S(2)}) %collective-permute-start.8) | collective-permute-done | bytes 245792 | tf_op jit(solution)/shard_map/ppermute | solution.py:393
  25.3 0.4 collective-permute-done.6.refs_7_.refs_5_
  25.7 0.4 collective-permute-done.4.refs_5_.refs_3_
  26.0 2.3 %prefill_partials.1 = (bf16[48,1152]{1,0:T(8,128)(2,1)S(1)}, bf16[48,1152]{1,0:T(8,128)(2,1)S(1)}) custom-call(s32[8,128]{1,0:T(8,128)S(1)} %broadcast_in_dim.3.off_ref, bf16[32,1024]{1,0:T(8,128)(2,1)S(1)} %get-tuple-element.24.refs_0_, bf16[32,1024]{1,0:T(8,128)(2,1)S(1)} %collective-permute-done.1.refs_1_, ...), custom_call_target="tpu_custom_call" | custom-call | flops 335544320 | bytes 4194304 | tf_op jit(solution)/shard_map/prefill_partials/pallas_call | solution.py:287
  28.3 2.8 %collective-permute-start.9 = (bf16[48,1152]{1,0:T(8,128)(2,1)S(1)}, bf16[48,1152]{1,0:T(8,128)(2,1)S(1)}, u32[]{:S(2)}, u32[]{:S(2)}) collective-permute-start(bf16[48,1152]{1,0:T(8,128)(2,1)S(1)} %get-tuple-element.30), channel_id=1, source_target_pairs={{0,16},{2,18},{4,20},{6,22},{8,24},{10,26},{12,28},{14,30},{16,0},... | collective-permute-start | bytes 331784 | tf_op jit(solution)/shard_map/ppermute | solution.py:393
  31.1 5.7 %collective-permute-done.9.refs_1_ = bf16[48,1152]{1,0:T(8,128)(2,1)S(1)} collective-permute-done((bf16[48,1152]{1,0:T(8,128)(2,1)S(1)}, bf16[48,1152]{1,0:T(8,128)(2,1)S(1)}, u32[]{:S(2)}, u32[]{:S(2)}) %collective-permute-start.9) | collective-permute-done | bytes 110624 | tf_op jit(solution)/shard_map/ppermute | solution.py:393
  36.8 0.3 join_parts.1.refs_0_
  37.1 1.7 %collective-permute-start.10 = (bf16[48,1024]{1,0:T(8,128)(2,1)S(1)}, bf16[48,1024]{1,0:T(8,128)(2,1)S(1)}, u32[]{:S(2)}, u32[]{:S(2)}) collective-permute-start(bf16[48,1024]{1,0:T(8,128)(2,1)S(1)} %join_parts.1.refs_0_), channel_id=1, source_target_pairs={{0,1},{1,0},{2,3},{3,2},{4,5},{5,4},{6,7},{7,6},{8,9},{9,8},{10,11... | collective-permute-start | bytes 294920 | tf_op jit(solution)/shard_map/ppermute | solution.py:427
  38.8 1.7 %update_cache.1 = bf16[1,128,512]{2,1,0:T(8,128)(2,1)} custom-call(s32[8,128]{1,0:T(8,128)S(1)} %broadcast_in_dim.3.off_ref, bf16[1,128,512]{2,1,0:T(8,128)(2,1)} %cache_hbm.3, bf16[240,512]{1,0:T(8,128)(2,1)S(1)} %constant_dynamic-update-slice_fusion.refs_2_.refs_0_, bf16[240,512]{1,0:T(8,128)(2,1)S(1)} %collective-permute-done.3.refs_3_.refs_1_, ...), custom_call_target="tpu_custom_call" | custom-call | tf_op jit(solution)/shard_map/update_cache/pallas_call | solution.py:334
  40.5 1.3 %collective-permute-done.10.refs_1_ = bf16[48,1024]{1,0:T(8,128)(2,1)S(1)} collective-permute-done((bf16[48,1024]{1,0:T(8,128)(2,1)S(1)}, bf16[48,1024]{1,0:T(8,128)(2,1)S(1)}, u32[]{:S(2)}, u32[]{:S(2)}) %collective-permute-start.10) | collective-permute-done | bytes 98336 | tf_op jit(solution)/shard_map/ppermute | solution.py:427
  41.8 0.8 %route_outputs.1 = (bf16[1,32,1024]{2,1,0:T(8,128)(2,1)}, bf16[16,1024]{1,0:T(8,128)(2,1)}) custom-call(f32[2,24,128]{2,1,0:T(8,128)S(1)} %get-tuple-element.19.route_ref, bf16[48,1024]{1,0:T(8,128)(2,1)S(1)} %join_parts.1.refs_0_, bf16[48,1024]{1,0:T(8,128)(2,1)S(1)} %collective-permute-done.10.refs_1_), custom_call_target="tpu_custom_call" | custom-call | tf_op jit(solution)/shard_map/route_outputs/pallas_call | solution.py:362
  (2 shorter events, 0.0 us)
Async XLA Ops:
  0.6 9.1 %collective-permute-start.1 = (bf16[32,1024]{1,0:T(8,128)(2,1)}, bf16[32,1024]{1,0:T(8,128)(2,1)S(1)}, u32[]{:S(2)}, u32[]{:S(2)}) collective-permute-start(bf16[32,1024]{1,0:T(8,128)(2,1)} %bitcast.4), channel_id=1, source_target_pairs={{0,16},{2,18},{4,20},{6,22},{8,24},{10,26},{12,28},{14,30},{16,0},... | collective-permute-start | bytes 196616 | tf_op jit(solution)/shard_map/ppermute | solution.py:393
  4.7 5.0 %collective-permute-start = (bf16[32,512]{1,0:T(8,128)(2,1)}, bf16[32,512]{1,0:T(8,128)(2,1)S(1)}, u32[]{:S(2)}, u32[]{:S(2)}) collective-permute-start(bf16[32,512]{1,0:T(8,128)(2,1)} %bitcast.5), channel_id=1, source_target_pairs={{0,16},{2,18},{4,20},{6,22},{8,24},{10,26},{12,28},{14,30},{16,0},... | collective-permute-start | bytes 98312 | tf_op jit(solution)/shard_map/ppermute | solution.py:393
  9.8 7.8 %collective-permute-start.2 = (bf16[240,512]{1,0:T(8,128)(2,1)S(1)}, bf16[240,512]{1,0:T(8,128)(2,1)S(1)}, u32[]{:S(2)}, u32[]{:S(2)}) collective-permute-start(bf16[240,512]{1,0:T(8,128)(2,1)S(1)} %constant_dynamic-update-slice_fusion.refs_2_.refs_0_), channel_id=1, source_target_pairs={{0,4},{2,6},{4,0},{6,2},{8,12},{10,14},{12,8},{14,10},{16,20},{18,... | collective-permute-start | bytes 737288 | tf_op jit(solution)/shard_map/ppermute | solution.py:393
  11.4 8.9 %collective-permute-start.5 = (bf16[240,512]{1,0:T(8,128)(2,1)S(1)}, bf16[240,512]{1,0:T(8,128)(2,1)S(1)}, u32[]{:S(2)}, u32[]{:S(2)}) collective-permute-start(bf16[240,512]{1,0:T(8,128)(2,1)S(1)} %constant_dynamic-update-slice_fusion.refs_2_.refs_0_), channel_id=1, source_target_pairs={{0,8},{2,10},{4,12},{6,14},{8,0},{10,2},{12,4},{14,6},{16,24},{18,... | collective-permute-start | bytes 737288 | tf_op jit(solution)/shard_map/ppermute | solution.py:393
  12.8 11.0 %collective-permute-start.7 = (bf16[240,512]{1,0:T(8,128)(2,1)S(1)}, bf16[240,512]{1,0:T(8,128)(2,1)S(1)}, u32[]{:S(2)}, u32[]{:S(2)}) collective-permute-start(bf16[240,512]{1,0:T(8,128)(2,1)S(1)} %constant_dynamic-update-slice_fusion.refs_2_.refs_0_), channel_id=1, source_target_pairs={{0,12},{2,14},{4,8},{6,10},{8,4},{10,6},{12,0},{14,2},{16,28},{18,... | collective-permute-start | bytes 737288 | tf_op jit(solution)/shard_map/ppermute | solution.py:393
  13.9 10.4 %collective-permute-start.3 = (bf16[240,512]{1,0:T(8,128)(2,1)S(1)}, bf16[240,512]{1,0:T(8,128)(2,1)S(1)}, u32[]{:S(2)}, u32[]{:S(2)}) collective-permute-start(bf16[240,512]{1,0:T(8,128)(2,1)S(1)} %constant_dynamic-update-slice_fusion.refs_2_.refs_0_), channel_id=1, source_target_pairs={{0,2},{2,0},{4,6},{6,4},{8,10},{10,8},{12,14},{14,12},{16,18},{18,... | collective-permute-start | bytes 737288 | tf_op jit(solution)/shard_map/ppermute | solution.py:393
  23.8 1.5 %collective-permute-start.8 = (bf16[240,512]{1,0:T(8,128)(2,1)S(1)}, bf16[240,512]{1,0:T(8,128)(2,1)S(1)}, u32[]{:S(2)}, u32[]{:S(2)}) collective-permute-start(bf16[240,512]{1,0:T(8,128)(2,1)S(1)} %collective-permute-done.7.refs_8_.refs_6_), channel_id=1, source_target_pairs={{0,2},{2,0},{4,6},{6,4},{8,10},{10,8},{12,14},{14,12},{16,18},{18,... | collective-permute-start | bytes 737288 | tf_op jit(solution)/shard_map/ppermute | solution.py:393
  23.8 1.9 %collective-permute-start.6 = (bf16[240,512]{1,0:T(8,128)(2,1)S(1)}, bf16[240,512]{1,0:T(8,128)(2,1)S(1)}, u32[]{:S(2)}, u32[]{:S(2)}) collective-permute-start(bf16[240,512]{1,0:T(8,128)(2,1)S(1)} %collective-permute-done.5.refs_6_.refs_4_), channel_id=1, source_target_pairs={{0,2},{2,0},{4,6},{6,4},{8,10},{10,8},{12,14},{14,12},{16,18},{18,... | collective-permute-start | bytes 737288 | tf_op jit(solution)/shard_map/ppermute | solution.py:393
  24.3 1.7 %collective-permute-start.4 = (bf16[240,512]{1,0:T(8,128)(2,1)S(1)}, bf16[240,512]{1,0:T(8,128)(2,1)S(1)}, u32[]{:S(2)}, u32[]{:S(2)}) collective-permute-start(bf16[240,512]{1,0:T(8,128)(2,1)S(1)} %collective-permute-done.2.refs_4_.refs_2_), channel_id=1, source_target_pairs={{0,2},{2,0},{4,6},{6,4},{8,10},{10,8},{12,14},{14,12},{16,18},{18,... | collective-permute-start | bytes 737288 | tf_op jit(solution)/shard_map/ppermute | solution.py:393
  28.3 8.5 %collective-permute-start.9 = (bf16[48,1152]{1,0:T(8,128)(2,1)S(1)}, bf16[48,1152]{1,0:T(8,128)(2,1)S(1)}, u32[]{:S(2)}, u32[]{:S(2)}) collective-permute-start(bf16[48,1152]{1,0:T(8,128)(2,1)S(1)} %get-tuple-element.30), channel_id=1, source_target_pairs={{0,16},{2,18},{4,20},{6,22},{8,24},{10,26},{12,28},{14,30},{16,0},... | collective-permute-start | bytes 331784 | tf_op jit(solution)/shard_map/ppermute | solution.py:393
  37.1 4.7 %collective-permute-start.10 = (bf16[48,1024]{1,0:T(8,128)(2,1)S(1)}, bf16[48,1024]{1,0:T(8,128)(2,1)S(1)}, u32[]{:S(2)}, u32[]{:S(2)}) collective-permute-start(bf16[48,1024]{1,0:T(8,128)(2,1)S(1)} %join_parts.1.refs_0_), channel_id=1, source_target_pairs={{0,1},{1,0},{2,3},{3,2},{4,5},{5,4},{6,7},{7,6},{8,9},{9,8},{10,11... | collective-permute-start | bytes 294920 | tf_op jit(solution)/shard_map/ppermute | solution.py:427

commit v7 on v6

--- a/solution.py
+++ b/solution.py
@@ -197,9 +197,9 @@
         copy.wait()
 
 
-def decode_partials(lengths, dealing, queries, new_rows, cache, pre_queries, pre_new, pre_cache, req, extra):
+def decode_partials(lengths, dealing, queries, new_rows, cache, pre_queries, pre_new, pre_cache, req):
     slots, ctx, width = cache.shape
-    rows = ctx + pre_new.shape[1] + (KEY_VALUE_HEADS + 1) * slots + extra
+    rows = ctx + pre_new.shape[1] + (KEY_VALUE_HEADS + 1) * slots
     inputs = (lengths, dealing, queries, new_rows, cache, pre_queries, pre_new, pre_cache)
     return pl.pallas_call(
         decode_kernel,
@@ -312,17 +312,22 @@
     )(*parts)
 
 
-def update_kernel(tokens, extra, off_ref, cache_hbm, *refs):
+def update_kernel(tokens, sets, off_ref, cache_hbm, near_ref, beside_ref, *refs):
     tables, (out_ref, cache_ref, sem) = refs[:KEY_SET], refs[-3:]
     load = pltpu.make_async_copy(cache_hbm.at[0], cache_ref, sem)
     load.start()
-    ctx, total = cache_ref.shape[0], tables[0].shape[0]
+    ctx = cache_ref.shape[0]
     me = lax.axis_index(BLK)
-    starts = [ctx] + list(range(total - extra, total, tokens))
-    rows = jnp.concatenate([t[pl.ds(start, tokens), :] for start in starts for t in tables], axis=0)
+    rows = [t[pl.ds(ctx, tokens), :] for t in tables]
+    rows = jnp.concatenate(rows + [near_ref[...], beside_ref[...]], axis=0)
     count = rows.shape[0]
     index = lax.broadcasted_iota(jnp.int32, (1, count), 1)
-    token = (me ^ (index // tokens)) * tokens + index % tokens
+    block = index // tokens
+    half = sets * KEY_SET // 2
+    far = block - KEY_SET
+    inner = far % half
+    distance = KEY_SET * (1 + inner % sets) + 2 * (inner // sets) + far // half
+    token = (me ^ jnp.where(block < KEY_SET, block, distance)) * tokens + index % tokens
     wanted = me * ctx + lax.broadcasted_iota(jnp.int32, (ctx, 1), 0) - off_ref[:1, :1]
     picked = dot(jnp.where(wanted == token, 1.0, 0.0).astype(BF16), rows).astype(BF16)
     inside = jnp.broadcast_to((wanted >= 0) & (wanted < count), cache_ref.shape)
@@ -330,16 +335,16 @@
     out_ref[0] = jnp.where(inside, picked, cache_ref[...])
 
 
-def update_cache(offset, cache, tables, tokens, extra):
+def update_cache(offset, cache, near, beside, tables, tokens, sets):
     return pl.pallas_call(
-        functools.partial(update_kernel, tokens, extra),
-        in_specs=[VMEM, HBM] + [VMEM] * len(tables),
+        functools.partial(update_kernel, tokens, sets),
+        in_specs=[VMEM, HBM] + [VMEM] * (2 + len(tables)),
         out_specs=VMEM,
         out_shape=jax.ShapeDtypeStruct(cache.shape, BF16),
         scratch_shapes=[pltpu.VMEM(cache.shape[1:], BF16), pltpu.SemaphoreType.DMA],
         compiler_params=pltpu.CompilerParams(vmem_limit_bytes=16 << 20),
         name="update_cache",
-    )(offset, pltpu.with_memory_space_constraint(cache, pltpu.HBM), *tables)
+    )(offset, pltpu.with_memory_space_constraint(cache, pltpu.HBM), near, beside, *tables)
 
 
 def route_kernel(count, route_ref, *refs):
@@ -392,9 +397,10 @@
     def swap(array, distance):
         return lax.ppermute(array, BLK, [(i, i ^ distance) for i in range(blk)])
 
+    def after(array, *marks):
+        return lax.optimization_barrier((array, *marks))[0]
+
     others = range(KEY_SET, blk, KEY_SET)
-    extra = len(others) * tokens
-    far_rows = [swap(new_prefill[0], k) for k in others]
     packs = [swap(prefill_queries[0], k) for k in others]
     decode_cache_out, table, queries, route = decode_partials(
         decode_lengths,
@@ -406,27 +412,32 @@
         new_prefill,
         prefill_cache,
         req,
-        extra,
-    )
-    far_rows, packs, table = lax.optimization_barrier((far_rows, packs, table))
-    for i, rows in enumerate(far_rows):
-        table = lax.dynamic_update_slice(table, rows, (table.shape[0] - extra + i * tokens, 0))
+    )
     lanes = [table] + [swap(table, k) for k in range(2, KEY_SET, 2)]
     offset = jnp.full((8, HEAD_SIZE), prefill_offsets[0], jnp.int32)
-    lanes[1], offset = lax.optimization_barrier((lanes[1], offset))
+    lanes[1], offset, *packs = lax.optimization_barrier((lanes[1], offset, *packs))
     for i in range(2, len(lanes)):
-        lanes[i], _ = lax.optimization_barrier((lanes[i], lanes[i - 1]))
+        lanes[i] = after(lanes[i], lanes[i - 1])
     tables = [t for lane in lanes for t in (lane, swap(lane, 1))]
 
     parts = prefill_partials(offset, [queries] + packs, tables, ctx, slots)
     attended = join_parts([parts[0]] + [swap(part, k * KEY_SET) for k, part in enumerate(parts) if k])
 
-    prefill_cache_out = update_cache(offset, prefill_cache, tables, tokens, extra)
+    own_rows = after(new_prefill[0], lanes[-1])
+    far = jnp.concatenate([swap(own_rows, k) for k in others], axis=0)
+    far = after(far, parts[0])
+    for k in range(2, KEY_SET, 2):
+        if k & (k - 1) == 0:
+            far = jnp.concatenate([far, swap(far, k)], axis=0)
+    prefill_cache_out = update_cache(
+        offset, prefill_cache, far, swap(far, 1), tables, tokens, len(others)
+    )
 
     if req == 2:
         held = [attended, lax.ppermute(attended, "req", [(0, 1), (1, 0)])]
     else:
         held = [lax.all_gather(attended, "req", axis=0)]
+    held[-1], prefill_cache_out = lax.optimization_barrier((held[-1], prefill_cache_out))
     prefill_out, decode_out = route_outputs(route, held, tokens, slots)
     return (prefill_out, decode_out, prefill_cache_out, decode_cache_out)
 

time: 42.7 us -> 40.7 us (0.953)
  waiting for transfers between devices: 20.6 us -> 12.9 us
  starting transfers between devices: 12.7 us -> 18.3 us
    ppermute x10 -> x13, waiting for transfers between devices: 19.3 us -> 11 us  [swap(): return lax.ppermute(array, BLK, [(i, i ^ distance) for i in range(blk)])]
    ppermute x10 -> x13, starting transfers between devices: 11.1 us -> 16.7 us  [swap(): return lax.ppermute(array, BLK, [(i, i ^ distance) for i in range(blk)])]
    ppermute x1, waiting for transfers between devices: 1.29 us -> 1.93 us  [per_device(): held = [attended, lax.ppermute(attended, 'req', [(0, 1), (1, 0)])]]
  transfers between devices with their start and end apart: 11 -> 14, of which waited for: 9 -> 5; matrix products, arithmetic and copies ran while one was open for 0% -> 0% of each run, Pallas kernels for 11% -> 10%
where the time goes in v7:
time: 40.7 us; the launch traced here: 40.5 us
  starting transfers between devices  18.3 us (45%)
  waiting for transfers between devices  12.9 us (32%)
  Pallas kernels  7.93 us (19%)
  between operations  1.38 us (3%)
    ppermute x13, starting transfers between devices, swap(): return lax.ppermute(array, BLK, [(i, i ^ distance) for i in range(blk)])  16.7 us
    ppermute x13, waiting for transfers between devices, swap(): return lax.ppermute(array, BLK, [(i, i ^ distance) for i in range(blk)])  11 us
    pallas_call x1, Pallas kernels, decode_partials(): pl.pallas_call(decode_kernel, in_specs=[HBM] * len(inputs), out_specs=[HB...  2.92 us
    pallas_call x1, Pallas kernels, prefill_partials(): pl.pallas_call(functools.partial(prefill_kernel, len(packs), ctx, slots),...  2.27 us
    ppermute x1, waiting for transfers between devices, per_device(): held = [attended, lax.ppermute(attended, 'req', [(0, 1), (1, 0)])]  1.93 us
    pallas_call x1, Pallas kernels, update_cache(): pl.pallas_call(functools.partial(update_kernel, tokens, sets), in_specs=[...  1.71 us
    ppermute x1, starting transfers between devices, per_device(): held = [attended, lax.ppermute(attended, 'req', [(0, 1), (1, 0)])]  1.6 us
  transfers between devices with their start and end apart: 14, of which 5 were waited for; matrix products, arithmetic and copies ran while one was open for 0% of the time, Pallas kernels for 10%

profile of v7, /device:TPU:0, one launch (start us, length us, event | category | flops | bytes accessed | tf_op | source)
XLA Modules:
  0.0 40.5 jit_solution(7417165296563614586)
XLA Ops:
  0.7 2.9 %decode_partials.1 = (bf16[16,128,512]{2,1,0:T(8,128)(2,1)}, bf16[208,512]{1,0:T(8,128)(2,1)S(1)}, bf16[32,1024]{1,0:T(8,128)(2,1)S(1)}, f32[2,24,128]{2,1,0:T(8,128)S(1)}) custom-call(s32[16]{0:T(128)} %len_hbm.1, s32[34]{0:T(128)} %deal_hbm.1, bf16[16,1024]{1,0:T(8,128)(2,1)} %q_hbm.1, bf16[16,512]{1,0:T(8,128)(2,1)} %new_hbm.1, ...), custom_call_target="tpu_custom_call" | custom-call | flops 8388608 | bytes 4194304 | tf_op jit(solution)/shard_map/decode_partials/pallas_call | solution.py:204
  3.6 3.0 %collective-permute-start = (bf16[208,512]{1,0:T(8,128)(2,1)S(1)}, bf16[208,512]{1,0:T(8,128)(2,1)S(1)}, u32[]{:S(2)}, u32[]{:S(2)}) collective-permute-start(bf16[208,512]{1,0:T(8,128)(2,1)S(1)} %get-tuple-element.22.refs_2_.refs_0_), channel_id=1, source_target_pairs={{0,4},{2,6},{4,0},{6,2},{8,12},{10,14},{12,8},{14,10},{16,20},{18,... | collective-permute-start | bytes 638984 | tf_op jit(solution)/shard_map/ppermute | solution.py:398
  6.6 1.6 %collective-permute-start.4 = (bf16[208,512]{1,0:T(8,128)(2,1)S(1)}, bf16[208,512]{1,0:T(8,128)(2,1)S(1)}, u32[]{:S(2)}, u32[]{:S(2)}) collective-permute-start(bf16[208,512]{1,0:T(8,128)(2,1)S(1)} %get-tuple-element.22.refs_2_.refs_0_), channel_id=1, source_target_pairs={{0,8},{2,10},{4,12},{6,14},{8,0},{10,2},{12,4},{14,6},{16,24},{18,... | collective-permute-start | bytes 638984 | tf_op jit(solution)/shard_map/ppermute | solution.py:398
  8.1 0.0 collective-permute-start.6
  8.1 3.0 %collective-permute-start.1 = (bf16[32,1024]{1,0:T(8,128)(2,1)S(1)}, bf16[32,1024]{1,0:T(8,128)(2,1)S(1)}, u32[]{:S(2)}, u32[]{:S(2)}) collective-permute-start(bf16[32,1024]{1,0:T(8,128)(2,1)S(1)} %bitcast.4), channel_id=1, source_target_pairs={{0,16},{2,18},{4,20},{6,22},{8,24},{10,26},{12,28},{14,30},{16,0},... | collective-permute-start | bytes 196616 | tf_op jit(solution)/shard_map/ppermute | solution.py:398
  11.2 0.0 collective-permute-start.2
  11.8 6.5 %collective-permute-done.1.refs_1_ = bf16[32,1024]{1,0:T(8,128)(2,1)S(1)} collective-permute-done((bf16[32,1024]{1,0:T(8,128)(2,1)S(1)}, bf16[32,1024]{1,0:T(8,128)(2,1)S(1)}, u32[]{:S(2)}, u32[]{:S(2)}) %collective-permute-start.1) | collective-permute-done | bytes 65568 | tf_op jit(solution)/shard_map/ppermute | solution.py:398
  18.3 0.0 collective-permute-done.refs_4_.refs_2_
  18.3 0.0 collective-permute-done.4.refs_6_.refs_4_
  18.3 0.7 %collective-permute-done.6.refs_8_.refs_6_ = bf16[208,512]{1,0:T(8,128)(2,1)S(1)} collective-permute-done((bf16[208,512]{1,0:T(8,128)(2,1)S(1)}, bf16[208,512]{1,0:T(8,128)(2,1)S(1)}, u32[]{:S(2)}, u32[]{:S(2)}) %collective-permute-start.6) | collective-permute-done | bytes 213024 | tf_op jit(solution)/shard_map/ppermute | solution.py:398
  19.0 0.0 collective-permute-start.7
  19.1 0.5 %collective-permute-start.5 = (bf16[208,512]{1,0:T(8,128)(2,1)S(1)}, bf16[208,512]{1,0:T(8,128)(2,1)S(1)}, u32[]{:S(2)}, u32[]{:S(2)}) collective-permute-start(bf16[208,512]{1,0:T(8,128)(2,1)S(1)} %collective-permute-done.4.refs_6_.refs_4_), channel_id=1, source_target_pairs={{0,2},{2,0},{4,6},{6,4},{8,10},{10,8},{12,14},{14,12},{16,18},{18,... | collective-permute-start | bytes 638984 | tf_op jit(solution)/shard_map/ppermute | solution.py:398
  19.6 0.0 collective-permute-start.3
  19.6 2.8 %collective-permute-start.10 = (bf16[32,512]{1,0:T(8,128)(2,1)S(1)}, bf16[32,512]{1,0:T(8,128)(2,1)S(1)}, u32[]{:S(2)}, u32[]{:S(2)}) collective-permute-start(bf16[32,512]{1,0:T(8,128)(2,1)S(1)} %bitcast.5), channel_id=1, source_target_pairs={{0,16},{2,18},{4,20},{6,22},{8,24},{10,26},{12,28},{14,30},{16,0},... | collective-permute-start | bytes 98312 | tf_op jit(solution)/shard_map/ppermute | solution.py:398
  22.4 0.0 collective-permute-done.2.refs_3_.refs_1_
  22.4 0.0 collective-permute-done.7.refs_9_.refs_7_
  22.4 0.0 collective-permute-done.5.refs_7_.refs_5_
  22.4 0.0 collective-permute-done.3.refs_5_.refs_3_
  22.4 2.3 %prefill_partials.1 = (bf16[48,1152]{1,0:T(8,128)(2,1)S(1)}, bf16[48,1152]{1,0:T(8,128)(2,1)S(1)}) custom-call(s32[8,128]{1,0:T(8,128)S(1)} %broadcast_in_dim.3.off_ref, bf16[32,1024]{1,0:T(8,128)(2,1)S(1)} %get-tuple-element.24.refs_0_, bf16[32,1024]{1,0:T(8,128)(2,1)S(1)} %collective-permute-done.1.refs_1_, ...), custom_call_target="tpu_custom_call" | custom-call | flops 335544320 | bytes 4194304 | tf_op jit(solution)/shard_map/prefill_partials/pallas_call | solution.py:287
  24.7 0.0 collective-permute-done.10
  24.7 1.3 %collective-permute-start.11 = (bf16[32,512]{1,0:T(8,128)(2,1)S(1)}, bf16[32,512]{1,0:T(8,128)(2,1)S(1)}, u32[]{:S(2)}, u32[]{:S(2)}) collective-permute-start(bf16[32,512]{1,0:T(8,128)(2,1)S(1)} %collective-permute-done.10), channel_id=1, source_target_pairs={{0,4},{2,6},{4,0},{6,2},{8,12},{10,14},{12,8},{14,10},{16,20},{18,... | collective-permute-start | bytes 98312 | tf_op jit(solution)/shard_map/ppermute | solution.py:398
  26.0 1.9 %collective-permute-start.8 = (bf16[48,1152]{1,0:T(8,128)(2,1)S(1)}, bf16[48,1152]{1,0:T(8,128)(2,1)S(1)}, u32[]{:S(2)}, u32[]{:S(2)}) collective-permute-start(bf16[48,1152]{1,0:T(8,128)(2,1)S(1)} %get-tuple-element.30), channel_id=1, source_target_pairs={{0,16},{2,18},{4,20},{6,22},{8,24},{10,26},{12,28},{14,30},{16,0},... | collective-permute-start | bytes 331784 | tf_op jit(solution)/shard_map/ppermute | solution.py:398
  27.9 0.8 %collective-permute-done.11 = bf16[32,512]{1,0:T(8,128)(2,1)S(1)} collective-permute-done((bf16[32,512]{1,0:T(8,128)(2,1)S(1)}, bf16[32,512]{1,0:T(8,128)(2,1)S(1)}, u32[]{:S(2)}, u32[]{:S(2)}) %collective-permute-start.11) | collective-permute-done | bytes 32800 | tf_op jit(solution)/shard_map/ppermute | solution.py:398
  28.7 2.6 %collective-permute-start.12 = (bf16[64,512]{1,0:T(8,128)(2,1)S(1)}, bf16[64,512]{1,0:T(8,128)(2,1)S(1)}, u32[]{:S(2)}, u32[]{:S(2)}) collective-permute-start(bf16[64,512]{1,0:T(8,128)(2,1)S(1)} %pad_maximum_fusion), channel_id=1, source_target_pairs={{0,8},{2,10},{4,12},{6,14},{8,0},{10,2},{12,4},{14,6},{16,24},{18,... | collective-permute-start | bytes 196616 | tf_op jit(solution)/shard_map/ppermute | solution.py:398
  31.2 3.0 %collective-permute-done.12 = bf16[64,512]{1,0:T(8,128)(2,1)S(1)} collective-permute-done((bf16[64,512]{1,0:T(8,128)(2,1)S(1)}, bf16[64,512]{1,0:T(8,128)(2,1)S(1)}, u32[]{:S(2)}, u32[]{:S(2)}) %collective-permute-start.12) | collective-permute-done | bytes 65568 | tf_op jit(solution)/shard_map/ppermute | solution.py:398
  34.2 0.0 collective-permute-done.8.refs_1_
  34.2 0.3 join_parts.1.refs_0_
  34.5 1.6 %collective-permute-start.9 = (bf16[48,1024]{1,0:T(8,128)(2,1)S(1)}, bf16[48,1024]{1,0:T(8,128)(2,1)S(1)}, u32[]{:S(2)}, u32[]{:S(2)}) collective-permute-start(bf16[48,1024]{1,0:T(8,128)(2,1)S(1)} %join_parts.1.refs_0_), channel_id=1, source_target_pairs={{0,1},{1,0},{2,3},{3,2},{4,5},{5,4},{6,7},{7,6},{8,9},{9,8},{10,11... | collective-permute-start | bytes 294920 | tf_op jit(solution)/shard_map/ppermute | solution.py:437
  36.1 0.0 collective-permute-done.13.beside_ref
  36.1 1.7 %update_cache.1 = bf16[1,128,512]{2,1,0:T(8,128)(2,1)} custom-call(s32[8,128]{1,0:T(8,128)S(1)} %broadcast_in_dim.3.off_ref, bf16[1,128,512]{2,1,0:T(8,128)(2,1)} %cache_hbm.3, bf16[128,512]{1,0:T(8,128)(2,1)S(1)} %constant_dynamic-update-slice_fusion.near_ref, bf16[128,512]{1,0:T(8,128)(2,1)S(1)} %collective-permute-done.13.beside_ref, ...), custom_call_target="tpu_custom_call" | custom-call | tf_op jit(solution)/shard_map/update_cache/pallas_call | solution.py:339
  37.8 1.9 %collective-permute-done.9.refs_1_ = bf16[48,1024]{1,0:T(8,128)(2,1)S(1)} collective-permute-done((bf16[48,1024]{1,0:T(8,128)(2,1)S(1)}, bf16[48,1024]{1,0:T(8,128)(2,1)S(1)}, u32[]{:S(2)}, u32[]{:S(2)}) %collective-permute-start.9) | collective-permute-done | bytes 98336 | tf_op jit(solution)/shard_map/ppermute | solution.py:437
  39.8 0.8 %route_outputs.1 = (bf16[1,32,1024]{2,1,0:T(8,128)(2,1)}, bf16[16,1024]{1,0:T(8,128)(2,1)}) custom-call(f32[2,24,128]{2,1,0:T(8,128)S(1)} %get-tuple-element.21.route_ref, bf16[48,1024]{1,0:T(8,128)(2,1)S(1)} %join_parts.1.refs_0_, bf16[48,1024]{1,0:T(8,128)(2,1)S(1)} %collective-permute-done.9.refs_1_), custom_call_target="tpu_custom_call" | custom-call | tf_op jit(solution)/shard_map/route_outputs/pallas_call | solution.py:367
  (10 shorter events, 0.0 us)
Async XLA Ops:
  0.6 18.9 %copy-start.1 = (bf16[1,32,512]{2,1,0:T(8,128)(2,1)S(1)}, bf16[1,32,512]{2,1,0:T(8,128)(2,1)}, u32[]{:S(2)}) copy-start(bf16[1,32,512]{2,1,0:T(8,128)(2,1)} %pre_new_hbm.1) | copy-start | bytes 98308
  0.6 7.5 %copy-start = (bf16[1,32,1024]{2,1,0:T(8,128)(2,1)S(1)}, bf16[1,32,1024]{2,1,0:T(8,128)(2,1)}, u32[]{:S(2)}) copy-start(bf16[1,32,1024]{2,1,0:T(8,128)(2,1)} %pre_q_hbm.1) | copy-start | bytes 196612
  3.6 14.8 %collective-permute-start = (bf16[208,512]{1,0:T(8,128)(2,1)S(1)}, bf16[208,512]{1,0:T(8,128)(2,1)S(1)}, u32[]{:S(2)}, u32[]{:S(2)}) collective-permute-start(bf16[208,512]{1,0:T(8,128)(2,1)S(1)} %get-tuple-element.22.refs_2_.refs_0_), channel_id=1, source_target_pairs={{0,4},{2,6},{4,0},{6,2},{8,12},{10,14},{12,8},{14,10},{16,20},{18,... | collective-permute-start | bytes 638984 | tf_op jit(solution)/shard_map/ppermute | solution.py:398
  6.6 11.8 %collective-permute-start.4 = (bf16[208,512]{1,0:T(8,128)(2,1)S(1)}, bf16[208,512]{1,0:T(8,128)(2,1)S(1)}, u32[]{:S(2)}, u32[]{:S(2)}) collective-permute-start(bf16[208,512]{1,0:T(8,128)(2,1)S(1)} %get-tuple-element.22.refs_2_.refs_0_), channel_id=1, source_target_pairs={{0,8},{2,10},{4,12},{6,14},{8,0},{10,2},{12,4},{14,6},{16,24},{18,... | collective-permute-start | bytes 638984 | tf_op jit(solution)/shard_map/ppermute | solution.py:398
  8.1 10.9 %collective-permute-start.6 = (bf16[208,512]{1,0:T(8,128)(2,1)S(1)}, bf16[208,512]{1,0:T(8,128)(2,1)S(1)}, u32[]{:S(2)}, u32[]{:S(2)}) collective-permute-start(bf16[208,512]{1,0:T(8,128)(2,1)S(1)} %get-tuple-element.22.refs_2_.refs_0_), channel_id=1, source_target_pairs={{0,12},{2,14},{4,8},{6,10},{8,4},{10,6},{12,0},{14,2},{16,28},{18,... | collective-permute-start | bytes 638984 | tf_op jit(solution)/shard_map/ppermute | solution.py:398
  8.1 10.2 %collective-permute-start.1 = (bf16[32,1024]{1,0:T(8,128)(2,1)S(1)}, bf16[32,1024]{1,0:T(8,128)(2,1)S(1)}, u32[]{:S(2)}, u32[]{:S(2)}) collective-permute-start(bf16[32,1024]{1,0:T(8,128)(2,1)S(1)} %bitcast.4), channel_id=1, source_target_pairs={{0,16},{2,18},{4,20},{6,22},{8,24},{10,26},{12,28},{14,30},{16,0},... | collective-permute-start | bytes 196616 | tf_op jit(solution)/shard_map/ppermute | solution.py:398
  11.2 11.2 %collective-permute-start.2 = (bf16[208,512]{1,0:T(8,128)(2,1)S(1)}, bf16[208,512]{1,0:T(8,128)(2,1)S(1)}, u32[]{:S(2)}, u32[]{:S(2)}) collective-permute-start(bf16[208,512]{1,0:T(8,128)(2,1)S(1)} %get-tuple-element.22.refs_2_.refs_0_), channel_id=1, source_target_pairs={{0,2},{2,0},{4,6},{6,4},{8,10},{10,8},{12,14},{14,12},{16,18},{18,... | collective-permute-start | bytes 638984 | tf_op jit(solution)/shard_map/ppermute | solution.py:398
  19.0 3.3 %collective-permute-start.7 = (bf16[208,512]{1,0:T(8,128)(2,1)S(1)}, bf16[208,512]{1,0:T(8,128)(2,1)S(1)}, u32[]{:S(2)}, u32[]{:S(2)}) collective-permute-start(bf16[208,512]{1,0:T(8,128)(2,1)S(1)} %collective-permute-done.6.refs_8_.refs_6_), channel_id=1, source_target_pairs={{0,2},{2,0},{4,6},{6,4},{8,10},{10,8},{12,14},{14,12},{16,18},{18,... | collective-permute-start | bytes 638984 | tf_op jit(solution)/shard_map/ppermute | solution.py:398
  19.1 3.3 %collective-permute-start.5 = (bf16[208,512]{1,0:T(8,128)(2,1)S(1)}, bf16[208,512]{1,0:T(8,128)(2,1)S(1)}, u32[]{:S(2)}, u32[]{:S(2)}) collective-permute-start(bf16[208,512]{1,0:T(8,128)(2,1)S(1)} %collective-permute-done.4.refs_6_.refs_4_), channel_id=1, source_target_pairs={{0,2},{2,0},{4,6},{6,4},{8,10},{10,8},{12,14},{14,12},{16,18},{18,... | collective-permute-start | bytes 638984 | tf_op jit(solution)/shard_map/ppermute | solution.py:398
  19.6 2.8 %collective-permute-start.3 = (bf16[208,512]{1,0:T(8,128)(2,1)S(1)}, bf16[208,512]{1,0:T(8,128)(2,1)S(1)}, u32[]{:S(2)}, u32[]{:S(2)}) collective-permute-start(bf16[208,512]{1,0:T(8,128)(2,1)S(1)} %collective-permute-done.refs_4_.refs_2_), channel_id=1, source_target_pairs={{0,2},{2,0},{4,6},{6,4},{8,10},{10,8},{12,14},{14,12},{16,18},{18,... | collective-permute-start | bytes 638984 | tf_op jit(solution)/shard_map/ppermute | solution.py:398
  19.6 5.1 %collective-permute-start.10 = (bf16[32,512]{1,0:T(8,128)(2,1)S(1)}, bf16[32,512]{1,0:T(8,128)(2,1)S(1)}, u32[]{:S(2)}, u32[]{:S(2)}) collective-permute-start(bf16[32,512]{1,0:T(8,128)(2,1)S(1)} %bitcast.5), channel_id=1, source_target_pairs={{0,16},{2,18},{4,20},{6,22},{8,24},{10,26},{12,28},{14,30},{16,0},... | collective-permute-start | bytes 98312 | tf_op jit(solution)/shard_map/ppermute | solution.py:398
  24.7 4.0 %collective-permute-start.11 = (bf16[32,512]{1,0:T(8,128)(2,1)S(1)}, bf16[32,512]{1,0:T(8,128)(2,1)S(1)}, u32[]{:S(2)}, u32[]{:S(2)}) collective-permute-start(bf16[32,512]{1,0:T(8,128)(2,1)S(1)} %collective-permute-done.10), channel_id=1, source_target_pairs={{0,4},{2,6},{4,0},{6,2},{8,12},{10,14},{12,8},{14,10},{16,20},{18,... | collective-permute-start | bytes 98312 | tf_op jit(solution)/shard_map/ppermute | solution.py:398
  26.0 8.2 %collective-permute-start.8 = (bf16[48,1152]{1,0:T(8,128)(2,1)S(1)}, bf16[48,1152]{1,0:T(8,128)(2,1)S(1)}, u32[]{:S(2)}, u32[]{:S(2)}) collective-permute-start(bf16[48,1152]{1,0:T(8,128)(2,1)S(1)} %get-tuple-element.30), channel_id=1, source_target_pairs={{0,16},{2,18},{4,20},{6,22},{8,24},{10,26},{12,28},{14,30},{16,0},... | collective-permute-start | bytes 331784 | tf_op jit(solution)/shard_map/ppermute | solution.py:398
  28.7 5.5 %collective-permute-start.12 = (bf16[64,512]{1,0:T(8,128)(2,1)S(1)}, bf16[64,512]{1,0:T(8,128)(2,1)S(1)}, u32[]{:S(2)}, u32[]{:S(2)}) collective-permute-start(bf16[64,512]{1,0:T(8,128)(2,1)S(1)} %pad_maximum_fusion), channel_id=1, source_target_pairs={{0,8},{2,10},{4,12},{6,14},{8,0},{10,2},{12,4},{14,6},{16,24},{18,... | collective-permute-start | bytes 196616 | tf_op jit(solution)/shard_map/ppermute | solution.py:398
  34.2 1.9 %collective-permute-start.13 = (bf16[128,512]{1,0:T(8,128)(2,1)S(1)}, bf16[128,512]{1,0:T(8,128)(2,1)S(1)}, u32[]{:S(2)}, u32[]{:S(2)}) collective-permute-start(bf16[128,512]{1,0:T(8,128)(2,1)S(1)} %constant_dynamic-update-slice_fusion.near_ref), channel_id=1, source_target_pairs={{0,2},{2,0},{4,6},{6,4},{8,10},{10,8},{12,14},{14,12},{16,18},{18,... | collective-permute-start | bytes 393224 | tf_op jit(solution)/shard_map/ppermute | solution.py:398
  34.5 5.3 %collective-permute-start.9 = (bf16[48,1024]{1,0:T(8,128)(2,1)S(1)}, bf16[48,1024]{1,0:T(8,128)(2,1)S(1)}, u32[]{:S(2)}, u32[]{:S(2)}) collective-permute-start(bf16[48,1024]{1,0:T(8,128)(2,1)S(1)} %join_parts.1.refs_0_), channel_id=1, source_target_pairs={{0,1},{1,0},{2,3},{3,2},{4,5},{5,4},{6,7},{7,6},{8,9},{9,8},{10,11... | collective-permute-start | bytes 294920 | tf_op jit(solution)/shard_map/ppermute | solution.py:437

commit v8 on v7

--- a/solution.py
+++ b/solution.py
@@ -16,6 +16,7 @@
 STATS = 128
 QUAD = 4
 KEY_SET = 8
+PART_ROWS = KEY_VALUE_HEADS + 1
 SCALE = HEAD_SIZE**-0.5
 MASKED = -1e30
 FLOOR = -1e20
@@ -86,10 +87,8 @@
     new_hbm,
     cache_hbm,
     pre_q_hbm,
-    pre_new_hbm,
-    pre_cache_hbm,
     out_hbm,
-    shared_ref,
+    part_ref,
     pre_q_ref,
     route_ref,
     lens,
@@ -103,23 +102,19 @@
     rows = GROUP * slots
     chunk = slots // CHUNKS
     base = lax.axis_index(BLK) * ctx
-    tokens = pre_new_hbm.shape[1]
-    first = ctx + tokens
     small = [
         (len_hbm, lens),
         (deal_hbm, deal),
         (q_hbm, query_ref),
         (new_hbm, new_ref),
         (pre_q_hbm.at[0], pre_q_ref),
-        (pre_cache_hbm.at[0], shared_ref.at[pl.ds(0, ctx), :]),
-        (pre_new_hbm.at[0], shared_ref.at[pl.ds(ctx, tokens), :]),
     ]
     small = [pltpu.make_async_copy(a, b, sems.at[i]) for i, (a, b) in enumerate(small)]
     loads, stores = [], []
     for c in range(CHUNKS):
         part = pl.ds(c * chunk, chunk)
-        loads.append(pltpu.make_async_copy(cache_hbm.at[part], table.at[part], sems.at[7 + c]))
-        stores.append(pltpu.make_async_copy(table.at[part], out_hbm.at[part], sems.at[7 + CHUNKS + c]))
+        loads.append(pltpu.make_async_copy(cache_hbm.at[part], table.at[part], sems.at[5 + c]))
+        stores.append(pltpu.make_async_copy(table.at[part], out_hbm.at[part], sems.at[5 + CHUNKS + c]))
     for copy in small + loads:
         copy.start()
     for copy in small:
@@ -188,26 +183,23 @@
         logs = jnp.where(seen, maxima + jnp.log(safe), MASKED)
         for h in range(GROUP):
             part = slice(h * slots, (h + 1) * slots)
-            shared_ref[pl.ds(first + g * slots, slots), pl.ds(h * HEAD_SIZE, HEAD_SIZE)] = normed[part]
+            part_ref[pl.ds(g * slots, slots), pl.ds(h * HEAD_SIZE, HEAD_SIZE)] = normed[part]
             columns.append(logs[part])
-    last = pl.ds(first + KEY_VALUE_HEADS * slots, slots)
-    shared_ref[last, pl.ds(0, STATS)] = stats_block(columns, slots)
-    shared_ref[last, pl.ds(STATS, KVW - STATS)] = jnp.zeros((slots, KVW - STATS), BF16)
+    put_stats(part_ref, columns, slots)
     for copy in stores:
         copy.wait()
 
 
-def decode_partials(lengths, dealing, queries, new_rows, cache, pre_queries, pre_new, pre_cache, req):
+def decode_partials(lengths, dealing, queries, new_rows, cache, pre_queries, req):
     slots, ctx, width = cache.shape
-    rows = ctx + pre_new.shape[1] + (KEY_VALUE_HEADS + 1) * slots
-    inputs = (lengths, dealing, queries, new_rows, cache, pre_queries, pre_new, pre_cache)
+    inputs = (lengths, dealing, queries, new_rows, cache, pre_queries)
     return pl.pallas_call(
         decode_kernel,
         in_specs=[HBM] * len(inputs),
         out_specs=[HBM, VMEM, VMEM, VMEM],
         out_shape=[
             pltpu.HBM(cache.shape, BF16),
-            pltpu.VMEM((rows, KVW), BF16),
+            pltpu.VMEM((PART_ROWS * slots, KVW), BF16),
             pltpu.VMEM(pre_queries.shape[1:], BF16),
             pltpu.VMEM((req, slots + 8, HEAD_SIZE), F32),
         ],
@@ -217,7 +209,7 @@
             pltpu.VMEM(queries.shape, BF16),
             pltpu.VMEM(new_rows.shape, BF16),
             pltpu.VMEM(cache.shape, BF16),
-            pltpu.SemaphoreType.DMA((7 + 2 * CHUNKS,)),
+            pltpu.SemaphoreType.DMA((5 + 2 * CHUNKS,)),
         ],
         compiler_params=pltpu.CompilerParams(vmem_limit_bytes=16 << 20),
         cost_estimate=pl.CostEstimate(
@@ -227,7 +219,47 @@
     )(*[pltpu.with_memory_space_constraint(x, pltpu.HBM) for x in inputs])
 
 
-def prefill_kernel(query_count, ctx, slots, off_ref, *refs):
+def put_stats(ref, columns, slots):
+    last = pl.ds(KEY_VALUE_HEADS * slots, slots)
+    ref[last, pl.ds(0, STATS)] = stats_block(columns, slots)
+    ref[last, pl.ds(STATS, KVW - STATS)] = jnp.zeros((slots, KVW - STATS), BF16)
+
+
+def decode_part(ref, slots):
+    blocks = [ref[pl.ds(g * slots, slots), :] for g in range(KEY_VALUE_HEADS)]
+    return jnp.concatenate(blocks + [ref[pl.ds(KEY_VALUE_HEADS * slots, slots), pl.ds(0, STATS)]], axis=1)
+
+
+def step_kernel(slots, own_ref, other_ref, *refs):
+    joined, logs = join([decode_part(own_ref, slots), decode_part(other_ref, slots)])
+    head = PART_ROWS * slots
+    rest = own_ref.shape[0] - head
+    out_ref = refs[0] if rest else refs[-1]
+    for g in range(KEY_VALUE_HEADS):
+        out_ref[pl.ds(g * slots, slots), :] = joined[:, g * KVW : (g + 1) * KVW]
+    put_stats(out_ref, [logs[:, h * HEAD_SIZE : h * HEAD_SIZE + 1] for h in range(QUERY_HEADS)], slots)
+    if not rest:
+        far_ref = refs[0]
+        out_ref[pl.ds(head, far_ref.shape[0]), :] = far_ref[...]
+        return
+    news_ref, at = (out_ref, head) if len(refs) == 1 else (refs[1], 0)
+    news_ref[pl.ds(at, rest), :] = own_ref[pl.ds(head, rest), :]
+    news_ref[pl.ds(at + rest, rest), :] = other_ref[pl.ds(head, rest), :]
+
+
+def join_step(own, other, slots, shapes, name, *extra):
+    return pl.pallas_call(
+        functools.partial(step_kernel, slots),
+        in_specs=[VMEM] * (2 + len(extra)),
+        out_specs=[VMEM] * len(shapes),
+        out_shape=[pltpu.VMEM((rows, KVW), BF16) for rows in shapes],
+        compiler_params=pltpu.CompilerParams(vmem_limit_bytes=16 << 20),
+        name=name,
+    )(own, other, *extra)
+
+
+def prefill_kernel(sets, ctx, off_ref, *refs):
+    query_count = len(sets)
     packs, tables, outs = refs[:query_count], refs[query_count:-query_count], refs[-query_count:]
     tokens = packs[0].shape[0]
     span = ctx + tokens
@@ -244,10 +276,10 @@
     lane = lax.broadcasted_iota(jnp.int32, (tokens, STATS), 1)
     stats = [jnp.zeros((tokens, STATS), F32) for _ in range(query_count)]
     for g in range(KEY_VALUE_HEADS):
-        keys = jnp.concatenate([t[pl.ds(0, span), pl.ds(g * HEAD_SIZE, HEAD_SIZE)] for t in tables], axis=0)
-        values = jnp.concatenate([t[pl.ds(0, span), pl.ds(KW + g * HEAD_SIZE, HEAD_SIZE)] for t in tables], axis=0)
+        keys = jnp.concatenate([t[:, pl.ds(g * HEAD_SIZE, HEAD_SIZE)] for t in tables], axis=0)
+        values = jnp.concatenate([t[:, pl.ds(KW + g * HEAD_SIZE, HEAD_SIZE)] for t in tables], axis=0)
         for k in range(query_count):
-            token = (me ^ (k * KEY_SET)) * tokens + in_block
+            token = (me ^ (sets[k] * KEY_SET)) * tokens + in_block
             query = jnp.concatenate(
                 [packs[k][:, pl.ds((g * GROUP + h) * HEAD_SIZE, HEAD_SIZE)] for h in range(GROUP)], axis=0
             )
@@ -262,33 +294,21 @@
             logs = jnp.where(seen, maxima + jnp.log(safe), MASKED)
             for h in range(GROUP):
                 part = slice(h * tokens, (h + 1) * tokens)
-                outs[k][pl.ds(0, tokens), pl.ds((g * GROUP + h) * HEAD_SIZE, HEAD_SIZE)] = normed[part]
+                outs[k][:, pl.ds((g * GROUP + h) * HEAD_SIZE, HEAD_SIZE)] = normed[part]
                 for term, value in enumerate(split3(logs[part])):
                     stats[k] = jnp.where(lane == term * QUERY_HEADS + g * GROUP + h, value, stats[k])
-    decodes = [
-        jnp.concatenate(
-            [t[pl.ds(span + g * slots, slots), :] for g in range(KEY_VALUE_HEADS)]
-            + [t[pl.ds(span + KEY_VALUE_HEADS * slots, slots), pl.ds(0, STATS)]],
-            axis=1,
-        )
-        for t in tables
-    ]
-    joined, logs = join(decodes)
-    joined_stats = stats_block([logs[:, h * HEAD_SIZE : h * HEAD_SIZE + 1] for h in range(QUERY_HEADS)], slots)
     for k in range(query_count):
-        outs[k][pl.ds(0, tokens), pl.ds(QW, STATS)] = stats[k].astype(BF16)
-        outs[k][pl.ds(tokens, slots), pl.ds(0, QW)] = joined
-        outs[k][pl.ds(tokens, slots), pl.ds(QW, STATS)] = joined_stats
-
-
-def prefill_partials(offset, packs, tables, ctx, slots):
+        outs[k][:, pl.ds(QW, STATS)] = stats[k].astype(BF16)
+
+
+def prefill_partials(offset, packs, tables, ctx, sets):
     tokens = packs[0].shape[0]
     pairs = len(packs) * tokens * KEY_SET * (ctx + tokens)
     return pl.pallas_call(
-        functools.partial(prefill_kernel, len(packs), ctx, slots),
+        functools.partial(prefill_kernel, sets, ctx),
         in_specs=[VMEM] * (1 + len(packs) + len(tables)),
         out_specs=[VMEM] * len(packs),
-        out_shape=[jax.ShapeDtypeStruct((tokens + slots, QW + STATS), BF16)] * len(packs),
+        out_shape=[jax.ShapeDtypeStruct((tokens, QW + STATS), BF16)] * len(packs),
         compiler_params=pltpu.CompilerParams(vmem_limit_bytes=32 << 20),
         cost_estimate=pl.CostEstimate(
             flops=4 * pairs * QW, bytes_accessed=4 << 20, transcendentals=pairs * QUERY_HEADS
@@ -297,19 +317,21 @@
     )(offset, *packs, *tables)
 
 
-def join_kernel(*refs):
-    refs[-1][...] = join([ref[...] for ref in refs[:-1]])[0]
-
-
-def join_parts(parts):
-    return pl.pallas_call(
-        join_kernel,
-        in_specs=[VMEM] * len(parts),
+def join_kernel(count, slots, *refs):
+    out_ref, tokens = refs[-1], refs[0].shape[0]
+    out_ref[pl.ds(0, tokens), :] = join([ref[...] for ref in refs[:count]])[0]
+    out_ref[pl.ds(tokens, slots), :] = join([decode_part(ref, slots) for ref in refs[count:-1]])[0]
+
+
+def join_parts(parts, decodes, slots):
+    return pl.pallas_call(
+        functools.partial(join_kernel, len(parts), slots),
+        in_specs=[VMEM] * (len(parts) + len(decodes)),
         out_specs=VMEM,
-        out_shape=jax.ShapeDtypeStruct((parts[0].shape[0], QW), BF16),
+        out_shape=jax.ShapeDtypeStruct((parts[0].shape[0] + slots, QW), BF16),
         compiler_params=pltpu.CompilerParams(vmem_limit_bytes=16 << 20),
         name="join_parts",
-    )(*parts)
+    )(*parts, *decodes)
 
 
 def update_kernel(tokens, sets, off_ref, cache_hbm, near_ref, beside_ref, *refs):
@@ -401,37 +423,35 @@
         return lax.optimization_barrier((array, *marks))[0]
 
     others = range(KEY_SET, blk, KEY_SET)
+    table = jnp.concatenate([prefill_cache[0], new_prefill[0]], axis=0)
+    lanes = [table] + [swap(table, k) for k in range(2, KEY_SET, 2)]
     packs = [swap(prefill_queries[0], k) for k in others]
-    decode_cache_out, table, queries, route = decode_partials(
-        decode_lengths,
-        dealing,
-        decode_queries,
-        new_decode,
-        decode_cache,
-        prefill_queries,
-        new_prefill,
-        prefill_cache,
-        req,
-    )
-    lanes = [table] + [swap(table, k) for k in range(2, KEY_SET, 2)]
+    far = jnp.concatenate([swap(new_prefill[0], k) for k in others], axis=0)
+
+    decode_cache_out, part, queries, route = decode_partials(
+        decode_lengths, dealing, decode_queries, new_decode, decode_cache, prefill_queries, req
+    )
+    head, rest = PART_ROWS * slots, far.shape[0]
+    (part,) = join_step(part, swap(part, 1), slots, [head + rest], "join_core", far)
+    part = after(part, *lanes[1:], *packs)
+    (part,) = join_step(part, swap(part, 2), slots, [head + 2 * rest], "join_x")
+    part, news = join_step(part, swap(part, 4), slots, [head, 4 * rest], "join_z")
+
     offset = jnp.full((8, HEAD_SIZE), prefill_offsets[0], jnp.int32)
-    lanes[1], offset, *packs = lax.optimization_barrier((lanes[1], offset, *packs))
+    lanes[1], offset = lax.optimization_barrier((lanes[1], offset))
     for i in range(2, len(lanes)):
         lanes[i] = after(lanes[i], lanes[i - 1])
     tables = [t for lane in lanes for t in (lane, swap(lane, 1))]
 
-    parts = prefill_partials(offset, [queries] + packs, tables, ctx, slots)
-    attended = join_parts([parts[0]] + [swap(part, k * KEY_SET) for k, part in enumerate(parts) if k])
-
-    own_rows = after(new_prefill[0], lanes[-1])
-    far = jnp.concatenate([swap(own_rows, k) for k in others], axis=0)
-    far = after(far, parts[0])
-    for k in range(2, KEY_SET, 2):
-        if k & (k - 1) == 0:
-            far = jnp.concatenate([far, swap(far, k)], axis=0)
-    prefill_cache_out = update_cache(
-        offset, prefill_cache, far, swap(far, 1), tables, tokens, len(others)
-    )
+    sent = prefill_partials(offset, packs, tables, ctx, [k // KEY_SET for k in others])
+    queries = after(queries, sent[0])
+    kept = prefill_partials(offset, [queries], tables, ctx, [0])
+    attended = join_parts(
+        [*kept] + [swap(p, k) for k, p in zip(others, sent)],
+        [part] + [swap(part, k) for k in others],
+        slots,
+    )
+    prefill_cache_out = update_cache(offset, prefill_cache, news, swap(news, 1), tables, tokens, len(others))
 
     if req == 2:
         held = [attended, lax.ppermute(attended, "req", [(0, 1), (1, 0)])]

time: 40.7 us -> 40.7 us (level)
  starting transfers between devices: 18.3 us -> 12.5 us
  waiting for transfers between devices: 12.9 us -> 17.2 us
  other arithmetic: 0.01 us -> 0.94 us
  Pallas kernels: 7.93 us -> 8.5 us
    ppermute x13 -> x15, starting transfers between devices: 16.7 us -> 10.8 us  [swap(): return lax.ppermute(array, BLK, [(i, i ^ distance) for i in range(blk)])]
    ppermute x13 -> x15, waiting for transfers between devices: 11 us -> 15.9 us  [swap(): return lax.ppermute(array, BLK, [(i, i ^ distance) for i in range(blk)])]
    concatenate x1, other arithmetic: 0.01 us -> 0.94 us  [per_device(): table = jnp.concatenate([prefill_cache[0], new_prefill[0]], axis=0)]
    pallas_call x2 -> x6, Pallas kernels: 2.54 us -> 3.25 us  [the longest x2 2.13 us: prefill_partials(): pl.pallas_call(functools.partial(prefill_kernel, sets, ctx), in_specs=[VM...]
    ppermute x1, waiting for transfers between devices: 1.93 us -> 1.25 us  [per_device(): held = [attended, lax.ppermute(attended, 'req', [(0, 1), (1, 0)])]]
  transfers between devices with their start and end apart: 14 -> 16, of which waited for: 5 -> 8; matrix products, arithmetic and copies ran while one was open for 0% -> 0% of each run, Pallas kernels for 10% -> 19%
where the time goes in v8:
time: 40.7 us; the launch traced here: 40.5 us
  waiting for transfers between devices  17.2 us (42%)
  starting transfers between devices  12.5 us (31%)
  Pallas kernels  8.5 us (21%)
  between operations  1.43 us (4%)
  other arithmetic  0.94 us (2%)
    ppermute x15, waiting for transfers between devices, swap(): return lax.ppermute(array, BLK, [(i, i ^ distance) for i in range(blk)])  15.9 us
    ppermute x15, starting transfers between devices, swap(): return lax.ppermute(array, BLK, [(i, i ^ distance) for i in range(blk)])  10.8 us
    pallas_call x1, Pallas kernels, decode_partials(): pl.pallas_call(decode_kernel, in_specs=[HBM] * len(inputs), out_specs=[HB...  2.77 us
    pallas_call x2, Pallas kernels, prefill_partials(): pl.pallas_call(functools.partial(prefill_kernel, sets, ctx), in_specs=[VM...  2.13 us
    pallas_call x1, Pallas kernels, update_cache(): pl.pallas_call(functools.partial(update_kernel, tokens, sets), in_specs=[...  1.71 us
    ppermute x1, starting transfers between devices, per_device(): held = [attended, lax.ppermute(attended, 'req', [(0, 1), (1, 0)])]  1.71 us
    ppermute x1, waiting for transfers between devices, per_device(): held = [attended, lax.ppermute(attended, 'req', [(0, 1), (1, 0)])]  1.25 us
    concatenate x1, other arithmetic, per_device(): table = jnp.concatenate([prefill_cache[0], new_prefill[0]], axis=0)  0.94 us
  transfers between devices with their start and end apart: 16, of which 8 were waited for; matrix products, arithmetic and copies ran while one was open for 0% of the time, Pallas kernels for 19%

profile of v8, /device:TPU:0, one launch (start us, length us, event | category | flops | bytes accessed | tf_op | source)
XLA Modules:
  0.0 40.5 jit_solution(17041033060932608621)
XLA Ops:
  0.6 0.9 %pad_maximum_fusion.refs_1_.refs_0_ = bf16[160,512]{1,0:T(8,128)(2,1)S(1)} fusion(bf16[32,512]{1,0:T(8,128)(2,1)} %bitcast.7, bf16[128,512]{1,0:T(8,128)(2,1)} %bitcast.5), kind=kLoop, calls=%fused_computation | loop fusion | flops 327680 | bytes 327680 | tf_op jit(solution)/shard_map/concatenate | solution.py:426
  1.6 3.0 %collective-permute-start = (bf16[160,512]{1,0:T(8,128)(2,1)S(1)}, bf16[160,512]{1,0:T(8,128)(2,1)S(1)}, u32[]{:S(2)}, u32[]{:S(2)}) collective-permute-start(bf16[160,512]{1,0:T(8,128)(2,1)S(1)} %pad_maximum_fusion.refs_1_.refs_0_), channel_id=1, source_target_pairs={{0,4},{2,6},{4,0},{6,2},{8,12},{10,14},{12,8},{14,10},{16,20},{18,... | collective-permute-start | bytes 491528 | tf_op jit(solution)/shard_map/ppermute | solution.py:420
  4.6 1.6 %collective-permute-start.4 = (bf16[160,512]{1,0:T(8,128)(2,1)S(1)}, bf16[160,512]{1,0:T(8,128)(2,1)S(1)}, u32[]{:S(2)}, u32[]{:S(2)}) collective-permute-start(bf16[160,512]{1,0:T(8,128)(2,1)S(1)} %pad_maximum_fusion.refs_1_.refs_0_), channel_id=1, source_target_pairs={{0,8},{2,10},{4,12},{6,14},{8,0},{10,2},{12,4},{14,6},{16,24},{18,... | collective-permute-start | bytes 491528 | tf_op jit(solution)/shard_map/ppermute | solution.py:420
  6.2 3.0 %collective-permute-start.1 = (bf16[32,1024]{1,0:T(8,128)(2,1)}, bf16[32,1024]{1,0:T(8,128)(2,1)S(1)}, u32[]{:S(2)}, u32[]{:S(2)}) collective-permute-start(bf16[32,1024]{1,0:T(8,128)(2,1)} %bitcast.6), channel_id=1, source_target_pairs={{0,16},{2,18},{4,20},{6,22},{8,24},{10,26},{12,28},{14,30},{16,0},... | collective-permute-start | bytes 196616 | tf_op jit(solution)/shard_map/ppermute | solution.py:420
  9.2 2.8 %decode_partials.1 = (bf16[16,128,512]{2,1,0:T(8,128)(2,1)}, bf16[48,512]{1,0:T(8,128)(2,1)S(1)}, bf16[32,1024]{1,0:T(8,128)(2,1)S(1)}, f32[2,24,128]{2,1,0:T(8,128)S(1)}) custom-call(s32[16]{0:T(128)} %len_hbm.1, s32[34]{0:T(128)} %deal_hbm.1, bf16[16,1024]{1,0:T(8,128)(2,1)} %q_hbm.1, bf16[16,512]{1,0:T(8,128)(2,1)} %new_hbm.1, ...), custom_call_target="tpu_custom_call" | custom-call | flops 8388608 | bytes 4194304 | tf_op jit(solution)/shard_map/decode_partials/pallas_call | solution.py:196
  12.0 0.1 collective-permute-start.9
  12.0 0.0 collective-permute-done.refs_3_.refs_2_
  12.1 0.1 collective-permute-start.10
  12.8 0.3 collective-permute-done.4.refs_5_.refs_4_
  13.1 0.2 collective-permute-start.2
  13.3 1.7 %collective-permute-done.6.refs_7_.refs_6_ = bf16[160,512]{1,0:T(8,128)(2,1)S(1)} collective-permute-done((bf16[160,512]{1,0:T(8,128)(2,1)S(1)}, bf16[160,512]{1,0:T(8,128)(2,1)S(1)}, u32[]{:S(2)}, u32[]{:S(2)}) %collective-permute-start.6) | collective-permute-done | bytes 163872 | tf_op jit(solution)/shard_map/ppermute | solution.py:420
  15.0 3.3 %collective-permute-done.10.refs_0_ = bf16[32,512]{1,0:T(8,128)(2,1)S(1)} collective-permute-done((bf16[32,512]{1,0:T(8,128)(2,1)S(1)}, bf16[32,512]{1,0:T(8,128)(2,1)S(1)}, u32[]{:S(2)}, u32[]{:S(2)}) %collective-permute-start.10) | collective-permute-done | bytes 32800 | tf_op jit(solution)/shard_map/ppermute | solution.py:420
  18.2 0.5 %collective-permute-start.3 = (bf16[160,512]{1,0:T(8,128)(2,1)S(1)}, bf16[160,512]{1,0:T(8,128)(2,1)S(1)}, u32[]{:S(2)}, u32[]{:S(2)}) collective-permute-start(bf16[160,512]{1,0:T(8,128)(2,1)S(1)} %collective-permute-done.refs_3_.refs_2_), channel_id=1, source_target_pairs={{0,2},{2,0},{4,6},{6,4},{8,10},{10,8},{12,14},{14,12},{16,18},{18,... | collective-permute-start | bytes 491528 | tf_op jit(solution)/shard_map/ppermute | solution.py:420
  18.8 0.3 join_core.1.own_ref
  19.1 0.2 collective-permute-start.11
  19.3 4.3 %collective-permute-done.11.other_ref = bf16[80,512]{1,0:T(8,128)(2,1)S(1)} collective-permute-done((bf16[80,512]{1,0:T(8,128)(2,1)S(1)}, bf16[80,512]{1,0:T(8,128)(2,1)S(1)}, u32[]{:S(2)}, u32[]{:S(2)}) %collective-permute-start.11) | collective-permute-done | bytes 81952 | tf_op jit(solution)/shard_map/ppermute | solution.py:420
  23.6 0.3 join_x.1.own_ref
  23.9 0.4 collective-permute-start.12
  24.3 1.1 %prefill_partials.2 = bf16[32,1152]{1,0:T(8,128)(2,1)S(1)} custom-call(s32[8,128]{1,0:T(8,128)S(1)} %broadcast_in_dim.3.off_ref, bf16[32,1024]{1,0:T(8,128)(2,1)S(1)} %collective-permute-done.1.refs_0_, bf16[160,512]{1,0:T(8,128)(2,1)S(1)} %pad_maximum_fusion.refs_1_.refs_0_, bf16[160,512]{1,0:T(8,128)(2,1)S(1)} %collective-permute-done.2.refs_2_.refs_1_, ...), custom_call_target="tpu_custom_call" | custom-call | flops 167772160 | bytes 4194304 | tf_op jit(solution)/shard_map/prefill_partials/pallas_call | solution.py:307
  25.3 1.6 %collective-permute-start.8 = (bf16[32,1152]{1,0:T(8,128)(2,1)S(1)}, bf16[32,1152]{1,0:T(8,128)(2,1)S(1)}, u32[]{:S(2)}, u32[]{:S(2)}) collective-permute-start(bf16[32,1152]{1,0:T(8,128)(2,1)S(1)} %prefill_partials.2), channel_id=1, source_target_pairs={{0,16},{2,18},{4,20},{6,22},{8,24},{10,26},{12,28},{14,30},{16,0},... | collective-permute-start | bytes 221192 | tf_op jit(solution)/shard_map/ppermute | solution.py:420
  26.9 2.5 %collective-permute-done.12.other_ref = bf16[112,512]{1,0:T(8,128)(2,1)S(1)} collective-permute-done((bf16[112,512]{1,0:T(8,128)(2,1)S(1)}, bf16[112,512]{1,0:T(8,128)(2,1)S(1)}, u32[]{:S(2)}, u32[]{:S(2)}) %collective-permute-start.12) | collective-permute-done | bytes 114720 | tf_op jit(solution)/shard_map/ppermute | solution.py:420
  29.5 0.3 join_z.1
  29.8 0.1 collective-permute-start.13
  29.9 0.1 collective-permute-start.15
  29.9 1.1 %prefill_partials.3.refs_0_ = bf16[32,1152]{1,0:T(8,128)(2,1)S(1)} custom-call(s32[8,128]{1,0:T(8,128)S(1)} %broadcast_in_dim.3.off_ref, bf16[32,1024]{1,0:T(8,128)(2,1)S(1)} %get-tuple-element.26.refs_0_, bf16[160,512]{1,0:T(8,128)(2,1)S(1)} %pad_maximum_fusion.refs_1_.refs_0_, bf16[160,512]{1,0:T(8,128)(2,1)S(1)} %collective-permute-done.2.refs_2_.refs_1_, ...), custom_call_target="tpu_custom_call" | custom-call | flops 167772160 | bytes 4194304 | tf_op jit(solution)/shard_map/prefill_partials/pallas_call | solution.py:307
  31.0 1.5 %collective-permute-done.8.refs_1_ = bf16[32,1152]{1,0:T(8,128)(2,1)S(1)} collective-permute-done((bf16[32,1152]{1,0:T(8,128)(2,1)S(1)}, bf16[32,1152]{1,0:T(8,128)(2,1)S(1)}, u32[]{:S(2)}, u32[]{:S(2)}) %collective-permute-start.8) | collective-permute-done | bytes 73760 | tf_op jit(solution)/shard_map/ppermute | solution.py:420
  32.5 2.3 %collective-permute-done.13.refs_3_ = bf16[48,512]{1,0:T(8,128)(2,1)S(1)} collective-permute-done((bf16[48,512]{1,0:T(8,128)(2,1)S(1)}, bf16[48,512]{1,0:T(8,128)(2,1)S(1)}, u32[]{:S(2)}, u32[]{:S(2)}) %collective-permute-start.13) | collective-permute-done | bytes 49184 | tf_op jit(solution)/shard_map/ppermute | solution.py:420
  34.8 0.3 join_parts.1.refs_0_
  35.1 1.7 %collective-permute-start.14 = (bf16[48,1024]{1,0:T(8,128)(2,1)S(1)}, bf16[48,1024]{1,0:T(8,128)(2,1)S(1)}, u32[]{:S(2)}, u32[]{:S(2)}) collective-permute-start(bf16[48,1024]{1,0:T(8,128)(2,1)S(1)} %join_parts.1.refs_0_), channel_id=1, source_target_pairs={{0,1},{1,0},{2,3},{3,2},{4,5},{5,4},{6,7},{7,6},{8,9},{9,8},{10,11... | collective-permute-start | bytes 294920 | tf_op jit(solution)/shard_map/ppermute | solution.py:457
  36.8 1.7 %update_cache.1 = bf16[1,128,512]{2,1,0:T(8,128)(2,1)} custom-call(s32[8,128]{1,0:T(8,128)S(1)} %broadcast_in_dim.3.off_ref, bf16[1,128,512]{2,1,0:T(8,128)(2,1)} %cache_hbm.3, bf16[128,512]{1,0:T(8,128)(2,1)S(1)} %get-tuple-element.30.near_ref, bf16[128,512]{1,0:T(8,128)(2,1)S(1)} %collective-permute-done.15.beside_ref, ...), custom_call_target="tpu_custom_call" | custom-call | tf_op jit(solution)/shard_map/update_cache/pallas_call | solution.py:361
  38.5 1.2 %collective-permute-done.14.refs_1_ = bf16[48,1024]{1,0:T(8,128)(2,1)S(1)} collective-permute-done((bf16[48,1024]{1,0:T(8,128)(2,1)S(1)}, bf16[48,1024]{1,0:T(8,128)(2,1)S(1)}, u32[]{:S(2)}, u32[]{:S(2)}) %collective-permute-start.14) | collective-permute-done | bytes 98336 | tf_op jit(solution)/shard_map/ppermute | solution.py:457
  39.8 0.8 %route_outputs.1 = (bf16[1,32,1024]{2,1,0:T(8,128)(2,1)}, bf16[16,1024]{1,0:T(8,128)(2,1)}) custom-call(f32[2,24,128]{2,1,0:T(8,128)S(1)} %get-tuple-element.20.route_ref, bf16[48,1024]{1,0:T(8,128)(2,1)S(1)} %join_parts.1.refs_0_, bf16[48,1024]{1,0:T(8,128)(2,1)S(1)} %collective-permute-done.14.refs_1_), custom_call_target="tpu_custom_call" | custom-call | tf_op jit(solution)/shard_map/route_outputs/pallas_call | solution.py:389
  (13 shorter events, 0.0 us)
Async XLA Ops:
  0.6 11.4 %copy-start = (bf16[1,32,512]{2,1,0:T(8,128)(2,1)S(1)}, bf16[1,32,512]{2,1,0:T(8,128)(2,1)}, u32[]{:S(2)}) copy-start(bf16[1,32,512]{2,1,0:T(8,128)(2,1)} %param.11) | copy-start | bytes 98308
  1.6 10.5 %collective-permute-start = (bf16[160,512]{1,0:T(8,128)(2,1)S(1)}, bf16[160,512]{1,0:T(8,128)(2,1)S(1)}, u32[]{:S(2)}, u32[]{:S(2)}) collective-permute-start(bf16[160,512]{1,0:T(8,128)(2,1)S(1)} %pad_maximum_fusion.refs_1_.refs_0_), channel_id=1, source_target_pairs={{0,4},{2,6},{4,0},{6,2},{8,12},{10,14},{12,8},{14,10},{16,20},{18,... | collective-permute-start | bytes 491528 | tf_op jit(solution)/shard_map/ppermute | solution.py:420
  4.6 8.5 %collective-permute-start.4 = (bf16[160,512]{1,0:T(8,128)(2,1)S(1)}, bf16[160,512]{1,0:T(8,128)(2,1)S(1)}, u32[]{:S(2)}, u32[]{:S(2)}) collective-permute-start(bf16[160,512]{1,0:T(8,128)(2,1)S(1)} %pad_maximum_fusion.refs_1_.refs_0_), channel_id=1, source_target_pairs={{0,8},{2,10},{4,12},{6,14},{8,0},{10,2},{12,4},{14,6},{16,24},{18,... | collective-permute-start | bytes 491528 | tf_op jit(solution)/shard_map/ppermute | solution.py:420
  6.2 8.8 %collective-permute-start.6 = (bf16[160,512]{1,0:T(8,128)(2,1)S(1)}, bf16[160,512]{1,0:T(8,128)(2,1)S(1)}, u32[]{:S(2)}, u32[]{:S(2)}) collective-permute-start(bf16[160,512]{1,0:T(8,128)(2,1)S(1)} %pad_maximum_fusion.refs_1_.refs_0_), channel_id=1, source_target_pairs={{0,12},{2,14},{4,8},{6,10},{8,4},{10,6},{12,0},{14,2},{16,28},{18,... | collective-permute-start | bytes 491528 | tf_op jit(solution)/shard_map/ppermute | solution.py:420
  6.2 12.9 %collective-permute-start.1 = (bf16[32,1024]{1,0:T(8,128)(2,1)}, bf16[32,1024]{1,0:T(8,128)(2,1)S(1)}, u32[]{:S(2)}, u32[]{:S(2)}) collective-permute-start(bf16[32,1024]{1,0:T(8,128)(2,1)} %bitcast.6), channel_id=1, source_target_pairs={{0,16},{2,18},{4,20},{6,22},{8,24},{10,26},{12,28},{14,30},{16,0},... | collective-permute-start | bytes 196616 | tf_op jit(solution)/shard_map/ppermute | solution.py:420
  12.0 6.3 %collective-permute-start.9 = (bf16[48,512]{1,0:T(8,128)(2,1)S(1)}, bf16[48,512]{1,0:T(8,128)(2,1)S(1)}, u32[]{:S(2)}, u32[]{:S(2)}) collective-permute-start(bf16[48,512]{1,0:T(8,128)(2,1)S(1)} %get-tuple-element.27.own_ref), channel_id=1, source_target_pairs={{0,2},{2,0},{4,6},{6,4},{8,10},{10,8},{12,14},{14,12},{16,18},{18,... | collective-permute-start | bytes 147464 | tf_op jit(solution)/shard_map/ppermute | solution.py:420
  12.1 6.2 %collective-permute-start.10 = (bf16[32,512]{1,0:T(8,128)(2,1)S(1)}, bf16[32,512]{1,0:T(8,128)(2,1)S(1)}, u32[]{:S(2)}, u32[]{:S(2)}) collective-permute-start(bf16[32,512]{1,0:T(8,128)(2,1)S(1)} %bitcast.8), channel_id=1, source_target_pairs={{0,16},{2,18},{4,20},{6,22},{8,24},{10,26},{12,28},{14,30},{16,0},... | collective-permute-start | bytes 98312 | tf_op jit(solution)/shard_map/ppermute | solution.py:420
  13.1 11.1 %collective-permute-start.2 = (bf16[160,512]{1,0:T(8,128)(2,1)S(1)}, bf16[160,512]{1,0:T(8,128)(2,1)S(1)}, u32[]{:S(2)}, u32[]{:S(2)}) collective-permute-start(bf16[160,512]{1,0:T(8,128)(2,1)S(1)} %pad_maximum_fusion.refs_1_.refs_0_), channel_id=1, source_target_pairs={{0,2},{2,0},{4,6},{6,4},{8,10},{10,8},{12,14},{14,12},{16,18},{18,... | collective-permute-start | bytes 491528 | tf_op jit(solution)/shard_map/ppermute | solution.py:420
  15.0 9.3 %collective-permute-start.5 = (bf16[160,512]{1,0:T(8,128)(2,1)S(1)}, bf16[160,512]{1,0:T(8,128)(2,1)S(1)}, u32[]{:S(2)}, u32[]{:S(2)}) collective-permute-start(bf16[160,512]{1,0:T(8,128)(2,1)S(1)} %collective-permute-done.4.refs_5_.refs_4_), channel_id=1, source_target_pairs={{0,2},{2,0},{4,6},{6,4},{8,10},{10,8},{12,14},{14,12},{16,18},{18,... | collective-permute-start | bytes 491528 | tf_op jit(solution)/shard_map/ppermute | solution.py:420
  18.2 6.0 %collective-permute-start.7 = (bf16[160,512]{1,0:T(8,128)(2,1)S(1)}, bf16[160,512]{1,0:T(8,128)(2,1)S(1)}, u32[]{:S(2)}, u32[]{:S(2)}) collective-permute-start(bf16[160,512]{1,0:T(8,128)(2,1)S(1)} %collective-permute-done.6.refs_7_.refs_6_), channel_id=1, source_target_pairs={{0,2},{2,0},{4,6},{6,4},{8,10},{10,8},{12,14},{14,12},{16,18},{18,... | collective-permute-start | bytes 491528 | tf_op jit(solution)/shard_map/ppermute | solution.py:420
  18.2 6.0 %collective-permute-start.3 = (bf16[160,512]{1,0:T(8,128)(2,1)S(1)}, bf16[160,512]{1,0:T(8,128)(2,1)S(1)}, u32[]{:S(2)}, u32[]{:S(2)}) collective-permute-start(bf16[160,512]{1,0:T(8,128)(2,1)S(1)} %collective-permute-done.refs_3_.refs_2_), channel_id=1, source_target_pairs={{0,2},{2,0},{4,6},{6,4},{8,10},{10,8},{12,14},{14,12},{16,18},{18,... | collective-permute-start | bytes 491528 | tf_op jit(solution)/shard_map/ppermute | solution.py:420
  19.1 4.5 %collective-permute-start.11 = (bf16[80,512]{1,0:T(8,128)(2,1)S(1)}, bf16[80,512]{1,0:T(8,128)(2,1)S(1)}, u32[]{:S(2)}, u32[]{:S(2)}) collective-permute-start(bf16[80,512]{1,0:T(8,128)(2,1)S(1)} %join_core.1.own_ref), channel_id=1, source_target_pairs={{0,4},{2,6},{4,0},{6,2},{8,12},{10,14},{12,8},{14,10},{16,20},{18,... | collective-permute-start | bytes 245768 | tf_op jit(solution)/shard_map/ppermute | solution.py:420
  23.9 5.6 %collective-permute-start.12 = (bf16[112,512]{1,0:T(8,128)(2,1)S(1)}, bf16[112,512]{1,0:T(8,128)(2,1)S(1)}, u32[]{:S(2)}, u32[]{:S(2)}) collective-permute-start(bf16[112,512]{1,0:T(8,128)(2,1)S(1)} %join_x.1.own_ref), channel_id=1, source_target_pairs={{0,8},{2,10},{4,12},{6,14},{8,0},{10,2},{12,4},{14,6},{16,24},{18,... | collective-permute-start | bytes 344072 | tf_op jit(solution)/shard_map/ppermute | solution.py:420
  25.3 7.2 %collective-permute-start.8 = (bf16[32,1152]{1,0:T(8,128)(2,1)S(1)}, bf16[32,1152]{1,0:T(8,128)(2,1)S(1)}, u32[]{:S(2)}, u32[]{:S(2)}) collective-permute-start(bf16[32,1152]{1,0:T(8,128)(2,1)S(1)} %prefill_partials.2), channel_id=1, source_target_pairs={{0,16},{2,18},{4,20},{6,22},{8,24},{10,26},{12,28},{14,30},{16,0},... | collective-permute-start | bytes 221192 | tf_op jit(solution)/shard_map/ppermute | solution.py:420
  29.8 5.1 %collective-permute-start.13 = (bf16[48,512]{1,0:T(8,128)(2,1)S(1)}, bf16[48,512]{1,0:T(8,128)(2,1)S(1)}, u32[]{:S(2)}, u32[]{:S(2)}) collective-permute-start(bf16[48,512]{1,0:T(8,128)(2,1)S(1)} %get-tuple-element.29.refs_2_), channel_id=1, source_target_pairs={{0,16},{2,18},{4,20},{6,22},{8,24},{10,26},{12,28},{14,30},{16,0},... | collective-permute-start | bytes 147464 | tf_op jit(solution)/shard_map/ppermute | solution.py:420
  29.9 7.0 %collective-permute-start.15 = (bf16[128,512]{1,0:T(8,128)(2,1)S(1)}, bf16[128,512]{1,0:T(8,128)(2,1)S(1)}, u32[]{:S(2)}, u32[]{:S(2)}) collective-permute-start(bf16[128,512]{1,0:T(8,128)(2,1)S(1)} %get-tuple-element.30.near_ref), channel_id=1, source_target_pairs={{0,2},{2,0},{4,6},{6,4},{8,10},{10,8},{12,14},{14,12},{16,18},{18,... | collective-permute-start | bytes 393224 | tf_op jit(solution)/shard_map/ppermute | solution.py:420
  35.1 4.7 %collective-permute-start.14 = (bf16[48,1024]{1,0:T(8,128)(2,1)S(1)}, bf16[48,1024]{1,0:T(8,128)(2,1)S(1)}, u32[]{:S(2)}, u32[]{:S(2)}) collective-permute-start(bf16[48,1024]{1,0:T(8,128)(2,1)S(1)} %join_parts.1.refs_0_), channel_id=1, source_target_pairs={{0,1},{1,0},{2,3},{3,2},{4,5},{5,4},{6,7},{7,6},{8,9},{9,8},{10,11... | collective-permute-start | bytes 294920 | tf_op jit(solution)/shard_map/ppermute | solution.py:457

commit v9 on v8

--- a/solution.py
+++ b/solution.py
@@ -432,18 +432,20 @@
         decode_lengths, dealing, decode_queries, new_decode, decode_cache, prefill_queries, req
     )
     head, rest = PART_ROWS * slots, far.shape[0]
-    (part,) = join_step(part, swap(part, 1), slots, [head + rest], "join_core", far)
-    part = after(part, *lanes[1:], *packs)
-    (part,) = join_step(part, swap(part, 2), slots, [head + 2 * rest], "join_x")
+    part, far = lax.optimization_barrier((part, far))
+    beside = swap(part, 1)
+    offset = jnp.full((8, HEAD_SIZE), prefill_offsets[0], jnp.int32)
+    lanes[1], offset, _ = lax.optimization_barrier((lanes[1], offset, part))
+    lanes[2], beside, _ = lax.optimization_barrier((lanes[2], beside, lanes[1]))
+    lanes[3], packs, _ = lax.optimization_barrier((lanes[3], packs, lanes[2]))
+    (part,) = join_step(part, beside, slots, [head + rest], "join_core", far)
+    across = swap(part, 2)
+    tables = [t for lane in lanes for t in (lane, swap(lane, 1))]
+
+    sent = prefill_partials(offset, packs, tables, ctx, [k // KEY_SET for k in others])
+    (part,) = join_step(part, after(across, sent[0]), slots, [head + 2 * rest], "join_x")
     part, news = join_step(part, swap(part, 4), slots, [head, 4 * rest], "join_z")
 
-    offset = jnp.full((8, HEAD_SIZE), prefill_offsets[0], jnp.int32)
-    lanes[1], offset = lax.optimization_barrier((lanes[1], offset))
-    for i in range(2, len(lanes)):
-        lanes[i] = after(lanes[i], lanes[i - 1])
-    tables = [t for lane in lanes for t in (lane, swap(lane, 1))]
-
-    sent = prefill_partials(offset, packs, tables, ctx, [k // KEY_SET for k in others])
     queries = after(queries, sent[0])
     kept = prefill_partials(offset, [queries], tables, ctx, [0])
     attended = join_parts(

time: 40.7 us -> 39.3 us (0.966)
  waiting for transfers between devices: 17.2 us -> 9.43 us
  starting transfers between devices: 12.5 us -> 18.9 us
    ppermute x15, waiting for transfers between devices: 15.9 us -> 8.06 us  [swap(): return lax.ppermute(array, BLK, [(i, i ^ distance) for i in range(blk)])]
    ppermute x15, starting transfers between devices: 10.8 us -> 17.3 us  [swap(): return lax.ppermute(array, BLK, [(i, i ^ distance) for i in range(blk)])]
  transfers between devices with their start and end apart: 16 -> 16, of which waited for: 8 -> 5; matrix products, arithmetic and copies ran while one was open for 0% -> 0% of each run, Pallas kernels for 19% -> 19%
where the time goes in v9:
time: 39.3 us; the launch traced here: 39.1 us
  starting transfers between devices  18.9 us (48%)
  waiting for transfers between devices  9.43 us (24%)
  Pallas kernels  8.52 us (22%)
  between operations  1.4 us (4%)
  other arithmetic  0.94 us (2%)
    ppermute x15, starting transfers between devices, swap(): return lax.ppermute(array, BLK, [(i, i ^ distance) for i in range(blk)])  17.3 us
    ppermute x15, waiting for transfers between devices, swap(): return lax.ppermute(array, BLK, [(i, i ^ distance) for i in range(blk)])  8.06 us
    pallas_call x1, Pallas kernels, decode_partials(): pl.pallas_call(decode_kernel, in_specs=[HBM] * len(inputs), out_specs=[HB...  2.79 us
    pallas_call x2, Pallas kernels, prefill_partials(): pl.pallas_call(functools.partial(prefill_kernel, sets, ctx), in_specs=[VM...  2.13 us
    pallas_call x1, Pallas kernels, update_cache(): pl.pallas_call(functools.partial(update_kernel, tokens, sets), in_specs=[...  1.71 us
    ppermute x1, starting transfers between devices, per_device(): held = [attended, lax.ppermute(attended, 'req', [(0, 1), (1, 0)])]  1.58 us
    ppermute x1, waiting for transfers between devices, per_device(): held = [attended, lax.ppermute(attended, 'req', [(0, 1), (1, 0)])]  1.37 us
    concatenate x1, other arithmetic, per_device(): table = jnp.concatenate([prefill_cache[0], new_prefill[0]], axis=0)  0.94 us
  transfers between devices with their start and end apart: 16, of which 5 were waited for; matrix products, arithmetic and copies ran while one was open for 0% of the time, Pallas kernels for 19%

profile of v9, /device:TPU:0, one launch (start us, length us, event | category | flops | bytes accessed | tf_op | source)
XLA Modules:
  0.0 39.1 jit_solution(8002506275482695207)
XLA Ops:
  0.6 0.9 %pad_maximum_fusion.refs_1_.refs_0_ = bf16[160,512]{1,0:T(8,128)(2,1)S(1)} fusion(bf16[32,512]{1,0:T(8,128)(2,1)} %bitcast.7, bf16[128,512]{1,0:T(8,128)(2,1)} %bitcast.5), kind=kLoop, calls=%fused_computation | loop fusion | flops 327680 | bytes 327680 | tf_op jit(solution)/shard_map/concatenate | solution.py:426
  1.6 3.0 %collective-permute-start = (bf16[160,512]{1,0:T(8,128)(2,1)S(1)}, bf16[160,512]{1,0:T(8,128)(2,1)S(1)}, u32[]{:S(2)}, u32[]{:S(2)}) collective-permute-start(bf16[160,512]{1,0:T(8,128)(2,1)S(1)} %pad_maximum_fusion.refs_1_.refs_0_), channel_id=1, source_target_pairs={{0,4},{2,6},{4,0},{6,2},{8,12},{10,14},{12,8},{14,10},{16,20},{18,... | collective-permute-start | bytes 491528 | tf_op jit(solution)/shard_map/ppermute | solution.py:420
  4.6 1.6 %collective-permute-start.4 = (bf16[160,512]{1,0:T(8,128)(2,1)S(1)}, bf16[160,512]{1,0:T(8,128)(2,1)S(1)}, u32[]{:S(2)}, u32[]{:S(2)}) collective-permute-start(bf16[160,512]{1,0:T(8,128)(2,1)S(1)} %pad_maximum_fusion.refs_1_.refs_0_), channel_id=1, source_target_pairs={{0,8},{2,10},{4,12},{6,14},{8,0},{10,2},{12,4},{14,6},{16,24},{18,... | collective-permute-start | bytes 491528 | tf_op jit(solution)/shard_map/ppermute | solution.py:420
  6.2 0.0 collective-permute-start.2
  6.2 3.0 %collective-permute-start.1 = (bf16[32,512]{1,0:T(8,128)(2,1)}, bf16[32,512]{1,0:T(8,128)(2,1)S(1)}, u32[]{:S(2)}, u32[]{:S(2)}) collective-permute-start(bf16[32,512]{1,0:T(8,128)(2,1)} %bitcast.8), channel_id=1, source_target_pairs={{0,16},{2,18},{4,20},{6,22},{8,24},{10,26},{12,28},{14,30},{16,0},... | collective-permute-start | bytes 98312 | tf_op jit(solution)/shard_map/ppermute | solution.py:420
  9.2 0.0 collective-permute-start.3
  9.2 2.8 %decode_partials.1 = (bf16[16,128,512]{2,1,0:T(8,128)(2,1)}, bf16[48,512]{1,0:T(8,128)(2,1)S(1)}, bf16[32,1024]{1,0:T(8,128)(2,1)S(1)}, f32[2,24,128]{2,1,0:T(8,128)S(1)}) custom-call(s32[16]{0:T(128)} %len_hbm.1, s32[34]{0:T(128)} %deal_hbm.1, bf16[16,1024]{1,0:T(8,128)(2,1)} %q_hbm.1, bf16[16,512]{1,0:T(8,128)(2,1)} %new_hbm.1, ...), custom_call_target="tpu_custom_call" | custom-call | flops 8388608 | bytes 4194304 | tf_op jit(solution)/shard_map/decode_partials/pallas_call | solution.py:196
  12.0 2.4 %collective-permute-done.1.refs_0_ = bf16[32,512]{1,0:T(8,128)(2,1)S(1)} collective-permute-done((bf16[32,512]{1,0:T(8,128)(2,1)}, bf16[32,512]{1,0:T(8,128)(2,1)S(1)}, u32[]{:S(2)}, u32[]{:S(2)}) %collective-permute-start.1) | collective-permute-done | bytes 32800 | tf_op jit(solution)/shard_map/ppermute | solution.py:420
  15.0 0.0 collective-permute-done.refs_3_.refs_2_
  15.0 0.6 %collective-permute-start.6 = (bf16[160,512]{1,0:T(8,128)(2,1)S(1)}, bf16[160,512]{1,0:T(8,128)(2,1)S(1)}, u32[]{:S(2)}, u32[]{:S(2)}) collective-permute-start(bf16[160,512]{1,0:T(8,128)(2,1)S(1)} %pad_maximum_fusion.refs_1_.refs_0_), channel_id=1, source_target_pairs={{0,2},{2,0},{4,6},{6,4},{8,10},{10,8},{12,14},{14,12},{16,18},{18,... | collective-permute-start | bytes 491528 | tf_op jit(solution)/shard_map/ppermute | solution.py:420
  15.6 0.0 collective-permute-done.4.refs_5_.refs_4_
  15.6 0.0 collective-permute-done.2.refs_7_.refs_6_
  15.6 0.2 collective-permute-start.9
  15.8 0.4 collective-permute-start.8
  16.2 0.1 collective-permute-start.7
  16.3 0.3 join_core.1.own_ref
  16.6 1.6 %collective-permute-start.11 = (bf16[80,512]{1,0:T(8,128)(2,1)S(1)}, bf16[80,512]{1,0:T(8,128)(2,1)S(1)}, u32[]{:S(2)}, u32[]{:S(2)}) collective-permute-start(bf16[80,512]{1,0:T(8,128)(2,1)S(1)} %join_core.1.own_ref), channel_id=1, source_target_pairs={{0,4},{2,6},{4,0},{6,2},{8,12},{10,14},{12,8},{14,10},{16,20},{18,... | collective-permute-start | bytes 245768 | tf_op jit(solution)/shard_map/ppermute | solution.py:420
  18.2 1.1 %prefill_partials.2 = bf16[32,1152]{1,0:T(8,128)(2,1)S(1)} custom-call(s32[8,128]{1,0:T(8,128)S(1)} %broadcast_in_dim.3.off_ref, bf16[32,1024]{1,0:T(8,128)(2,1)S(1)} %collective-permute-done.3.refs_0_, bf16[160,512]{1,0:T(8,128)(2,1)S(1)} %pad_maximum_fusion.refs_1_.refs_0_, bf16[160,512]{1,0:T(8,128)(2,1)S(1)} %collective-permute-done.6.refs_2_.refs_1_, ...), custom_call_target="tpu_custom_call" | custom-call | flops 167772160 | bytes 4194304 | tf_op jit(solution)/shard_map/prefill_partials/pallas_call | solution.py:307
  19.3 2.1 %collective-permute-done.11.other_ref = bf16[80,512]{1,0:T(8,128)(2,1)S(1)} collective-permute-done((bf16[80,512]{1,0:T(8,128)(2,1)S(1)}, bf16[80,512]{1,0:T(8,128)(2,1)S(1)}, u32[]{:S(2)}, u32[]{:S(2)}) %collective-permute-start.11) | collective-permute-done | bytes 81952 | tf_op jit(solution)/shard_map/ppermute | solution.py:420
  21.4 0.3 join_x.1.own_ref
  21.7 3.5 %collective-permute-start.12 = (bf16[112,512]{1,0:T(8,128)(2,1)S(1)}, bf16[112,512]{1,0:T(8,128)(2,1)S(1)}, u32[]{:S(2)}, u32[]{:S(2)}) collective-permute-start(bf16[112,512]{1,0:T(8,128)(2,1)S(1)} %join_x.1.own_ref), channel_id=1, source_target_pairs={{0,8},{2,10},{4,12},{6,14},{8,0},{10,2},{12,4},{14,6},{16,24},{18,... | collective-permute-start | bytes 344072 | tf_op jit(solution)/shard_map/ppermute | solution.py:420
  25.2 0.9 %collective-permute-start.10 = (bf16[32,1152]{1,0:T(8,128)(2,1)S(1)}, bf16[32,1152]{1,0:T(8,128)(2,1)S(1)}, u32[]{:S(2)}, u32[]{:S(2)}) collective-permute-start(bf16[32,1152]{1,0:T(8,128)(2,1)S(1)} %prefill_partials.2), channel_id=1, source_target_pairs={{0,16},{2,18},{4,20},{6,22},{8,24},{10,26},{12,28},{14,30},{16,0},... | collective-permute-start | bytes 221192 | tf_op jit(solution)/shard_map/ppermute | solution.py:420
  26.1 2.0 %collective-permute-done.12.other_ref = bf16[112,512]{1,0:T(8,128)(2,1)S(1)} collective-permute-done((bf16[112,512]{1,0:T(8,128)(2,1)S(1)}, bf16[112,512]{1,0:T(8,128)(2,1)S(1)}, u32[]{:S(2)}, u32[]{:S(2)}) %collective-permute-start.12) | collective-permute-done | bytes 114720 | tf_op jit(solution)/shard_map/ppermute | solution.py:420
  28.1 0.3 join_z.1
  28.4 2.4 %collective-permute-start.13 = (bf16[48,512]{1,0:T(8,128)(2,1)S(1)}, bf16[48,512]{1,0:T(8,128)(2,1)S(1)}, u32[]{:S(2)}, u32[]{:S(2)}) collective-permute-start(bf16[48,512]{1,0:T(8,128)(2,1)S(1)} %get-tuple-element.37.refs_2_), channel_id=1, source_target_pairs={{0,16},{2,18},{4,20},{6,22},{8,24},{10,26},{12,28},{14,30},{16,0},... | collective-permute-start | bytes 147464 | tf_op jit(solution)/shard_map/ppermute | solution.py:420
  30.8 1.1 %prefill_partials.3.refs_0_ = bf16[32,1152]{1,0:T(8,128)(2,1)S(1)} custom-call(s32[8,128]{1,0:T(8,128)S(1)} %broadcast_in_dim.3.off_ref, bf16[32,1024]{1,0:T(8,128)(2,1)S(1)} %get-tuple-element.33.refs_0_, bf16[160,512]{1,0:T(8,128)(2,1)S(1)} %pad_maximum_fusion.refs_1_.refs_0_, bf16[160,512]{1,0:T(8,128)(2,1)S(1)} %collective-permute-done.6.refs_2_.refs_1_, ...), custom_call_target="tpu_custom_call" | custom-call | flops 167772160 | bytes 4194304 | tf_op jit(solution)/shard_map/prefill_partials/pallas_call | solution.py:307
  31.9 1.5 %collective-permute-done.13.refs_3_ = bf16[48,512]{1,0:T(8,128)(2,1)S(1)} collective-permute-done((bf16[48,512]{1,0:T(8,128)(2,1)S(1)}, bf16[48,512]{1,0:T(8,128)(2,1)S(1)}, u32[]{:S(2)}, u32[]{:S(2)}) %collective-permute-start.13) | collective-permute-done | bytes 49184 | tf_op jit(solution)/shard_map/ppermute | solution.py:420
  33.4 0.3 join_parts.1.refs_0_
  33.7 1.6 %collective-permute-start.14 = (bf16[48,1024]{1,0:T(8,128)(2,1)S(1)}, bf16[48,1024]{1,0:T(8,128)(2,1)S(1)}, u32[]{:S(2)}, u32[]{:S(2)}) collective-permute-start(bf16[48,1024]{1,0:T(8,128)(2,1)S(1)} %join_parts.1.refs_0_), channel_id=1, source_target_pairs={{0,1},{1,0},{2,3},{3,2},{4,5},{5,4},{6,7},{7,6},{8,9},{9,8},{10,11... | collective-permute-start | bytes 294920 | tf_op jit(solution)/shard_map/ppermute | solution.py:459
  35.3 1.7 %update_cache.1 = bf16[1,128,512]{2,1,0:T(8,128)(2,1)} custom-call(s32[8,128]{1,0:T(8,128)S(1)} %broadcast_in_dim.3.off_ref, bf16[1,128,512]{2,1,0:T(8,128)(2,1)} %cache_hbm.3, bf16[128,512]{1,0:T(8,128)(2,1)S(1)} %get-tuple-element.38.near_ref, bf16[128,512]{1,0:T(8,128)(2,1)S(1)} %collective-permute-done.15.beside_ref, ...), custom_call_target="tpu_custom_call" | custom-call | tf_op jit(solution)/shard_map/update_cache/pallas_call | solution.py:361
  37.0 1.4 %collective-permute-done.14.refs_1_ = bf16[48,1024]{1,0:T(8,128)(2,1)S(1)} collective-permute-done((bf16[48,1024]{1,0:T(8,128)(2,1)S(1)}, bf16[48,1024]{1,0:T(8,128)(2,1)S(1)}, u32[]{:S(2)}, u32[]{:S(2)}) %collective-permute-start.14) | collective-permute-done | bytes 98336 | tf_op jit(solution)/shard_map/ppermute | solution.py:459
  38.4 0.8 %route_outputs.1 = (bf16[1,32,1024]{2,1,0:T(8,128)(2,1)}, bf16[16,1024]{1,0:T(8,128)(2,1)}) custom-call(f32[2,24,128]{2,1,0:T(8,128)S(1)} %get-tuple-element.24.route_ref, bf16[48,1024]{1,0:T(8,128)(2,1)S(1)} %join_parts.1.refs_0_, bf16[48,1024]{1,0:T(8,128)(2,1)S(1)} %collective-permute-done.14.refs_1_), custom_call_target="tpu_custom_call" | custom-call | tf_op jit(solution)/shard_map/route_outputs/pallas_call | solution.py:389
  (11 shorter events, 0.0 us)
Async XLA Ops:
  1.6 13.4 %collective-permute-start = (bf16[160,512]{1,0:T(8,128)(2,1)S(1)}, bf16[160,512]{1,0:T(8,128)(2,1)S(1)}, u32[]{:S(2)}, u32[]{:S(2)}) collective-permute-start(bf16[160,512]{1,0:T(8,128)(2,1)S(1)} %pad_maximum_fusion.refs_1_.refs_0_), channel_id=1, source_target_pairs={{0,4},{2,6},{4,0},{6,2},{8,12},{10,14},{12,8},{14,10},{16,20},{18,... | collective-permute-start | bytes 491528 | tf_op jit(solution)/shard_map/ppermute | solution.py:420
  4.6 11.0 %collective-permute-start.4 = (bf16[160,512]{1,0:T(8,128)(2,1)S(1)}, bf16[160,512]{1,0:T(8,128)(2,1)S(1)}, u32[]{:S(2)}, u32[]{:S(2)}) collective-permute-start(bf16[160,512]{1,0:T(8,128)(2,1)S(1)} %pad_maximum_fusion.refs_1_.refs_0_), channel_id=1, source_target_pairs={{0,8},{2,10},{4,12},{6,14},{8,0},{10,2},{12,4},{14,6},{16,24},{18,... | collective-permute-start | bytes 491528 | tf_op jit(solution)/shard_map/ppermute | solution.py:420
  6.2 9.5 %collective-permute-start.2 = (bf16[160,512]{1,0:T(8,128)(2,1)S(1)}, bf16[160,512]{1,0:T(8,128)(2,1)S(1)}, u32[]{:S(2)}, u32[]{:S(2)}) collective-permute-start(bf16[160,512]{1,0:T(8,128)(2,1)S(1)} %pad_maximum_fusion.refs_1_.refs_0_), channel_id=1, source_target_pairs={{0,12},{2,14},{4,8},{6,10},{8,4},{10,6},{12,0},{14,2},{16,28},{18,... | collective-permute-start | bytes 491528 | tf_op jit(solution)/shard_map/ppermute | solution.py:420
  6.2 8.2 %collective-permute-start.1 = (bf16[32,512]{1,0:T(8,128)(2,1)}, bf16[32,512]{1,0:T(8,128)(2,1)S(1)}, u32[]{:S(2)}, u32[]{:S(2)}) collective-permute-start(bf16[32,512]{1,0:T(8,128)(2,1)} %bitcast.8), channel_id=1, source_target_pairs={{0,16},{2,18},{4,20},{6,22},{8,24},{10,26},{12,28},{14,30},{16,0},... | collective-permute-start | bytes 98312 | tf_op jit(solution)/shard_map/ppermute | solution.py:420
  9.2 6.4 %collective-permute-start.3 = (bf16[32,1024]{1,0:T(8,128)(2,1)}, bf16[32,1024]{1,0:T(8,128)(2,1)S(1)}, u32[]{:S(2)}, u32[]{:S(2)}) collective-permute-start(bf16[32,1024]{1,0:T(8,128)(2,1)} %bitcast.6), channel_id=1, source_target_pairs={{0,16},{2,18},{4,20},{6,22},{8,24},{10,26},{12,28},{14,30},{16,0},... | collective-permute-start | bytes 196616 | tf_op jit(solution)/shard_map/ppermute | solution.py:420
  14.4 1.2 %collective-permute-start.5 = (bf16[48,512]{1,0:T(8,128)(2,1)S(1)}, bf16[48,512]{1,0:T(8,128)(2,1)S(1)}, u32[]{:S(2)}, u32[]{:S(2)}) collective-permute-start(bf16[48,512]{1,0:T(8,128)(2,1)S(1)} %get-tuple-element.26.own_ref), channel_id=1, source_target_pairs={{0,2},{2,0},{4,6},{6,4},{8,10},{10,8},{12,14},{14,12},{16,18},{18,... | collective-permute-start | bytes 147464 | tf_op jit(solution)/shard_map/ppermute | solution.py:420
  15.0 3.2 %collective-permute-start.6 = (bf16[160,512]{1,0:T(8,128)(2,1)S(1)}, bf16[160,512]{1,0:T(8,128)(2,1)S(1)}, u32[]{:S(2)}, u32[]{:S(2)}) collective-permute-start(bf16[160,512]{1,0:T(8,128)(2,1)S(1)} %pad_maximum_fusion.refs_1_.refs_0_), channel_id=1, source_target_pairs={{0,2},{2,0},{4,6},{6,4},{8,10},{10,8},{12,14},{14,12},{16,18},{18,... | collective-permute-start | bytes 491528 | tf_op jit(solution)/shard_map/ppermute | solution.py:420
  15.6 2.6 %collective-permute-start.9 = (bf16[160,512]{1,0:T(8,128)(2,1)S(1)}, bf16[160,512]{1,0:T(8,128)(2,1)S(1)}, u32[]{:S(2)}, u32[]{:S(2)}) collective-permute-start(bf16[160,512]{1,0:T(8,128)(2,1)S(1)} %collective-permute-done.2.refs_7_.refs_6_), channel_id=1, source_target_pairs={{0,2},{2,0},{4,6},{6,4},{8,10},{10,8},{12,14},{14,12},{16,18},{18,... | collective-permute-start | bytes 491528 | tf_op jit(solution)/shard_map/ppermute | solution.py:420
  15.8 2.4 %collective-permute-start.8 = (bf16[160,512]{1,0:T(8,128)(2,1)S(1)}, bf16[160,512]{1,0:T(8,128)(2,1)S(1)}, u32[]{:S(2)}, u32[]{:S(2)}) collective-permute-start(bf16[160,512]{1,0:T(8,128)(2,1)S(1)} %collective-permute-done.4.refs_5_.refs_4_), channel_id=1, source_target_pairs={{0,2},{2,0},{4,6},{6,4},{8,10},{10,8},{12,14},{14,12},{16,18},{18,... | collective-permute-start | bytes 491528 | tf_op jit(solution)/shard_map/ppermute | solution.py:420
  16.2 2.0 %collective-permute-start.7 = (bf16[160,512]{1,0:T(8,128)(2,1)S(1)}, bf16[160,512]{1,0:T(8,128)(2,1)S(1)}, u32[]{:S(2)}, u32[]{:S(2)}) collective-permute-start(bf16[160,512]{1,0:T(8,128)(2,1)S(1)} %collective-permute-done.refs_3_.refs_2_), channel_id=1, source_target_pairs={{0,2},{2,0},{4,6},{6,4},{8,10},{10,8},{12,14},{14,12},{16,18},{18,... | collective-permute-start | bytes 491528 | tf_op jit(solution)/shard_map/ppermute | solution.py:420
  16.6 4.8 %collective-permute-start.11 = (bf16[80,512]{1,0:T(8,128)(2,1)S(1)}, bf16[80,512]{1,0:T(8,128)(2,1)S(1)}, u32[]{:S(2)}, u32[]{:S(2)}) collective-permute-start(bf16[80,512]{1,0:T(8,128)(2,1)S(1)} %join_core.1.own_ref), channel_id=1, source_target_pairs={{0,4},{2,6},{4,0},{6,2},{8,12},{10,14},{12,8},{14,10},{16,20},{18,... | collective-permute-start | bytes 245768 | tf_op jit(solution)/shard_map/ppermute | solution.py:420
  21.7 6.4 %collective-permute-start.12 = (bf16[112,512]{1,0:T(8,128)(2,1)S(1)}, bf16[112,512]{1,0:T(8,128)(2,1)S(1)}, u32[]{:S(2)}, u32[]{:S(2)}) collective-permute-start(bf16[112,512]{1,0:T(8,128)(2,1)S(1)} %join_x.1.own_ref), channel_id=1, source_target_pairs={{0,8},{2,10},{4,12},{6,14},{8,0},{10,2},{12,4},{14,6},{16,24},{18,... | collective-permute-start | bytes 344072 | tf_op jit(solution)/shard_map/ppermute | solution.py:420
  25.2 6.7 %collective-permute-start.10 = (bf16[32,1152]{1,0:T(8,128)(2,1)S(1)}, bf16[32,1152]{1,0:T(8,128)(2,1)S(1)}, u32[]{:S(2)}, u32[]{:S(2)}) collective-permute-start(bf16[32,1152]{1,0:T(8,128)(2,1)S(1)} %prefill_partials.2), channel_id=1, source_target_pairs={{0,16},{2,18},{4,20},{6,22},{8,24},{10,26},{12,28},{14,30},{16,0},... | collective-permute-start | bytes 221192 | tf_op jit(solution)/shard_map/ppermute | solution.py:420
  28.4 5.1 %collective-permute-start.13 = (bf16[48,512]{1,0:T(8,128)(2,1)S(1)}, bf16[48,512]{1,0:T(8,128)(2,1)S(1)}, u32[]{:S(2)}, u32[]{:S(2)}) collective-permute-start(bf16[48,512]{1,0:T(8,128)(2,1)S(1)} %get-tuple-element.37.refs_2_), channel_id=1, source_target_pairs={{0,16},{2,18},{4,20},{6,22},{8,24},{10,26},{12,28},{14,30},{16,0},... | collective-permute-start | bytes 147464 | tf_op jit(solution)/shard_map/ppermute | solution.py:420
  30.8 4.5 %collective-permute-start.15 = (bf16[128,512]{1,0:T(8,128)(2,1)S(1)}, bf16[128,512]{1,0:T(8,128)(2,1)S(1)}, u32[]{:S(2)}, u32[]{:S(2)}) collective-permute-start(bf16[128,512]{1,0:T(8,128)(2,1)S(1)} %get-tuple-element.38.near_ref), channel_id=1, source_target_pairs={{0,2},{2,0},{4,6},{6,4},{8,10},{10,8},{12,14},{14,12},{16,18},{18,... | collective-permute-start | bytes 393224 | tf_op jit(solution)/shard_map/ppermute | solution.py:420
  33.7 4.7 %collective-permute-start.14 = (bf16[48,1024]{1,0:T(8,128)(2,1)S(1)}, bf16[48,1024]{1,0:T(8,128)(2,1)S(1)}, u32[]{:S(2)}, u32[]{:S(2)}) collective-permute-start(bf16[48,1024]{1,0:T(8,128)(2,1)S(1)} %join_parts.1.refs_0_), channel_id=1, source_target_pairs={{0,1},{1,0},{2,3},{3,2},{4,5},{5,4},{6,7},{7,6},{8,9},{9,8},{10,11... | collective-permute-start | bytes 294920 | tf_op jit(solution)/shard_map/ppermute | solution.py:459

commit v10 on v9

--- a/solution.py
+++ b/solution.py
@@ -230,26 +230,24 @@
     return jnp.concatenate(blocks + [ref[pl.ds(KEY_VALUE_HEADS * slots, slots), pl.ds(0, STATS)]], axis=1)
 
 
-def step_kernel(slots, own_ref, other_ref, *refs):
+def step_kernel(slots, appends, own_ref, other_ref, *refs):
     joined, logs = join([decode_part(own_ref, slots), decode_part(other_ref, slots)])
     head = PART_ROWS * slots
     rest = own_ref.shape[0] - head
-    out_ref = refs[0] if rest else refs[-1]
+    out_ref = refs[1] if appends else refs[0]
     for g in range(KEY_VALUE_HEADS):
         out_ref[pl.ds(g * slots, slots), :] = joined[:, g * KVW : (g + 1) * KVW]
     put_stats(out_ref, [logs[:, h * HEAD_SIZE : h * HEAD_SIZE + 1] for h in range(QUERY_HEADS)], slots)
-    if not rest:
-        far_ref = refs[0]
-        out_ref[pl.ds(head, far_ref.shape[0]), :] = far_ref[...]
-        return
-    news_ref, at = (out_ref, head) if len(refs) == 1 else (refs[1], 0)
-    news_ref[pl.ds(at, rest), :] = own_ref[pl.ds(head, rest), :]
-    news_ref[pl.ds(at + rest, rest), :] = other_ref[pl.ds(head, rest), :]
+    if appends:
+        out_ref[pl.ds(head, refs[0].shape[0]), :] = refs[0][...]
+    if rest:
+        refs[1][pl.ds(0, rest), :] = own_ref[pl.ds(head, rest), :]
+        refs[1][pl.ds(rest, rest), :] = other_ref[pl.ds(head, rest), :]
 
 
 def join_step(own, other, slots, shapes, name, *extra):
     return pl.pallas_call(
-        functools.partial(step_kernel, slots),
+        functools.partial(step_kernel, slots, bool(extra)),
         in_specs=[VMEM] * (2 + len(extra)),
         out_specs=[VMEM] * len(shapes),
         out_shape=[pltpu.VMEM((rows, KVW), BF16) for rows in shapes],
@@ -348,7 +346,8 @@
     half = sets * KEY_SET // 2
     far = block - KEY_SET
     inner = far % half
-    distance = KEY_SET * (1 + inner % sets) + 2 * (inner // sets) + far // half
+    lane = inner // sets
+    distance = KEY_SET * (1 + inner % sets) + lane % 2 * 4 + lane // 2 * 2 + far // half
     token = (me ^ jnp.where(block < KEY_SET, block, distance)) * tokens + index % tokens
     wanted = me * ctx + lax.broadcasted_iota(jnp.int32, (ctx, 1), 0) - off_ref[:1, :1]
     picked = dot(jnp.where(wanted == token, 1.0, 0.0).astype(BF16), rows).astype(BF16)
@@ -432,27 +431,26 @@
         decode_lengths, dealing, decode_queries, new_decode, decode_cache, prefill_queries, req
     )
     head, rest = PART_ROWS * slots, far.shape[0]
-    part, far = lax.optimization_barrier((part, far))
     beside = swap(part, 1)
     offset = jnp.full((8, HEAD_SIZE), prefill_offsets[0], jnp.int32)
     lanes[1], offset, _ = lax.optimization_barrier((lanes[1], offset, part))
     lanes[2], beside, _ = lax.optimization_barrier((lanes[2], beside, lanes[1]))
-    lanes[3], packs, _ = lax.optimization_barrier((lanes[3], packs, lanes[2]))
-    (part,) = join_step(part, beside, slots, [head + rest], "join_core", far)
+    (part,) = join_step(part, beside, slots, [head], "join_core")
     across = swap(part, 2)
+    lanes[3], packs, far, _ = lax.optimization_barrier((lanes[3], packs, far, lanes[2]))
     tables = [t for lane in lanes for t in (lane, swap(lane, 1))]
 
     sent = prefill_partials(offset, packs, tables, ctx, [k // KEY_SET for k in others])
-    (part,) = join_step(part, after(across, sent[0]), slots, [head + 2 * rest], "join_x")
-    part, news = join_step(part, swap(part, 4), slots, [head, 4 * rest], "join_z")
-
+    (part,) = join_step(part, after(across, sent[0]), slots, [head + rest], "join_x", far)
     queries = after(queries, sent[0])
     kept = prefill_partials(offset, [queries], tables, ctx, [0])
+    part, news = join_step(part, after(swap(part, 4), kept[0]), slots, [head, 2 * rest], "join_z")
     attended = join_parts(
         [*kept] + [swap(p, k) for k, p in zip(others, sent)],
         [part] + [swap(part, k) for k in others],
         slots,
     )
+    news = jnp.concatenate([news, swap(news, 2)], axis=0)
     prefill_cache_out = update_cache(offset, prefill_cache, news, swap(news, 1), tables, tokens, len(others))
 
     if req == 2:

time: 39.3 us -> 39.9 us (1.015)
  waiting for transfers between devices: 9.43 us -> 15.2 us
  starting transfers between devices: 18.9 us -> 13.6 us
    ppermute x15 -> x16, waiting for transfers between devices: 8.06 us -> 13.9 us  [swap(): return lax.ppermute(array, BLK, [(i, i ^ distance) for i in range(blk)])]
    ppermute x15 -> x16, starting transfers between devices: 17.3 us -> 12 us  [swap(): return lax.ppermute(array, BLK, [(i, i ^ distance) for i in range(blk)])]
  transfers between devices with their start and end apart: 16 -> 17, of which waited for: 5 -> 10; matrix products, arithmetic and copies ran while one was open for 0% -> 0% of each run, Pallas kernels for 19% -> 19%
where the time goes in v10:
time: 39.9 us; the launch traced here: 39.7 us
  waiting for transfers between devices  15.2 us (38%)
  starting transfers between devices  13.6 us (34%)
  Pallas kernels  8.55 us (21%)
  between operations  1.42 us (4%)
  other arithmetic  0.94 us (2%)
    ppermute x16, waiting for transfers between devices, swap(): return lax.ppermute(array, BLK, [(i, i ^ distance) for i in range(blk)])  13.9 us
    ppermute x16, starting transfers between devices, swap(): return lax.ppermute(array, BLK, [(i, i ^ distance) for i in range(blk)])  12 us
    pallas_call x1, Pallas kernels, decode_partials(): pl.pallas_call(decode_kernel, in_specs=[HBM] * len(inputs), out_specs=[HB...  2.82 us
    pallas_call x2, Pallas kernels, prefill_partials(): pl.pallas_call(functools.partial(prefill_kernel, sets, ctx), in_specs=[VM...  2.12 us
    pallas_call x1, Pallas kernels, update_cache(): pl.pallas_call(functools.partial(update_kernel, tokens, sets), in_specs=[...  1.72 us
    ppermute x1, starting transfers between devices, per_device(): held = [attended, lax.ppermute(attended, 'req', [(0, 1), (1, 0)])]  1.59 us
    ppermute x1, waiting for transfers between devices, per_device(): held = [attended, lax.ppermute(attended, 'req', [(0, 1), (1, 0)])]  1.36 us
    concatenate x1, other arithmetic, per_device(): table = jnp.concatenate([prefill_cache[0], new_prefill[0]], axis=0)  0.94 us
  transfers between devices with their start and end apart: 17, of which 10 were waited for; matrix products, arithmetic and copies ran while one was open for 0% of the time, Pallas kernels for 19%

profile of v10, /device:TPU:0, one launch (start us, length us, event | category | flops | bytes accessed | tf_op | source)
XLA Modules:
  0.0 39.7 jit_solution(1152820410355621474)
XLA Ops:
  0.6 0.9 %pad_maximum_fusion.refs_1_.refs_0_ = bf16[160,512]{1,0:T(8,128)(2,1)S(1)} fusion(bf16[32,512]{1,0:T(8,128)(2,1)} %bitcast.7, bf16[128,512]{1,0:T(8,128)(2,1)} %bitcast.5), kind=kLoop, calls=%fused_computation | loop fusion | flops 327680 | bytes 327680 | tf_op jit(solution)/shard_map/concatenate | solution.py:425
  1.6 3.0 %collective-permute-start = (bf16[160,512]{1,0:T(8,128)(2,1)S(1)}, bf16[160,512]{1,0:T(8,128)(2,1)S(1)}, u32[]{:S(2)}, u32[]{:S(2)}) collective-permute-start(bf16[160,512]{1,0:T(8,128)(2,1)S(1)} %pad_maximum_fusion.refs_1_.refs_0_), channel_id=1, source_target_pairs={{0,4},{2,6},{4,0},{6,2},{8,12},{10,14},{12,8},{14,10},{16,20},{18,... | collective-permute-start | bytes 491528 | tf_op jit(solution)/shard_map/ppermute | solution.py:419
  4.6 1.6 %collective-permute-start.4 = (bf16[160,512]{1,0:T(8,128)(2,1)S(1)}, bf16[160,512]{1,0:T(8,128)(2,1)S(1)}, u32[]{:S(2)}, u32[]{:S(2)}) collective-permute-start(bf16[160,512]{1,0:T(8,128)(2,1)S(1)} %pad_maximum_fusion.refs_1_.refs_0_), channel_id=1, source_target_pairs={{0,8},{2,10},{4,12},{6,14},{8,0},{10,2},{12,4},{14,6},{16,24},{18,... | collective-permute-start | bytes 491528 | tf_op jit(solution)/shard_map/ppermute | solution.py:419
  6.2 3.0 %collective-permute-start.2 = (bf16[32,1024]{1,0:T(8,128)(2,1)}, bf16[32,1024]{1,0:T(8,128)(2,1)S(1)}, u32[]{:S(2)}, u32[]{:S(2)}) collective-permute-start(bf16[32,1024]{1,0:T(8,128)(2,1)} %bitcast.6), channel_id=1, source_target_pairs={{0,16},{2,18},{4,20},{6,22},{8,24},{10,26},{12,28},{14,30},{16,0},... | collective-permute-start | bytes 196616 | tf_op jit(solution)/shard_map/ppermute | solution.py:419
  9.2 2.8 %decode_partials.1 = (bf16[16,128,512]{2,1,0:T(8,128)(2,1)}, bf16[48,512]{1,0:T(8,128)(2,1)S(1)}, bf16[32,1024]{1,0:T(8,128)(2,1)S(1)}, f32[2,24,128]{2,1,0:T(8,128)S(1)}) custom-call(s32[16]{0:T(128)} %len_hbm.1, s32[34]{0:T(128)} %deal_hbm.1, bf16[16,1024]{1,0:T(8,128)(2,1)} %q_hbm.1, bf16[16,512]{1,0:T(8,128)(2,1)} %new_hbm.1, ...), custom_call_target="tpu_custom_call" | custom-call | flops 8388608 | bytes 4194304 | tf_op jit(solution)/shard_map/decode_partials/pallas_call | solution.py:196
  12.8 0.5 %collective-permute-done.5.other_ref = bf16[48,512]{1,0:T(8,128)(2,1)S(1)} collective-permute-done((bf16[48,512]{1,0:T(8,128)(2,1)S(1)}, bf16[48,512]{1,0:T(8,128)(2,1)S(1)}, u32[]{:S(2)}, u32[]{:S(2)}) %collective-permute-start.5) | collective-permute-done | bytes 49184 | tf_op jit(solution)/shard_map/ppermute | solution.py:419
  13.3 0.2 collective-permute-start.6
  13.5 4.8 %collective-permute-done.3.refs_0_ = bf16[32,512]{1,0:T(8,128)(2,1)S(1)} collective-permute-done((bf16[32,512]{1,0:T(8,128)(2,1)S(1)}, bf16[32,512]{1,0:T(8,128)(2,1)S(1)}, u32[]{:S(2)}, u32[]{:S(2)}) %collective-permute-start.3) | collective-permute-done | bytes 32800 | tf_op jit(solution)/shard_map/ppermute | solution.py:419
  18.3 0.5 %collective-permute-start.8 = (bf16[160,512]{1,0:T(8,128)(2,1)S(1)}, bf16[160,512]{1,0:T(8,128)(2,1)S(1)}, u32[]{:S(2)}, u32[]{:S(2)}) collective-permute-start(bf16[160,512]{1,0:T(8,128)(2,1)S(1)} %collective-permute-done.4.refs_5_.refs_4_), channel_id=1, source_target_pairs={{0,2},{2,0},{4,6},{6,4},{8,10},{10,8},{12,14},{14,12},{16,18},{18,... | collective-permute-start | bytes 491528 | tf_op jit(solution)/shard_map/ppermute | solution.py:419
  18.8 0.1 collective-permute-start.7
  18.8 0.3 join_core.1.own_ref
  19.1 0.2 collective-permute-start.11
  19.4 0.3 collective-permute-done.9.refs_8_.refs_7_
  19.6 0.2 collective-permute-done.8.refs_6_.refs_5_
  19.9 0.3 collective-permute-done.7.refs_4_.refs_3_
  20.2 1.1 %prefill_partials.2 = bf16[32,1152]{1,0:T(8,128)(2,1)S(1)} custom-call(s32[8,128]{1,0:T(8,128)S(1)} %broadcast_in_dim.3.off_ref, bf16[32,1024]{1,0:T(8,128)(2,1)S(1)} %collective-permute-done.2.refs_0_, bf16[160,512]{1,0:T(8,128)(2,1)S(1)} %pad_maximum_fusion.refs_1_.refs_0_, bf16[160,512]{1,0:T(8,128)(2,1)S(1)} %collective-permute-done.6.refs_2_.refs_1_, ...), custom_call_target="tpu_custom_call" | custom-call | flops 167772160 | bytes 4194304 | tf_op jit(solution)/shard_map/prefill_partials/pallas_call | solution.py:305
  21.2 2.1 %collective-permute-done.11.other_ref = bf16[48,512]{1,0:T(8,128)(2,1)S(1)} collective-permute-done((bf16[48,512]{1,0:T(8,128)(2,1)S(1)}, bf16[48,512]{1,0:T(8,128)(2,1)S(1)}, u32[]{:S(2)}, u32[]{:S(2)}) %collective-permute-start.11) | collective-permute-done | bytes 49184 | tf_op jit(solution)/shard_map/ppermute | solution.py:419
  23.3 0.3 join_x.1.own_ref
  23.6 0.4 collective-permute-start.12
  24.0 1.5 %collective-permute-start.10 = (bf16[32,1152]{1,0:T(8,128)(2,1)S(1)}, bf16[32,1152]{1,0:T(8,128)(2,1)S(1)}, u32[]{:S(2)}, u32[]{:S(2)}) collective-permute-start(bf16[32,1152]{1,0:T(8,128)(2,1)S(1)} %prefill_partials.2), channel_id=1, source_target_pairs={{0,16},{2,18},{4,20},{6,22},{8,24},{10,26},{12,28},{14,30},{16,0},... | collective-permute-start | bytes 221192 | tf_op jit(solution)/shard_map/ppermute | solution.py:419
  25.4 1.1 %prefill_partials.3.refs_0_ = bf16[32,1152]{1,0:T(8,128)(2,1)S(1)} custom-call(s32[8,128]{1,0:T(8,128)S(1)} %broadcast_in_dim.3.off_ref, bf16[32,1024]{1,0:T(8,128)(2,1)S(1)} %get-tuple-element.32.refs_0_, bf16[160,512]{1,0:T(8,128)(2,1)S(1)} %pad_maximum_fusion.refs_1_.refs_0_, bf16[160,512]{1,0:T(8,128)(2,1)S(1)} %collective-permute-done.6.refs_2_.refs_1_, ...), custom_call_target="tpu_custom_call" | custom-call | flops 167772160 | bytes 4194304 | tf_op jit(solution)/shard_map/prefill_partials/pallas_call | solution.py:305
  26.5 1.7 %collective-permute-done.12.other_ref = bf16[80,512]{1,0:T(8,128)(2,1)S(1)} collective-permute-done((bf16[80,512]{1,0:T(8,128)(2,1)S(1)}, bf16[80,512]{1,0:T(8,128)(2,1)S(1)}, u32[]{:S(2)}, u32[]{:S(2)}) %collective-permute-start.12) | collective-permute-done | bytes 81952 | tf_op jit(solution)/shard_map/ppermute | solution.py:419
  28.2 0.3 join_z.1
  28.5 0.3 collective-permute-start.13
  28.8 1.1 %collective-permute-start.15 = (bf16[64,512]{1,0:T(8,128)(2,1)S(1)}, bf16[64,512]{1,0:T(8,128)(2,1)S(1)}, u32[]{:S(2)}, u32[]{:S(2)}) collective-permute-start(bf16[64,512]{1,0:T(8,128)(2,1)S(1)} %get-tuple-element.38), channel_id=1, source_target_pairs={{0,4},{2,6},{4,0},{6,2},{8,12},{10,14},{12,8},{14,10},{16,20},{18,... | collective-permute-start | bytes 196616 | tf_op jit(solution)/shard_map/ppermute | solution.py:419
  29.9 3.2 %collective-permute-done.15 = bf16[64,512]{1,0:T(8,128)(2,1)S(1)} collective-permute-done((bf16[64,512]{1,0:T(8,128)(2,1)S(1)}, bf16[64,512]{1,0:T(8,128)(2,1)S(1)}, u32[]{:S(2)}, u32[]{:S(2)}) %collective-permute-start.15) | collective-permute-done | bytes 65568 | tf_op jit(solution)/shard_map/ppermute | solution.py:419
  33.1 0.9 %collective-permute-done.13.refs_3_ = bf16[48,512]{1,0:T(8,128)(2,1)S(1)} collective-permute-done((bf16[48,512]{1,0:T(8,128)(2,1)S(1)}, bf16[48,512]{1,0:T(8,128)(2,1)S(1)}, u32[]{:S(2)}, u32[]{:S(2)}) %collective-permute-start.13) | collective-permute-done | bytes 49184 | tf_op jit(solution)/shard_map/ppermute | solution.py:419
  34.0 0.3 join_parts.1.refs_0_
  34.3 1.6 %collective-permute-start.14 = (bf16[48,1024]{1,0:T(8,128)(2,1)S(1)}, bf16[48,1024]{1,0:T(8,128)(2,1)S(1)}, u32[]{:S(2)}, u32[]{:S(2)}) collective-permute-start(bf16[48,1024]{1,0:T(8,128)(2,1)S(1)} %join_parts.1.refs_0_), channel_id=1, source_target_pairs={{0,1},{1,0},{2,3},{3,2},{4,5},{5,4},{6,7},{7,6},{8,9},{9,8},{10,11... | collective-permute-start | bytes 294920 | tf_op jit(solution)/shard_map/ppermute | solution.py:457
  35.9 1.7 %update_cache.1 = bf16[1,128,512]{2,1,0:T(8,128)(2,1)} custom-call(s32[8,128]{1,0:T(8,128)S(1)} %broadcast_in_dim.3.off_ref, bf16[1,128,512]{2,1,0:T(8,128)(2,1)} %cache_hbm.3, bf16[128,512]{1,0:T(8,128)(2,1)S(1)} %constant_dynamic-update-slice_fusion.near_ref, bf16[128,512]{1,0:T(8,128)(2,1)S(1)} %collective-permute-done.16.beside_ref, ...), custom_call_target="tpu_custom_call" | custom-call | tf_op jit(solution)/shard_map/update_cache/pallas_call | solution.py:360
  37.6 1.4 %collective-permute-done.14.refs_1_ = bf16[48,1024]{1,0:T(8,128)(2,1)S(1)} collective-permute-done((bf16[48,1024]{1,0:T(8,128)(2,1)S(1)}, bf16[48,1024]{1,0:T(8,128)(2,1)S(1)}, u32[]{:S(2)}, u32[]{:S(2)}) %collective-permute-start.14) | collective-permute-done | bytes 98336 | tf_op jit(solution)/shard_map/ppermute | solution.py:457
  39.0 0.8 %route_outputs.1 = (bf16[1,32,1024]{2,1,0:T(8,128)(2,1)}, bf16[16,1024]{1,0:T(8,128)(2,1)}) custom-call(f32[2,24,128]{2,1,0:T(8,128)S(1)} %get-tuple-element.24.route_ref, bf16[48,1024]{1,0:T(8,128)(2,1)S(1)} %join_parts.1.refs_0_, bf16[48,1024]{1,0:T(8,128)(2,1)S(1)} %collective-permute-done.14.refs_1_), custom_call_target="tpu_custom_call" | custom-call | tf_op jit(solution)/shard_map/route_outputs/pallas_call | solution.py:388
  (17 shorter events, 0.2 us)
Async XLA Ops:
  0.6 11.5 %copy-start = (bf16[1,32,512]{2,1,0:T(8,128)(2,1)S(1)}, bf16[1,32,512]{2,1,0:T(8,128)(2,1)}, u32[]{:S(2)}) copy-start(bf16[1,32,512]{2,1,0:T(8,128)(2,1)} %param.11) | copy-start | bytes 98308
  1.6 10.5 %collective-permute-start = (bf16[160,512]{1,0:T(8,128)(2,1)S(1)}, bf16[160,512]{1,0:T(8,128)(2,1)S(1)}, u32[]{:S(2)}, u32[]{:S(2)}) collective-permute-start(bf16[160,512]{1,0:T(8,128)(2,1)S(1)} %pad_maximum_fusion.refs_1_.refs_0_), channel_id=1, source_target_pairs={{0,4},{2,6},{4,0},{6,2},{8,12},{10,14},{12,8},{14,10},{16,20},{18,... | collective-permute-start | bytes 491528 | tf_op jit(solution)/shard_map/ppermute | solution.py:419
  4.6 8.9 %collective-permute-start.4 = (bf16[160,512]{1,0:T(8,128)(2,1)S(1)}, bf16[160,512]{1,0:T(8,128)(2,1)S(1)}, u32[]{:S(2)}, u32[]{:S(2)}) collective-permute-start(bf16[160,512]{1,0:T(8,128)(2,1)S(1)} %pad_maximum_fusion.refs_1_.refs_0_), channel_id=1, source_target_pairs={{0,8},{2,10},{4,12},{6,14},{8,0},{10,2},{12,4},{14,6},{16,24},{18,... | collective-permute-start | bytes 491528 | tf_op jit(solution)/shard_map/ppermute | solution.py:419
  6.2 12.1 %collective-permute-start.1 = (bf16[160,512]{1,0:T(8,128)(2,1)S(1)}, bf16[160,512]{1,0:T(8,128)(2,1)S(1)}, u32[]{:S(2)}, u32[]{:S(2)}) collective-permute-start(bf16[160,512]{1,0:T(8,128)(2,1)S(1)} %pad_maximum_fusion.refs_1_.refs_0_), channel_id=1, source_target_pairs={{0,12},{2,14},{4,8},{6,10},{8,4},{10,6},{12,0},{14,2},{16,28},{18,... | collective-permute-start | bytes 491528 | tf_op jit(solution)/shard_map/ppermute | solution.py:419
  6.2 12.1 %collective-permute-start.2 = (bf16[32,1024]{1,0:T(8,128)(2,1)}, bf16[32,1024]{1,0:T(8,128)(2,1)S(1)}, u32[]{:S(2)}, u32[]{:S(2)}) collective-permute-start(bf16[32,1024]{1,0:T(8,128)(2,1)} %bitcast.6), channel_id=1, source_target_pairs={{0,16},{2,18},{4,20},{6,22},{8,24},{10,26},{12,28},{14,30},{16,0},... | collective-permute-start | bytes 196616 | tf_op jit(solution)/shard_map/ppermute | solution.py:419
  12.0 1.3 %collective-permute-start.5 = (bf16[48,512]{1,0:T(8,128)(2,1)S(1)}, bf16[48,512]{1,0:T(8,128)(2,1)S(1)}, u32[]{:S(2)}, u32[]{:S(2)}) collective-permute-start(bf16[48,512]{1,0:T(8,128)(2,1)S(1)} %get-tuple-element.25.own_ref), channel_id=1, source_target_pairs={{0,2},{2,0},{4,6},{6,4},{8,10},{10,8},{12,14},{14,12},{16,18},{18,... | collective-permute-start | bytes 147464 | tf_op jit(solution)/shard_map/ppermute | solution.py:419
  12.1 6.1 %collective-permute-start.3 = (bf16[32,512]{1,0:T(8,128)(2,1)S(1)}, bf16[32,512]{1,0:T(8,128)(2,1)S(1)}, u32[]{:S(2)}, u32[]{:S(2)}) collective-permute-start(bf16[32,512]{1,0:T(8,128)(2,1)S(1)} %bitcast.8), channel_id=1, source_target_pairs={{0,16},{2,18},{4,20},{6,22},{8,24},{10,26},{12,28},{14,30},{16,0},... | collective-permute-start | bytes 98312 | tf_op jit(solution)/shard_map/ppermute | solution.py:419
  13.3 6.1 %collective-permute-start.6 = (bf16[160,512]{1,0:T(8,128)(2,1)S(1)}, bf16[160,512]{1,0:T(8,128)(2,1)S(1)}, u32[]{:S(2)}, u32[]{:S(2)}) collective-permute-start(bf16[160,512]{1,0:T(8,128)(2,1)S(1)} %pad_maximum_fusion.refs_1_.refs_0_), channel_id=1, source_target_pairs={{0,2},{2,0},{4,6},{6,4},{8,10},{10,8},{12,14},{14,12},{16,18},{18,... | collective-permute-start | bytes 491528 | tf_op jit(solution)/shard_map/ppermute | solution.py:419
  18.2 1.4 %collective-permute-start.9 = (bf16[160,512]{1,0:T(8,128)(2,1)S(1)}, bf16[160,512]{1,0:T(8,128)(2,1)S(1)}, u32[]{:S(2)}, u32[]{:S(2)}) collective-permute-start(bf16[160,512]{1,0:T(8,128)(2,1)S(1)} %collective-permute-done.1.refs_7_.refs_6_), channel_id=1, source_target_pairs={{0,2},{2,0},{4,6},{6,4},{8,10},{10,8},{12,14},{14,12},{16,18},{18,... | collective-permute-start | bytes 491528 | tf_op jit(solution)/shard_map/ppermute | solution.py:419
  18.3 1.6 %collective-permute-start.8 = (bf16[160,512]{1,0:T(8,128)(2,1)S(1)}, bf16[160,512]{1,0:T(8,128)(2,1)S(1)}, u32[]{:S(2)}, u32[]{:S(2)}) collective-permute-start(bf16[160,512]{1,0:T(8,128)(2,1)S(1)} %collective-permute-done.4.refs_5_.refs_4_), channel_id=1, source_target_pairs={{0,2},{2,0},{4,6},{6,4},{8,10},{10,8},{12,14},{14,12},{16,18},{18,... | collective-permute-start | bytes 491528 | tf_op jit(solution)/shard_map/ppermute | solution.py:419
  18.8 1.4 %collective-permute-start.7 = (bf16[160,512]{1,0:T(8,128)(2,1)S(1)}, bf16[160,512]{1,0:T(8,128)(2,1)S(1)}, u32[]{:S(2)}, u32[]{:S(2)}) collective-permute-start(bf16[160,512]{1,0:T(8,128)(2,1)S(1)} %collective-permute-done.refs_3_.refs_2_), channel_id=1, source_target_pairs={{0,2},{2,0},{4,6},{6,4},{8,10},{10,8},{12,14},{14,12},{16,18},{18,... | collective-permute-start | bytes 491528 | tf_op jit(solution)/shard_map/ppermute | solution.py:419
  19.1 4.2 %collective-permute-start.11 = (bf16[48,512]{1,0:T(8,128)(2,1)S(1)}, bf16[48,512]{1,0:T(8,128)(2,1)S(1)}, u32[]{:S(2)}, u32[]{:S(2)}) collective-permute-start(bf16[48,512]{1,0:T(8,128)(2,1)S(1)} %join_core.1.own_ref), channel_id=1, source_target_pairs={{0,4},{2,6},{4,0},{6,2},{8,12},{10,14},{12,8},{14,10},{16,20},{18,... | collective-permute-start | bytes 147464 | tf_op jit(solution)/shard_map/ppermute | solution.py:419
  23.6 4.6 %collective-permute-start.12 = (bf16[80,512]{1,0:T(8,128)(2,1)S(1)}, bf16[80,512]{1,0:T(8,128)(2,1)S(1)}, u32[]{:S(2)}, u32[]{:S(2)}) collective-permute-start(bf16[80,512]{1,0:T(8,128)(2,1)S(1)} %join_x.1.own_ref), channel_id=1, source_target_pairs={{0,8},{2,10},{4,12},{6,14},{8,0},{10,2},{12,4},{14,6},{16,24},{18,... | collective-permute-start | bytes 245768 | tf_op jit(solution)/shard_map/ppermute | solution.py:419
  24.0 9.1 %collective-permute-start.10 = (bf16[32,1152]{1,0:T(8,128)(2,1)S(1)}, bf16[32,1152]{1,0:T(8,128)(2,1)S(1)}, u32[]{:S(2)}, u32[]{:S(2)}) collective-permute-start(bf16[32,1152]{1,0:T(8,128)(2,1)S(1)} %prefill_partials.2), channel_id=1, source_target_pairs={{0,16},{2,18},{4,20},{6,22},{8,24},{10,26},{12,28},{14,30},{16,0},... | collective-permute-start | bytes 221192 | tf_op jit(solution)/shard_map/ppermute | solution.py:419
  28.5 5.5 %collective-permute-start.13 = (bf16[48,512]{1,0:T(8,128)(2,1)S(1)}, bf16[48,512]{1,0:T(8,128)(2,1)S(1)}, u32[]{:S(2)}, u32[]{:S(2)}) collective-permute-start(bf16[48,512]{1,0:T(8,128)(2,1)S(1)} %get-tuple-element.37.refs_2_), channel_id=1, source_target_pairs={{0,16},{2,18},{4,20},{6,22},{8,24},{10,26},{12,28},{14,30},{16,0},... | collective-permute-start | bytes 147464 | tf_op jit(solution)/shard_map/ppermute | solution.py:419
  28.8 4.3 %collective-permute-start.15 = (bf16[64,512]{1,0:T(8,128)(2,1)S(1)}, bf16[64,512]{1,0:T(8,128)(2,1)S(1)}, u32[]{:S(2)}, u32[]{:S(2)}) collective-permute-start(bf16[64,512]{1,0:T(8,128)(2,1)S(1)} %get-tuple-element.38), channel_id=1, source_target_pairs={{0,4},{2,6},{4,0},{6,2},{8,12},{10,14},{12,8},{14,10},{16,20},{18,... | collective-permute-start | bytes 196616 | tf_op jit(solution)/shard_map/ppermute | solution.py:419
  33.0 2.8 %collective-permute-start.16 = (bf16[128,512]{1,0:T(8,128)(2,1)S(1)}, bf16[128,512]{1,0:T(8,128)(2,1)S(1)}, u32[]{:S(2)}, u32[]{:S(2)}) collective-permute-start(bf16[128,512]{1,0:T(8,128)(2,1)S(1)} %constant_dynamic-update-slice_fusion.near_ref), channel_id=1, source_target_pairs={{0,2},{2,0},{4,6},{6,4},{8,10},{10,8},{12,14},{14,12},{16,18},{18,... | collective-permute-start | bytes 393224 | tf_op jit(solution)/shard_map/ppermute | solution.py:419
  34.3 4.7 %collective-permute-start.14 = (bf16[48,1024]{1,0:T(8,128)(2,1)S(1)}, bf16[48,1024]{1,0:T(8,128)(2,1)S(1)}, u32[]{:S(2)}, u32[]{:S(2)}) collective-permute-start(bf16[48,1024]{1,0:T(8,128)(2,1)S(1)} %join_parts.1.refs_0_), channel_id=1, source_target_pairs={{0,1},{1,0},{2,3},{3,2},{4,5},{5,4},{6,7},{7,6},{8,9},{9,8},{10,11... | collective-permute-start | bytes 294920 | tf_op jit(solution)/shard_map/ppermute | solution.py:457

commit v11 on v10

--- a/solution.py
+++ b/solution.py
@@ -346,8 +346,7 @@
     half = sets * KEY_SET // 2
     far = block - KEY_SET
     inner = far % half
-    lane = inner // sets
-    distance = KEY_SET * (1 + inner % sets) + lane % 2 * 4 + lane // 2 * 2 + far // half
+    distance = KEY_SET * (1 + inner % sets) + 2 * (inner // sets) + far // half
     token = (me ^ jnp.where(block < KEY_SET, block, distance)) * tokens + index % tokens
     wanted = me * ctx + lax.broadcasted_iota(jnp.int32, (ctx, 1), 0) - off_ref[:1, :1]
     picked = dot(jnp.where(wanted == token, 1.0, 0.0).astype(BF16), rows).astype(BF16)
@@ -434,23 +433,25 @@
     beside = swap(part, 1)
     offset = jnp.full((8, HEAD_SIZE), prefill_offsets[0], jnp.int32)
     lanes[1], offset, _ = lax.optimization_barrier((lanes[1], offset, part))
-    lanes[2], beside, _ = lax.optimization_barrier((lanes[2], beside, lanes[1]))
+    lanes[2], beside, far, _ = lax.optimization_barrier((lanes[2], beside, far, lanes[1]))
     (part,) = join_step(part, beside, slots, [head], "join_core")
+    far_across = swap(far, 2)
     across = swap(part, 2)
-    lanes[3], packs, far, _ = lax.optimization_barrier((lanes[3], packs, far, lanes[2]))
+    lanes[3], packs, across, _ = lax.optimization_barrier((lanes[3], packs, across, lanes[2]))
     tables = [t for lane in lanes for t in (lane, swap(lane, 1))]
 
+    far = jnp.concatenate([far, far_across], axis=0)
+    (part,) = join_step(part, across, slots, [head + 2 * rest], "join_x", far)
+    packs, _ = lax.optimization_barrier((packs, part))
     sent = prefill_partials(offset, packs, tables, ctx, [k // KEY_SET for k in others])
-    (part,) = join_step(part, after(across, sent[0]), slots, [head + rest], "join_x", far)
     queries = after(queries, sent[0])
     kept = prefill_partials(offset, [queries], tables, ctx, [0])
-    part, news = join_step(part, after(swap(part, 4), kept[0]), slots, [head, 2 * rest], "join_z")
+    part, news = join_step(part, after(swap(part, 4), kept[0]), slots, [head, 4 * rest], "join_z")
     attended = join_parts(
         [*kept] + [swap(p, k) for k, p in zip(others, sent)],
         [part] + [swap(part, k) for k in others],
         slots,
     )
-    news = jnp.concatenate([news, swap(news, 2)], axis=0)
     prefill_cache_out = update_cache(offset, prefill_cache, news, swap(news, 1), tables, tokens, len(others))
 
     if req == 2:

time: 39.9 us -> 40.3 us (1.010)
  starting transfers between devices: 13.6 us -> 19.8 us
  waiting for transfers between devices: 15.2 us -> 9.33 us
    ppermute x16, starting transfers between devices: 12 us -> 18.2 us  [swap(): return lax.ppermute(array, BLK, [(i, i ^ distance) for i in range(blk)])]
    ppermute x16, waiting for transfers between devices: 13.9 us -> 7.96 us  [swap(): return lax.ppermute(array, BLK, [(i, i ^ distance) for i in range(blk)])]
  transfers between devices with their start and end apart: 17 -> 17, of which waited for: 10 -> 5; matrix products, arithmetic and copies ran while one was open for 0% -> 0% of each run, Pallas kernels for 19% -> 19%
where the time goes in v11:
time: 40.3 us; the launch traced here: 40.1 us
  starting transfers between devices  19.8 us (49%)
  waiting for transfers between devices  9.33 us (23%)
  Pallas kernels  8.52 us (21%)
  between operations  1.41 us (3%)
  other arithmetic  0.97 us (2%)
    ppermute x16, starting transfers between devices, swap(): return lax.ppermute(array, BLK, [(i, i ^ distance) for i in range(blk)])  18.2 us
    ppermute x16, waiting for transfers between devices, swap(): return lax.ppermute(array, BLK, [(i, i ^ distance) for i in range(blk)])  7.96 us
    pallas_call x1, Pallas kernels, decode_partials(): pl.pallas_call(decode_kernel, in_specs=[HBM] * len(inputs), out_specs=[HB...  2.8 us
    pallas_call x2, Pallas kernels, prefill_partials(): pl.pallas_call(functools.partial(prefill_kernel, sets, ctx), in_specs=[VM...  2.12 us
    pallas_call x1, Pallas kernels, update_cache(): pl.pallas_call(functools.partial(update_kernel, tokens, sets), in_specs=[...  1.71 us
    ppermute x1, starting transfers between devices, per_device(): held = [attended, lax.ppermute(attended, 'req', [(0, 1), (1, 0)])]  1.59 us
    ppermute x1, waiting for transfers between devices, per_device(): held = [attended, lax.ppermute(attended, 'req', [(0, 1), (1, 0)])]  1.37 us
    concatenate x1, other arithmetic, per_device(): table = jnp.concatenate([prefill_cache[0], new_prefill[0]], axis=0)  0.97 us
  transfers between devices with their start and end apart: 17, of which 5 were waited for; matrix products, arithmetic and copies ran while one was open for 0% of the time, Pallas kernels for 19%

profile of v11, /device:TPU:0, one launch (start us, length us, event | category | flops | bytes accessed | tf_op | source)
XLA Modules:
  0.0 40.1 jit_solution(10140050582994166934)
XLA Ops:
  0.6 0.0 copy-start
  0.7 1.0 %pad_maximum_fusion.refs_1_.refs_0_ = bf16[160,512]{1,0:T(8,128)(2,1)S(1)} fusion(bf16[32,512]{1,0:T(8,128)(2,1)} %bitcast.7, bf16[128,512]{1,0:T(8,128)(2,1)} %bitcast.5), kind=kLoop, calls=%fused_computation | loop fusion | flops 327680 | bytes 327680 | tf_op jit(solution)/shard_map/concatenate | solution.py:424
  1.6 3.0 %collective-permute-start = (bf16[160,512]{1,0:T(8,128)(2,1)S(1)}, bf16[160,512]{1,0:T(8,128)(2,1)S(1)}, u32[]{:S(2)}, u32[]{:S(2)}) collective-permute-start(bf16[160,512]{1,0:T(8,128)(2,1)S(1)} %pad_maximum_fusion.refs_1_.refs_0_), channel_id=1, source_target_pairs={{0,4},{2,6},{4,0},{6,2},{8,12},{10,14},{12,8},{14,10},{16,20},{18,... | collective-permute-start | bytes 491528 | tf_op jit(solution)/shard_map/ppermute | solution.py:418
  4.6 1.6 %collective-permute-start.3 = (bf16[160,512]{1,0:T(8,128)(2,1)S(1)}, bf16[160,512]{1,0:T(8,128)(2,1)S(1)}, u32[]{:S(2)}, u32[]{:S(2)}) collective-permute-start(bf16[160,512]{1,0:T(8,128)(2,1)S(1)} %pad_maximum_fusion.refs_1_.refs_0_), channel_id=1, source_target_pairs={{0,8},{2,10},{4,12},{6,14},{8,0},{10,2},{12,4},{14,6},{16,24},{18,... | collective-permute-start | bytes 491528 | tf_op jit(solution)/shard_map/ppermute | solution.py:418
  6.2 0.0 collective-permute-start.1
  6.2 2.8 %decode_partials.1 = (bf16[16,128,512]{2,1,0:T(8,128)(2,1)}, bf16[48,512]{1,0:T(8,128)(2,1)S(1)}, bf16[32,1024]{1,0:T(8,128)(2,1)S(1)}, f32[2,24,128]{2,1,0:T(8,128)S(1)}) custom-call(s32[16]{0:T(128)} %len_hbm.1, s32[34]{0:T(128)} %deal_hbm.1, bf16[16,1024]{1,0:T(8,128)(2,1)} %q_hbm.1, bf16[16,512]{1,0:T(8,128)(2,1)} %new_hbm.1, ...), custom_call_target="tpu_custom_call" | custom-call | flops 8388608 | bytes 4194304 | tf_op jit(solution)/shard_map/decode_partials/pallas_call | solution.py:196
  9.0 0.1 collective-permute-start.4
  9.1 3.0 %collective-permute-start.5 = (bf16[32,512]{1,0:T(8,128)(2,1)S(1)}, bf16[32,512]{1,0:T(8,128)(2,1)S(1)}, u32[]{:S(2)}, u32[]{:S(2)}) collective-permute-start(bf16[32,512]{1,0:T(8,128)(2,1)S(1)} %bitcast.8), channel_id=1, source_target_pairs={{0,16},{2,18},{4,20},{6,22},{8,24},{10,26},{12,28},{14,30},{16,0},... | collective-permute-start | bytes 98312 | tf_op jit(solution)/shard_map/ppermute | solution.py:418
  12.1 0.0 collective-permute-done.refs_3_.refs_2_
  12.1 0.1 collective-permute-start.2
  12.9 1.3 %collective-permute-done.5 = bf16[32,512]{1,0:T(8,128)(2,1)S(1)} collective-permute-done((bf16[32,512]{1,0:T(8,128)(2,1)S(1)}, bf16[32,512]{1,0:T(8,128)(2,1)S(1)}, u32[]{:S(2)}, u32[]{:S(2)}) %collective-permute-start.5) | collective-permute-done | bytes 32800 | tf_op jit(solution)/shard_map/ppermute | solution.py:418
  14.2 0.0 collective-permute-done.4.other_ref
  14.2 0.3 join_core.1.own_ref
  14.5 1.7 %collective-permute-start.6 = (bf16[48,512]{1,0:T(8,128)(2,1)S(1)}, bf16[48,512]{1,0:T(8,128)(2,1)S(1)}, u32[]{:S(2)}, u32[]{:S(2)}) collective-permute-start(bf16[48,512]{1,0:T(8,128)(2,1)S(1)} %join_core.1.own_ref), channel_id=1, source_target_pairs={{0,4},{2,6},{4,0},{6,2},{8,12},{10,14},{12,8},{14,10},{16,20},{18,... | collective-permute-start | bytes 147464 | tf_op jit(solution)/shard_map/ppermute | solution.py:418
  16.2 0.4 collective-permute-start.7
  16.6 2.3 %collective-permute-done.2.refs_0_ = bf16[32,1024]{1,0:T(8,128)(2,1)S(1)} collective-permute-done((bf16[32,1024]{1,0:T(8,128)(2,1)S(1)}, bf16[32,1024]{1,0:T(8,128)(2,1)S(1)}, u32[]{:S(2)}, u32[]{:S(2)}) %collective-permute-start.2) | collective-permute-done | bytes 65568 | tf_op jit(solution)/shard_map/ppermute | solution.py:418
  19.0 0.5 %collective-permute-start.10 = (bf16[160,512]{1,0:T(8,128)(2,1)S(1)}, bf16[160,512]{1,0:T(8,128)(2,1)S(1)}, u32[]{:S(2)}, u32[]{:S(2)}) collective-permute-start(bf16[160,512]{1,0:T(8,128)(2,1)S(1)} %collective-permute-done.3.refs_5_.refs_4_), channel_id=1, source_target_pairs={{0,2},{2,0},{4,6},{6,4},{8,10},{10,8},{12,14},{14,12},{16,18},{18,... | collective-permute-start | bytes 491528 | tf_op jit(solution)/shard_map/ppermute | solution.py:418
  19.5 0.1 collective-permute-start.11
  19.5 0.6 %collective-permute-done.7 = bf16[32,512]{1,0:T(8,128)(2,1)S(1)} collective-permute-done((bf16[32,512]{1,0:T(8,128)(2,1)S(1)}, bf16[32,512]{1,0:T(8,128)(2,1)S(1)}, u32[]{:S(2)}, u32[]{:S(2)}) %collective-permute-start.7) | collective-permute-done | bytes 32800 | tf_op jit(solution)/shard_map/ppermute | solution.py:418
  20.1 0.3 join_x.1.own_ref
  20.4 2.7 %collective-permute-start.13 = (bf16[112,512]{1,0:T(8,128)(2,1)S(1)}, bf16[112,512]{1,0:T(8,128)(2,1)S(1)}, u32[]{:S(2)}, u32[]{:S(2)}) collective-permute-start(bf16[112,512]{1,0:T(8,128)(2,1)S(1)} %join_x.1.own_ref), channel_id=1, source_target_pairs={{0,8},{2,10},{4,12},{6,14},{8,0},{10,2},{12,4},{14,6},{16,24},{18,... | collective-permute-start | bytes 344072 | tf_op jit(solution)/shard_map/ppermute | solution.py:418
  23.1 1.1 %prefill_partials.2 = bf16[32,1152]{1,0:T(8,128)(2,1)S(1)} custom-call(s32[8,128]{1,0:T(8,128)S(1)} %broadcast_in_dim.3.off_ref, bf16[32,1024]{1,0:T(8,128)(2,1)S(1)} %collective-permute-done.2.refs_0_, bf16[160,512]{1,0:T(8,128)(2,1)S(1)} %pad_maximum_fusion.refs_1_.refs_0_, bf16[160,512]{1,0:T(8,128)(2,1)S(1)} %collective-permute-done.8.refs_2_.refs_1_, ...), custom_call_target="tpu_custom_call" | custom-call | flops 167772160 | bytes 4194304 | tf_op jit(solution)/shard_map/prefill_partials/pallas_call | solution.py:305
  24.2 3.5 %collective-permute-start.12 = (bf16[32,1152]{1,0:T(8,128)(2,1)S(1)}, bf16[32,1152]{1,0:T(8,128)(2,1)S(1)}, u32[]{:S(2)}, u32[]{:S(2)}) collective-permute-start(bf16[32,1152]{1,0:T(8,128)(2,1)S(1)} %prefill_partials.2), channel_id=1, source_target_pairs={{0,16},{2,18},{4,20},{6,22},{8,24},{10,26},{12,28},{14,30},{16,0},... | collective-permute-start | bytes 221192 | tf_op jit(solution)/shard_map/ppermute | solution.py:418
  27.7 1.1 %prefill_partials.3.refs_0_ = bf16[32,1152]{1,0:T(8,128)(2,1)S(1)} custom-call(s32[8,128]{1,0:T(8,128)S(1)} %broadcast_in_dim.3.off_ref, bf16[32,1024]{1,0:T(8,128)(2,1)S(1)} %get-tuple-element.37.refs_0_, bf16[160,512]{1,0:T(8,128)(2,1)S(1)} %pad_maximum_fusion.refs_1_.refs_0_, bf16[160,512]{1,0:T(8,128)(2,1)S(1)} %collective-permute-done.8.refs_2_.refs_1_, ...), custom_call_target="tpu_custom_call" | custom-call | flops 167772160 | bytes 4194304 | tf_op jit(solution)/shard_map/prefill_partials/pallas_call | solution.py:305
  28.7 0.3 join_z.1
  29.0 1.6 %collective-permute-start.14 = (bf16[48,512]{1,0:T(8,128)(2,1)S(1)}, bf16[48,512]{1,0:T(8,128)(2,1)S(1)}, u32[]{:S(2)}, u32[]{:S(2)}) collective-permute-start(bf16[48,512]{1,0:T(8,128)(2,1)S(1)} %get-tuple-element.39.refs_2_), channel_id=1, source_target_pairs={{0,16},{2,18},{4,20},{6,22},{8,24},{10,26},{12,28},{14,30},{16,0},... | collective-permute-start | bytes 147464 | tf_op jit(solution)/shard_map/ppermute | solution.py:418
  30.7 3.7 %collective-permute-done.14.refs_3_ = bf16[48,512]{1,0:T(8,128)(2,1)S(1)} collective-permute-done((bf16[48,512]{1,0:T(8,128)(2,1)S(1)}, bf16[48,512]{1,0:T(8,128)(2,1)S(1)}, u32[]{:S(2)}, u32[]{:S(2)}) %collective-permute-start.14) | collective-permute-done | bytes 49184 | tf_op jit(solution)/shard_map/ppermute | solution.py:418
  34.4 0.3 join_parts.1.refs_0_
  34.6 1.6 %collective-permute-start.15 = (bf16[48,1024]{1,0:T(8,128)(2,1)S(1)}, bf16[48,1024]{1,0:T(8,128)(2,1)S(1)}, u32[]{:S(2)}, u32[]{:S(2)}) collective-permute-start(bf16[48,1024]{1,0:T(8,128)(2,1)S(1)} %join_parts.1.refs_0_), channel_id=1, source_target_pairs={{0,1},{1,0},{2,3},{3,2},{4,5},{5,4},{6,7},{7,6},{8,9},{9,8},{10,11... | collective-permute-start | bytes 294920 | tf_op jit(solution)/shard_map/ppermute | solution.py:458
  36.2 1.7 %update_cache.1 = bf16[1,128,512]{2,1,0:T(8,128)(2,1)} custom-call(s32[8,128]{1,0:T(8,128)S(1)} %broadcast_in_dim.3.off_ref, bf16[1,128,512]{2,1,0:T(8,128)(2,1)} %cache_hbm.3, bf16[128,512]{1,0:T(8,128)(2,1)S(1)} %get-tuple-element.40.near_ref, bf16[128,512]{1,0:T(8,128)(2,1)S(1)} %collective-permute-done.16.beside_ref, ...), custom_call_target="tpu_custom_call" | custom-call | tf_op jit(solution)/shard_map/update_cache/pallas_call | solution.py:359
  38.0 1.4 %collective-permute-done.15.refs_1_ = bf16[48,1024]{1,0:T(8,128)(2,1)S(1)} collective-permute-done((bf16[48,1024]{1,0:T(8,128)(2,1)S(1)}, bf16[48,1024]{1,0:T(8,128)(2,1)S(1)}, u32[]{:S(2)}, u32[]{:S(2)}) %collective-permute-start.15) | collective-permute-done | bytes 98336 | tf_op jit(solution)/shard_map/ppermute | solution.py:458
  39.3 0.8 %route_outputs.1 = (bf16[1,32,1024]{2,1,0:T(8,128)(2,1)}, bf16[16,1024]{1,0:T(8,128)(2,1)}) custom-call(f32[2,24,128]{2,1,0:T(8,128)S(1)} %get-tuple-element.25.route_ref, bf16[48,1024]{1,0:T(8,128)(2,1)S(1)} %join_parts.1.refs_0_, bf16[48,1024]{1,0:T(8,128)(2,1)S(1)} %collective-permute-done.15.refs_1_), custom_call_target="tpu_custom_call" | custom-call | tf_op jit(solution)/shard_map/route_outputs/pallas_call | solution.py:387
  (18 shorter events, 0.0 us)
Async XLA Ops:
  0.6 8.5 %copy-start.1 = (bf16[1,32,512]{2,1,0:T(8,128)(2,1)S(1)}, bf16[1,32,512]{2,1,0:T(8,128)(2,1)}, u32[]{:S(2)}) copy-start(bf16[1,32,512]{2,1,0:T(8,128)(2,1)} %param.11) | copy-start | bytes 98308
  0.6 11.5 %copy-start = (bf16[1,32,1024]{2,1,0:T(8,128)(2,1)S(1)}, bf16[1,32,1024]{2,1,0:T(8,128)(2,1)}, u32[]{:S(2)}) copy-start(bf16[1,32,1024]{2,1,0:T(8,128)(2,1)} %pre_q_hbm.1) | copy-start | bytes 196612
  1.6 10.5 %collective-permute-start = (bf16[160,512]{1,0:T(8,128)(2,1)S(1)}, bf16[160,512]{1,0:T(8,128)(2,1)S(1)}, u32[]{:S(2)}, u32[]{:S(2)}) collective-permute-start(bf16[160,512]{1,0:T(8,128)(2,1)S(1)} %pad_maximum_fusion.refs_1_.refs_0_), channel_id=1, source_target_pairs={{0,4},{2,6},{4,0},{6,2},{8,12},{10,14},{12,8},{14,10},{16,20},{18,... | collective-permute-start | bytes 491528 | tf_op jit(solution)/shard_map/ppermute | solution.py:418
  4.6 9.6 %collective-permute-start.3 = (bf16[160,512]{1,0:T(8,128)(2,1)S(1)}, bf16[160,512]{1,0:T(8,128)(2,1)S(1)}, u32[]{:S(2)}, u32[]{:S(2)}) collective-permute-start(bf16[160,512]{1,0:T(8,128)(2,1)S(1)} %pad_maximum_fusion.refs_1_.refs_0_), channel_id=1, source_target_pairs={{0,8},{2,10},{4,12},{6,14},{8,0},{10,2},{12,4},{14,6},{16,24},{18,... | collective-permute-start | bytes 491528 | tf_op jit(solution)/shard_map/ppermute | solution.py:418
  6.2 12.7 %collective-permute-start.1 = (bf16[160,512]{1,0:T(8,128)(2,1)S(1)}, bf16[160,512]{1,0:T(8,128)(2,1)S(1)}, u32[]{:S(2)}, u32[]{:S(2)}) collective-permute-start(bf16[160,512]{1,0:T(8,128)(2,1)S(1)} %pad_maximum_fusion.refs_1_.refs_0_), channel_id=1, source_target_pairs={{0,12},{2,14},{4,8},{6,10},{8,4},{10,6},{12,0},{14,2},{16,28},{18,... | collective-permute-start | bytes 491528 | tf_op jit(solution)/shard_map/ppermute | solution.py:418
  9.0 5.2 %collective-permute-start.4 = (bf16[48,512]{1,0:T(8,128)(2,1)S(1)}, bf16[48,512]{1,0:T(8,128)(2,1)S(1)}, u32[]{:S(2)}, u32[]{:S(2)}) collective-permute-start(bf16[48,512]{1,0:T(8,128)(2,1)S(1)} %get-tuple-element.26.own_ref), channel_id=1, source_target_pairs={{0,2},{2,0},{4,6},{6,4},{8,10},{10,8},{12,14},{14,12},{16,18},{18,... | collective-permute-start | bytes 147464 | tf_op jit(solution)/shard_map/ppermute | solution.py:418
  9.1 5.1 %collective-permute-start.5 = (bf16[32,512]{1,0:T(8,128)(2,1)S(1)}, bf16[32,512]{1,0:T(8,128)(2,1)S(1)}, u32[]{:S(2)}, u32[]{:S(2)}) collective-permute-start(bf16[32,512]{1,0:T(8,128)(2,1)S(1)} %bitcast.8), channel_id=1, source_target_pairs={{0,16},{2,18},{4,20},{6,22},{8,24},{10,26},{12,28},{14,30},{16,0},... | collective-permute-start | bytes 98312 | tf_op jit(solution)/shard_map/ppermute | solution.py:418
  12.1 6.8 %collective-permute-start.2 = (bf16[32,1024]{1,0:T(8,128)(2,1)S(1)}, bf16[32,1024]{1,0:T(8,128)(2,1)S(1)}, u32[]{:S(2)}, u32[]{:S(2)}) collective-permute-start(bf16[32,1024]{1,0:T(8,128)(2,1)S(1)} %bitcast.6), channel_id=1, source_target_pairs={{0,16},{2,18},{4,20},{6,22},{8,24},{10,26},{12,28},{14,30},{16,0},... | collective-permute-start | bytes 196616 | tf_op jit(solution)/shard_map/ppermute | solution.py:418
  14.5 5.0 %collective-permute-start.6 = (bf16[48,512]{1,0:T(8,128)(2,1)S(1)}, bf16[48,512]{1,0:T(8,128)(2,1)S(1)}, u32[]{:S(2)}, u32[]{:S(2)}) collective-permute-start(bf16[48,512]{1,0:T(8,128)(2,1)S(1)} %join_core.1.own_ref), channel_id=1, source_target_pairs={{0,4},{2,6},{4,0},{6,2},{8,12},{10,14},{12,8},{14,10},{16,20},{18,... | collective-permute-start | bytes 147464 | tf_op jit(solution)/shard_map/ppermute | solution.py:418
  16.2 3.9 %collective-permute-start.7 = (bf16[32,512]{1,0:T(8,128)(2,1)S(1)}, bf16[32,512]{1,0:T(8,128)(2,1)S(1)}, u32[]{:S(2)}, u32[]{:S(2)}) collective-permute-start(bf16[32,512]{1,0:T(8,128)(2,1)S(1)} %collective-permute-done.5), channel_id=1, source_target_pairs={{0,4},{2,6},{4,0},{6,2},{8,12},{10,14},{12,8},{14,10},{16,20},{18,... | collective-permute-start | bytes 98312 | tf_op jit(solution)/shard_map/ppermute | solution.py:418
  16.6 6.5 %collective-permute-start.8 = (bf16[160,512]{1,0:T(8,128)(2,1)S(1)}, bf16[160,512]{1,0:T(8,128)(2,1)S(1)}, u32[]{:S(2)}, u32[]{:S(2)}) collective-permute-start(bf16[160,512]{1,0:T(8,128)(2,1)S(1)} %pad_maximum_fusion.refs_1_.refs_0_), channel_id=1, source_target_pairs={{0,2},{2,0},{4,6},{6,4},{8,10},{10,8},{12,14},{14,12},{16,18},{18,... | collective-permute-start | bytes 491528 | tf_op jit(solution)/shard_map/ppermute | solution.py:418
  18.9 4.2 %collective-permute-start.9 = (bf16[160,512]{1,0:T(8,128)(2,1)S(1)}, bf16[160,512]{1,0:T(8,128)(2,1)S(1)}, u32[]{:S(2)}, u32[]{:S(2)}) collective-permute-start(bf16[160,512]{1,0:T(8,128)(2,1)S(1)} %collective-permute-done.refs_3_.refs_2_), channel_id=1, source_target_pairs={{0,2},{2,0},{4,6},{6,4},{8,10},{10,8},{12,14},{14,12},{16,18},{18,... | collective-permute-start | bytes 491528 | tf_op jit(solution)/shard_map/ppermute | solution.py:418
  19.0 4.2 %collective-permute-start.10 = (bf16[160,512]{1,0:T(8,128)(2,1)S(1)}, bf16[160,512]{1,0:T(8,128)(2,1)S(1)}, u32[]{:S(2)}, u32[]{:S(2)}) collective-permute-start(bf16[160,512]{1,0:T(8,128)(2,1)S(1)} %collective-permute-done.3.refs_5_.refs_4_), channel_id=1, source_target_pairs={{0,2},{2,0},{4,6},{6,4},{8,10},{10,8},{12,14},{14,12},{16,18},{18,... | collective-permute-start | bytes 491528 | tf_op jit(solution)/shard_map/ppermute | solution.py:418
  19.5 3.7 %collective-permute-start.11 = (bf16[160,512]{1,0:T(8,128)(2,1)S(1)}, bf16[160,512]{1,0:T(8,128)(2,1)S(1)}, u32[]{:S(2)}, u32[]{:S(2)}) collective-permute-start(bf16[160,512]{1,0:T(8,128)(2,1)S(1)} %collective-permute-done.1.refs_7_.refs_6_), channel_id=1, source_target_pairs={{0,2},{2,0},{4,6},{6,4},{8,10},{10,8},{12,14},{14,12},{16,18},{18,... | collective-permute-start | bytes 491528 | tf_op jit(solution)/shard_map/ppermute | solution.py:418
  20.4 8.3 %collective-permute-start.13 = (bf16[112,512]{1,0:T(8,128)(2,1)S(1)}, bf16[112,512]{1,0:T(8,128)(2,1)S(1)}, u32[]{:S(2)}, u32[]{:S(2)}) collective-permute-start(bf16[112,512]{1,0:T(8,128)(2,1)S(1)} %join_x.1.own_ref), channel_id=1, source_target_pairs={{0,8},{2,10},{4,12},{6,14},{8,0},{10,2},{12,4},{14,6},{16,24},{18,... | collective-permute-start | bytes 344072 | tf_op jit(solution)/shard_map/ppermute | solution.py:418
  24.2 10.2 %collective-permute-start.12 = (bf16[32,1152]{1,0:T(8,128)(2,1)S(1)}, bf16[32,1152]{1,0:T(8,128)(2,1)S(1)}, u32[]{:S(2)}, u32[]{:S(2)}) collective-permute-start(bf16[32,1152]{1,0:T(8,128)(2,1)S(1)} %prefill_partials.2), channel_id=1, source_target_pairs={{0,16},{2,18},{4,20},{6,22},{8,24},{10,26},{12,28},{14,30},{16,0},... | collective-permute-start | bytes 221192 | tf_op jit(solution)/shard_map/ppermute | solution.py:418
  29.0 5.3 %collective-permute-start.14 = (bf16[48,512]{1,0:T(8,128)(2,1)S(1)}, bf16[48,512]{1,0:T(8,128)(2,1)S(1)}, u32[]{:S(2)}, u32[]{:S(2)}) collective-permute-start(bf16[48,512]{1,0:T(8,128)(2,1)S(1)} %get-tuple-element.39.refs_2_), channel_id=1, source_target_pairs={{0,16},{2,18},{4,20},{6,22},{8,24},{10,26},{12,28},{14,30},{16,0},... | collective-permute-start | bytes 147464 | tf_op jit(solution)/shard_map/ppermute | solution.py:418
  30.7 5.6 %collective-permute-start.16 = (bf16[128,512]{1,0:T(8,128)(2,1)S(1)}, bf16[128,512]{1,0:T(8,128)(2,1)S(1)}, u32[]{:S(2)}, u32[]{:S(2)}) collective-permute-start(bf16[128,512]{1,0:T(8,128)(2,1)S(1)} %get-tuple-element.40.near_ref), channel_id=1, source_target_pairs={{0,2},{2,0},{4,6},{6,4},{8,10},{10,8},{12,14},{14,12},{16,18},{18,... | collective-permute-start | bytes 393224 | tf_op jit(solution)/shard_map/ppermute | solution.py:418
  34.6 4.7 %collective-permute-start.15 = (bf16[48,1024]{1,0:T(8,128)(2,1)S(1)}, bf16[48,1024]{1,0:T(8,128)(2,1)S(1)}, u32[]{:S(2)}, u32[]{:S(2)}) collective-permute-start(bf16[48,1024]{1,0:T(8,128)(2,1)S(1)} %join_parts.1.refs_0_), channel_id=1, source_target_pairs={{0,1},{1,0},{2,3},{3,2},{4,5},{5,4},{6,7},{7,6},{8,9},{9,8},{10,11... | collective-permute-start | bytes 294920 | tf_op jit(solution)/shard_map/ppermute | solution.py:458

commit v12 on v7

--- a/solution.py
+++ b/solution.py
@@ -88,7 +88,7 @@
     pre_q_hbm,
     pre_new_hbm,
     pre_cache_hbm,
-    out_hbm,
+    table,
     shared_ref,
     pre_q_ref,
     route_ref,
@@ -96,7 +96,6 @@
     deal,
     query_ref,
     new_ref,
-    table,
     sems,
 ):
     slots, ctx, _ = table.shape
@@ -115,11 +114,10 @@
         (pre_new_hbm.at[0], shared_ref.at[pl.ds(ctx, tokens), :]),
     ]
     small = [pltpu.make_async_copy(a, b, sems.at[i]) for i, (a, b) in enumerate(small)]
-    loads, stores = [], []
+    loads = []
     for c in range(CHUNKS):
         part = pl.ds(c * chunk, chunk)
         loads.append(pltpu.make_async_copy(cache_hbm.at[part], table.at[part], sems.at[7 + c]))
-        stores.append(pltpu.make_async_copy(table.at[part], out_hbm.at[part], sems.at[7 + CHUNKS + c]))
     for copy in small + loads:
         copy.start()
     for copy in small:
@@ -162,7 +160,6 @@
                     in_tile == relative - start, new_ref[s : s + 1, :], tile
                 )
 
-        stores[c].start()
         for g in range(KEY_VALUE_HEADS):
             key = table[pl.ds(c * chunk, chunk), :, pl.ds(g * HEAD_SIZE, HEAD_SIZE)]
             wide = dot_t(queries[g], key.reshape(chunk * ctx, HEAD_SIZE))
@@ -193,8 +190,6 @@
     last = pl.ds(first + KEY_VALUE_HEADS * slots, slots)
     shared_ref[last, pl.ds(0, STATS)] = stats_block(columns, slots)
     shared_ref[last, pl.ds(STATS, KVW - STATS)] = jnp.zeros((slots, KVW - STATS), BF16)
-    for copy in stores:
-        copy.wait()
 
 
 def decode_partials(lengths, dealing, queries, new_rows, cache, pre_queries, pre_new, pre_cache, req):
@@ -204,9 +199,9 @@
     return pl.pallas_call(
         decode_kernel,
         in_specs=[HBM] * len(inputs),
-        out_specs=[HBM, VMEM, VMEM, VMEM],
+        out_specs=[VMEM] * 4,
         out_shape=[
-            pltpu.HBM(cache.shape, BF16),
+            pltpu.VMEM(cache.shape, BF16),
             pltpu.VMEM((rows, KVW), BF16),
             pltpu.VMEM(pre_queries.shape[1:], BF16),
             pltpu.VMEM((req, slots + 8, HEAD_SIZE), F32),
@@ -216,8 +211,7 @@
             pltpu.SMEM(dealing.shape, jnp.int32),
             pltpu.VMEM(queries.shape, BF16),
             pltpu.VMEM(new_rows.shape, BF16),
-            pltpu.VMEM(cache.shape, BF16),
-            pltpu.SemaphoreType.DMA((7 + 2 * CHUNKS,)),
+            pltpu.SemaphoreType.DMA((7 + CHUNKS,)),
         ],
         compiler_params=pltpu.CompilerParams(vmem_limit_bytes=16 << 20),
         cost_estimate=pl.CostEstimate(
@@ -227,7 +221,32 @@
     )(*[pltpu.with_memory_space_constraint(x, pltpu.HBM) for x in inputs])
 
 
-def prefill_kernel(query_count, ctx, slots, off_ref, *refs):
+def store_kernel(cache_ref, out_hbm, sems):
+    chunk = cache_ref.shape[0] // CHUNKS
+    copies = []
+    for c in range(CHUNKS):
+        part = pl.ds(c * chunk, chunk)
+        copies.append(pltpu.make_async_copy(cache_ref.at[part], out_hbm.at[part], sems.at[c]))
+    for copy in copies:
+        copy.start()
+    for copy in copies:
+        copy.wait()
+
+
+def store_cache(cache):
+    return pl.pallas_call(
+        store_kernel,
+        in_specs=[VMEM],
+        out_specs=HBM,
+        out_shape=pltpu.HBM(cache.shape, BF16),
+        scratch_shapes=[pltpu.SemaphoreType.DMA((CHUNKS,))],
+        compiler_params=pltpu.CompilerParams(vmem_limit_bytes=16 << 20),
+        name="store_cache",
+    )(pltpu.with_memory_space_constraint(cache, pltpu.VMEM))
+
+
+def prefill_kernel(sets, ctx, slots, off_ref, *refs):
+    query_count = len(sets)
     packs, tables, outs = refs[:query_count], refs[query_count:-query_count], refs[-query_count:]
     tokens = packs[0].shape[0]
     span = ctx + tokens
@@ -247,7 +266,7 @@
         keys = jnp.concatenate([t[pl.ds(0, span), pl.ds(g * HEAD_SIZE, HEAD_SIZE)] for t in tables], axis=0)
         values = jnp.concatenate([t[pl.ds(0, span), pl.ds(KW + g * HEAD_SIZE, HEAD_SIZE)] for t in tables], axis=0)
         for k in range(query_count):
-            token = (me ^ (k * KEY_SET)) * tokens + in_block
+            token = (me ^ (sets[k] * KEY_SET)) * tokens + in_block
             query = jnp.concatenate(
                 [packs[k][:, pl.ds((g * GROUP + h) * HEAD_SIZE, HEAD_SIZE)] for h in range(GROUP)], axis=0
             )
@@ -265,6 +284,10 @@
                 outs[k][pl.ds(0, tokens), pl.ds((g * GROUP + h) * HEAD_SIZE, HEAD_SIZE)] = normed[part]
                 for term, value in enumerate(split3(logs[part])):
                     stats[k] = jnp.where(lane == term * QUERY_HEADS + g * GROUP + h, value, stats[k])
+    for k in range(query_count):
+        outs[k][pl.ds(0, tokens), pl.ds(QW, STATS)] = stats[k].astype(BF16)
+    if outs[0].shape[0] == tokens:
+        return
     decodes = [
         jnp.concatenate(
             [t[pl.ds(span + g * slots, slots), :] for g in range(KEY_VALUE_HEADS)]
@@ -276,19 +299,19 @@
     joined, logs = join(decodes)
     joined_stats = stats_block([logs[:, h * HEAD_SIZE : h * HEAD_SIZE + 1] for h in range(QUERY_HEADS)], slots)
     for k in range(query_count):
-        outs[k][pl.ds(0, tokens), pl.ds(QW, STATS)] = stats[k].astype(BF16)
         outs[k][pl.ds(tokens, slots), pl.ds(0, QW)] = joined
         outs[k][pl.ds(tokens, slots), pl.ds(QW, STATS)] = joined_stats
 
 
-def prefill_partials(offset, packs, tables, ctx, slots):
+def prefill_partials(offset, packs, tables, ctx, slots, sets, with_decode):
     tokens = packs[0].shape[0]
+    rows = tokens + slots if with_decode else tokens
     pairs = len(packs) * tokens * KEY_SET * (ctx + tokens)
     return pl.pallas_call(
-        functools.partial(prefill_kernel, len(packs), ctx, slots),
+        functools.partial(prefill_kernel, sets, ctx, slots),
         in_specs=[VMEM] * (1 + len(packs) + len(tables)),
         out_specs=[VMEM] * len(packs),
-        out_shape=[jax.ShapeDtypeStruct((tokens + slots, QW + STATS), BF16)] * len(packs),
+        out_shape=[pltpu.VMEM((rows, QW + STATS), BF16)] * len(packs),
         compiler_params=pltpu.CompilerParams(vmem_limit_bytes=32 << 20),
         cost_estimate=pl.CostEstimate(
             flops=4 * pairs * QW, bytes_accessed=4 << 20, transcendentals=pairs * QUERY_HEADS
@@ -297,19 +320,23 @@
     )(offset, *packs, *tables)
 
 
-def join_kernel(*refs):
-    refs[-1][...] = join([ref[...] for ref in refs[:-1]])[0]
-
-
-def join_parts(parts):
+def join_kernel(kept_ref, *refs):
+    parts, out_ref = refs[:-1], refs[-1]
+    tokens = kept_ref.shape[0]
+    slots = out_ref.shape[0] - tokens
+    out_ref[pl.ds(0, tokens), :] = join([kept_ref[...]] + [p[pl.ds(0, tokens), :] for p in parts[1:]])[0]
+    out_ref[pl.ds(tokens, slots), :] = join([p[pl.ds(tokens, slots), :] for p in parts])[0]
+
+
+def join_parts(kept, parts):
     return pl.pallas_call(
         join_kernel,
-        in_specs=[VMEM] * len(parts),
+        in_specs=[VMEM] * (1 + len(parts)),
         out_specs=VMEM,
         out_shape=jax.ShapeDtypeStruct((parts[0].shape[0], QW), BF16),
         compiler_params=pltpu.CompilerParams(vmem_limit_bytes=16 << 20),
         name="join_parts",
-    )(*parts)
+    )(kept, *parts)
 
 
 def update_kernel(tokens, sets, off_ref, cache_hbm, near_ref, beside_ref, *refs):
@@ -402,6 +429,7 @@
 
     others = range(KEY_SET, blk, KEY_SET)
     packs = [swap(prefill_queries[0], k) for k in others]
+    far = jnp.concatenate([swap(new_prefill[0], k) for k in others], axis=0)
     decode_cache_out, table, queries, route = decode_partials(
         decode_lengths,
         dealing,
@@ -415,20 +443,21 @@
     )
     lanes = [table] + [swap(table, k) for k in range(2, KEY_SET, 2)]
     offset = jnp.full((8, HEAD_SIZE), prefill_offsets[0], jnp.int32)
-    lanes[1], offset, *packs = lax.optimization_barrier((lanes[1], offset, *packs))
-    for i in range(2, len(lanes)):
-        lanes[i] = after(lanes[i], lanes[i - 1])
+    decode_cache_out = store_cache(decode_cache_out)
+    lanes[1], offset, far, _ = lax.optimization_barrier((lanes[1], offset, far, decode_cache_out))
+    lanes[2] = after(lanes[2], lanes[1])
+    far_across = swap(far, 2)
+    lanes[3], packs, far_across, _ = lax.optimization_barrier((lanes[3], packs, far_across, lanes[2]))
     tables = [t for lane in lanes for t in (lane, swap(lane, 1))]
 
-    parts = prefill_partials(offset, [queries] + packs, tables, ctx, slots)
-    attended = join_parts([parts[0]] + [swap(part, k * KEY_SET) for k, part in enumerate(parts) if k])
-
-    own_rows = after(new_prefill[0], lanes[-1])
-    far = jnp.concatenate([swap(own_rows, k) for k in others], axis=0)
-    far = after(far, parts[0])
-    for k in range(2, KEY_SET, 2):
-        if k & (k - 1) == 0:
-            far = jnp.concatenate([far, swap(far, k)], axis=0)
+    sent = prefill_partials(offset, packs, tables, ctx, slots, [k // KEY_SET for k in others], True)
+    queries = after(queries, sent[0])
+    (kept,) = prefill_partials(offset, [queries], tables, ctx, slots, [0], False)
+    attended = join_parts(kept, [sent[0]] + [swap(p, k) for k, p in zip(others, sent)])
+
+    far = jnp.concatenate([far, far_across], axis=0)
+    far = after(far, sent[0])
+    far = jnp.concatenate([far, after(swap(far, 4), kept)], axis=0)
     prefill_cache_out = update_cache(
         offset, prefill_cache, far, swap(far, 1), tables, tokens, len(others)
     )

time: 40.7 us -> 39.4 us (0.968)
  starting transfers between devices: 18.3 us -> 14 us
  waiting for transfers between devices: 12.9 us -> 14.8 us
  Pallas kernels: 7.93 us -> 9.1 us
    ppermute x13, starting transfers between devices: 16.7 us -> 12.4 us  [swap(): return lax.ppermute(array, BLK, [(i, i ^ distance) for i in range(blk)])]
    ppermute x13, waiting for transfers between devices: 11 us -> 13.2 us  [swap(): return lax.ppermute(array, BLK, [(i, i ^ distance) for i in range(blk)])]
    pallas_call x3 -> x5, Pallas kernels: 5.45 us -> 6.63 us  [the longest x1 2.6 us: decode_partials(): pl.pallas_call(decode_kernel, in_specs=[HBM] * len(inputs), out_specs=[VM...]
  transfers between devices with their start and end apart: 14 -> 14, of which waited for: 5 -> 7; matrix products, arithmetic and copies ran while one was open for 0% -> 0% of each run, Pallas kernels for 10% -> 11%
where the time goes in v12:
time: 39.4 us; the launch traced here: 39.2 us
  waiting for transfers between devices  14.8 us (38%)
  starting transfers between devices  14 us (36%)
  Pallas kernels  9.1 us (23%)
  between operations  1.39 us (4%)
    ppermute x13, waiting for transfers between devices, swap(): return lax.ppermute(array, BLK, [(i, i ^ distance) for i in range(blk)])  13.2 us
    ppermute x13, starting transfers between devices, swap(): return lax.ppermute(array, BLK, [(i, i ^ distance) for i in range(blk)])  12.4 us
    pallas_call x1, Pallas kernels, decode_partials(): pl.pallas_call(decode_kernel, in_specs=[HBM] * len(inputs), out_specs=[VM...  2.6 us
    pallas_call x2, Pallas kernels, prefill_partials(): pl.pallas_call(functools.partial(prefill_kernel, sets, ctx, slots), in_sp...  2.42 us
    pallas_call x1, Pallas kernels, update_cache(): pl.pallas_call(functools.partial(update_kernel, tokens, sets), in_specs=[...  1.71 us
    ppermute x1, waiting for transfers between devices, per_device(): held = [attended, lax.ppermute(attended, 'req', [(0, 1), (1, 0)])]  1.59 us
    ppermute x1, starting transfers between devices, per_device(): held = [attended, lax.ppermute(attended, 'req', [(0, 1), (1, 0)])]  1.57 us
    pallas_call x1, Pallas kernels, store_cache(): pl.pallas_call(store_kernel, in_specs=[VMEM], out_specs=HBM, out_shape=pl...  1.34 us
  transfers between devices with their start and end apart: 14, of which 7 were waited for; matrix products, arithmetic and copies ran while one was open for 0% of the time, Pallas kernels for 11%

profile of v12, /device:TPU:0, one launch (start us, length us, event | category | flops | bytes accessed | tf_op | source)
XLA Modules:
  0.0 39.2 jit_solution(920475651072929626)
XLA Ops:
  0.7 2.6 %decode_partials.1 = (bf16[16,128,512]{2,1,0:T(8,128)(2,1)S(1)}, bf16[208,512]{1,0:T(8,128)(2,1)S(1)}, bf16[32,1024]{1,0:T(8,128)(2,1)S(1)}, f32[2,24,128]{2,1,0:T(8,128)S(1)}) custom-call(s32[16]{0:T(128)} %len_hbm.1, s32[34]{0:T(128)} %deal_hbm.1, bf16[16,1024]{1,0:T(8,128)(2,1)} %q_hbm.1, bf16[16,512]{1,0:T(8,128)(2,1)} %new_hbm.1, ...), custom_call_target="tpu_custom_call" | custom-call | flops 8388608 | bytes 4194304 | tf_op jit(solution)/shard_map/decode_partials/pallas_call | solution.py:199
  3.3 3.0 %collective-permute-start = (bf16[208,512]{1,0:T(8,128)(2,1)S(1)}, bf16[208,512]{1,0:T(8,128)(2,1)S(1)}, u32[]{:S(2)}, u32[]{:S(2)}) collective-permute-start(bf16[208,512]{1,0:T(8,128)(2,1)S(1)} %get-tuple-element.23.refs_1_.refs_0_), channel_id=1, source_target_pairs={{0,4},{2,6},{4,0},{6,2},{8,12},{10,14},{12,8},{14,10},{16,20},{18,... | collective-permute-start | bytes 638984 | tf_op jit(solution)/shard_map/ppermute | solution.py:425
  6.2 1.6 %collective-permute-start.5 = (bf16[208,512]{1,0:T(8,128)(2,1)S(1)}, bf16[208,512]{1,0:T(8,128)(2,1)S(1)}, u32[]{:S(2)}, u32[]{:S(2)}) collective-permute-start(bf16[208,512]{1,0:T(8,128)(2,1)S(1)} %get-tuple-element.23.refs_1_.refs_0_), channel_id=1, source_target_pairs={{0,8},{2,10},{4,12},{6,14},{8,0},{10,2},{12,4},{14,6},{16,24},{18,... | collective-permute-start | bytes 638984 | tf_op jit(solution)/shard_map/ppermute | solution.py:425
  7.9 0.0 collective-permute-start.2
  7.9 3.0 %collective-permute-start.1 = (bf16[32,512]{1,0:T(8,128)(2,1)S(1)}, bf16[32,512]{1,0:T(8,128)(2,1)S(1)}, u32[]{:S(2)}, u32[]{:S(2)}) collective-permute-start(bf16[32,512]{1,0:T(8,128)(2,1)S(1)} %bitcast.5), channel_id=1, source_target_pairs={{0,16},{2,18},{4,20},{6,22},{8,24},{10,26},{12,28},{14,30},{16,0},... | collective-permute-start | bytes 98312 | tf_op jit(solution)/shard_map/ppermute | solution.py:425
  10.8 0.1 collective-permute-start.3
  10.9 1.3 %store_cache.1 = bf16[16,128,512]{2,1,0:T(8,128)(2,1)} custom-call(bf16[16,128,512]{2,1,0:T(8,128)(2,1)S(1)} %get-tuple-element.24.cache_ref), custom_call_target="tpu_custom_call" | custom-call | tf_op jit(solution)/shard_map/store_cache/pallas_call | solution.py:237
  12.9 5.1 %collective-permute-done.1 = bf16[32,512]{1,0:T(8,128)(2,1)S(1)} collective-permute-done((bf16[32,512]{1,0:T(8,128)(2,1)S(1)}, bf16[32,512]{1,0:T(8,128)(2,1)S(1)}, u32[]{:S(2)}, u32[]{:S(2)}) %collective-permute-start.1) | collective-permute-done | bytes 32800 | tf_op jit(solution)/shard_map/ppermute | solution.py:425
  18.0 0.0 collective-permute-done.refs_3_.refs_2_
  18.0 0.5 %collective-permute-start.4 = (bf16[32,512]{1,0:T(8,128)(2,1)S(1)}, bf16[32,512]{1,0:T(8,128)(2,1)S(1)}, u32[]{:S(2)}, u32[]{:S(2)}) collective-permute-start(bf16[32,512]{1,0:T(8,128)(2,1)S(1)} %collective-permute-done.1), channel_id=1, source_target_pairs={{0,4},{2,6},{4,0},{6,2},{8,12},{10,14},{12,8},{14,10},{16,20},{18,... | collective-permute-start | bytes 98312 | tf_op jit(solution)/shard_map/ppermute | solution.py:425
  18.6 0.0 collective-permute-start.6
  18.6 0.0 collective-permute-done.5.refs_5_.refs_4_
  18.6 0.5 %collective-permute-start.7 = (bf16[208,512]{1,0:T(8,128)(2,1)S(1)}, bf16[208,512]{1,0:T(8,128)(2,1)S(1)}, u32[]{:S(2)}, u32[]{:S(2)}) collective-permute-start(bf16[208,512]{1,0:T(8,128)(2,1)S(1)} %collective-permute-done.refs_3_.refs_2_), channel_id=1, source_target_pairs={{0,2},{2,0},{4,6},{6,4},{8,10},{10,8},{12,14},{14,12},{16,18},{18,... | collective-permute-start | bytes 638984 | tf_op jit(solution)/shard_map/ppermute | solution.py:425
  19.1 0.0 collective-permute-done.3.refs_0_
  19.1 0.1 collective-permute-start.8
  19.2 0.4 collective-permute-done.2.refs_7_.refs_6_
  19.5 2.4 %collective-permute-done.4 = bf16[32,512]{1,0:T(8,128)(2,1)S(1)} collective-permute-done((bf16[32,512]{1,0:T(8,128)(2,1)S(1)}, bf16[32,512]{1,0:T(8,128)(2,1)S(1)}, u32[]{:S(2)}, u32[]{:S(2)}) %collective-permute-start.4) | collective-permute-done | bytes 32800 | tf_op jit(solution)/shard_map/ppermute | solution.py:425
  22.0 0.0 collective-permute-start.9
  22.0 0.0 collective-permute-done.8.refs_6_.refs_5_
  22.0 0.0 collective-permute-done.7.refs_4_.refs_3_
  22.0 1.4 %collective-permute-done.9.refs_8_.refs_7_ = bf16[208,512]{1,0:T(8,128)(2,1)S(1)} collective-permute-done((bf16[208,512]{1,0:T(8,128)(2,1)S(1)}, bf16[208,512]{1,0:T(8,128)(2,1)S(1)}, u32[]{:S(2)}, u32[]{:S(2)}) %collective-permute-start.9) | collective-permute-done | bytes 213024 | tf_op jit(solution)/shard_map/ppermute | solution.py:425
  23.4 1.4 %prefill_partials.2.refs_0_ = bf16[48,1152]{1,0:T(8,128)(2,1)S(1)} custom-call(s32[8,128]{1,0:T(8,128)S(1)} %broadcast_in_dim.3.off_ref, bf16[32,1024]{1,0:T(8,128)(2,1)S(1)} %collective-permute-done.3.refs_0_, bf16[208,512]{1,0:T(8,128)(2,1)S(1)} %get-tuple-element.23.refs_1_.refs_0_, bf16[208,512]{1,0:T(8,128)(2,1)S(1)} %collective-permute-done.6.refs_2_.refs_1_, ...), custom_call_target="tpu_custom_call" | custom-call | flops 167772160 | bytes 4194304 | tf_op jit(solution)/shard_map/prefill_partials/pallas_call | solution.py:310
  24.8 3.4 %collective-permute-start.10 = (bf16[48,1152]{1,0:T(8,128)(2,1)S(1)}, bf16[48,1152]{1,0:T(8,128)(2,1)S(1)}, u32[]{:S(2)}, u32[]{:S(2)}) collective-permute-start(bf16[48,1152]{1,0:T(8,128)(2,1)S(1)} %prefill_partials.2.refs_0_), channel_id=1, source_target_pairs={{0,16},{2,18},{4,20},{6,22},{8,24},{10,26},{12,28},{14,30},{16,0},... | collective-permute-start | bytes 331784 | tf_op jit(solution)/shard_map/ppermute | solution.py:425
  28.3 0.2 collective-permute-start.12
  28.4 1.0 %prefill_partials.3.kept_ref = bf16[32,1152]{1,0:T(8,128)(2,1)S(1)} custom-call(s32[8,128]{1,0:T(8,128)S(1)} %broadcast_in_dim.3.off_ref, bf16[32,1024]{1,0:T(8,128)(2,1)S(1)} %get-tuple-element.32.refs_0_, bf16[208,512]{1,0:T(8,128)(2,1)S(1)} %get-tuple-element.23.refs_1_.refs_0_, bf16[208,512]{1,0:T(8,128)(2,1)S(1)} %collective-permute-done.6.refs_2_.refs_1_, ...), custom_call_target="tpu_custom_call" | custom-call | flops 167772160 | bytes 4194304 | tf_op jit(solution)/shard_map/prefill_partials/pallas_call | solution.py:310
  29.5 3.4 %collective-permute-done.12 = bf16[64,512]{1,0:T(8,128)(2,1)S(1)} collective-permute-done((bf16[64,512]{1,0:T(8,128)(2,1)S(1)}, bf16[64,512]{1,0:T(8,128)(2,1)S(1)}, u32[]{:S(2)}, u32[]{:S(2)}) %collective-permute-start.12) | collective-permute-done | bytes 65568 | tf_op jit(solution)/shard_map/ppermute | solution.py:425
  32.9 0.4 collective-permute-done.10.refs_1_
  33.3 0.3 join_parts.1.refs_0_
  33.6 1.6 %collective-permute-start.11 = (bf16[48,1024]{1,0:T(8,128)(2,1)S(1)}, bf16[48,1024]{1,0:T(8,128)(2,1)S(1)}, u32[]{:S(2)}, u32[]{:S(2)}) collective-permute-start(bf16[48,1024]{1,0:T(8,128)(2,1)S(1)} %join_parts.1.refs_0_), channel_id=1, source_target_pairs={{0,1},{1,0},{2,3},{3,2},{4,5},{5,4},{6,7},{7,6},{8,9},{9,8},{10,11... | collective-permute-start | bytes 294920 | tf_op jit(solution)/shard_map/ppermute | solution.py:466
  35.2 1.7 %update_cache.1 = bf16[1,128,512]{2,1,0:T(8,128)(2,1)} custom-call(s32[8,128]{1,0:T(8,128)S(1)} %broadcast_in_dim.3.off_ref, bf16[1,128,512]{2,1,0:T(8,128)(2,1)} %cache_hbm.3, bf16[128,512]{1,0:T(8,128)(2,1)S(1)} %constant_dynamic-update-slice_fusion.near_ref, bf16[128,512]{1,0:T(8,128)(2,1)S(1)} %collective-permute-done.13.beside_ref, ...), custom_call_target="tpu_custom_call" | custom-call | tf_op jit(solution)/shard_map/update_cache/pallas_call | solution.py:366
  36.9 1.6 %collective-permute-done.11.refs_1_ = bf16[48,1024]{1,0:T(8,128)(2,1)S(1)} collective-permute-done((bf16[48,1024]{1,0:T(8,128)(2,1)S(1)}, bf16[48,1024]{1,0:T(8,128)(2,1)S(1)}, u32[]{:S(2)}, u32[]{:S(2)}) %collective-permute-start.11) | collective-permute-done | bytes 98336 | tf_op jit(solution)/shard_map/ppermute | solution.py:466
  38.5 0.8 %route_outputs.1 = (bf16[1,32,1024]{2,1,0:T(8,128)(2,1)}, bf16[16,1024]{1,0:T(8,128)(2,1)}) custom-call(f32[2,24,128]{2,1,0:T(8,128)S(1)} %get-tuple-element.22.route_ref, bf16[48,1024]{1,0:T(8,128)(2,1)S(1)} %join_parts.1.refs_0_, bf16[48,1024]{1,0:T(8,128)(2,1)S(1)} %collective-permute-done.11.refs_1_), custom_call_target="tpu_custom_call" | custom-call | tf_op jit(solution)/shard_map/route_outputs/pallas_call | solution.py:394
  (11 shorter events, 0.0 us)
Async XLA Ops:
  0.6 7.2 %copy-start.1 = (bf16[1,32,512]{2,1,0:T(8,128)(2,1)S(1)}, bf16[1,32,512]{2,1,0:T(8,128)(2,1)}, u32[]{:S(2)}) copy-start(bf16[1,32,512]{2,1,0:T(8,128)(2,1)} %pre_new_hbm.1) | copy-start | bytes 98308
  0.6 10.2 %copy-start = (bf16[1,32,1024]{2,1,0:T(8,128)(2,1)S(1)}, bf16[1,32,1024]{2,1,0:T(8,128)(2,1)}, u32[]{:S(2)}) copy-start(bf16[1,32,1024]{2,1,0:T(8,128)(2,1)} %pre_q_hbm.1) | copy-start | bytes 196612
  3.3 14.8 %collective-permute-start = (bf16[208,512]{1,0:T(8,128)(2,1)S(1)}, bf16[208,512]{1,0:T(8,128)(2,1)S(1)}, u32[]{:S(2)}, u32[]{:S(2)}) collective-permute-start(bf16[208,512]{1,0:T(8,128)(2,1)S(1)} %get-tuple-element.23.refs_1_.refs_0_), channel_id=1, source_target_pairs={{0,4},{2,6},{4,0},{6,2},{8,12},{10,14},{12,8},{14,10},{16,20},{18,... | collective-permute-start | bytes 638984 | tf_op jit(solution)/shard_map/ppermute | solution.py:425
  6.2 12.3 %collective-permute-start.5 = (bf16[208,512]{1,0:T(8,128)(2,1)S(1)}, bf16[208,512]{1,0:T(8,128)(2,1)S(1)}, u32[]{:S(2)}, u32[]{:S(2)}) collective-permute-start(bf16[208,512]{1,0:T(8,128)(2,1)S(1)} %get-tuple-element.23.refs_1_.refs_0_), channel_id=1, source_target_pairs={{0,8},{2,10},{4,12},{6,14},{8,0},{10,2},{12,4},{14,6},{16,24},{18,... | collective-permute-start | bytes 638984 | tf_op jit(solution)/shard_map/ppermute | solution.py:425
  7.9 11.7 %collective-permute-start.2 = (bf16[208,512]{1,0:T(8,128)(2,1)S(1)}, bf16[208,512]{1,0:T(8,128)(2,1)S(1)}, u32[]{:S(2)}, u32[]{:S(2)}) collective-permute-start(bf16[208,512]{1,0:T(8,128)(2,1)S(1)} %get-tuple-element.23.refs_1_.refs_0_), channel_id=1, source_target_pairs={{0,12},{2,14},{4,8},{6,10},{8,4},{10,6},{12,0},{14,2},{16,28},{18,... | collective-permute-start | bytes 638984 | tf_op jit(solution)/shard_map/ppermute | solution.py:425
  7.9 10.2 %collective-permute-start.1 = (bf16[32,512]{1,0:T(8,128)(2,1)S(1)}, bf16[32,512]{1,0:T(8,128)(2,1)S(1)}, u32[]{:S(2)}, u32[]{:S(2)}) collective-permute-start(bf16[32,512]{1,0:T(8,128)(2,1)S(1)} %bitcast.5), channel_id=1, source_target_pairs={{0,16},{2,18},{4,20},{6,22},{8,24},{10,26},{12,28},{14,30},{16,0},... | collective-permute-start | bytes 98312 | tf_op jit(solution)/shard_map/ppermute | solution.py:425
  10.8 8.2 %collective-permute-start.3 = (bf16[32,1024]{1,0:T(8,128)(2,1)S(1)}, bf16[32,1024]{1,0:T(8,128)(2,1)S(1)}, u32[]{:S(2)}, u32[]{:S(2)}) collective-permute-start(bf16[32,1024]{1,0:T(8,128)(2,1)S(1)} %bitcast.4), channel_id=1, source_target_pairs={{0,16},{2,18},{4,20},{6,22},{8,24},{10,26},{12,28},{14,30},{16,0},... | collective-permute-start | bytes 196616 | tf_op jit(solution)/shard_map/ppermute | solution.py:425
  18.0 3.9 %collective-permute-start.4 = (bf16[32,512]{1,0:T(8,128)(2,1)S(1)}, bf16[32,512]{1,0:T(8,128)(2,1)S(1)}, u32[]{:S(2)}, u32[]{:S(2)}) collective-permute-start(bf16[32,512]{1,0:T(8,128)(2,1)S(1)} %collective-permute-done.1), channel_id=1, source_target_pairs={{0,4},{2,6},{4,0},{6,2},{8,12},{10,14},{12,8},{14,10},{16,20},{18,... | collective-permute-start | bytes 98312 | tf_op jit(solution)/shard_map/ppermute | solution.py:425
  18.6 3.4 %collective-permute-start.6 = (bf16[208,512]{1,0:T(8,128)(2,1)S(1)}, bf16[208,512]{1,0:T(8,128)(2,1)S(1)}, u32[]{:S(2)}, u32[]{:S(2)}) collective-permute-start(bf16[208,512]{1,0:T(8,128)(2,1)S(1)} %get-tuple-element.23.refs_1_.refs_0_), channel_id=1, source_target_pairs={{0,2},{2,0},{4,6},{6,4},{8,10},{10,8},{12,14},{14,12},{16,18},{18,... | collective-permute-start | bytes 638984 | tf_op jit(solution)/shard_map/ppermute | solution.py:425
  18.6 3.4 %collective-permute-start.7 = (bf16[208,512]{1,0:T(8,128)(2,1)S(1)}, bf16[208,512]{1,0:T(8,128)(2,1)S(1)}, u32[]{:S(2)}, u32[]{:S(2)}) collective-permute-start(bf16[208,512]{1,0:T(8,128)(2,1)S(1)} %collective-permute-done.refs_3_.refs_2_), channel_id=1, source_target_pairs={{0,2},{2,0},{4,6},{6,4},{8,10},{10,8},{12,14},{14,12},{16,18},{18,... | collective-permute-start | bytes 638984 | tf_op jit(solution)/shard_map/ppermute | solution.py:425
  19.1 2.9 %collective-permute-start.8 = (bf16[208,512]{1,0:T(8,128)(2,1)S(1)}, bf16[208,512]{1,0:T(8,128)(2,1)S(1)}, u32[]{:S(2)}, u32[]{:S(2)}) collective-permute-start(bf16[208,512]{1,0:T(8,128)(2,1)S(1)} %collective-permute-done.5.refs_5_.refs_4_), channel_id=1, source_target_pairs={{0,2},{2,0},{4,6},{6,4},{8,10},{10,8},{12,14},{14,12},{16,18},{18,... | collective-permute-start | bytes 638984 | tf_op jit(solution)/shard_map/ppermute | solution.py:425
  22.0 1.5 %collective-permute-start.9 = (bf16[208,512]{1,0:T(8,128)(2,1)S(1)}, bf16[208,512]{1,0:T(8,128)(2,1)S(1)}, u32[]{:S(2)}, u32[]{:S(2)}) collective-permute-start(bf16[208,512]{1,0:T(8,128)(2,1)S(1)} %collective-permute-done.2.refs_7_.refs_6_), channel_id=1, source_target_pairs={{0,2},{2,0},{4,6},{6,4},{8,10},{10,8},{12,14},{14,12},{16,18},{18,... | collective-permute-start | bytes 638984 | tf_op jit(solution)/shard_map/ppermute | solution.py:425
  24.8 8.5 %collective-permute-start.10 = (bf16[48,1152]{1,0:T(8,128)(2,1)S(1)}, bf16[48,1152]{1,0:T(8,128)(2,1)S(1)}, u32[]{:S(2)}, u32[]{:S(2)}) collective-permute-start(bf16[48,1152]{1,0:T(8,128)(2,1)S(1)} %prefill_partials.2.refs_0_), channel_id=1, source_target_pairs={{0,16},{2,18},{4,20},{6,22},{8,24},{10,26},{12,28},{14,30},{16,0},... | collective-permute-start | bytes 331784 | tf_op jit(solution)/shard_map/ppermute | solution.py:425
  28.3 4.7 %collective-permute-start.12 = (bf16[64,512]{1,0:T(8,128)(2,1)S(1)}, bf16[64,512]{1,0:T(8,128)(2,1)S(1)}, u32[]{:S(2)}, u32[]{:S(2)}) collective-permute-start(bf16[64,512]{1,0:T(8,128)(2,1)S(1)} %pad_maximum_fusion), channel_id=1, source_target_pairs={{0,8},{2,10},{4,12},{6,14},{8,0},{10,2},{12,4},{14,6},{16,24},{18,... | collective-permute-start | bytes 196616 | tf_op jit(solution)/shard_map/ppermute | solution.py:425
  32.9 2.2 %collective-permute-start.13 = (bf16[128,512]{1,0:T(8,128)(2,1)S(1)}, bf16[128,512]{1,0:T(8,128)(2,1)S(1)}, u32[]{:S(2)}, u32[]{:S(2)}) collective-permute-start(bf16[128,512]{1,0:T(8,128)(2,1)S(1)} %constant_dynamic-update-slice_fusion.near_ref), channel_id=1, source_target_pairs={{0,2},{2,0},{4,6},{6,4},{8,10},{10,8},{12,14},{14,12},{16,18},{18,... | collective-permute-start | bytes 393224 | tf_op jit(solution)/shard_map/ppermute | solution.py:425
  33.6 4.9 %collective-permute-start.11 = (bf16[48,1024]{1,0:T(8,128)(2,1)S(1)}, bf16[48,1024]{1,0:T(8,128)(2,1)S(1)}, u32[]{:S(2)}, u32[]{:S(2)}) collective-permute-start(bf16[48,1024]{1,0:T(8,128)(2,1)S(1)} %join_parts.1.refs_0_), channel_id=1, source_target_pairs={{0,1},{1,0},{2,3},{3,2},{4,5},{5,4},{6,7},{7,6},{8,9},{9,8},{10,11... | collective-permute-start | bytes 294920 | tf_op jit(solution)/shard_map/ppermute | solution.py:466

commit v13 on v11

--- a/solution.py
+++ b/solution.py
@@ -87,6 +87,7 @@
     new_hbm,
     cache_hbm,
     pre_q_hbm,
+    pre_new_hbm,
     out_hbm,
     part_ref,
     pre_q_ref,
@@ -108,13 +109,14 @@
         (q_hbm, query_ref),
         (new_hbm, new_ref),
         (pre_q_hbm.at[0], pre_q_ref),
+        (pre_new_hbm.at[0], part_ref.at[pl.ds(PART_ROWS * slots, pre_new_hbm.shape[1]), :]),
     ]
     small = [pltpu.make_async_copy(a, b, sems.at[i]) for i, (a, b) in enumerate(small)]
     loads, stores = [], []
     for c in range(CHUNKS):
         part = pl.ds(c * chunk, chunk)
-        loads.append(pltpu.make_async_copy(cache_hbm.at[part], table.at[part], sems.at[5 + c]))
-        stores.append(pltpu.make_async_copy(table.at[part], out_hbm.at[part], sems.at[5 + CHUNKS + c]))
+        loads.append(pltpu.make_async_copy(cache_hbm.at[part], table.at[part], sems.at[6 + c]))
+        stores.append(pltpu.make_async_copy(table.at[part], out_hbm.at[part], sems.at[6 + CHUNKS + c]))
     for copy in small + loads:
         copy.start()
     for copy in small:
@@ -190,16 +192,16 @@
         copy.wait()
 
 
-def decode_partials(lengths, dealing, queries, new_rows, cache, pre_queries, req):
+def decode_partials(lengths, dealing, queries, new_rows, cache, pre_queries, pre_new, req):
     slots, ctx, width = cache.shape
-    inputs = (lengths, dealing, queries, new_rows, cache, pre_queries)
+    inputs = (lengths, dealing, queries, new_rows, cache, pre_queries, pre_new)
     return pl.pallas_call(
         decode_kernel,
         in_specs=[HBM] * len(inputs),
         out_specs=[HBM, VMEM, VMEM, VMEM],
         out_shape=[
             pltpu.HBM(cache.shape, BF16),
-            pltpu.VMEM((PART_ROWS * slots, KVW), BF16),
+            pltpu.VMEM((PART_ROWS * slots + pre_new.shape[1], KVW), BF16),
             pltpu.VMEM(pre_queries.shape[1:], BF16),
             pltpu.VMEM((req, slots + 8, HEAD_SIZE), F32),
         ],
@@ -209,7 +211,7 @@
             pltpu.VMEM(queries.shape, BF16),
             pltpu.VMEM(new_rows.shape, BF16),
             pltpu.VMEM(cache.shape, BF16),
-            pltpu.SemaphoreType.DMA((5 + 2 * CHUNKS,)),
+            pltpu.SemaphoreType.DMA((6 + 2 * CHUNKS,)),
         ],
         compiler_params=pltpu.CompilerParams(vmem_limit_bytes=16 << 20),
         cost_estimate=pl.CostEstimate(
@@ -230,30 +232,30 @@
     return jnp.concatenate(blocks + [ref[pl.ds(KEY_VALUE_HEADS * slots, slots), pl.ds(0, STATS)]], axis=1)
 
 
-def step_kernel(slots, appends, own_ref, other_ref, *refs):
-    joined, logs = join([decode_part(own_ref, slots), decode_part(other_ref, slots)])
+def step_kernel(slots, keep, *refs):
+    parts, out_ref = refs[:-1], refs[-1]
+    joined, logs = join([decode_part(ref, slots) for ref in parts])
     head = PART_ROWS * slots
-    rest = own_ref.shape[0] - head
-    out_ref = refs[1] if appends else refs[0]
+    rest = parts[0].shape[0] - head
     for g in range(KEY_VALUE_HEADS):
         out_ref[pl.ds(g * slots, slots), :] = joined[:, g * KVW : (g + 1) * KVW]
     put_stats(out_ref, [logs[:, h * HEAD_SIZE : h * HEAD_SIZE + 1] for h in range(QUERY_HEADS)], slots)
-    if appends:
-        out_ref[pl.ds(head, refs[0].shape[0]), :] = refs[0][...]
-    if rest:
-        refs[1][pl.ds(0, rest), :] = own_ref[pl.ds(head, rest), :]
-        refs[1][pl.ds(rest, rest), :] = other_ref[pl.ds(head, rest), :]
-
-
-def join_step(own, other, slots, shapes, name, *extra):
-    return pl.pallas_call(
-        functools.partial(step_kernel, slots, bool(extra)),
-        in_specs=[VMEM] * (2 + len(extra)),
-        out_specs=[VMEM] * len(shapes),
-        out_shape=[pltpu.VMEM((rows, KVW), BF16) for rows in shapes],
+    for i, ref in enumerate(parts if keep else parts[1:]):
+        out_ref[pl.ds(head + i * rest, rest), :] = ref[pl.ds(head, rest), :]
+
+
+def join_step(parts, slots, keep, name):
+    head = PART_ROWS * slots
+    rest = parts[0].shape[0] - head
+    rows = head + rest * (len(parts) if keep else len(parts) - 1)
+    return pl.pallas_call(
+        functools.partial(step_kernel, slots, keep),
+        in_specs=[VMEM] * len(parts),
+        out_specs=VMEM,
+        out_shape=pltpu.VMEM((rows, KVW), BF16),
         compiler_params=pltpu.CompilerParams(vmem_limit_bytes=16 << 20),
         name=name,
-    )(own, other, *extra)
+    )(*parts)
 
 
 def prefill_kernel(sets, ctx, off_ref, *refs):
@@ -332,18 +334,21 @@
     )(*parts, *decodes)
 
 
-def update_kernel(tokens, sets, off_ref, cache_hbm, near_ref, beside_ref, *refs):
+def update_kernel(tokens, slots, off_ref, cache_hbm, near_ref, beside_ref, *refs):
     tables, (out_ref, cache_ref, sem) = refs[:KEY_SET], refs[-3:]
     load = pltpu.make_async_copy(cache_hbm.at[0], cache_ref, sem)
     load.start()
     ctx = cache_ref.shape[0]
+    head = PART_ROWS * slots
+    rest = near_ref.shape[0] - head
     me = lax.axis_index(BLK)
     rows = [t[pl.ds(ctx, tokens), :] for t in tables]
-    rows = jnp.concatenate(rows + [near_ref[...], beside_ref[...]], axis=0)
+    rows = jnp.concatenate(rows + [r[pl.ds(head, rest), :] for r in (near_ref, beside_ref)], axis=0)
     count = rows.shape[0]
     index = lax.broadcasted_iota(jnp.int32, (1, count), 1)
     block = index // tokens
-    half = sets * KEY_SET // 2
+    half = rest // tokens
+    sets = half * 2 // KEY_SET
     far = block - KEY_SET
     inner = far % half
     distance = KEY_SET * (1 + inner % sets) + 2 * (inner // sets) + far // half
@@ -355,9 +360,9 @@
     out_ref[0] = jnp.where(inside, picked, cache_ref[...])
 
 
-def update_cache(offset, cache, near, beside, tables, tokens, sets):
-    return pl.pallas_call(
-        functools.partial(update_kernel, tokens, sets),
+def update_cache(offset, cache, near, beside, tables, tokens, slots):
+    return pl.pallas_call(
+        functools.partial(update_kernel, tokens, slots),
         in_specs=[VMEM, HBM] + [VMEM] * (2 + len(tables)),
         out_specs=VMEM,
         out_shape=jax.ShapeDtypeStruct(cache.shape, BF16),
@@ -424,35 +429,35 @@
     table = jnp.concatenate([prefill_cache[0], new_prefill[0]], axis=0)
     lanes = [table] + [swap(table, k) for k in range(2, KEY_SET, 2)]
     packs = [swap(prefill_queries[0], k) for k in others]
-    far = jnp.concatenate([swap(new_prefill[0], k) for k in others], axis=0)
 
     decode_cache_out, part, queries, route = decode_partials(
-        decode_lengths, dealing, decode_queries, new_decode, decode_cache, prefill_queries, req
+        decode_lengths,
+        dealing,
+        decode_queries,
+        new_decode,
+        decode_cache,
+        prefill_queries,
+        new_prefill,
+        req,
     )
-    head, rest = PART_ROWS * slots, far.shape[0]
-    beside = swap(part, 1)
+    far = [swap(part, k) for k in others]
     offset = jnp.full((8, HEAD_SIZE), prefill_offsets[0], jnp.int32)
     lanes[1], offset, _ = lax.optimization_barrier((lanes[1], offset, part))
-    lanes[2], beside, far, _ = lax.optimization_barrier((lanes[2], beside, far, lanes[1]))
-    (part,) = join_step(part, beside, slots, [head], "join_core")
-    far_across = swap(far, 2)
+    lanes[2], packs, _ = lax.optimization_barrier((lanes[2], packs, lanes[1]))
+    lanes[3], far, _ = lax.optimization_barrier((lanes[3], far, lanes[2]))
+    part = join_step([part] + far, slots, False, "join_far")
+    tables = [t for lane in lanes for t in (lane, swap(lane, 1))]
     across = swap(part, 2)
-    lanes[3], packs, across, _ = lax.optimization_barrier((lanes[3], packs, across, lanes[2]))
-    tables = [t for lane in lanes for t in (lane, swap(lane, 1))]
-
-    far = jnp.concatenate([far, far_across], axis=0)
-    (part,) = join_step(part, across, slots, [head + 2 * rest], "join_x", far)
-    packs, _ = lax.optimization_barrier((packs, part))
+
     sent = prefill_partials(offset, packs, tables, ctx, [k // KEY_SET for k in others])
+    part = join_step([part, after(across, sent[0])], slots, True, "join_x")
     queries = after(queries, sent[0])
     kept = prefill_partials(offset, [queries], tables, ctx, [0])
-    part, news = join_step(part, after(swap(part, 4), kept[0]), slots, [head, 4 * rest], "join_z")
-    attended = join_parts(
-        [*kept] + [swap(p, k) for k, p in zip(others, sent)],
-        [part] + [swap(part, k) for k in others],
-        slots,
-    )
-    prefill_cache_out = update_cache(offset, prefill_cache, news, swap(news, 1), tables, tokens, len(others))
+    part = join_step([part, after(swap(part, 4), kept[0])], slots, True, "join_z")
+    arrived = [swap(p, k) for k, p in zip(others, sent)]
+    beside = swap(after(part, *arrived), 1)
+    attended = join_parts([*kept] + arrived, [part, beside], slots)
+    prefill_cache_out = update_cache(offset, prefill_cache, part, beside, tables, tokens, slots)
 
     if req == 2:
         held = [attended, lax.ppermute(attended, "req", [(0, 1), (1, 0)])]

time: 40.3 us -> 39.6 us (0.983)
  starting transfers between devices: 19.8 us -> 15 us
  waiting for transfers between devices: 9.33 us -> 13.5 us
    ppermute x16 -> x13, starting transfers between devices: 18.2 us -> 13.1 us  [swap(): return lax.ppermute(array, BLK, [(i, i ^ distance) for i in range(blk)])]
    ppermute x16 -> x13, waiting for transfers between devices: 7.96 us -> 12.1 us  [swap(): return lax.ppermute(array, BLK, [(i, i ^ distance) for i in range(blk)])]
  transfers between devices with their start and end apart: 17 -> 14, of which waited for: 5 -> 5; matrix products, arithmetic and copies ran while one was open for 0% -> 0% of each run, Pallas kernels for 19% -> 18%
where the time goes in v13:
time: 39.6 us; the launch traced here: 39.4 us
  starting transfers between devices  15 us (38%)
  waiting for transfers between devices  13.5 us (34%)
  Pallas kernels  8.57 us (22%)
  between operations  1.42 us (4%)
  other arithmetic  0.97 us (2%)
    ppermute x13, starting transfers between devices, swap(): return lax.ppermute(array, BLK, [(i, i ^ distance) for i in range(blk)])  13.1 us
    ppermute x13, waiting for transfers between devices, swap(): return lax.ppermute(array, BLK, [(i, i ^ distance) for i in range(blk)])  12.1 us
    pallas_call x1, Pallas kernels, decode_partials(): pl.pallas_call(decode_kernel, in_specs=[HBM] * len(inputs), out_specs=[HB...  2.85 us
    pallas_call x2, Pallas kernels, prefill_partials(): pl.pallas_call(functools.partial(prefill_kernel, sets, ctx), in_specs=[VM...  2.13 us
    ppermute x1, starting transfers between devices, per_device(): held = [attended, lax.ppermute(attended, 'req', [(0, 1), (1, 0)])]  1.87 us
    pallas_call x1, Pallas kernels, update_cache(): pl.pallas_call(functools.partial(update_kernel, tokens, slots), in_specs=...  1.71 us
    ppermute x1, waiting for transfers between devices, per_device(): held = [attended, lax.ppermute(attended, 'req', [(0, 1), (1, 0)])]  1.38 us
    concatenate x1, other arithmetic, per_device(): table = jnp.concatenate([prefill_cache[0], new_prefill[0]], axis=0)  0.97 us
  transfers between devices with their start and end apart: 14, of which 5 were waited for; matrix products, arithmetic and copies ran while one was open for 0% of the time, Pallas kernels for 18%

profile of v13, /device:TPU:0, one launch (start us, length us, event | category | flops | bytes accessed | tf_op | source)
XLA Modules:
  0.0 39.4 jit_solution(10689277714533157766)
XLA Ops:
  0.6 0.0 copy-start
  0.6 1.0 %pad_maximum_fusion.refs_1_.refs_0_ = bf16[160,512]{1,0:T(8,128)(2,1)S(1)} fusion(bf16[32,512]{1,0:T(8,128)(2,1)} %bitcast.6, bf16[128,512]{1,0:T(8,128)(2,1)} %bitcast.5), kind=kLoop, calls=%fused_computation | loop fusion | flops 327680 | bytes 327680 | tf_op jit(solution)/shard_map/concatenate | solution.py:429
  1.6 3.0 %collective-permute-start = (bf16[160,512]{1,0:T(8,128)(2,1)S(1)}, bf16[160,512]{1,0:T(8,128)(2,1)S(1)}, u32[]{:S(2)}, u32[]{:S(2)}) collective-permute-start(bf16[160,512]{1,0:T(8,128)(2,1)S(1)} %pad_maximum_fusion.refs_1_.refs_0_), channel_id=1, source_target_pairs={{0,4},{2,6},{4,0},{6,2},{8,12},{10,14},{12,8},{14,10},{16,20},{18,... | collective-permute-start | bytes 491528 | tf_op jit(solution)/shard_map/ppermute | solution.py:423
  4.6 1.6 %collective-permute-start.1 = (bf16[160,512]{1,0:T(8,128)(2,1)S(1)}, bf16[160,512]{1,0:T(8,128)(2,1)S(1)}, u32[]{:S(2)}, u32[]{:S(2)}) collective-permute-start(bf16[160,512]{1,0:T(8,128)(2,1)S(1)} %pad_maximum_fusion.refs_1_.refs_0_), channel_id=1, source_target_pairs={{0,8},{2,10},{4,12},{6,14},{8,0},{10,2},{12,4},{14,6},{16,24},{18,... | collective-permute-start | bytes 491528 | tf_op jit(solution)/shard_map/ppermute | solution.py:423
  6.2 2.8 %decode_partials.1 = (bf16[16,128,512]{2,1,0:T(8,128)(2,1)}, bf16[80,512]{1,0:T(8,128)(2,1)S(1)}, bf16[32,1024]{1,0:T(8,128)(2,1)S(1)}, f32[2,24,128]{2,1,0:T(8,128)S(1)}) custom-call(s32[16]{0:T(128)} %len_hbm.1, s32[34]{0:T(128)} %deal_hbm.1, bf16[16,1024]{1,0:T(8,128)(2,1)} %q_hbm.1, bf16[16,512]{1,0:T(8,128)(2,1)} %new_hbm.1, ...), custom_call_target="tpu_custom_call" | custom-call | flops 8388608 | bytes 4194304 | tf_op jit(solution)/shard_map/decode_partials/pallas_call | solution.py:198
  9.1 3.0 %collective-permute-start.7 = (bf16[80,512]{1,0:T(8,128)(2,1)S(1)}, bf16[80,512]{1,0:T(8,128)(2,1)S(1)}, u32[]{:S(2)}, u32[]{:S(2)}) collective-permute-start(bf16[80,512]{1,0:T(8,128)(2,1)S(1)} %get-tuple-element.23.refs_0_), channel_id=1, source_target_pairs={{0,16},{2,18},{4,20},{6,22},{8,24},{10,26},{12,28},{14,30},{16,0},... | collective-permute-start | bytes 245768 | tf_op jit(solution)/shard_map/ppermute | solution.py:423
  12.1 0.1 collective-permute-start.2
  12.8 0.0 collective-permute-done.refs_3_.refs_2_
  12.8 0.1 collective-permute-start.3
  12.9 6.4 %collective-permute-done.2.refs_0_ = bf16[32,1024]{1,0:T(8,128)(2,1)S(1)} collective-permute-done((bf16[32,1024]{1,0:T(8,128)(2,1)S(1)}, bf16[32,1024]{1,0:T(8,128)(2,1)S(1)}, u32[]{:S(2)}, u32[]{:S(2)}) %collective-permute-start.2) | collective-permute-done | bytes 65568 | tf_op jit(solution)/shard_map/ppermute | solution.py:423
  19.3 0.0 collective-permute-done.1.refs_5_.refs_4_
  19.3 0.0 collective-permute-done.7.refs_1_
  19.3 0.1 collective-permute-start.8
  19.4 0.5 %collective-permute-start.5 = (bf16[160,512]{1,0:T(8,128)(2,1)S(1)}, bf16[160,512]{1,0:T(8,128)(2,1)S(1)}, u32[]{:S(2)}, u32[]{:S(2)}) collective-permute-start(bf16[160,512]{1,0:T(8,128)(2,1)S(1)} %collective-permute-done.1.refs_5_.refs_4_), channel_id=1, source_target_pairs={{0,2},{2,0},{4,6},{6,4},{8,10},{10,8},{12,14},{14,12},{16,18},{18,... | collective-permute-start | bytes 491528 | tf_op jit(solution)/shard_map/ppermute | solution.py:423
  19.9 0.1 collective-permute-start.4
  20.0 0.3 join_far.1.refs_0_
  20.3 1.4 %collective-permute-start.10 = (bf16[80,512]{1,0:T(8,128)(2,1)S(1)}, bf16[80,512]{1,0:T(8,128)(2,1)S(1)}, u32[]{:S(2)}, u32[]{:S(2)}) collective-permute-start(bf16[80,512]{1,0:T(8,128)(2,1)S(1)} %join_far.1.refs_0_), channel_id=1, source_target_pairs={{0,4},{2,6},{4,0},{6,2},{8,12},{10,14},{12,8},{14,10},{16,20},{18,... | collective-permute-start | bytes 245768 | tf_op jit(solution)/shard_map/ppermute | solution.py:423
  21.7 1.1 %prefill_partials.2 = bf16[32,1152]{1,0:T(8,128)(2,1)S(1)} custom-call(s32[8,128]{1,0:T(8,128)S(1)} %broadcast_in_dim.3.off_ref, bf16[32,1024]{1,0:T(8,128)(2,1)S(1)} %collective-permute-done.2.refs_0_, bf16[160,512]{1,0:T(8,128)(2,1)S(1)} %pad_maximum_fusion.refs_1_.refs_0_, bf16[160,512]{1,0:T(8,128)(2,1)S(1)} %collective-permute-done.3.refs_2_.refs_1_, ...), custom_call_target="tpu_custom_call" | custom-call | flops 167772160 | bytes 4194304 | tf_op jit(solution)/shard_map/prefill_partials/pallas_call | solution.py:307
  22.8 2.3 %collective-permute-done.10.refs_1_ = bf16[80,512]{1,0:T(8,128)(2,1)S(1)} collective-permute-done((bf16[80,512]{1,0:T(8,128)(2,1)S(1)}, bf16[80,512]{1,0:T(8,128)(2,1)S(1)}, u32[]{:S(2)}, u32[]{:S(2)}) %collective-permute-start.10) | collective-permute-done | bytes 81952 | tf_op jit(solution)/shard_map/ppermute | solution.py:423
  25.1 0.3 join_x.1.refs_0_
  25.4 0.4 %collective-permute-start.11 = (bf16[112,512]{1,0:T(8,128)(2,1)S(1)}, bf16[112,512]{1,0:T(8,128)(2,1)S(1)}, u32[]{:S(2)}, u32[]{:S(2)}) collective-permute-start(bf16[112,512]{1,0:T(8,128)(2,1)S(1)} %join_x.1.refs_0_), channel_id=1, source_target_pairs={{0,8},{2,10},{4,12},{6,14},{8,0},{10,2},{12,4},{14,6},{16,24},{18,... | collective-permute-start | bytes 344072 | tf_op jit(solution)/shard_map/ppermute | solution.py:423
  25.8 2.8 %collective-permute-start.9 = (bf16[32,1152]{1,0:T(8,128)(2,1)S(1)}, bf16[32,1152]{1,0:T(8,128)(2,1)S(1)}, u32[]{:S(2)}, u32[]{:S(2)}) collective-permute-start(bf16[32,1152]{1,0:T(8,128)(2,1)S(1)} %prefill_partials.2), channel_id=1, source_target_pairs={{0,16},{2,18},{4,20},{6,22},{8,24},{10,26},{12,28},{14,30},{16,0},... | collective-permute-start | bytes 221192 | tf_op jit(solution)/shard_map/ppermute | solution.py:423
  28.6 1.1 %prefill_partials.3.refs_0_ = bf16[32,1152]{1,0:T(8,128)(2,1)S(1)} custom-call(s32[8,128]{1,0:T(8,128)S(1)} %broadcast_in_dim.3.off_ref, bf16[32,1024]{1,0:T(8,128)(2,1)S(1)} %get-tuple-element.30.refs_0_, bf16[160,512]{1,0:T(8,128)(2,1)S(1)} %pad_maximum_fusion.refs_1_.refs_0_, bf16[160,512]{1,0:T(8,128)(2,1)S(1)} %collective-permute-done.3.refs_2_.refs_1_, ...), custom_call_target="tpu_custom_call" | custom-call | flops 167772160 | bytes 4194304 | tf_op jit(solution)/shard_map/prefill_partials/pallas_call | solution.py:307
  29.7 1.9 %collective-permute-done.11.refs_1_ = bf16[112,512]{1,0:T(8,128)(2,1)S(1)} collective-permute-done((bf16[112,512]{1,0:T(8,128)(2,1)S(1)}, bf16[112,512]{1,0:T(8,128)(2,1)S(1)}, u32[]{:S(2)}, u32[]{:S(2)}) %collective-permute-start.11) | collective-permute-done | bytes 114720 | tf_op jit(solution)/shard_map/ppermute | solution.py:423
  31.6 0.3 join_z.1.refs_2_.near_ref
  31.9 0.1 collective-permute-start.12
  32.0 1.4 %collective-permute-done.12.refs_3_.beside_ref = bf16[176,512]{1,0:T(8,128)(2,1)S(1)} collective-permute-done((bf16[176,512]{1,0:T(8,128)(2,1)S(1)}, bf16[176,512]{1,0:T(8,128)(2,1)S(1)}, u32[]{:S(2)}, u32[]{:S(2)}) %collective-permute-start.12) | collective-permute-done | bytes 180256 | tf_op jit(solution)/shard_map/ppermute | solution.py:423
  33.4 0.3 join_parts.1.refs_0_
  33.7 1.9 %collective-permute-start.13 = (bf16[48,1024]{1,0:T(8,128)(2,1)S(1)}, bf16[48,1024]{1,0:T(8,128)(2,1)S(1)}, u32[]{:S(2)}, u32[]{:S(2)}) collective-permute-start(bf16[48,1024]{1,0:T(8,128)(2,1)S(1)} %join_parts.1.refs_0_), channel_id=1, source_target_pairs={{0,1},{1,0},{2,3},{3,2},{4,5},{5,4},{6,7},{7,6},{8,9},{9,8},{10,11... | collective-permute-start | bytes 294920 | tf_op jit(solution)/shard_map/ppermute | solution.py:463
  35.6 1.7 %update_cache.1 = bf16[1,128,512]{2,1,0:T(8,128)(2,1)} custom-call(s32[8,128]{1,0:T(8,128)S(1)} %broadcast_in_dim.3.off_ref, bf16[1,128,512]{2,1,0:T(8,128)(2,1)} %cache_hbm.3, bf16[176,512]{1,0:T(8,128)(2,1)S(1)} %join_z.1.refs_2_.near_ref, bf16[176,512]{1,0:T(8,128)(2,1)S(1)} %collective-permute-done.12.refs_3_.beside_ref, ...), custom_call_target="tpu_custom_call" | custom-call | tf_op jit(solution)/shard_map/update_cache/pallas_call | solution.py:364
  37.3 1.4 %collective-permute-done.13.refs_1_ = bf16[48,1024]{1,0:T(8,128)(2,1)S(1)} collective-permute-done((bf16[48,1024]{1,0:T(8,128)(2,1)S(1)}, bf16[48,1024]{1,0:T(8,128)(2,1)S(1)}, u32[]{:S(2)}, u32[]{:S(2)}) %collective-permute-start.13) | collective-permute-done | bytes 98336 | tf_op jit(solution)/shard_map/ppermute | solution.py:463
  38.7 0.8 %route_outputs.1 = (bf16[1,32,1024]{2,1,0:T(8,128)(2,1)}, bf16[16,1024]{1,0:T(8,128)(2,1)}) custom-call(f32[2,24,128]{2,1,0:T(8,128)S(1)} %get-tuple-element.22.route_ref, bf16[48,1024]{1,0:T(8,128)(2,1)S(1)} %join_parts.1.refs_0_, bf16[48,1024]{1,0:T(8,128)(2,1)S(1)} %collective-permute-done.13.refs_1_), custom_call_target="tpu_custom_call" | custom-call | tf_op jit(solution)/shard_map/route_outputs/pallas_call | solution.py:392
  (9 shorter events, 0.0 us)
Async XLA Ops:
  0.6 11.4 %copy-start = (bf16[1,32,1024]{2,1,0:T(8,128)(2,1)S(1)}, bf16[1,32,1024]{2,1,0:T(8,128)(2,1)}, u32[]{:S(2)}) copy-start(bf16[1,32,1024]{2,1,0:T(8,128)(2,1)} %pre_q_hbm.1) | copy-start | bytes 196612
  1.6 11.2 %collective-permute-start = (bf16[160,512]{1,0:T(8,128)(2,1)S(1)}, bf16[160,512]{1,0:T(8,128)(2,1)S(1)}, u32[]{:S(2)}, u32[]{:S(2)}) collective-permute-start(bf16[160,512]{1,0:T(8,128)(2,1)S(1)} %pad_maximum_fusion.refs_1_.refs_0_), channel_id=1, source_target_pairs={{0,4},{2,6},{4,0},{6,2},{8,12},{10,14},{12,8},{14,10},{16,20},{18,... | collective-permute-start | bytes 491528 | tf_op jit(solution)/shard_map/ppermute | solution.py:423
  4.6 14.7 %collective-permute-start.1 = (bf16[160,512]{1,0:T(8,128)(2,1)S(1)}, bf16[160,512]{1,0:T(8,128)(2,1)S(1)}, u32[]{:S(2)}, u32[]{:S(2)}) collective-permute-start(bf16[160,512]{1,0:T(8,128)(2,1)S(1)} %pad_maximum_fusion.refs_1_.refs_0_), channel_id=1, source_target_pairs={{0,8},{2,10},{4,12},{6,14},{8,0},{10,2},{12,4},{14,6},{16,24},{18,... | collective-permute-start | bytes 491528 | tf_op jit(solution)/shard_map/ppermute | solution.py:423
  6.2 13.1 %collective-permute-start.6 = (bf16[160,512]{1,0:T(8,128)(2,1)S(1)}, bf16[160,512]{1,0:T(8,128)(2,1)S(1)}, u32[]{:S(2)}, u32[]{:S(2)}) collective-permute-start(bf16[160,512]{1,0:T(8,128)(2,1)S(1)} %pad_maximum_fusion.refs_1_.refs_0_), channel_id=1, source_target_pairs={{0,12},{2,14},{4,8},{6,10},{8,4},{10,6},{12,0},{14,2},{16,28},{18,... | collective-permute-start | bytes 491528 | tf_op jit(solution)/shard_map/ppermute | solution.py:423
  9.1 10.3 %collective-permute-start.7 = (bf16[80,512]{1,0:T(8,128)(2,1)S(1)}, bf16[80,512]{1,0:T(8,128)(2,1)S(1)}, u32[]{:S(2)}, u32[]{:S(2)}) collective-permute-start(bf16[80,512]{1,0:T(8,128)(2,1)S(1)} %get-tuple-element.23.refs_0_), channel_id=1, source_target_pairs={{0,16},{2,18},{4,20},{6,22},{8,24},{10,26},{12,28},{14,30},{16,0},... | collective-permute-start | bytes 245768 | tf_op jit(solution)/shard_map/ppermute | solution.py:423
  12.1 7.2 %collective-permute-start.2 = (bf16[32,1024]{1,0:T(8,128)(2,1)S(1)}, bf16[32,1024]{1,0:T(8,128)(2,1)S(1)}, u32[]{:S(2)}, u32[]{:S(2)}) collective-permute-start(bf16[32,1024]{1,0:T(8,128)(2,1)S(1)} %bitcast.7), channel_id=1, source_target_pairs={{0,16},{2,18},{4,20},{6,22},{8,24},{10,26},{12,28},{14,30},{16,0},... | collective-permute-start | bytes 196616 | tf_op jit(solution)/shard_map/ppermute | solution.py:423
  12.8 8.9 %collective-permute-start.3 = (bf16[160,512]{1,0:T(8,128)(2,1)S(1)}, bf16[160,512]{1,0:T(8,128)(2,1)S(1)}, u32[]{:S(2)}, u32[]{:S(2)}) collective-permute-start(bf16[160,512]{1,0:T(8,128)(2,1)S(1)} %pad_maximum_fusion.refs_1_.refs_0_), channel_id=1, source_target_pairs={{0,2},{2,0},{4,6},{6,4},{8,10},{10,8},{12,14},{14,12},{16,18},{18,... | collective-permute-start | bytes 491528 | tf_op jit(solution)/shard_map/ppermute | solution.py:423
  19.3 2.4 %collective-permute-start.8 = (bf16[160,512]{1,0:T(8,128)(2,1)S(1)}, bf16[160,512]{1,0:T(8,128)(2,1)S(1)}, u32[]{:S(2)}, u32[]{:S(2)}) collective-permute-start(bf16[160,512]{1,0:T(8,128)(2,1)S(1)} %collective-permute-done.6.refs_7_.refs_6_), channel_id=1, source_target_pairs={{0,2},{2,0},{4,6},{6,4},{8,10},{10,8},{12,14},{14,12},{16,18},{18,... | collective-permute-start | bytes 491528 | tf_op jit(solution)/shard_map/ppermute | solution.py:423
  19.4 2.3 %collective-permute-start.5 = (bf16[160,512]{1,0:T(8,128)(2,1)S(1)}, bf16[160,512]{1,0:T(8,128)(2,1)S(1)}, u32[]{:S(2)}, u32[]{:S(2)}) collective-permute-start(bf16[160,512]{1,0:T(8,128)(2,1)S(1)} %collective-permute-done.1.refs_5_.refs_4_), channel_id=1, source_target_pairs={{0,2},{2,0},{4,6},{6,4},{8,10},{10,8},{12,14},{14,12},{16,18},{18,... | collective-permute-start | bytes 491528 | tf_op jit(solution)/shard_map/ppermute | solution.py:423
  19.9 1.8 %collective-permute-start.4 = (bf16[160,512]{1,0:T(8,128)(2,1)S(1)}, bf16[160,512]{1,0:T(8,128)(2,1)S(1)}, u32[]{:S(2)}, u32[]{:S(2)}) collective-permute-start(bf16[160,512]{1,0:T(8,128)(2,1)S(1)} %collective-permute-done.refs_3_.refs_2_), channel_id=1, source_target_pairs={{0,2},{2,0},{4,6},{6,4},{8,10},{10,8},{12,14},{14,12},{16,18},{18,... | collective-permute-start | bytes 491528 | tf_op jit(solution)/shard_map/ppermute | solution.py:423
  20.3 4.9 %collective-permute-start.10 = (bf16[80,512]{1,0:T(8,128)(2,1)S(1)}, bf16[80,512]{1,0:T(8,128)(2,1)S(1)}, u32[]{:S(2)}, u32[]{:S(2)}) collective-permute-start(bf16[80,512]{1,0:T(8,128)(2,1)S(1)} %join_far.1.refs_0_), channel_id=1, source_target_pairs={{0,4},{2,6},{4,0},{6,2},{8,12},{10,14},{12,8},{14,10},{16,20},{18,... | collective-permute-start | bytes 245768 | tf_op jit(solution)/shard_map/ppermute | solution.py:423
  25.4 6.2 %collective-permute-start.11 = (bf16[112,512]{1,0:T(8,128)(2,1)S(1)}, bf16[112,512]{1,0:T(8,128)(2,1)S(1)}, u32[]{:S(2)}, u32[]{:S(2)}) collective-permute-start(bf16[112,512]{1,0:T(8,128)(2,1)S(1)} %join_x.1.refs_0_), channel_id=1, source_target_pairs={{0,8},{2,10},{4,12},{6,14},{8,0},{10,2},{12,4},{14,6},{16,24},{18,... | collective-permute-start | bytes 344072 | tf_op jit(solution)/shard_map/ppermute | solution.py:423
  25.8 6.1 %collective-permute-start.9 = (bf16[32,1152]{1,0:T(8,128)(2,1)S(1)}, bf16[32,1152]{1,0:T(8,128)(2,1)S(1)}, u32[]{:S(2)}, u32[]{:S(2)}) collective-permute-start(bf16[32,1152]{1,0:T(8,128)(2,1)S(1)} %prefill_partials.2), channel_id=1, source_target_pairs={{0,16},{2,18},{4,20},{6,22},{8,24},{10,26},{12,28},{14,30},{16,0},... | collective-permute-start | bytes 221192 | tf_op jit(solution)/shard_map/ppermute | solution.py:423
  31.9 1.5 %collective-permute-start.12 = (bf16[176,512]{1,0:T(8,128)(2,1)S(1)}, bf16[176,512]{1,0:T(8,128)(2,1)S(1)}, u32[]{:S(2)}, u32[]{:S(2)}) collective-permute-start(bf16[176,512]{1,0:T(8,128)(2,1)S(1)} %join_z.1.refs_2_.near_ref), channel_id=1, source_target_pairs={{0,2},{2,0},{4,6},{6,4},{8,10},{10,8},{12,14},{14,12},{16,18},{18,... | collective-permute-start | bytes 540680 | tf_op jit(solution)/shard_map/ppermute | solution.py:423
  33.7 5.0 %collective-permute-start.13 = (bf16[48,1024]{1,0:T(8,128)(2,1)S(1)}, bf16[48,1024]{1,0:T(8,128)(2,1)S(1)}, u32[]{:S(2)}, u32[]{:S(2)}) collective-permute-start(bf16[48,1024]{1,0:T(8,128)(2,1)S(1)} %join_parts.1.refs_0_), channel_id=1, source_target_pairs={{0,1},{1,0},{2,3},{3,2},{4,5},{5,4},{6,7},{7,6},{8,9},{9,8},{10,11... | collective-permute-start | bytes 294920 | tf_op jit(solution)/shard_map/ppermute | solution.py:463

commit v14 on v13

--- a/solution.py
+++ b/solution.py
@@ -440,20 +440,21 @@
         new_prefill,
         req,
     )
+    part = after(part, *packs)
     far = [swap(part, k) for k in others]
     offset = jnp.full((8, HEAD_SIZE), prefill_offsets[0], jnp.int32)
     lanes[1], offset, _ = lax.optimization_barrier((lanes[1], offset, part))
-    lanes[2], packs, _ = lax.optimization_barrier((lanes[2], packs, lanes[1]))
+    lanes[2] = after(lanes[2], lanes[1])
     lanes[3], far, _ = lax.optimization_barrier((lanes[3], far, lanes[2]))
     part = join_step([part] + far, slots, False, "join_far")
     tables = [t for lane in lanes for t in (lane, swap(lane, 1))]
-    across = swap(part, 2)
+    around = [swap(part, k) for k in range(2, KEY_SET, 2)]
 
     sent = prefill_partials(offset, packs, tables, ctx, [k // KEY_SET for k in others])
-    part = join_step([part, after(across, sent[0])], slots, True, "join_x")
     queries = after(queries, sent[0])
     kept = prefill_partials(offset, [queries], tables, ctx, [0])
-    part = join_step([part, after(swap(part, 4), kept[0])], slots, True, "join_z")
+    around[0] = after(around[0], kept[0])
+    part = join_step([part] + around, slots, True, "join_lanes")
     arrived = [swap(p, k) for k, p in zip(others, sent)]
     beside = swap(after(part, *arrived), 1)
     attended = join_parts([*kept] + arrived, [part, beside], slots)

time: 39.6 us -> 41 us (1.035)
  starting transfers between devices: 15 us -> 18.8 us
  waiting for transfers between devices: 13.5 us -> 11.4 us
    ppermute x13 -> x14, starting transfers between devices: 13.1 us -> 17.2 us  [swap(): return lax.ppermute(array, BLK, [(i, i ^ distance) for i in range(blk)])]
    ppermute x13 -> x14, waiting for transfers between devices: 12.1 us -> 9.81 us  [swap(): return lax.ppermute(array, BLK, [(i, i ^ distance) for i in range(blk)])]
    pallas_call x3 -> x2, Pallas kernels: 0.86 us -> 0.64 us  [join_step(): pl.pallas_call(functools.partial(step_kernel, slots, keep), in_specs=[VME...]
  transfers between devices with their start and end apart: 14 -> 15, of which waited for: 5 -> 5; matrix products, arithmetic and copies ran while one was open for 0% -> 0% of each run, Pallas kernels for 18% -> 18%
where the time goes in v14:
time: 41 us; the launch traced here: 40.8 us
  starting transfers between devices  18.8 us (46%)
  waiting for transfers between devices  11.4 us (28%)
  Pallas kernels  8.32 us (20%)
  between operations  1.39 us (3%)
  other arithmetic  0.94 us (2%)
    ppermute x14, starting transfers between devices, swap(): return lax.ppermute(array, BLK, [(i, i ^ distance) for i in range(blk)])  17.2 us
    ppermute x14, waiting for transfers between devices, swap(): return lax.ppermute(array, BLK, [(i, i ^ distance) for i in range(blk)])  9.81 us
    pallas_call x1, Pallas kernels, decode_partials(): pl.pallas_call(decode_kernel, in_specs=[HBM] * len(inputs), out_specs=[HB...  2.81 us
    pallas_call x2, Pallas kernels, prefill_partials(): pl.pallas_call(functools.partial(prefill_kernel, sets, ctx), in_specs=[VM...  2.12 us
    pallas_call x1, Pallas kernels, update_cache(): pl.pallas_call(functools.partial(update_kernel, tokens, slots), in_specs=...  1.71 us
    ppermute x1, waiting for transfers between devices, per_device(): held = [attended, lax.ppermute(attended, 'req', [(0, 1), (1, 0)])]  1.6 us
    ppermute x1, starting transfers between devices, per_device(): held = [attended, lax.ppermute(attended, 'req', [(0, 1), (1, 0)])]  1.59 us
    concatenate x1, other arithmetic, per_device(): table = jnp.concatenate([prefill_cache[0], new_prefill[0]], axis=0)  0.94 us
  transfers between devices with their start and end apart: 15, of which 5 were waited for; matrix products, arithmetic and copies ran while one was open for 0% of the time, Pallas kernels for 18%

profile of v14, /device:TPU:0, one launch (start us, length us, event | category | flops | bytes accessed | tf_op | source)
XLA Modules:
  0.0 40.8 jit_solution(14449257531264949430)
XLA Ops:
  0.6 0.9 %pad_maximum_fusion.refs_1_.refs_0_ = bf16[160,512]{1,0:T(8,128)(2,1)S(1)} fusion(bf16[32,512]{1,0:T(8,128)(2,1)} %bitcast.6, bf16[128,512]{1,0:T(8,128)(2,1)} %bitcast.5), kind=kLoop, calls=%fused_computation | loop fusion | flops 327680 | bytes 327680 | tf_op jit(solution)/shard_map/concatenate | solution.py:429
  1.6 3.0 %collective-permute-start = (bf16[160,512]{1,0:T(8,128)(2,1)S(1)}, bf16[160,512]{1,0:T(8,128)(2,1)S(1)}, u32[]{:S(2)}, u32[]{:S(2)}) collective-permute-start(bf16[160,512]{1,0:T(8,128)(2,1)S(1)} %pad_maximum_fusion.refs_1_.refs_0_), channel_id=1, source_target_pairs={{0,4},{2,6},{4,0},{6,2},{8,12},{10,14},{12,8},{14,10},{16,20},{18,... | collective-permute-start | bytes 491528 | tf_op jit(solution)/shard_map/ppermute | solution.py:423
  4.6 1.6 %collective-permute-start.4 = (bf16[160,512]{1,0:T(8,128)(2,1)S(1)}, bf16[160,512]{1,0:T(8,128)(2,1)S(1)}, u32[]{:S(2)}, u32[]{:S(2)}) collective-permute-start(bf16[160,512]{1,0:T(8,128)(2,1)S(1)} %pad_maximum_fusion.refs_1_.refs_0_), channel_id=1, source_target_pairs={{0,8},{2,10},{4,12},{6,14},{8,0},{10,2},{12,4},{14,6},{16,24},{18,... | collective-permute-start | bytes 491528 | tf_op jit(solution)/shard_map/ppermute | solution.py:423
  6.2 0.0 collective-permute-start.6
  6.2 3.0 %collective-permute-start.1 = (bf16[32,1024]{1,0:T(8,128)(2,1)}, bf16[32,1024]{1,0:T(8,128)(2,1)S(1)}, u32[]{:S(2)}, u32[]{:S(2)}) collective-permute-start(bf16[32,1024]{1,0:T(8,128)(2,1)} %bitcast.7), channel_id=1, source_target_pairs={{0,16},{2,18},{4,20},{6,22},{8,24},{10,26},{12,28},{14,30},{16,0},... | collective-permute-start | bytes 196616 | tf_op jit(solution)/shard_map/ppermute | solution.py:423
  9.2 2.8 %decode_partials.1 = (bf16[16,128,512]{2,1,0:T(8,128)(2,1)}, bf16[80,512]{1,0:T(8,128)(2,1)S(1)}, bf16[32,1024]{1,0:T(8,128)(2,1)S(1)}, f32[2,24,128]{2,1,0:T(8,128)S(1)}) custom-call(s32[16]{0:T(128)} %len_hbm.1, s32[34]{0:T(128)} %deal_hbm.1, bf16[16,1024]{1,0:T(8,128)(2,1)} %q_hbm.1, bf16[16,512]{1,0:T(8,128)(2,1)} %new_hbm.1, ...), custom_call_target="tpu_custom_call" | custom-call | flops 8388608 | bytes 4194304 | tf_op jit(solution)/shard_map/decode_partials/pallas_call | solution.py:198
  12.0 2.4 %collective-permute-done.1.refs_0_ = bf16[32,1024]{1,0:T(8,128)(2,1)S(1)} collective-permute-done((bf16[32,1024]{1,0:T(8,128)(2,1)}, bf16[32,1024]{1,0:T(8,128)(2,1)S(1)}, u32[]{:S(2)}, u32[]{:S(2)}) %collective-permute-start.1) | collective-permute-done | bytes 65568 | tf_op jit(solution)/shard_map/ppermute | solution.py:423
  14.4 3.3 %collective-permute-start.7 = (bf16[80,512]{1,0:T(8,128)(2,1)S(1)}, bf16[80,512]{1,0:T(8,128)(2,1)S(1)}, u32[]{:S(2)}, u32[]{:S(2)}) collective-permute-start(bf16[80,512]{1,0:T(8,128)(2,1)S(1)} %get-tuple-element.23.refs_0_), channel_id=1, source_target_pairs={{0,16},{2,18},{4,20},{6,22},{8,24},{10,26},{12,28},{14,30},{16,0},... | collective-permute-start | bytes 245768 | tf_op jit(solution)/shard_map/ppermute | solution.py:423
  18.3 0.0 collective-permute-done.refs_3_.refs_2_
  18.3 0.0 collective-permute-done.4.refs_5_.refs_4_
  18.3 2.5 %collective-permute-done.7.refs_1_ = bf16[80,512]{1,0:T(8,128)(2,1)S(1)} collective-permute-done((bf16[80,512]{1,0:T(8,128)(2,1)S(1)}, bf16[80,512]{1,0:T(8,128)(2,1)S(1)}, u32[]{:S(2)}, u32[]{:S(2)}) %collective-permute-start.7) | collective-permute-done | bytes 81952 | tf_op jit(solution)/shard_map/ppermute | solution.py:423
  20.8 0.5 %collective-permute-start.5 = (bf16[160,512]{1,0:T(8,128)(2,1)S(1)}, bf16[160,512]{1,0:T(8,128)(2,1)S(1)}, u32[]{:S(2)}, u32[]{:S(2)}) collective-permute-start(bf16[160,512]{1,0:T(8,128)(2,1)S(1)} %collective-permute-done.4.refs_5_.refs_4_), channel_id=1, source_target_pairs={{0,2},{2,0},{4,6},{6,4},{8,10},{10,8},{12,14},{14,12},{16,18},{18,... | collective-permute-start | bytes 491528 | tf_op jit(solution)/shard_map/ppermute | solution.py:423
  21.3 0.0 collective-permute-start.3
  21.3 0.3 join_far.1.refs_0_
  21.6 2.3 %collective-permute-start.12 = (bf16[80,512]{1,0:T(8,128)(2,1)S(1)}, bf16[80,512]{1,0:T(8,128)(2,1)S(1)}, u32[]{:S(2)}, u32[]{:S(2)}) collective-permute-start(bf16[80,512]{1,0:T(8,128)(2,1)S(1)} %join_far.1.refs_0_), channel_id=1, source_target_pairs={{0,12},{2,14},{4,8},{6,10},{8,4},{10,6},{12,0},{14,2},{16,28},{18,... | collective-permute-start | bytes 245768 | tf_op jit(solution)/shard_map/ppermute | solution.py:423
  23.9 0.0 collective-permute-done.2.refs_2_.refs_1_
  23.9 0.1 collective-permute-start.11
  24.0 0.0 collective-permute-done.8.refs_8_.refs_7_
  24.0 1.4 %collective-permute-start.10 = (bf16[80,512]{1,0:T(8,128)(2,1)S(1)}, bf16[80,512]{1,0:T(8,128)(2,1)S(1)}, u32[]{:S(2)}, u32[]{:S(2)}) collective-permute-start(bf16[80,512]{1,0:T(8,128)(2,1)S(1)} %join_far.1.refs_0_), channel_id=1, source_target_pairs={{0,4},{2,6},{4,0},{6,2},{8,12},{10,14},{12,8},{14,10},{16,20},{18,... | collective-permute-start | bytes 245768 | tf_op jit(solution)/shard_map/ppermute | solution.py:423
  25.5 1.1 %prefill_partials.2 = bf16[32,1152]{1,0:T(8,128)(2,1)S(1)} custom-call(s32[8,128]{1,0:T(8,128)S(1)} %broadcast_in_dim.3.off_ref, bf16[32,1024]{1,0:T(8,128)(2,1)S(1)} %collective-permute-done.1.refs_0_, bf16[160,512]{1,0:T(8,128)(2,1)S(1)} %pad_maximum_fusion.refs_1_.refs_0_, bf16[160,512]{1,0:T(8,128)(2,1)S(1)} %collective-permute-done.2.refs_2_.refs_1_, ...), custom_call_target="tpu_custom_call" | custom-call | flops 167772160 | bytes 4194304 | tf_op jit(solution)/shard_map/prefill_partials/pallas_call | solution.py:307
  26.6 1.9 %collective-permute-start.9 = (bf16[32,1152]{1,0:T(8,128)(2,1)S(1)}, bf16[32,1152]{1,0:T(8,128)(2,1)S(1)}, u32[]{:S(2)}, u32[]{:S(2)}) collective-permute-start(bf16[32,1152]{1,0:T(8,128)(2,1)S(1)} %prefill_partials.2), channel_id=1, source_target_pairs={{0,16},{2,18},{4,20},{6,22},{8,24},{10,26},{12,28},{14,30},{16,0},... | collective-permute-start | bytes 221192 | tf_op jit(solution)/shard_map/ppermute | solution.py:423
  28.5 1.1 %prefill_partials.3.refs_0_ = bf16[32,1152]{1,0:T(8,128)(2,1)S(1)} custom-call(s32[8,128]{1,0:T(8,128)S(1)} %broadcast_in_dim.3.off_ref, bf16[32,1024]{1,0:T(8,128)(2,1)S(1)} %get-tuple-element.29.refs_0_, bf16[160,512]{1,0:T(8,128)(2,1)S(1)} %pad_maximum_fusion.refs_1_.refs_0_, bf16[160,512]{1,0:T(8,128)(2,1)S(1)} %collective-permute-done.2.refs_2_.refs_1_, ...), custom_call_target="tpu_custom_call" | custom-call | flops 167772160 | bytes 4194304 | tf_op jit(solution)/shard_map/prefill_partials/pallas_call | solution.py:307
  29.6 0.0 collective-permute-done.12.refs_3_
  29.6 0.0 collective-permute-done.11.refs_2_
  29.6 0.4 join_lanes.1.refs_2_.near_ref
  29.9 3.5 %collective-permute-done.9.refs_1_ = bf16[32,1152]{1,0:T(8,128)(2,1)S(1)} collective-permute-done((bf16[32,1152]{1,0:T(8,128)(2,1)S(1)}, bf16[32,1152]{1,0:T(8,128)(2,1)S(1)}, u32[]{:S(2)}, u32[]{:S(2)}) %collective-permute-start.9) | collective-permute-done | bytes 73760 | tf_op jit(solution)/shard_map/ppermute | solution.py:423
  33.5 1.4 %collective-permute-done.13.refs_3_.beside_ref = bf16[176,512]{1,0:T(8,128)(2,1)S(1)} collective-permute-done((bf16[176,512]{1,0:T(8,128)(2,1)S(1)}, bf16[176,512]{1,0:T(8,128)(2,1)S(1)}, u32[]{:S(2)}, u32[]{:S(2)}) %collective-permute-start.13) | collective-permute-done | bytes 180256 | tf_op jit(solution)/shard_map/ppermute | solution.py:423
  34.9 0.3 join_parts.1.refs_0_
  35.2 1.6 %collective-permute-start.14 = (bf16[48,1024]{1,0:T(8,128)(2,1)S(1)}, bf16[48,1024]{1,0:T(8,128)(2,1)S(1)}, u32[]{:S(2)}, u32[]{:S(2)}) collective-permute-start(bf16[48,1024]{1,0:T(8,128)(2,1)S(1)} %join_parts.1.refs_0_), channel_id=1, source_target_pairs={{0,1},{1,0},{2,3},{3,2},{4,5},{5,4},{6,7},{7,6},{8,9},{9,8},{10,11... | collective-permute-start | bytes 294920 | tf_op jit(solution)/shard_map/ppermute | solution.py:464
  36.7 1.7 %update_cache.1 = bf16[1,128,512]{2,1,0:T(8,128)(2,1)} custom-call(s32[8,128]{1,0:T(8,128)S(1)} %broadcast_in_dim.3.off_ref, bf16[1,128,512]{2,1,0:T(8,128)(2,1)} %cache_hbm.3, bf16[176,512]{1,0:T(8,128)(2,1)S(1)} %join_lanes.1.refs_2_.near_ref, bf16[176,512]{1,0:T(8,128)(2,1)S(1)} %collective-permute-done.13.refs_3_.beside_ref, ...), custom_call_target="tpu_custom_call" | custom-call | tf_op jit(solution)/shard_map/update_cache/pallas_call | solution.py:364
  38.5 1.6 %collective-permute-done.14.refs_1_ = bf16[48,1024]{1,0:T(8,128)(2,1)S(1)} collective-permute-done((bf16[48,1024]{1,0:T(8,128)(2,1)S(1)}, bf16[48,1024]{1,0:T(8,128)(2,1)S(1)}, u32[]{:S(2)}, u32[]{:S(2)}) %collective-permute-start.14) | collective-permute-done | bytes 98336 | tf_op jit(solution)/shard_map/ppermute | solution.py:464
  40.1 0.8 %route_outputs.1 = (bf16[1,32,1024]{2,1,0:T(8,128)(2,1)}, bf16[16,1024]{1,0:T(8,128)(2,1)}) custom-call(f32[2,24,128]{2,1,0:T(8,128)S(1)} %get-tuple-element.21.route_ref, bf16[48,1024]{1,0:T(8,128)(2,1)S(1)} %join_parts.1.refs_0_, bf16[48,1024]{1,0:T(8,128)(2,1)S(1)} %collective-permute-done.14.refs_1_), custom_call_target="tpu_custom_call" | custom-call | tf_op jit(solution)/shard_map/route_outputs/pallas_call | solution.py:392
  (8 shorter events, 0.0 us)
Async XLA Ops:
  1.6 16.7 %collective-permute-start = (bf16[160,512]{1,0:T(8,128)(2,1)S(1)}, bf16[160,512]{1,0:T(8,128)(2,1)S(1)}, u32[]{:S(2)}, u32[]{:S(2)}) collective-permute-start(bf16[160,512]{1,0:T(8,128)(2,1)S(1)} %pad_maximum_fusion.refs_1_.refs_0_), channel_id=1, source_target_pairs={{0,4},{2,6},{4,0},{6,2},{8,12},{10,14},{12,8},{14,10},{16,20},{18,... | collective-permute-start | bytes 491528 | tf_op jit(solution)/shard_map/ppermute | solution.py:423
  4.6 13.7 %collective-permute-start.4 = (bf16[160,512]{1,0:T(8,128)(2,1)S(1)}, bf16[160,512]{1,0:T(8,128)(2,1)S(1)}, u32[]{:S(2)}, u32[]{:S(2)}) collective-permute-start(bf16[160,512]{1,0:T(8,128)(2,1)S(1)} %pad_maximum_fusion.refs_1_.refs_0_), channel_id=1, source_target_pairs={{0,8},{2,10},{4,12},{6,14},{8,0},{10,2},{12,4},{14,6},{16,24},{18,... | collective-permute-start | bytes 491528 | tf_op jit(solution)/shard_map/ppermute | solution.py:423
  6.2 14.6 %collective-permute-start.6 = (bf16[160,512]{1,0:T(8,128)(2,1)S(1)}, bf16[160,512]{1,0:T(8,128)(2,1)S(1)}, u32[]{:S(2)}, u32[]{:S(2)}) collective-permute-start(bf16[160,512]{1,0:T(8,128)(2,1)S(1)} %pad_maximum_fusion.refs_1_.refs_0_), channel_id=1, source_target_pairs={{0,12},{2,14},{4,8},{6,10},{8,4},{10,6},{12,0},{14,2},{16,28},{18,... | collective-permute-start | bytes 491528 | tf_op jit(solution)/shard_map/ppermute | solution.py:423
  6.2 8.2 %collective-permute-start.1 = (bf16[32,1024]{1,0:T(8,128)(2,1)}, bf16[32,1024]{1,0:T(8,128)(2,1)S(1)}, u32[]{:S(2)}, u32[]{:S(2)}) collective-permute-start(bf16[32,1024]{1,0:T(8,128)(2,1)} %bitcast.7), channel_id=1, source_target_pairs={{0,16},{2,18},{4,20},{6,22},{8,24},{10,26},{12,28},{14,30},{16,0},... | collective-permute-start | bytes 196616 | tf_op jit(solution)/shard_map/ppermute | solution.py:423
  14.4 6.4 %collective-permute-start.7 = (bf16[80,512]{1,0:T(8,128)(2,1)S(1)}, bf16[80,512]{1,0:T(8,128)(2,1)S(1)}, u32[]{:S(2)}, u32[]{:S(2)}) collective-permute-start(bf16[80,512]{1,0:T(8,128)(2,1)S(1)} %get-tuple-element.23.refs_0_), channel_id=1, source_target_pairs={{0,16},{2,18},{4,20},{6,22},{8,24},{10,26},{12,28},{14,30},{16,0},... | collective-permute-start | bytes 245768 | tf_op jit(solution)/shard_map/ppermute | solution.py:423
  17.6 6.3 %collective-permute-start.2 = (bf16[160,512]{1,0:T(8,128)(2,1)S(1)}, bf16[160,512]{1,0:T(8,128)(2,1)S(1)}, u32[]{:S(2)}, u32[]{:S(2)}) collective-permute-start(bf16[160,512]{1,0:T(8,128)(2,1)S(1)} %pad_maximum_fusion.refs_1_.refs_0_), channel_id=1, source_target_pairs={{0,2},{2,0},{4,6},{6,4},{8,10},{10,8},{12,14},{14,12},{16,18},{18,... | collective-permute-start | bytes 491528 | tf_op jit(solution)/shard_map/ppermute | solution.py:423
  20.8 3.2 %collective-permute-start.8 = (bf16[160,512]{1,0:T(8,128)(2,1)S(1)}, bf16[160,512]{1,0:T(8,128)(2,1)S(1)}, u32[]{:S(2)}, u32[]{:S(2)}) collective-permute-start(bf16[160,512]{1,0:T(8,128)(2,1)S(1)} %collective-permute-done.6.refs_7_.refs_6_), channel_id=1, source_target_pairs={{0,2},{2,0},{4,6},{6,4},{8,10},{10,8},{12,14},{14,12},{16,18},{18,... | collective-permute-start | bytes 491528 | tf_op jit(solution)/shard_map/ppermute | solution.py:423
  20.8 4.7 %collective-permute-start.5 = (bf16[160,512]{1,0:T(8,128)(2,1)S(1)}, bf16[160,512]{1,0:T(8,128)(2,1)S(1)}, u32[]{:S(2)}, u32[]{:S(2)}) collective-permute-start(bf16[160,512]{1,0:T(8,128)(2,1)S(1)} %collective-permute-done.4.refs_5_.refs_4_), channel_id=1, source_target_pairs={{0,2},{2,0},{4,6},{6,4},{8,10},{10,8},{12,14},{14,12},{16,18},{18,... | collective-permute-start | bytes 491528 | tf_op jit(solution)/shard_map/ppermute | solution.py:423
  21.3 4.2 %collective-permute-start.3 = (bf16[160,512]{1,0:T(8,128)(2,1)S(1)}, bf16[160,512]{1,0:T(8,128)(2,1)S(1)}, u32[]{:S(2)}, u32[]{:S(2)}) collective-permute-start(bf16[160,512]{1,0:T(8,128)(2,1)S(1)} %collective-permute-done.refs_3_.refs_2_), channel_id=1, source_target_pairs={{0,2},{2,0},{4,6},{6,4},{8,10},{10,8},{12,14},{14,12},{16,18},{18,... | collective-permute-start | bytes 491528 | tf_op jit(solution)/shard_map/ppermute | solution.py:423
  21.6 8.0 %collective-permute-start.12 = (bf16[80,512]{1,0:T(8,128)(2,1)S(1)}, bf16[80,512]{1,0:T(8,128)(2,1)S(1)}, u32[]{:S(2)}, u32[]{:S(2)}) collective-permute-start(bf16[80,512]{1,0:T(8,128)(2,1)S(1)} %join_far.1.refs_0_), channel_id=1, source_target_pairs={{0,12},{2,14},{4,8},{6,10},{8,4},{10,6},{12,0},{14,2},{16,28},{18,... | collective-permute-start | bytes 245768 | tf_op jit(solution)/shard_map/ppermute | solution.py:423
  23.9 5.6 %collective-permute-start.11 = (bf16[80,512]{1,0:T(8,128)(2,1)S(1)}, bf16[80,512]{1,0:T(8,128)(2,1)S(1)}, u32[]{:S(2)}, u32[]{:S(2)}) collective-permute-start(bf16[80,512]{1,0:T(8,128)(2,1)S(1)} %join_far.1.refs_0_), channel_id=1, source_target_pairs={{0,8},{2,10},{4,12},{6,14},{8,0},{10,2},{12,4},{14,6},{16,24},{18,... | collective-permute-start | bytes 245768 | tf_op jit(solution)/shard_map/ppermute | solution.py:423
  24.0 5.5 %collective-permute-start.10 = (bf16[80,512]{1,0:T(8,128)(2,1)S(1)}, bf16[80,512]{1,0:T(8,128)(2,1)S(1)}, u32[]{:S(2)}, u32[]{:S(2)}) collective-permute-start(bf16[80,512]{1,0:T(8,128)(2,1)S(1)} %join_far.1.refs_0_), channel_id=1, source_target_pairs={{0,4},{2,6},{4,0},{6,2},{8,12},{10,14},{12,8},{14,10},{16,20},{18,... | collective-permute-start | bytes 245768 | tf_op jit(solution)/shard_map/ppermute | solution.py:423
  26.6 6.9 %collective-permute-start.9 = (bf16[32,1152]{1,0:T(8,128)(2,1)S(1)}, bf16[32,1152]{1,0:T(8,128)(2,1)S(1)}, u32[]{:S(2)}, u32[]{:S(2)}) collective-permute-start(bf16[32,1152]{1,0:T(8,128)(2,1)S(1)} %prefill_partials.2), channel_id=1, source_target_pairs={{0,16},{2,18},{4,20},{6,22},{8,24},{10,26},{12,28},{14,30},{16,0},... | collective-permute-start | bytes 221192 | tf_op jit(solution)/shard_map/ppermute | solution.py:423
  33.5 1.4 %collective-permute-start.13 = (bf16[176,512]{1,0:T(8,128)(2,1)S(1)}, bf16[176,512]{1,0:T(8,128)(2,1)S(1)}, u32[]{:S(2)}, u32[]{:S(2)}) collective-permute-start(bf16[176,512]{1,0:T(8,128)(2,1)S(1)} %join_lanes.1.refs_2_.near_ref), channel_id=1, source_target_pairs={{0,2},{2,0},{4,6},{6,4},{8,10},{10,8},{12,14},{14,12},{16,18},{18,... | collective-permute-start | bytes 540680 | tf_op jit(solution)/shard_map/ppermute | solution.py:423
  35.2 4.9 %collective-permute-start.14 = (bf16[48,1024]{1,0:T(8,128)(2,1)S(1)}, bf16[48,1024]{1,0:T(8,128)(2,1)S(1)}, u32[]{:S(2)}, u32[]{:S(2)}) collective-permute-start(bf16[48,1024]{1,0:T(8,128)(2,1)S(1)} %join_parts.1.refs_0_), channel_id=1, source_target_pairs={{0,1},{1,0},{2,3},{3,2},{4,5},{5,4},{6,7},{7,6},{8,9},{9,8},{10,11... | collective-permute-start | bytes 294920 | tf_op jit(solution)/shard_map/ppermute | solution.py:464

commit v15 on v13

--- a/solution.py
+++ b/solution.py
@@ -232,30 +232,31 @@
     return jnp.concatenate(blocks + [ref[pl.ds(KEY_VALUE_HEADS * slots, slots), pl.ds(0, STATS)]], axis=1)
 
 
-def step_kernel(slots, keep, *refs):
-    parts, out_ref = refs[:-1], refs[-1]
-    joined, logs = join([decode_part(ref, slots) for ref in parts])
+def step_kernel(slots, count, *refs):
+    out_ref = refs[-1]
+    joined, logs = join([decode_part(ref, slots) for ref in refs[:count]])
     head = PART_ROWS * slots
-    rest = parts[0].shape[0] - head
     for g in range(KEY_VALUE_HEADS):
         out_ref[pl.ds(g * slots, slots), :] = joined[:, g * KVW : (g + 1) * KVW]
     put_stats(out_ref, [logs[:, h * HEAD_SIZE : h * HEAD_SIZE + 1] for h in range(QUERY_HEADS)], slots)
-    for i, ref in enumerate(parts if keep else parts[1:]):
-        out_ref[pl.ds(head + i * rest, rest), :] = ref[pl.ds(head, rest), :]
-
-
-def join_step(parts, slots, keep, name):
+    at = head
+    for ref in refs[count:-1]:
+        rest = ref.shape[0] - head
+        out_ref[pl.ds(at, rest), :] = ref[pl.ds(head, rest), :]
+        at += rest
+
+
+def join_step(parts, carriers, slots, name):
     head = PART_ROWS * slots
-    rest = parts[0].shape[0] - head
-    rows = head + rest * (len(parts) if keep else len(parts) - 1)
-    return pl.pallas_call(
-        functools.partial(step_kernel, slots, keep),
-        in_specs=[VMEM] * len(parts),
+    rows = head + sum(c.shape[0] - head for c in carriers)
+    return pl.pallas_call(
+        functools.partial(step_kernel, slots, len(parts)),
+        in_specs=[VMEM] * (len(parts) + len(carriers)),
         out_specs=VMEM,
         out_shape=pltpu.VMEM((rows, KVW), BF16),
         compiler_params=pltpu.CompilerParams(vmem_limit_bytes=16 << 20),
         name=name,
-    )(*parts)
+    )(*parts, *carriers)
 
 
 def prefill_kernel(sets, ctx, off_ref, *refs):
@@ -317,38 +318,51 @@
     )(offset, *packs, *tables)
 
 
-def join_kernel(count, slots, *refs):
-    out_ref, tokens = refs[-1], refs[0].shape[0]
-    out_ref[pl.ds(0, tokens), :] = join([ref[...] for ref in refs[:count]])[0]
-    out_ref[pl.ds(tokens, slots), :] = join([decode_part(ref, slots) for ref in refs[count:-1]])[0]
-
-
-def join_parts(parts, decodes, slots):
-    return pl.pallas_call(
-        functools.partial(join_kernel, len(parts), slots),
-        in_specs=[VMEM] * (len(parts) + len(decodes)),
+def join_kernel(*refs):
+    refs[-1][...] = join([ref[...] for ref in refs[:-1]])[0]
+
+
+def join_parts(parts):
+    return pl.pallas_call(
+        join_kernel,
+        in_specs=[VMEM] * len(parts),
         out_specs=VMEM,
-        out_shape=jax.ShapeDtypeStruct((parts[0].shape[0] + slots, QW), BF16),
+        out_shape=pltpu.VMEM((parts[0].shape[0], QW), BF16),
         compiler_params=pltpu.CompilerParams(vmem_limit_bytes=16 << 20),
         name="join_parts",
-    )(*parts, *decodes)
-
-
-def update_kernel(tokens, slots, off_ref, cache_hbm, near_ref, beside_ref, *refs):
+    )(*parts)
+
+
+def finish_kernel(slots, prefill_ref, *refs):
+    decodes, out_ref = refs[:-1], refs[-1]
+    tokens = prefill_ref.shape[0]
+    out_ref[pl.ds(0, tokens), :] = prefill_ref[...]
+    out_ref[pl.ds(tokens, slots), :] = join([decode_part(ref, slots) for ref in decodes])[0]
+
+
+def finish(prefill, decodes, slots):
+    return pl.pallas_call(
+        functools.partial(finish_kernel, slots),
+        in_specs=[VMEM] * (1 + len(decodes)),
+        out_specs=VMEM,
+        out_shape=pltpu.VMEM((prefill.shape[0] + slots, QW), BF16),
+        compiler_params=pltpu.CompilerParams(vmem_limit_bytes=16 << 20),
+        name="finish",
+    )(prefill, *decodes)
+
+
+def update_kernel(tokens, sets, off_ref, cache_hbm, near_ref, beside_ref, *refs):
     tables, (out_ref, cache_ref, sem) = refs[:KEY_SET], refs[-3:]
     load = pltpu.make_async_copy(cache_hbm.at[0], cache_ref, sem)
     load.start()
     ctx = cache_ref.shape[0]
-    head = PART_ROWS * slots
-    rest = near_ref.shape[0] - head
     me = lax.axis_index(BLK)
     rows = [t[pl.ds(ctx, tokens), :] for t in tables]
-    rows = jnp.concatenate(rows + [r[pl.ds(head, rest), :] for r in (near_ref, beside_ref)], axis=0)
+    rows = jnp.concatenate(rows + [near_ref[...], beside_ref[...]], axis=0)
     count = rows.shape[0]
     index = lax.broadcasted_iota(jnp.int32, (1, count), 1)
     block = index // tokens
-    half = rest // tokens
-    sets = half * 2 // KEY_SET
+    half = sets * KEY_SET // 2
     far = block - KEY_SET
     inner = far % half
     distance = KEY_SET * (1 + inner % sets) + 2 * (inner // sets) + far // half
@@ -360,9 +374,9 @@
     out_ref[0] = jnp.where(inside, picked, cache_ref[...])
 
 
-def update_cache(offset, cache, near, beside, tables, tokens, slots):
-    return pl.pallas_call(
-        functools.partial(update_kernel, tokens, slots),
+def update_cache(offset, cache, near, beside, tables, tokens, sets):
+    return pl.pallas_call(
+        functools.partial(update_kernel, tokens, sets),
         in_specs=[VMEM, HBM] + [VMEM] * (2 + len(tables)),
         out_specs=VMEM,
         out_shape=jax.ShapeDtypeStruct(cache.shape, BF16),
@@ -442,22 +456,24 @@
     )
     far = [swap(part, k) for k in others]
     offset = jnp.full((8, HEAD_SIZE), prefill_offsets[0], jnp.int32)
-    lanes[1], offset, _ = lax.optimization_barrier((lanes[1], offset, part))
-    lanes[2], packs, _ = lax.optimization_barrier((lanes[2], packs, lanes[1]))
+    lanes[2], offset, _ = lax.optimization_barrier((lanes[2], offset, part))
     lanes[3], far, _ = lax.optimization_barrier((lanes[3], far, lanes[2]))
-    part = join_step([part] + far, slots, False, "join_far")
+    lanes[1], packs, _ = lax.optimization_barrier((lanes[1], packs, lanes[2]))
+    part = join_step([part] + far, [], slots, "join_far")
     tables = [t for lane in lanes for t in (lane, swap(lane, 1))]
-    across = swap(part, 2)
+    beside = swap(part, 1)
 
     sent = prefill_partials(offset, packs, tables, ctx, [k // KEY_SET for k in others])
-    part = join_step([part, after(across, sent[0])], slots, True, "join_x")
+    arrived = [swap(p, k) for k, p in zip(others, sent)]
     queries = after(queries, sent[0])
     kept = prefill_partials(offset, [queries], tables, ctx, [0])
-    part = join_step([part, after(swap(part, 4), kept[0])], slots, True, "join_z")
-    arrived = [swap(p, k) for k, p in zip(others, sent)]
-    beside = swap(after(part, *arrived), 1)
-    attended = join_parts([*kept] + arrived, [part, beside], slots)
-    prefill_cache_out = update_cache(offset, prefill_cache, part, beside, tables, tokens, slots)
+    part = join_step([part, after(beside, sent[0])], far, slots, "join_core")
+    around = [part] + [swap(part, k) for k in range(2, KEY_SET, 2)]
+    attended = join_parts([*kept] + arrived)
+    attended = finish(attended, around, slots)
+    around[0], attended = lax.optimization_barrier((around[0], attended))
+    news = jnp.concatenate([after(a, attended)[PART_ROWS * slots :] for a in around], axis=0)
+    prefill_cache_out = update_cache(offset, prefill_cache, news, swap(news, 1), tables, tokens, len(others))
 
     if req == 2:
         held = [attended, lax.ppermute(attended, "req", [(0, 1), (1, 0)])]

time: 39.6 us -> 38.3 us (0.967)
  waiting for transfers between devices: 13.5 us -> 12.1 us
    ppermute x13 -> x15, waiting for transfers between devices: 12.1 us -> 10.3 us  [swap(): return lax.ppermute(array, BLK, [(i, i ^ distance) for i in range(blk)])]
    ppermute x1, waiting for transfers between devices: 1.38 us -> 1.79 us  [per_device(): held = [attended, lax.ppermute(attended, 'req', [(0, 1), (1, 0)])]]
    ppermute x13 -> x15, starting transfers between devices: 13.1 us -> 13.4 us  [swap(): return lax.ppermute(array, BLK, [(i, i ^ distance) for i in range(blk)])]
  transfers between devices with their start and end apart: 14 -> 16, of which waited for: 5 -> 6; matrix products, arithmetic and copies ran while one was open for 0% -> 0% of each run, Pallas kernels for 18% -> 19%
where the time goes in v15:
time: 38.3 us; the launch traced here: 38.1 us
  starting transfers between devices  15.1 us (39%)
  waiting for transfers between devices  12.1 us (32%)
  Pallas kernels  8.47 us (22%)
  between operations  1.48 us (4%)
  other arithmetic  0.98 us (3%)
    ppermute x15, starting transfers between devices, swap(): return lax.ppermute(array, BLK, [(i, i ^ distance) for i in range(blk)])  13.4 us
    ppermute x15, waiting for transfers between devices, swap(): return lax.ppermute(array, BLK, [(i, i ^ distance) for i in range(blk)])  10.3 us
    pallas_call x1, Pallas kernels, decode_partials(): pl.pallas_call(decode_kernel, in_specs=[HBM] * len(inputs), out_specs=[HB...  2.81 us
    pallas_call x2, Pallas kernels, prefill_partials(): pl.pallas_call(functools.partial(prefill_kernel, sets, ctx), in_specs=[VM...  2.13 us
    ppermute x1, waiting for transfers between devices, per_device(): held = [attended, lax.ppermute(attended, 'req', [(0, 1), (1, 0)])]  1.79 us
    pallas_call x1, Pallas kernels, update_cache(): pl.pallas_call(functools.partial(update_kernel, tokens, sets), in_specs=[...  1.71 us
    ppermute x1, starting transfers between devices, per_device(): held = [attended, lax.ppermute(attended, 'req', [(0, 1), (1, 0)])]  1.7 us
    concatenate x1, other arithmetic, per_device(): table = jnp.concatenate([prefill_cache[0], new_prefill[0]], axis=0)  0.97 us
  transfers between devices with their start and end apart: 16, of which 6 were waited for; matrix products, arithmetic and copies ran while one was open for 0% of the time, Pallas kernels for 19%

profile of v15, /device:TPU:0, one launch (start us, length us, event | category | flops | bytes accessed | tf_op | source)
XLA Modules:
  0.0 38.1 jit_solution(17234649072488998327)
XLA Ops:
  0.6 0.0 copy-start
  0.6 1.0 %pad_maximum_fusion.refs_1_.refs_0_ = bf16[160,512]{1,0:T(8,128)(2,1)S(1)} fusion(bf16[32,512]{1,0:T(8,128)(2,1)} %bitcast.6, bf16[128,512]{1,0:T(8,128)(2,1)} %bitcast.5), kind=kLoop, calls=%fused_computation | loop fusion | flops 327680 | bytes 327680 | tf_op jit(solution)/shard_map/concatenate | solution.py:443
  1.6 3.1 %collective-permute-start.2 = (bf16[160,512]{1,0:T(8,128)(2,1)S(1)}, bf16[160,512]{1,0:T(8,128)(2,1)S(1)}, u32[]{:S(2)}, u32[]{:S(2)}) collective-permute-start(bf16[160,512]{1,0:T(8,128)(2,1)S(1)} %pad_maximum_fusion.refs_1_.refs_0_), channel_id=1, source_target_pairs={{0,8},{2,10},{4,12},{6,14},{8,0},{10,2},{12,4},{14,6},{16,24},{18,... | collective-permute-start | bytes 491528 | tf_op jit(solution)/shard_map/ppermute | solution.py:437
  4.7 1.4 %collective-permute-start = (bf16[160,512]{1,0:T(8,128)(2,1)S(1)}, bf16[160,512]{1,0:T(8,128)(2,1)S(1)}, u32[]{:S(2)}, u32[]{:S(2)}) collective-permute-start(bf16[160,512]{1,0:T(8,128)(2,1)S(1)} %pad_maximum_fusion.refs_1_.refs_0_), channel_id=1, source_target_pairs={{0,12},{2,14},{4,8},{6,10},{8,4},{10,6},{12,0},{14,2},{16,28},{18,... | collective-permute-start | bytes 491528 | tf_op jit(solution)/shard_map/ppermute | solution.py:437
  6.1 0.2 collective-permute-start.4
  6.2 2.8 %decode_partials.1 = (bf16[16,128,512]{2,1,0:T(8,128)(2,1)}, bf16[80,512]{1,0:T(8,128)(2,1)S(1)}, bf16[32,1024]{1,0:T(8,128)(2,1)S(1)}, f32[2,24,128]{2,1,0:T(8,128)S(1)}) custom-call(s32[16]{0:T(128)} %len_hbm.1, s32[34]{0:T(128)} %deal_hbm.1, bf16[16,1024]{1,0:T(8,128)(2,1)} %q_hbm.1, bf16[16,512]{1,0:T(8,128)(2,1)} %new_hbm.1, ...), custom_call_target="tpu_custom_call" | custom-call | flops 8388608 | bytes 4194304 | tf_op jit(solution)/shard_map/decode_partials/pallas_call | solution.py:198
  9.1 3.0 %collective-permute-start.1 = (bf16[80,512]{1,0:T(8,128)(2,1)S(1)}, bf16[80,512]{1,0:T(8,128)(2,1)S(1)}, u32[]{:S(2)}, u32[]{:S(2)}) collective-permute-start(bf16[80,512]{1,0:T(8,128)(2,1)S(1)} %get-tuple-element.27.refs_0_), channel_id=1, source_target_pairs={{0,16},{2,18},{4,20},{6,22},{8,24},{10,26},{12,28},{14,30},{16,0},... | collective-permute-start | bytes 245768 | tf_op jit(solution)/shard_map/ppermute | solution.py:437
  12.1 0.1 collective-permute-start.5
  12.8 0.0 collective-permute-done.2.refs_5_.refs_4_
  12.8 0.1 collective-permute-start.6
  12.9 4.5 %collective-permute-done.1.refs_1_.refs_2_ = bf16[80,512]{1,0:T(8,128)(2,1)S(1)} collective-permute-done((bf16[80,512]{1,0:T(8,128)(2,1)S(1)}, bf16[80,512]{1,0:T(8,128)(2,1)S(1)}, u32[]{:S(2)}, u32[]{:S(2)}) %collective-permute-start.1) | collective-permute-done | bytes 81952 | tf_op jit(solution)/shard_map/ppermute | solution.py:437
  17.4 0.0 collective-permute-done.refs_7_.refs_6_
  17.4 1.6 %collective-permute-done.5.refs_0_ = bf16[32,1024]{1,0:T(8,128)(2,1)S(1)} collective-permute-done((bf16[32,1024]{1,0:T(8,128)(2,1)S(1)}, bf16[32,1024]{1,0:T(8,128)(2,1)S(1)}, u32[]{:S(2)}, u32[]{:S(2)}) %collective-permute-start.5) | collective-permute-done | bytes 65568 | tf_op jit(solution)/shard_map/ppermute | solution.py:437
  19.0 0.5 %collective-permute-start.8 = (bf16[160,512]{1,0:T(8,128)(2,1)S(1)}, bf16[160,512]{1,0:T(8,128)(2,1)S(1)}, u32[]{:S(2)}, u32[]{:S(2)}) collective-permute-start(bf16[160,512]{1,0:T(8,128)(2,1)S(1)} %collective-permute-done.2.refs_5_.refs_4_), channel_id=1, source_target_pairs={{0,2},{2,0},{4,6},{6,4},{8,10},{10,8},{12,14},{14,12},{16,18},{18,... | collective-permute-start | bytes 491528 | tf_op jit(solution)/shard_map/ppermute | solution.py:437
  19.5 0.3 join_far.1.refs_0_
  19.8 0.1 collective-permute-start.3
  19.9 0.5 %collective-permute-done.7.refs_4_.refs_3_ = bf16[160,512]{1,0:T(8,128)(2,1)S(1)} collective-permute-done((bf16[160,512]{1,0:T(8,128)(2,1)S(1)}, bf16[160,512]{1,0:T(8,128)(2,1)S(1)}, u32[]{:S(2)}, u32[]{:S(2)}) %collective-permute-start.7) | collective-permute-done | bytes 163872 | tf_op jit(solution)/shard_map/ppermute | solution.py:437
  20.4 0.2 collective-permute-done.8.refs_6_.refs_5_
  20.6 1.1 %prefill_partials.2 = bf16[32,1152]{1,0:T(8,128)(2,1)S(1)} custom-call(s32[8,128]{1,0:T(8,128)S(1)} %broadcast_in_dim.3.off_ref, bf16[32,1024]{1,0:T(8,128)(2,1)S(1)} %collective-permute-done.5.refs_0_, bf16[160,512]{1,0:T(8,128)(2,1)S(1)} %pad_maximum_fusion.refs_1_.refs_0_, bf16[160,512]{1,0:T(8,128)(2,1)S(1)} %collective-permute-done.6.refs_2_.refs_1_, ...), custom_call_target="tpu_custom_call" | custom-call | flops 167772160 | bytes 4194304 | tf_op jit(solution)/shard_map/prefill_partials/pallas_call | solution.py:308
  21.7 0.3 join_core.1.refs_0_
  22.0 1.7 %collective-permute-start.11 = (bf16[80,512]{1,0:T(8,128)(2,1)S(1)}, bf16[80,512]{1,0:T(8,128)(2,1)S(1)}, u32[]{:S(2)}, u32[]{:S(2)}) collective-permute-start(bf16[80,512]{1,0:T(8,128)(2,1)S(1)} %join_core.1.refs_0_), channel_id=1, source_target_pairs={{0,4},{2,6},{4,0},{6,2},{8,12},{10,14},{12,8},{14,10},{16,20},{18,... | collective-permute-start | bytes 245768 | tf_op jit(solution)/shard_map/ppermute | solution.py:437
  23.7 1.8 %collective-permute-start.13 = (bf16[80,512]{1,0:T(8,128)(2,1)S(1)}, bf16[80,512]{1,0:T(8,128)(2,1)S(1)}, u32[]{:S(2)}, u32[]{:S(2)}) collective-permute-start(bf16[80,512]{1,0:T(8,128)(2,1)S(1)} %join_core.1.refs_0_), channel_id=1, source_target_pairs={{0,12},{2,14},{4,8},{6,10},{8,4},{10,6},{12,0},{14,2},{16,28},{18,... | collective-permute-start | bytes 245768 | tf_op jit(solution)/shard_map/ppermute | solution.py:437
  25.6 1.4 %collective-permute-start.10 = (bf16[32,1152]{1,0:T(8,128)(2,1)S(1)}, bf16[32,1152]{1,0:T(8,128)(2,1)S(1)}, u32[]{:S(2)}, u32[]{:S(2)}) collective-permute-start(bf16[32,1152]{1,0:T(8,128)(2,1)S(1)} %prefill_partials.2), channel_id=1, source_target_pairs={{0,16},{2,18},{4,20},{6,22},{8,24},{10,26},{12,28},{14,30},{16,0},... | collective-permute-start | bytes 221192 | tf_op jit(solution)/shard_map/ppermute | solution.py:437
  27.0 1.1 %prefill_partials.3.refs_0_ = bf16[32,1152]{1,0:T(8,128)(2,1)S(1)} custom-call(s32[8,128]{1,0:T(8,128)S(1)} %broadcast_in_dim.3.off_ref, bf16[32,1024]{1,0:T(8,128)(2,1)S(1)} %get-tuple-element.36.refs_0_, bf16[160,512]{1,0:T(8,128)(2,1)S(1)} %pad_maximum_fusion.refs_1_.refs_0_, bf16[160,512]{1,0:T(8,128)(2,1)S(1)} %collective-permute-done.6.refs_2_.refs_1_, ...), custom_call_target="tpu_custom_call" | custom-call | flops 167772160 | bytes 4194304 | tf_op jit(solution)/shard_map/prefill_partials/pallas_call | solution.py:308
  28.1 3.4 %collective-permute-done.10.refs_1_ = bf16[32,1152]{1,0:T(8,128)(2,1)S(1)} collective-permute-done((bf16[32,1152]{1,0:T(8,128)(2,1)S(1)}, bf16[32,1152]{1,0:T(8,128)(2,1)S(1)}, u32[]{:S(2)}, u32[]{:S(2)}) %collective-permute-start.10) | collective-permute-done | bytes 73760 | tf_op jit(solution)/shard_map/ppermute | solution.py:437
  31.5 0.2 join_parts.1.prefill_ref
  31.8 0.3 finish.1.refs_0_
  32.1 0.1 collective-permute-start.15
  32.2 1.7 %collective-permute-start.14 = (bf16[48,1024]{1,0:T(8,128)(2,1)S(1)}, bf16[48,1024]{1,0:T(8,128)(2,1)S(1)}, u32[]{:S(2)}, u32[]{:S(2)}) collective-permute-start(bf16[48,1024]{1,0:T(8,128)(2,1)S(1)} %finish.1.refs_0_), channel_id=1, source_target_pairs={{0,1},{1,0},{2,3},{3,2},{4,5},{5,4},{6,7},{7,6},{8,9},{9,8},{10,11... | collective-permute-start | bytes 294920 | tf_op jit(solution)/shard_map/ppermute | solution.py:479
  33.9 1.7 %update_cache.1 = bf16[1,128,512]{2,1,0:T(8,128)(2,1)} custom-call(s32[8,128]{1,0:T(8,128)S(1)} %broadcast_in_dim.3.off_ref, bf16[1,128,512]{2,1,0:T(8,128)(2,1)} %cache_hbm.3, bf16[128,512]{1,0:T(8,128)(2,1)S(1)} %pad_maximum_fusion.1.near_ref, bf16[128,512]{1,0:T(8,128)(2,1)S(1)} %collective-permute-done.15.beside_ref, ...), custom_call_target="tpu_custom_call" | custom-call | tf_op jit(solution)/shard_map/update_cache/pallas_call | solution.py:378
  35.6 1.8 %collective-permute-done.14.refs_1_ = bf16[48,1024]{1,0:T(8,128)(2,1)S(1)} collective-permute-done((bf16[48,1024]{1,0:T(8,128)(2,1)S(1)}, bf16[48,1024]{1,0:T(8,128)(2,1)S(1)}, u32[]{:S(2)}, u32[]{:S(2)}) %collective-permute-start.14) | collective-permute-done | bytes 98336 | tf_op jit(solution)/shard_map/ppermute | solution.py:479
  37.4 0.8 %route_outputs.1 = (bf16[1,32,1024]{2,1,0:T(8,128)(2,1)}, bf16[16,1024]{1,0:T(8,128)(2,1)}) custom-call(f32[2,24,128]{2,1,0:T(8,128)S(1)} %get-tuple-element.26.route_ref, bf16[48,1024]{1,0:T(8,128)(2,1)S(1)} %finish.1.refs_0_, bf16[48,1024]{1,0:T(8,128)(2,1)S(1)} %collective-permute-done.14.refs_1_), custom_call_target="tpu_custom_call" | custom-call | tf_op jit(solution)/shard_map/route_outputs/pallas_call | solution.py:406
  (18 shorter events, 0.1 us)
Async XLA Ops:
  0.6 11.4 %copy-start = (bf16[1,32,1024]{2,1,0:T(8,128)(2,1)S(1)}, bf16[1,32,1024]{2,1,0:T(8,128)(2,1)}, u32[]{:S(2)}) copy-start(bf16[1,32,1024]{2,1,0:T(8,128)(2,1)} %pre_q_hbm.1) | copy-start | bytes 196612
  1.6 11.2 %collective-permute-start.2 = (bf16[160,512]{1,0:T(8,128)(2,1)S(1)}, bf16[160,512]{1,0:T(8,128)(2,1)S(1)}, u32[]{:S(2)}, u32[]{:S(2)}) collective-permute-start(bf16[160,512]{1,0:T(8,128)(2,1)S(1)} %pad_maximum_fusion.refs_1_.refs_0_), channel_id=1, source_target_pairs={{0,8},{2,10},{4,12},{6,14},{8,0},{10,2},{12,4},{14,6},{16,24},{18,... | collective-permute-start | bytes 491528 | tf_op jit(solution)/shard_map/ppermute | solution.py:437
  4.7 12.7 %collective-permute-start = (bf16[160,512]{1,0:T(8,128)(2,1)S(1)}, bf16[160,512]{1,0:T(8,128)(2,1)S(1)}, u32[]{:S(2)}, u32[]{:S(2)}) collective-permute-start(bf16[160,512]{1,0:T(8,128)(2,1)S(1)} %pad_maximum_fusion.refs_1_.refs_0_), channel_id=1, source_target_pairs={{0,12},{2,14},{4,8},{6,10},{8,4},{10,6},{12,0},{14,2},{16,28},{18,... | collective-permute-start | bytes 491528 | tf_op jit(solution)/shard_map/ppermute | solution.py:437
  6.1 12.9 %collective-permute-start.4 = (bf16[160,512]{1,0:T(8,128)(2,1)S(1)}, bf16[160,512]{1,0:T(8,128)(2,1)S(1)}, u32[]{:S(2)}, u32[]{:S(2)}) collective-permute-start(bf16[160,512]{1,0:T(8,128)(2,1)S(1)} %pad_maximum_fusion.refs_1_.refs_0_), channel_id=1, source_target_pairs={{0,4},{2,6},{4,0},{6,2},{8,12},{10,14},{12,8},{14,10},{16,20},{18,... | collective-permute-start | bytes 491528 | tf_op jit(solution)/shard_map/ppermute | solution.py:437
  9.1 8.4 %collective-permute-start.1 = (bf16[80,512]{1,0:T(8,128)(2,1)S(1)}, bf16[80,512]{1,0:T(8,128)(2,1)S(1)}, u32[]{:S(2)}, u32[]{:S(2)}) collective-permute-start(bf16[80,512]{1,0:T(8,128)(2,1)S(1)} %get-tuple-element.27.refs_0_), channel_id=1, source_target_pairs={{0,16},{2,18},{4,20},{6,22},{8,24},{10,26},{12,28},{14,30},{16,0},... | collective-permute-start | bytes 245768 | tf_op jit(solution)/shard_map/ppermute | solution.py:437
  12.1 6.9 %collective-permute-start.5 = (bf16[32,1024]{1,0:T(8,128)(2,1)S(1)}, bf16[32,1024]{1,0:T(8,128)(2,1)S(1)}, u32[]{:S(2)}, u32[]{:S(2)}) collective-permute-start(bf16[32,1024]{1,0:T(8,128)(2,1)S(1)} %bitcast.7), channel_id=1, source_target_pairs={{0,16},{2,18},{4,20},{6,22},{8,24},{10,26},{12,28},{14,30},{16,0},... | collective-permute-start | bytes 196616 | tf_op jit(solution)/shard_map/ppermute | solution.py:437
  12.8 7.1 %collective-permute-start.6 = (bf16[160,512]{1,0:T(8,128)(2,1)S(1)}, bf16[160,512]{1,0:T(8,128)(2,1)S(1)}, u32[]{:S(2)}, u32[]{:S(2)}) collective-permute-start(bf16[160,512]{1,0:T(8,128)(2,1)S(1)} %pad_maximum_fusion.refs_1_.refs_0_), channel_id=1, source_target_pairs={{0,2},{2,0},{4,6},{6,4},{8,10},{10,8},{12,14},{14,12},{16,18},{18,... | collective-permute-start | bytes 491528 | tf_op jit(solution)/shard_map/ppermute | solution.py:437
  17.4 2.5 %collective-permute-start.9 = (bf16[160,512]{1,0:T(8,128)(2,1)S(1)}, bf16[160,512]{1,0:T(8,128)(2,1)S(1)}, u32[]{:S(2)}, u32[]{:S(2)}) collective-permute-start(bf16[160,512]{1,0:T(8,128)(2,1)S(1)} %collective-permute-done.refs_7_.refs_6_), channel_id=1, source_target_pairs={{0,2},{2,0},{4,6},{6,4},{8,10},{10,8},{12,14},{14,12},{16,18},{18,... | collective-permute-start | bytes 491528 | tf_op jit(solution)/shard_map/ppermute | solution.py:437
  19.0 1.4 %collective-permute-start.7 = (bf16[160,512]{1,0:T(8,128)(2,1)S(1)}, bf16[160,512]{1,0:T(8,128)(2,1)S(1)}, u32[]{:S(2)}, u32[]{:S(2)}) collective-permute-start(bf16[160,512]{1,0:T(8,128)(2,1)S(1)} %collective-permute-done.4.refs_3_.refs_2_), channel_id=1, source_target_pairs={{0,2},{2,0},{4,6},{6,4},{8,10},{10,8},{12,14},{14,12},{16,18},{18,... | collective-permute-start | bytes 491528 | tf_op jit(solution)/shard_map/ppermute | solution.py:437
  19.0 1.6 %collective-permute-start.8 = (bf16[160,512]{1,0:T(8,128)(2,1)S(1)}, bf16[160,512]{1,0:T(8,128)(2,1)S(1)}, u32[]{:S(2)}, u32[]{:S(2)}) collective-permute-start(bf16[160,512]{1,0:T(8,128)(2,1)S(1)} %collective-permute-done.2.refs_5_.refs_4_), channel_id=1, source_target_pairs={{0,2},{2,0},{4,6},{6,4},{8,10},{10,8},{12,14},{14,12},{16,18},{18,... | collective-permute-start | bytes 491528 | tf_op jit(solution)/shard_map/ppermute | solution.py:437
  19.8 1.9 %collective-permute-start.3 = (bf16[48,512]{1,0:T(8,128)(2,1)S(1)}, bf16[48,512]{1,0:T(8,128)(2,1)S(1)}, u32[]{:S(2)}, u32[]{:S(2)}) collective-permute-start(bf16[48,512]{1,0:T(8,128)(2,1)S(1)} %join_far.1.refs_0_), channel_id=1, source_target_pairs={{0,2},{2,0},{4,6},{6,4},{8,10},{10,8},{12,14},{14,12},{16,18},{18,... | collective-permute-start | bytes 147464 | tf_op jit(solution)/shard_map/ppermute | solution.py:437
  22.0 9.7 %collective-permute-start.11 = (bf16[80,512]{1,0:T(8,128)(2,1)S(1)}, bf16[80,512]{1,0:T(8,128)(2,1)S(1)}, u32[]{:S(2)}, u32[]{:S(2)}) collective-permute-start(bf16[80,512]{1,0:T(8,128)(2,1)S(1)} %join_core.1.refs_0_), channel_id=1, source_target_pairs={{0,4},{2,6},{4,0},{6,2},{8,12},{10,14},{12,8},{14,10},{16,20},{18,... | collective-permute-start | bytes 245768 | tf_op jit(solution)/shard_map/ppermute | solution.py:437
  23.7 8.0 %collective-permute-start.12 = (bf16[80,512]{1,0:T(8,128)(2,1)S(1)}, bf16[80,512]{1,0:T(8,128)(2,1)S(1)}, u32[]{:S(2)}, u32[]{:S(2)}) collective-permute-start(bf16[80,512]{1,0:T(8,128)(2,1)S(1)} %join_core.1.refs_0_), channel_id=1, source_target_pairs={{0,8},{2,10},{4,12},{6,14},{8,0},{10,2},{12,4},{14,6},{16,24},{18,... | collective-permute-start | bytes 245768 | tf_op jit(solution)/shard_map/ppermute | solution.py:437
  23.7 8.0 %collective-permute-start.13 = (bf16[80,512]{1,0:T(8,128)(2,1)S(1)}, bf16[80,512]{1,0:T(8,128)(2,1)S(1)}, u32[]{:S(2)}, u32[]{:S(2)}) collective-permute-start(bf16[80,512]{1,0:T(8,128)(2,1)S(1)} %join_core.1.refs_0_), channel_id=1, source_target_pairs={{0,12},{2,14},{4,8},{6,10},{8,4},{10,6},{12,0},{14,2},{16,28},{18,... | collective-permute-start | bytes 245768 | tf_op jit(solution)/shard_map/ppermute | solution.py:437
  25.6 5.9 %collective-permute-start.10 = (bf16[32,1152]{1,0:T(8,128)(2,1)S(1)}, bf16[32,1152]{1,0:T(8,128)(2,1)S(1)}, u32[]{:S(2)}, u32[]{:S(2)}) collective-permute-start(bf16[32,1152]{1,0:T(8,128)(2,1)S(1)} %prefill_partials.2), channel_id=1, source_target_pairs={{0,16},{2,18},{4,20},{6,22},{8,24},{10,26},{12,28},{14,30},{16,0},... | collective-permute-start | bytes 221192 | tf_op jit(solution)/shard_map/ppermute | solution.py:437
  32.1 1.8 %collective-permute-start.15 = (bf16[128,512]{1,0:T(8,128)(2,1)S(1)}, bf16[128,512]{1,0:T(8,128)(2,1)S(1)}, u32[]{:S(2)}, u32[]{:S(2)}) collective-permute-start(bf16[128,512]{1,0:T(8,128)(2,1)S(1)} %pad_maximum_fusion.1.near_ref), channel_id=1, source_target_pairs={{0,2},{2,0},{4,6},{6,4},{8,10},{10,8},{12,14},{14,12},{16,18},{18,... | collective-permute-start | bytes 393224 | tf_op jit(solution)/shard_map/ppermute | solution.py:437
  32.2 5.2 %collective-permute-start.14 = (bf16[48,1024]{1,0:T(8,128)(2,1)S(1)}, bf16[48,1024]{1,0:T(8,128)(2,1)S(1)}, u32[]{:S(2)}, u32[]{:S(2)}) collective-permute-start(bf16[48,1024]{1,0:T(8,128)(2,1)S(1)} %finish.1.refs_0_), channel_id=1, source_target_pairs={{0,1},{1,0},{2,3},{3,2},{4,5},{5,4},{6,7},{7,6},{8,9},{9,8},{10,11... | collective-permute-start | bytes 294920 | tf_op jit(solution)/shard_map/ppermute | solution.py:479

commit v16 on v15

--- a/solution.py
+++ b/solution.py
@@ -456,9 +456,9 @@
     )
     far = [swap(part, k) for k in others]
     offset = jnp.full((8, HEAD_SIZE), prefill_offsets[0], jnp.int32)
-    lanes[2], offset, _ = lax.optimization_barrier((lanes[2], offset, part))
-    lanes[3], far, _ = lax.optimization_barrier((lanes[3], far, lanes[2]))
-    lanes[1], packs, _ = lax.optimization_barrier((lanes[1], packs, lanes[2]))
+    lanes[1], offset, _ = lax.optimization_barrier((lanes[1], offset, part))
+    lanes[2] = after(lanes[2], lanes[1])
+    lanes[3], far, packs, _ = lax.optimization_barrier((lanes[3], far, packs, lanes[2]))
     part = join_step([part] + far, [], slots, "join_far")
     tables = [t for lane in lanes for t in (lane, swap(lane, 1))]
     beside = swap(part, 1)
@@ -471,8 +471,7 @@
     around = [part] + [swap(part, k) for k in range(2, KEY_SET, 2)]
     attended = join_parts([*kept] + arrived)
     attended = finish(attended, around, slots)
-    around[0], attended = lax.optimization_barrier((around[0], attended))
-    news = jnp.concatenate([after(a, attended)[PART_ROWS * slots :] for a in around], axis=0)
+    news = jnp.concatenate([a[PART_ROWS * slots :] for a in around], axis=0)
     prefill_cache_out = update_cache(offset, prefill_cache, news, swap(news, 1), tables, tokens, len(others))
 
     if req == 2:

time: 38.3 us -> 38.5 us (level)
    ppermute x15, waiting for transfers between devices: 10.3 us -> 10.8 us  [swap(): return lax.ppermute(array, BLK, [(i, i ^ distance) for i in range(blk)])]
    ppermute x1, waiting for transfers between devices: 1.79 us -> 1.31 us  [per_device(): held = [attended, lax.ppermute(attended, 'req', [(0, 1), (1, 0)])]]
  transfers between devices with their start and end apart: 16 -> 16, of which waited for: 6 -> 7; matrix products, arithmetic and copies ran while one was open for 0% -> 0% of each run, Pallas kernels for 19% -> 19%
where the time goes in v16:
time: 38.5 us; the launch traced here: 38.3 us
  starting transfers between devices  15.4 us (40%)
  waiting for transfers between devices  12.1 us (31%)
  Pallas kernels  8.46 us (22%)
  between operations  1.43 us (4%)
  other arithmetic  0.98 us (3%)
    ppermute x15, starting transfers between devices, swap(): return lax.ppermute(array, BLK, [(i, i ^ distance) for i in range(blk)])  13.7 us
    ppermute x15, waiting for transfers between devices, swap(): return lax.ppermute(array, BLK, [(i, i ^ distance) for i in range(blk)])  10.8 us
    pallas_call x1, Pallas kernels, decode_partials(): pl.pallas_call(decode_kernel, in_specs=[HBM] * len(inputs), out_specs=[HB...  2.8 us
    pallas_call x2, Pallas kernels, prefill_partials(): pl.pallas_call(functools.partial(prefill_kernel, sets, ctx), in_specs=[VM...  2.12 us
    pallas_call x1, Pallas kernels, update_cache(): pl.pallas_call(functools.partial(update_kernel, tokens, sets), in_specs=[...  1.71 us
    ppermute x1, starting transfers between devices, per_device(): held = [attended, lax.ppermute(attended, 'req', [(0, 1), (1, 0)])]  1.65 us
    ppermute x1, waiting for transfers between devices, per_device(): held = [attended, lax.ppermute(attended, 'req', [(0, 1), (1, 0)])]  1.31 us
    concatenate x1, other arithmetic, per_device(): table = jnp.concatenate([prefill_cache[0], new_prefill[0]], axis=0)  0.97 us
  transfers between devices with their start and end apart: 16, of which 7 were waited for; matrix products, arithmetic and copies ran while one was open for 0% of the time, Pallas kernels for 19%

profile of v16, /device:TPU:0, one launch (start us, length us, event | category | flops | bytes accessed | tf_op | source)
XLA Modules:
  0.0 38.3 jit_solution(2939426540419351828)
XLA Ops:
  0.6 1.0 %pad_maximum_fusion.refs_1_.refs_0_ = bf16[160,512]{1,0:T(8,128)(2,1)S(1)} fusion(bf16[32,512]{1,0:T(8,128)(2,1)} %bitcast.6, bf16[128,512]{1,0:T(8,128)(2,1)} %bitcast.5), kind=kLoop, calls=%fused_computation | loop fusion | flops 327680 | bytes 327680 | tf_op jit(solution)/shard_map/concatenate | solution.py:443
  1.6 3.0 %collective-permute-start = (bf16[160,512]{1,0:T(8,128)(2,1)S(1)}, bf16[160,512]{1,0:T(8,128)(2,1)S(1)}, u32[]{:S(2)}, u32[]{:S(2)}) collective-permute-start(bf16[160,512]{1,0:T(8,128)(2,1)S(1)} %pad_maximum_fusion.refs_1_.refs_0_), channel_id=1, source_target_pairs={{0,4},{2,6},{4,0},{6,2},{8,12},{10,14},{12,8},{14,10},{16,20},{18,... | collective-permute-start | bytes 491528 | tf_op jit(solution)/shard_map/ppermute | solution.py:437
  4.6 1.6 %collective-permute-start.4 = (bf16[160,512]{1,0:T(8,128)(2,1)S(1)}, bf16[160,512]{1,0:T(8,128)(2,1)S(1)}, u32[]{:S(2)}, u32[]{:S(2)}) collective-permute-start(bf16[160,512]{1,0:T(8,128)(2,1)S(1)} %pad_maximum_fusion.refs_1_.refs_0_), channel_id=1, source_target_pairs={{0,8},{2,10},{4,12},{6,14},{8,0},{10,2},{12,4},{14,6},{16,24},{18,... | collective-permute-start | bytes 491528 | tf_op jit(solution)/shard_map/ppermute | solution.py:437
  6.2 2.8 %decode_partials.1 = (bf16[16,128,512]{2,1,0:T(8,128)(2,1)}, bf16[80,512]{1,0:T(8,128)(2,1)S(1)}, bf16[32,1024]{1,0:T(8,128)(2,1)S(1)}, f32[2,24,128]{2,1,0:T(8,128)S(1)}) custom-call(s32[16]{0:T(128)} %len_hbm.1, s32[34]{0:T(128)} %deal_hbm.1, bf16[16,1024]{1,0:T(8,128)(2,1)} %q_hbm.1, bf16[16,512]{1,0:T(8,128)(2,1)} %new_hbm.1, ...), custom_call_target="tpu_custom_call" | custom-call | flops 8388608 | bytes 4194304 | tf_op jit(solution)/shard_map/decode_partials/pallas_call | solution.py:198
  9.0 3.1 %collective-permute-start.2 = (bf16[80,512]{1,0:T(8,128)(2,1)S(1)}, bf16[80,512]{1,0:T(8,128)(2,1)S(1)}, u32[]{:S(2)}, u32[]{:S(2)}) collective-permute-start(bf16[80,512]{1,0:T(8,128)(2,1)S(1)} %get-tuple-element.21.refs_0_), channel_id=1, source_target_pairs={{0,16},{2,18},{4,20},{6,22},{8,24},{10,26},{12,28},{14,30},{16,0},... | collective-permute-start | bytes 245768 | tf_op jit(solution)/shard_map/ppermute | solution.py:437
  12.1 0.1 collective-permute-start.3
  12.8 0.1 collective-permute-start.5
  12.9 6.4 %collective-permute-done.3.refs_0_ = bf16[32,1024]{1,0:T(8,128)(2,1)S(1)} collective-permute-done((bf16[32,1024]{1,0:T(8,128)(2,1)S(1)}, bf16[32,1024]{1,0:T(8,128)(2,1)S(1)}, u32[]{:S(2)}, u32[]{:S(2)}) %collective-permute-start.3) | collective-permute-done | bytes 65568 | tf_op jit(solution)/shard_map/ppermute | solution.py:437
  19.3 0.5 %collective-permute-start.7 = (bf16[160,512]{1,0:T(8,128)(2,1)S(1)}, bf16[160,512]{1,0:T(8,128)(2,1)S(1)}, u32[]{:S(2)}, u32[]{:S(2)}) collective-permute-start(bf16[160,512]{1,0:T(8,128)(2,1)S(1)} %collective-permute-done.4.refs_5_.refs_4_), channel_id=1, source_target_pairs={{0,2},{2,0},{4,6},{6,4},{8,10},{10,8},{12,14},{14,12},{16,18},{18,... | collective-permute-start | bytes 491528 | tf_op jit(solution)/shard_map/ppermute | solution.py:437
  19.8 0.1 collective-permute-start.6
  19.9 0.3 join_far.1.refs_0_
  20.2 0.5 %collective-permute-start.10 = (bf16[48,512]{1,0:T(8,128)(2,1)S(1)}, bf16[48,512]{1,0:T(8,128)(2,1)S(1)}, u32[]{:S(2)}, u32[]{:S(2)}) collective-permute-start(bf16[48,512]{1,0:T(8,128)(2,1)S(1)} %join_far.1.refs_0_), channel_id=1, source_target_pairs={{0,2},{2,0},{4,6},{6,4},{8,10},{10,8},{12,14},{14,12},{16,18},{18,... | collective-permute-start | bytes 147464 | tf_op jit(solution)/shard_map/ppermute | solution.py:437
  20.7 0.0 collective-permute-done.8.refs_8_.refs_7_
  20.7 0.2 collective-permute-done.7.refs_6_.refs_5_
  20.9 0.3 collective-permute-done.6.refs_4_.refs_3_
  21.2 1.1 %prefill_partials.2 = bf16[32,1152]{1,0:T(8,128)(2,1)S(1)} custom-call(s32[8,128]{1,0:T(8,128)S(1)} %broadcast_in_dim.3.off_ref, bf16[32,1024]{1,0:T(8,128)(2,1)S(1)} %collective-permute-done.3.refs_0_, bf16[160,512]{1,0:T(8,128)(2,1)S(1)} %pad_maximum_fusion.refs_1_.refs_0_, bf16[160,512]{1,0:T(8,128)(2,1)S(1)} %collective-permute-done.5.refs_2_.refs_1_, ...), custom_call_target="tpu_custom_call" | custom-call | flops 167772160 | bytes 4194304 | tf_op jit(solution)/shard_map/prefill_partials/pallas_call | solution.py:308
  22.3 0.3 join_core.1.refs_0_
  22.6 0.8 %collective-permute-start.13 = (bf16[80,512]{1,0:T(8,128)(2,1)S(1)}, bf16[80,512]{1,0:T(8,128)(2,1)S(1)}, u32[]{:S(2)}, u32[]{:S(2)}) collective-permute-start(bf16[80,512]{1,0:T(8,128)(2,1)S(1)} %join_core.1.refs_0_), channel_id=1, source_target_pairs={{0,12},{2,14},{4,8},{6,10},{8,4},{10,6},{12,0},{14,2},{16,28},{18,... | collective-permute-start | bytes 245768 | tf_op jit(solution)/shard_map/ppermute | solution.py:437
  23.3 2.2 %collective-permute-start.12 = (bf16[80,512]{1,0:T(8,128)(2,1)S(1)}, bf16[80,512]{1,0:T(8,128)(2,1)S(1)}, u32[]{:S(2)}, u32[]{:S(2)}) collective-permute-start(bf16[80,512]{1,0:T(8,128)(2,1)S(1)} %join_core.1.refs_0_), channel_id=1, source_target_pairs={{0,8},{2,10},{4,12},{6,14},{8,0},{10,2},{12,4},{14,6},{16,24},{18,... | collective-permute-start | bytes 245768 | tf_op jit(solution)/shard_map/ppermute | solution.py:437
  25.5 0.6 %collective-permute-start.11 = (bf16[80,512]{1,0:T(8,128)(2,1)S(1)}, bf16[80,512]{1,0:T(8,128)(2,1)S(1)}, u32[]{:S(2)}, u32[]{:S(2)}) collective-permute-start(bf16[80,512]{1,0:T(8,128)(2,1)S(1)} %join_core.1.refs_0_), channel_id=1, source_target_pairs={{0,4},{2,6},{4,0},{6,2},{8,12},{10,14},{12,8},{14,10},{16,20},{18,... | collective-permute-start | bytes 245768 | tf_op jit(solution)/shard_map/ppermute | solution.py:437
  26.1 1.2 %collective-permute-start.9 = (bf16[32,1152]{1,0:T(8,128)(2,1)S(1)}, bf16[32,1152]{1,0:T(8,128)(2,1)S(1)}, u32[]{:S(2)}, u32[]{:S(2)}) collective-permute-start(bf16[32,1152]{1,0:T(8,128)(2,1)S(1)} %prefill_partials.2), channel_id=1, source_target_pairs={{0,16},{2,18},{4,20},{6,22},{8,24},{10,26},{12,28},{14,30},{16,0},... | collective-permute-start | bytes 221192 | tf_op jit(solution)/shard_map/ppermute | solution.py:437
  27.4 1.5 %collective-permute-done.13.refs_3_ = bf16[80,512]{1,0:T(8,128)(2,1)S(1)} collective-permute-done((bf16[80,512]{1,0:T(8,128)(2,1)S(1)}, bf16[80,512]{1,0:T(8,128)(2,1)S(1)}, u32[]{:S(2)}, u32[]{:S(2)}) %collective-permute-start.13) | collective-permute-done | bytes 81952 | tf_op jit(solution)/shard_map/ppermute | solution.py:437
  28.8 1.8 %collective-permute-done.12.refs_2_ = bf16[80,512]{1,0:T(8,128)(2,1)S(1)} collective-permute-done((bf16[80,512]{1,0:T(8,128)(2,1)S(1)}, bf16[80,512]{1,0:T(8,128)(2,1)S(1)}, u32[]{:S(2)}, u32[]{:S(2)}) %collective-permute-start.12) | collective-permute-done | bytes 81952 | tf_op jit(solution)/shard_map/ppermute | solution.py:437
  30.7 0.1 collective-permute-start.15
  30.7 1.1 %prefill_partials.3.refs_0_ = bf16[32,1152]{1,0:T(8,128)(2,1)S(1)} custom-call(s32[8,128]{1,0:T(8,128)S(1)} %broadcast_in_dim.3.off_ref, bf16[32,1024]{1,0:T(8,128)(2,1)S(1)} %get-tuple-element.28.refs_0_, bf16[160,512]{1,0:T(8,128)(2,1)S(1)} %pad_maximum_fusion.refs_1_.refs_0_, bf16[160,512]{1,0:T(8,128)(2,1)S(1)} %collective-permute-done.5.refs_2_.refs_1_, ...), custom_call_target="tpu_custom_call" | custom-call | flops 167772160 | bytes 4194304 | tf_op jit(solution)/shard_map/prefill_partials/pallas_call | solution.py:308
  31.8 0.6 %collective-permute-done.9.refs_1_ = bf16[32,1152]{1,0:T(8,128)(2,1)S(1)} collective-permute-done((bf16[32,1152]{1,0:T(8,128)(2,1)S(1)}, bf16[32,1152]{1,0:T(8,128)(2,1)S(1)}, u32[]{:S(2)}, u32[]{:S(2)}) %collective-permute-start.9) | collective-permute-done | bytes 73760 | tf_op jit(solution)/shard_map/ppermute | solution.py:437
  32.4 0.2 join_parts.1.prefill_ref
  32.6 0.3 finish.1.refs_0_
  32.9 1.6 %collective-permute-start.14 = (bf16[48,1024]{1,0:T(8,128)(2,1)S(1)}, bf16[48,1024]{1,0:T(8,128)(2,1)S(1)}, u32[]{:S(2)}, u32[]{:S(2)}) collective-permute-start(bf16[48,1024]{1,0:T(8,128)(2,1)S(1)} %finish.1.refs_0_), channel_id=1, source_target_pairs={{0,1},{1,0},{2,3},{3,2},{4,5},{5,4},{6,7},{7,6},{8,9},{9,8},{10,11... | collective-permute-start | bytes 294920 | tf_op jit(solution)/shard_map/ppermute | solution.py:478
  34.5 1.7 %update_cache.1 = bf16[1,128,512]{2,1,0:T(8,128)(2,1)} custom-call(s32[8,128]{1,0:T(8,128)S(1)} %broadcast_in_dim.3.off_ref, bf16[1,128,512]{2,1,0:T(8,128)(2,1)} %cache_hbm.3, bf16[128,512]{1,0:T(8,128)(2,1)S(1)} %pad_maximum_fusion.1.near_ref, bf16[128,512]{1,0:T(8,128)(2,1)S(1)} %collective-permute-done.15.beside_ref, ...), custom_call_target="tpu_custom_call" | custom-call | tf_op jit(solution)/shard_map/update_cache/pallas_call | solution.py:378
  36.3 1.3 %collective-permute-done.14.refs_1_ = bf16[48,1024]{1,0:T(8,128)(2,1)S(1)} collective-permute-done((bf16[48,1024]{1,0:T(8,128)(2,1)S(1)}, bf16[48,1024]{1,0:T(8,128)(2,1)S(1)}, u32[]{:S(2)}, u32[]{:S(2)}) %collective-permute-start.14) | collective-permute-done | bytes 98336 | tf_op jit(solution)/shard_map/ppermute | solution.py:478
  37.6 0.8 %route_outputs.1 = (bf16[1,32,1024]{2,1,0:T(8,128)(2,1)}, bf16[16,1024]{1,0:T(8,128)(2,1)}) custom-call(f32[2,24,128]{2,1,0:T(8,128)S(1)} %get-tuple-element.20.route_ref, bf16[48,1024]{1,0:T(8,128)(2,1)S(1)} %finish.1.refs_0_, bf16[48,1024]{1,0:T(8,128)(2,1)S(1)} %collective-permute-done.14.refs_1_), custom_call_target="tpu_custom_call" | custom-call | tf_op jit(solution)/shard_map/route_outputs/pallas_call | solution.py:406
  (18 shorter events, 0.1 us)
Async XLA Ops:
  0.6 11.4 %copy-start = (bf16[1,32,1024]{2,1,0:T(8,128)(2,1)S(1)}, bf16[1,32,1024]{2,1,0:T(8,128)(2,1)}, u32[]{:S(2)}) copy-start(bf16[1,32,1024]{2,1,0:T(8,128)(2,1)} %pre_q_hbm.1) | copy-start | bytes 196612
  1.6 11.2 %collective-permute-start = (bf16[160,512]{1,0:T(8,128)(2,1)S(1)}, bf16[160,512]{1,0:T(8,128)(2,1)S(1)}, u32[]{:S(2)}, u32[]{:S(2)}) collective-permute-start(bf16[160,512]{1,0:T(8,128)(2,1)S(1)} %pad_maximum_fusion.refs_1_.refs_0_), channel_id=1, source_target_pairs={{0,4},{2,6},{4,0},{6,2},{8,12},{10,14},{12,8},{14,10},{16,20},{18,... | collective-permute-start | bytes 491528 | tf_op jit(solution)/shard_map/ppermute | solution.py:437
  4.6 8.3 %collective-permute-start.4 = (bf16[160,512]{1,0:T(8,128)(2,1)S(1)}, bf16[160,512]{1,0:T(8,128)(2,1)S(1)}, u32[]{:S(2)}, u32[]{:S(2)}) collective-permute-start(bf16[160,512]{1,0:T(8,128)(2,1)S(1)} %pad_maximum_fusion.refs_1_.refs_0_), channel_id=1, source_target_pairs={{0,8},{2,10},{4,12},{6,14},{8,0},{10,2},{12,4},{14,6},{16,24},{18,... | collective-permute-start | bytes 491528 | tf_op jit(solution)/shard_map/ppermute | solution.py:437
  6.2 13.1 %collective-permute-start.1 = (bf16[160,512]{1,0:T(8,128)(2,1)S(1)}, bf16[160,512]{1,0:T(8,128)(2,1)S(1)}, u32[]{:S(2)}, u32[]{:S(2)}) collective-permute-start(bf16[160,512]{1,0:T(8,128)(2,1)S(1)} %pad_maximum_fusion.refs_1_.refs_0_), channel_id=1, source_target_pairs={{0,12},{2,14},{4,8},{6,10},{8,4},{10,6},{12,0},{14,2},{16,28},{18,... | collective-permute-start | bytes 491528 | tf_op jit(solution)/shard_map/ppermute | solution.py:437
  9.0 10.3 %collective-permute-start.2 = (bf16[80,512]{1,0:T(8,128)(2,1)S(1)}, bf16[80,512]{1,0:T(8,128)(2,1)S(1)}, u32[]{:S(2)}, u32[]{:S(2)}) collective-permute-start(bf16[80,512]{1,0:T(8,128)(2,1)S(1)} %get-tuple-element.21.refs_0_), channel_id=1, source_target_pairs={{0,16},{2,18},{4,20},{6,22},{8,24},{10,26},{12,28},{14,30},{16,0},... | collective-permute-start | bytes 245768 | tf_op jit(solution)/shard_map/ppermute | solution.py:437
  12.1 7.2 %collective-permute-start.3 = (bf16[32,1024]{1,0:T(8,128)(2,1)S(1)}, bf16[32,1024]{1,0:T(8,128)(2,1)S(1)}, u32[]{:S(2)}, u32[]{:S(2)}) collective-permute-start(bf16[32,1024]{1,0:T(8,128)(2,1)S(1)} %bitcast.7), channel_id=1, source_target_pairs={{0,16},{2,18},{4,20},{6,22},{8,24},{10,26},{12,28},{14,30},{16,0},... | collective-permute-start | bytes 196616 | tf_op jit(solution)/shard_map/ppermute | solution.py:437
  12.8 7.9 %collective-permute-start.5 = (bf16[160,512]{1,0:T(8,128)(2,1)S(1)}, bf16[160,512]{1,0:T(8,128)(2,1)S(1)}, u32[]{:S(2)}, u32[]{:S(2)}) collective-permute-start(bf16[160,512]{1,0:T(8,128)(2,1)S(1)} %pad_maximum_fusion.refs_1_.refs_0_), channel_id=1, source_target_pairs={{0,2},{2,0},{4,6},{6,4},{8,10},{10,8},{12,14},{14,12},{16,18},{18,... | collective-permute-start | bytes 491528 | tf_op jit(solution)/shard_map/ppermute | solution.py:437
  19.3 1.4 %collective-permute-start.8 = (bf16[160,512]{1,0:T(8,128)(2,1)S(1)}, bf16[160,512]{1,0:T(8,128)(2,1)S(1)}, u32[]{:S(2)}, u32[]{:S(2)}) collective-permute-start(bf16[160,512]{1,0:T(8,128)(2,1)S(1)} %collective-permute-done.1.refs_7_.refs_6_), channel_id=1, source_target_pairs={{0,2},{2,0},{4,6},{6,4},{8,10},{10,8},{12,14},{14,12},{16,18},{18,... | collective-permute-start | bytes 491528 | tf_op jit(solution)/shard_map/ppermute | solution.py:437
  19.3 1.6 %collective-permute-start.7 = (bf16[160,512]{1,0:T(8,128)(2,1)S(1)}, bf16[160,512]{1,0:T(8,128)(2,1)S(1)}, u32[]{:S(2)}, u32[]{:S(2)}) collective-permute-start(bf16[160,512]{1,0:T(8,128)(2,1)S(1)} %collective-permute-done.4.refs_5_.refs_4_), channel_id=1, source_target_pairs={{0,2},{2,0},{4,6},{6,4},{8,10},{10,8},{12,14},{14,12},{16,18},{18,... | collective-permute-start | bytes 491528 | tf_op jit(solution)/shard_map/ppermute | solution.py:437
  19.8 1.4 %collective-permute-start.6 = (bf16[160,512]{1,0:T(8,128)(2,1)S(1)}, bf16[160,512]{1,0:T(8,128)(2,1)S(1)}, u32[]{:S(2)}, u32[]{:S(2)}) collective-permute-start(bf16[160,512]{1,0:T(8,128)(2,1)S(1)} %collective-permute-done.refs_3_.refs_2_), channel_id=1, source_target_pairs={{0,2},{2,0},{4,6},{6,4},{8,10},{10,8},{12,14},{14,12},{16,18},{18,... | collective-permute-start | bytes 491528 | tf_op jit(solution)/shard_map/ppermute | solution.py:437
  20.2 2.1 %collective-permute-start.10 = (bf16[48,512]{1,0:T(8,128)(2,1)S(1)}, bf16[48,512]{1,0:T(8,128)(2,1)S(1)}, u32[]{:S(2)}, u32[]{:S(2)}) collective-permute-start(bf16[48,512]{1,0:T(8,128)(2,1)S(1)} %join_far.1.refs_0_), channel_id=1, source_target_pairs={{0,2},{2,0},{4,6},{6,4},{8,10},{10,8},{12,14},{14,12},{16,18},{18,... | collective-permute-start | bytes 147464 | tf_op jit(solution)/shard_map/ppermute | solution.py:437
  22.6 6.2 %collective-permute-start.13 = (bf16[80,512]{1,0:T(8,128)(2,1)S(1)}, bf16[80,512]{1,0:T(8,128)(2,1)S(1)}, u32[]{:S(2)}, u32[]{:S(2)}) collective-permute-start(bf16[80,512]{1,0:T(8,128)(2,1)S(1)} %join_core.1.refs_0_), channel_id=1, source_target_pairs={{0,12},{2,14},{4,8},{6,10},{8,4},{10,6},{12,0},{14,2},{16,28},{18,... | collective-permute-start | bytes 245768 | tf_op jit(solution)/shard_map/ppermute | solution.py:437
  23.3 7.3 %collective-permute-start.12 = (bf16[80,512]{1,0:T(8,128)(2,1)S(1)}, bf16[80,512]{1,0:T(8,128)(2,1)S(1)}, u32[]{:S(2)}, u32[]{:S(2)}) collective-permute-start(bf16[80,512]{1,0:T(8,128)(2,1)S(1)} %join_core.1.refs_0_), channel_id=1, source_target_pairs={{0,8},{2,10},{4,12},{6,14},{8,0},{10,2},{12,4},{14,6},{16,24},{18,... | collective-permute-start | bytes 245768 | tf_op jit(solution)/shard_map/ppermute | solution.py:437
  25.5 5.1 %collective-permute-start.11 = (bf16[80,512]{1,0:T(8,128)(2,1)S(1)}, bf16[80,512]{1,0:T(8,128)(2,1)S(1)}, u32[]{:S(2)}, u32[]{:S(2)}) collective-permute-start(bf16[80,512]{1,0:T(8,128)(2,1)S(1)} %join_core.1.refs_0_), channel_id=1, source_target_pairs={{0,4},{2,6},{4,0},{6,2},{8,12},{10,14},{12,8},{14,10},{16,20},{18,... | collective-permute-start | bytes 245768 | tf_op jit(solution)/shard_map/ppermute | solution.py:437
  26.1 6.3 %collective-permute-start.9 = (bf16[32,1152]{1,0:T(8,128)(2,1)S(1)}, bf16[32,1152]{1,0:T(8,128)(2,1)S(1)}, u32[]{:S(2)}, u32[]{:S(2)}) collective-permute-start(bf16[32,1152]{1,0:T(8,128)(2,1)S(1)} %prefill_partials.2), channel_id=1, source_target_pairs={{0,16},{2,18},{4,20},{6,22},{8,24},{10,26},{12,28},{14,30},{16,0},... | collective-permute-start | bytes 221192 | tf_op jit(solution)/shard_map/ppermute | solution.py:437
  30.7 3.9 %collective-permute-start.15 = (bf16[128,512]{1,0:T(8,128)(2,1)S(1)}, bf16[128,512]{1,0:T(8,128)(2,1)S(1)}, u32[]{:S(2)}, u32[]{:S(2)}) collective-permute-start(bf16[128,512]{1,0:T(8,128)(2,1)S(1)} %pad_maximum_fusion.1.near_ref), channel_id=1, source_target_pairs={{0,2},{2,0},{4,6},{6,4},{8,10},{10,8},{12,14},{14,12},{16,18},{18,... | collective-permute-start | bytes 393224 | tf_op jit(solution)/shard_map/ppermute | solution.py:437
  32.9 4.7 %collective-permute-start.14 = (bf16[48,1024]{1,0:T(8,128)(2,1)S(1)}, bf16[48,1024]{1,0:T(8,128)(2,1)S(1)}, u32[]{:S(2)}, u32[]{:S(2)}) collective-permute-start(bf16[48,1024]{1,0:T(8,128)(2,1)S(1)} %finish.1.refs_0_), channel_id=1, source_target_pairs={{0,1},{1,0},{2,3},{3,2},{4,5},{5,4},{6,7},{7,6},{8,9},{9,8},{10,11... | collective-permute-start | bytes 294920 | tf_op jit(solution)/shard_map/ppermute | solution.py:478

commit v17 on v15

--- a/solution.py
+++ b/solution.py
@@ -318,37 +318,22 @@
     )(offset, *packs, *tables)
 
 
-def join_kernel(*refs):
-    refs[-1][...] = join([ref[...] for ref in refs[:-1]])[0]
-
-
-def join_parts(parts):
-    return pl.pallas_call(
-        join_kernel,
-        in_specs=[VMEM] * len(parts),
+def join_kernel(count, slots, *refs):
+    parts, decodes, out_ref = refs[:count], refs[count:-1], refs[-1]
+    tokens = parts[0].shape[0]
+    out_ref[pl.ds(0, tokens), :] = join([ref[...] for ref in parts])[0]
+    out_ref[pl.ds(tokens, slots), :] = join([decode_part(ref, slots) for ref in decodes])[0]
+
+
+def join_parts(parts, decodes, slots):
+    return pl.pallas_call(
+        functools.partial(join_kernel, len(parts), slots),
+        in_specs=[VMEM] * (len(parts) + len(decodes)),
         out_specs=VMEM,
-        out_shape=pltpu.VMEM((parts[0].shape[0], QW), BF16),
+        out_shape=pltpu.VMEM((parts[0].shape[0] + slots, QW), BF16),
         compiler_params=pltpu.CompilerParams(vmem_limit_bytes=16 << 20),
         name="join_parts",
-    )(*parts)
-
-
-def finish_kernel(slots, prefill_ref, *refs):
-    decodes, out_ref = refs[:-1], refs[-1]
-    tokens = prefill_ref.shape[0]
-    out_ref[pl.ds(0, tokens), :] = prefill_ref[...]
-    out_ref[pl.ds(tokens, slots), :] = join([decode_part(ref, slots) for ref in decodes])[0]
-
-
-def finish(prefill, decodes, slots):
-    return pl.pallas_call(
-        functools.partial(finish_kernel, slots),
-        in_specs=[VMEM] * (1 + len(decodes)),
-        out_specs=VMEM,
-        out_shape=pltpu.VMEM((prefill.shape[0] + slots, QW), BF16),
-        compiler_params=pltpu.CompilerParams(vmem_limit_bytes=16 << 20),
-        name="finish",
-    )(prefill, *decodes)
+    )(*parts, *decodes)
 
 
 def update_kernel(tokens, sets, off_ref, cache_hbm, near_ref, beside_ref, *refs):
@@ -469,10 +454,8 @@
     kept = prefill_partials(offset, [queries], tables, ctx, [0])
     part = join_step([part, after(beside, sent[0])], far, slots, "join_core")
     around = [part] + [swap(part, k) for k in range(2, KEY_SET, 2)]
-    attended = join_parts([*kept] + arrived)
-    attended = finish(attended, around, slots)
-    around[0], attended = lax.optimization_barrier((around[0], attended))
-    news = jnp.concatenate([after(a, attended)[PART_ROWS * slots :] for a in around], axis=0)
+    attended = join_parts([*kept] + arrived, around, slots)
+    news = jnp.concatenate([a[PART_ROWS * slots :] for a in around], axis=0)
     prefill_cache_out = update_cache(offset, prefill_cache, news, swap(news, 1), tables, tokens, len(others))
 
     if req == 2:

time: 38.3 us -> 38.6 us (level)
  starting transfers between devices: 15.1 us -> 15.6 us
    ppermute x15, starting transfers between devices: 13.4 us -> 13.9 us  [swap(): return lax.ppermute(array, BLK, [(i, i ^ distance) for i in range(blk)])]
  transfers between devices with their start and end apart: 16 -> 16, of which waited for: 6 -> 7; matrix products, arithmetic and copies ran while one was open for 0% -> 0% of each run, Pallas kernels for 19% -> 19%
where the time goes in v17:
time: 38.6 us; the launch traced here: 38.5 us
  starting transfers between devices  15.6 us (40%)
  waiting for transfers between devices  12.1 us (31%)
  Pallas kernels  8.32 us (22%)
  between operations  1.41 us (4%)
  other arithmetic  0.98 us (3%)
    ppermute x15, starting transfers between devices, swap(): return lax.ppermute(array, BLK, [(i, i ^ distance) for i in range(blk)])  13.9 us
    ppermute x15, waiting for transfers between devices, swap(): return lax.ppermute(array, BLK, [(i, i ^ distance) for i in range(blk)])  10.4 us
    pallas_call x1, Pallas kernels, decode_partials(): pl.pallas_call(decode_kernel, in_specs=[HBM] * len(inputs), out_specs=[HB...  2.84 us
    pallas_call x2, Pallas kernels, prefill_partials(): pl.pallas_call(functools.partial(prefill_kernel, sets, ctx), in_specs=[VM...  2.13 us
    ppermute x1, waiting for transfers between devices, per_device(): held = [attended, lax.ppermute(attended, 'req', [(0, 1), (1, 0)])]  1.73 us
    pallas_call x1, Pallas kernels, update_cache(): pl.pallas_call(functools.partial(update_kernel, tokens, sets), in_specs=[...  1.71 us
    ppermute x1, starting transfers between devices, per_device(): held = [attended, lax.ppermute(attended, 'req', [(0, 1), (1, 0)])]  1.67 us
    concatenate x1, other arithmetic, per_device(): table = jnp.concatenate([prefill_cache[0], new_prefill[0]], axis=0)  0.97 us
  transfers between devices with their start and end apart: 16, of which 7 were waited for; matrix products, arithmetic and copies ran while one was open for 0% of the time, Pallas kernels for 19%

profile of v17, /device:TPU:0, one launch (start us, length us, event | category | flops | bytes accessed | tf_op | source)
XLA Modules:
  0.0 38.5 jit_solution(695245623973490820)
XLA Ops:
  0.6 0.0 copy-start
  0.6 1.0 %pad_maximum_fusion.refs_1_.refs_0_ = bf16[160,512]{1,0:T(8,128)(2,1)S(1)} fusion(bf16[32,512]{1,0:T(8,128)(2,1)} %bitcast.6, bf16[128,512]{1,0:T(8,128)(2,1)} %bitcast.5), kind=kLoop, calls=%fused_computation | loop fusion | flops 327680 | bytes 327680 | tf_op jit(solution)/shard_map/concatenate | solution.py:428
  1.6 3.1 %collective-permute-start = (bf16[160,512]{1,0:T(8,128)(2,1)S(1)}, bf16[160,512]{1,0:T(8,128)(2,1)S(1)}, u32[]{:S(2)}, u32[]{:S(2)}) collective-permute-start(bf16[160,512]{1,0:T(8,128)(2,1)S(1)} %pad_maximum_fusion.refs_1_.refs_0_), channel_id=1, source_target_pairs={{0,8},{2,10},{4,12},{6,14},{8,0},{10,2},{12,4},{14,6},{16,24},{18,... | collective-permute-start | bytes 491528 | tf_op jit(solution)/shard_map/ppermute | solution.py:422
  4.7 1.5 %collective-permute-start.1 = (bf16[160,512]{1,0:T(8,128)(2,1)S(1)}, bf16[160,512]{1,0:T(8,128)(2,1)S(1)}, u32[]{:S(2)}, u32[]{:S(2)}) collective-permute-start(bf16[160,512]{1,0:T(8,128)(2,1)S(1)} %pad_maximum_fusion.refs_1_.refs_0_), channel_id=1, source_target_pairs={{0,4},{2,6},{4,0},{6,2},{8,12},{10,14},{12,8},{14,10},{16,20},{18,... | collective-permute-start | bytes 491528 | tf_op jit(solution)/shard_map/ppermute | solution.py:422
  6.2 0.0 collective-permute-start.6
  6.2 2.8 %decode_partials.1 = (bf16[16,128,512]{2,1,0:T(8,128)(2,1)}, bf16[80,512]{1,0:T(8,128)(2,1)S(1)}, bf16[32,1024]{1,0:T(8,128)(2,1)S(1)}, f32[2,24,128]{2,1,0:T(8,128)S(1)}) custom-call(s32[16]{0:T(128)} %len_hbm.1, s32[34]{0:T(128)} %deal_hbm.1, bf16[16,1024]{1,0:T(8,128)(2,1)} %q_hbm.1, bf16[16,512]{1,0:T(8,128)(2,1)} %new_hbm.1, ...), custom_call_target="tpu_custom_call" | custom-call | flops 8388608 | bytes 4194304 | tf_op jit(solution)/shard_map/decode_partials/pallas_call | solution.py:198
  9.1 3.0 %collective-permute-start.7 = (bf16[80,512]{1,0:T(8,128)(2,1)S(1)}, bf16[80,512]{1,0:T(8,128)(2,1)S(1)}, u32[]{:S(2)}, u32[]{:S(2)}) collective-permute-start(bf16[80,512]{1,0:T(8,128)(2,1)S(1)} %get-tuple-element.21.refs_0_), channel_id=1, source_target_pairs={{0,16},{2,18},{4,20},{6,22},{8,24},{10,26},{12,28},{14,30},{16,0},... | collective-permute-start | bytes 245768 | tf_op jit(solution)/shard_map/ppermute | solution.py:422
  12.1 0.1 collective-permute-start.2
  12.8 0.1 collective-permute-start.3
  12.9 6.2 %collective-permute-done.2.refs_0_ = bf16[32,1024]{1,0:T(8,128)(2,1)S(1)} collective-permute-done((bf16[32,1024]{1,0:T(8,128)(2,1)S(1)}, bf16[32,1024]{1,0:T(8,128)(2,1)S(1)}, u32[]{:S(2)}, u32[]{:S(2)}) %collective-permute-start.2) | collective-permute-done | bytes 65568 | tf_op jit(solution)/shard_map/ppermute | solution.py:422
  19.1 0.5 %collective-permute-start.4 = (bf16[160,512]{1,0:T(8,128)(2,1)S(1)}, bf16[160,512]{1,0:T(8,128)(2,1)S(1)}, u32[]{:S(2)}, u32[]{:S(2)}) collective-permute-start(bf16[160,512]{1,0:T(8,128)(2,1)S(1)} %collective-permute-done.1.refs_3_.refs_2_), channel_id=1, source_target_pairs={{0,2},{2,0},{4,6},{6,4},{8,10},{10,8},{12,14},{14,12},{16,18},{18,... | collective-permute-start | bytes 491528 | tf_op jit(solution)/shard_map/ppermute | solution.py:422
  19.6 0.1 collective-permute-start.8
  19.7 0.3 join_far.1.refs_0_
  20.0 0.5 %collective-permute-start.10 = (bf16[48,512]{1,0:T(8,128)(2,1)S(1)}, bf16[48,512]{1,0:T(8,128)(2,1)S(1)}, u32[]{:S(2)}, u32[]{:S(2)}) collective-permute-start(bf16[48,512]{1,0:T(8,128)(2,1)S(1)} %join_far.1.refs_0_), channel_id=1, source_target_pairs={{0,2},{2,0},{4,6},{6,4},{8,10},{10,8},{12,14},{14,12},{16,18},{18,... | collective-permute-start | bytes 147464 | tf_op jit(solution)/shard_map/ppermute | solution.py:422
  20.5 0.2 collective-permute-done.4.refs_4_.refs_3_
  20.7 0.3 collective-permute-done.8.refs_8_.refs_7_
  21.0 1.1 %prefill_partials.2 = bf16[32,1152]{1,0:T(8,128)(2,1)S(1)} custom-call(s32[8,128]{1,0:T(8,128)S(1)} %broadcast_in_dim.3.off_ref, bf16[32,1024]{1,0:T(8,128)(2,1)S(1)} %collective-permute-done.2.refs_0_, bf16[160,512]{1,0:T(8,128)(2,1)S(1)} %pad_maximum_fusion.refs_1_.refs_0_, bf16[160,512]{1,0:T(8,128)(2,1)S(1)} %collective-permute-done.3.refs_2_.refs_1_, ...), custom_call_target="tpu_custom_call" | custom-call | flops 167772160 | bytes 4194304 | tf_op jit(solution)/shard_map/prefill_partials/pallas_call | solution.py:308
  22.1 0.3 join_core.1.refs_2_
  22.4 1.0 %collective-permute-start.13 = (bf16[80,512]{1,0:T(8,128)(2,1)S(1)}, bf16[80,512]{1,0:T(8,128)(2,1)S(1)}, u32[]{:S(2)}, u32[]{:S(2)}) collective-permute-start(bf16[80,512]{1,0:T(8,128)(2,1)S(1)} %join_core.1.refs_2_), channel_id=1, source_target_pairs={{0,12},{2,14},{4,8},{6,10},{8,4},{10,6},{12,0},{14,2},{16,28},{18,... | collective-permute-start | bytes 245768 | tf_op jit(solution)/shard_map/ppermute | solution.py:422
  23.3 2.2 %collective-permute-start.12 = (bf16[80,512]{1,0:T(8,128)(2,1)S(1)}, bf16[80,512]{1,0:T(8,128)(2,1)S(1)}, u32[]{:S(2)}, u32[]{:S(2)}) collective-permute-start(bf16[80,512]{1,0:T(8,128)(2,1)S(1)} %join_core.1.refs_2_), channel_id=1, source_target_pairs={{0,8},{2,10},{4,12},{6,14},{8,0},{10,2},{12,4},{14,6},{16,24},{18,... | collective-permute-start | bytes 245768 | tf_op jit(solution)/shard_map/ppermute | solution.py:422
  25.6 0.3 collective-permute-start.11
  25.9 1.4 %collective-permute-start.9 = (bf16[32,1152]{1,0:T(8,128)(2,1)S(1)}, bf16[32,1152]{1,0:T(8,128)(2,1)S(1)}, u32[]{:S(2)}, u32[]{:S(2)}) collective-permute-start(bf16[32,1152]{1,0:T(8,128)(2,1)S(1)} %prefill_partials.2), channel_id=1, source_target_pairs={{0,16},{2,18},{4,20},{6,22},{8,24},{10,26},{12,28},{14,30},{16,0},... | collective-permute-start | bytes 221192 | tf_op jit(solution)/shard_map/ppermute | solution.py:422
  27.4 1.2 %collective-permute-done.13.refs_5_ = bf16[80,512]{1,0:T(8,128)(2,1)S(1)} collective-permute-done((bf16[80,512]{1,0:T(8,128)(2,1)S(1)}, bf16[80,512]{1,0:T(8,128)(2,1)S(1)}, u32[]{:S(2)}, u32[]{:S(2)}) %collective-permute-start.13) | collective-permute-done | bytes 81952 | tf_op jit(solution)/shard_map/ppermute | solution.py:422
  28.6 2.3 %collective-permute-done.12.refs_4_ = bf16[80,512]{1,0:T(8,128)(2,1)S(1)} collective-permute-done((bf16[80,512]{1,0:T(8,128)(2,1)S(1)}, bf16[80,512]{1,0:T(8,128)(2,1)S(1)}, u32[]{:S(2)}, u32[]{:S(2)}) %collective-permute-start.12) | collective-permute-done | bytes 81952 | tf_op jit(solution)/shard_map/ppermute | solution.py:422
  31.0 0.1 collective-permute-start.15
  31.0 1.1 %prefill_partials.3.refs_0_ = bf16[32,1152]{1,0:T(8,128)(2,1)S(1)} custom-call(s32[8,128]{1,0:T(8,128)S(1)} %broadcast_in_dim.3.off_ref, bf16[32,1024]{1,0:T(8,128)(2,1)S(1)} %get-tuple-element.28.refs_0_, bf16[160,512]{1,0:T(8,128)(2,1)S(1)} %pad_maximum_fusion.refs_1_.refs_0_, bf16[160,512]{1,0:T(8,128)(2,1)S(1)} %collective-permute-done.3.refs_2_.refs_1_, ...), custom_call_target="tpu_custom_call" | custom-call | flops 167772160 | bytes 4194304 | tf_op jit(solution)/shard_map/prefill_partials/pallas_call | solution.py:308
  32.1 0.1 collective-permute-done.9.refs_1_
  32.3 0.3 join_parts.1.refs_0_
  32.6 1.7 %collective-permute-start.14 = (bf16[48,1024]{1,0:T(8,128)(2,1)S(1)}, bf16[48,1024]{1,0:T(8,128)(2,1)S(1)}, u32[]{:S(2)}, u32[]{:S(2)}) collective-permute-start(bf16[48,1024]{1,0:T(8,128)(2,1)S(1)} %join_parts.1.refs_0_), channel_id=1, source_target_pairs={{0,1},{1,0},{2,3},{3,2},{4,5},{5,4},{6,7},{7,6},{8,9},{9,8},{10,11... | collective-permute-start | bytes 294920 | tf_op jit(solution)/shard_map/ppermute | solution.py:462
  34.2 1.7 %update_cache.1 = bf16[1,128,512]{2,1,0:T(8,128)(2,1)} custom-call(s32[8,128]{1,0:T(8,128)S(1)} %broadcast_in_dim.3.off_ref, bf16[1,128,512]{2,1,0:T(8,128)(2,1)} %cache_hbm.3, bf16[128,512]{1,0:T(8,128)(2,1)S(1)} %pad_maximum_fusion.1.near_ref, bf16[128,512]{1,0:T(8,128)(2,1)S(1)} %collective-permute-done.15.beside_ref, ...), custom_call_target="tpu_custom_call" | custom-call | tf_op jit(solution)/shard_map/update_cache/pallas_call | solution.py:363
  36.0 1.7 %collective-permute-done.14.refs_1_ = bf16[48,1024]{1,0:T(8,128)(2,1)S(1)} collective-permute-done((bf16[48,1024]{1,0:T(8,128)(2,1)S(1)}, bf16[48,1024]{1,0:T(8,128)(2,1)S(1)}, u32[]{:S(2)}, u32[]{:S(2)}) %collective-permute-start.14) | collective-permute-done | bytes 98336 | tf_op jit(solution)/shard_map/ppermute | solution.py:462
  37.7 0.8 %route_outputs.1 = (bf16[1,32,1024]{2,1,0:T(8,128)(2,1)}, bf16[16,1024]{1,0:T(8,128)(2,1)}) custom-call(f32[2,24,128]{2,1,0:T(8,128)S(1)} %get-tuple-element.20.route_ref, bf16[48,1024]{1,0:T(8,128)(2,1)S(1)} %join_parts.1.refs_0_, bf16[48,1024]{1,0:T(8,128)(2,1)S(1)} %collective-permute-done.14.refs_1_), custom_call_target="tpu_custom_call" | custom-call | tf_op jit(solution)/shard_map/route_outputs/pallas_call | solution.py:391
  (17 shorter events, 0.1 us)
Async XLA Ops:
  0.6 11.4 %copy-start = (bf16[1,32,1024]{2,1,0:T(8,128)(2,1)S(1)}, bf16[1,32,1024]{2,1,0:T(8,128)(2,1)}, u32[]{:S(2)}) copy-start(bf16[1,32,1024]{2,1,0:T(8,128)(2,1)} %pre_q_hbm.1) | copy-start | bytes 196612
  1.6 11.2 %collective-permute-start = (bf16[160,512]{1,0:T(8,128)(2,1)S(1)}, bf16[160,512]{1,0:T(8,128)(2,1)S(1)}, u32[]{:S(2)}, u32[]{:S(2)}) collective-permute-start(bf16[160,512]{1,0:T(8,128)(2,1)S(1)} %pad_maximum_fusion.refs_1_.refs_0_), channel_id=1, source_target_pairs={{0,8},{2,10},{4,12},{6,14},{8,0},{10,2},{12,4},{14,6},{16,24},{18,... | collective-permute-start | bytes 491528 | tf_op jit(solution)/shard_map/ppermute | solution.py:422
  4.7 14.4 %collective-permute-start.1 = (bf16[160,512]{1,0:T(8,128)(2,1)S(1)}, bf16[160,512]{1,0:T(8,128)(2,1)S(1)}, u32[]{:S(2)}, u32[]{:S(2)}) collective-permute-start(bf16[160,512]{1,0:T(8,128)(2,1)S(1)} %pad_maximum_fusion.refs_1_.refs_0_), channel_id=1, source_target_pairs={{0,4},{2,6},{4,0},{6,2},{8,12},{10,14},{12,8},{14,10},{16,20},{18,... | collective-permute-start | bytes 491528 | tf_op jit(solution)/shard_map/ppermute | solution.py:422
  6.2 13.4 %collective-permute-start.6 = (bf16[160,512]{1,0:T(8,128)(2,1)S(1)}, bf16[160,512]{1,0:T(8,128)(2,1)S(1)}, u32[]{:S(2)}, u32[]{:S(2)}) collective-permute-start(bf16[160,512]{1,0:T(8,128)(2,1)S(1)} %pad_maximum_fusion.refs_1_.refs_0_), channel_id=1, source_target_pairs={{0,12},{2,14},{4,8},{6,10},{8,4},{10,6},{12,0},{14,2},{16,28},{18,... | collective-permute-start | bytes 491528 | tf_op jit(solution)/shard_map/ppermute | solution.py:422
  9.1 10.5 %collective-permute-start.7 = (bf16[80,512]{1,0:T(8,128)(2,1)S(1)}, bf16[80,512]{1,0:T(8,128)(2,1)S(1)}, u32[]{:S(2)}, u32[]{:S(2)}) collective-permute-start(bf16[80,512]{1,0:T(8,128)(2,1)S(1)} %get-tuple-element.21.refs_0_), channel_id=1, source_target_pairs={{0,16},{2,18},{4,20},{6,22},{8,24},{10,26},{12,28},{14,30},{16,0},... | collective-permute-start | bytes 245768 | tf_op jit(solution)/shard_map/ppermute | solution.py:422
  12.1 7.0 %collective-permute-start.2 = (bf16[32,1024]{1,0:T(8,128)(2,1)S(1)}, bf16[32,1024]{1,0:T(8,128)(2,1)S(1)}, u32[]{:S(2)}, u32[]{:S(2)}) collective-permute-start(bf16[32,1024]{1,0:T(8,128)(2,1)S(1)} %bitcast.7), channel_id=1, source_target_pairs={{0,16},{2,18},{4,20},{6,22},{8,24},{10,26},{12,28},{14,30},{16,0},... | collective-permute-start | bytes 196616 | tf_op jit(solution)/shard_map/ppermute | solution.py:422
  12.8 7.6 %collective-permute-start.3 = (bf16[160,512]{1,0:T(8,128)(2,1)S(1)}, bf16[160,512]{1,0:T(8,128)(2,1)S(1)}, u32[]{:S(2)}, u32[]{:S(2)}) collective-permute-start(bf16[160,512]{1,0:T(8,128)(2,1)S(1)} %pad_maximum_fusion.refs_1_.refs_0_), channel_id=1, source_target_pairs={{0,2},{2,0},{4,6},{6,4},{8,10},{10,8},{12,14},{14,12},{16,18},{18,... | collective-permute-start | bytes 491528 | tf_op jit(solution)/shard_map/ppermute | solution.py:422
  19.1 1.6 %collective-permute-start.5 = (bf16[160,512]{1,0:T(8,128)(2,1)S(1)}, bf16[160,512]{1,0:T(8,128)(2,1)S(1)}, u32[]{:S(2)}, u32[]{:S(2)}) collective-permute-start(bf16[160,512]{1,0:T(8,128)(2,1)S(1)} %collective-permute-done.refs_5_.refs_4_), channel_id=1, source_target_pairs={{0,2},{2,0},{4,6},{6,4},{8,10},{10,8},{12,14},{14,12},{16,18},{18,... | collective-permute-start | bytes 491528 | tf_op jit(solution)/shard_map/ppermute | solution.py:422
  19.1 1.6 %collective-permute-start.4 = (bf16[160,512]{1,0:T(8,128)(2,1)S(1)}, bf16[160,512]{1,0:T(8,128)(2,1)S(1)}, u32[]{:S(2)}, u32[]{:S(2)}) collective-permute-start(bf16[160,512]{1,0:T(8,128)(2,1)S(1)} %collective-permute-done.1.refs_3_.refs_2_), channel_id=1, source_target_pairs={{0,2},{2,0},{4,6},{6,4},{8,10},{10,8},{12,14},{14,12},{16,18},{18,... | collective-permute-start | bytes 491528 | tf_op jit(solution)/shard_map/ppermute | solution.py:422
  19.6 1.4 %collective-permute-start.8 = (bf16[160,512]{1,0:T(8,128)(2,1)S(1)}, bf16[160,512]{1,0:T(8,128)(2,1)S(1)}, u32[]{:S(2)}, u32[]{:S(2)}) collective-permute-start(bf16[160,512]{1,0:T(8,128)(2,1)S(1)} %collective-permute-done.6.refs_7_.refs_6_), channel_id=1, source_target_pairs={{0,2},{2,0},{4,6},{6,4},{8,10},{10,8},{12,14},{14,12},{16,18},{18,... | collective-permute-start | bytes 491528 | tf_op jit(solution)/shard_map/ppermute | solution.py:422
  20.0 2.1 %collective-permute-start.10 = (bf16[48,512]{1,0:T(8,128)(2,1)S(1)}, bf16[48,512]{1,0:T(8,128)(2,1)S(1)}, u32[]{:S(2)}, u32[]{:S(2)}) collective-permute-start(bf16[48,512]{1,0:T(8,128)(2,1)S(1)} %join_far.1.refs_0_), channel_id=1, source_target_pairs={{0,2},{2,0},{4,6},{6,4},{8,10},{10,8},{12,14},{14,12},{16,18},{18,... | collective-permute-start | bytes 147464 | tf_op jit(solution)/shard_map/ppermute | solution.py:422
  22.4 6.2 %collective-permute-start.13 = (bf16[80,512]{1,0:T(8,128)(2,1)S(1)}, bf16[80,512]{1,0:T(8,128)(2,1)S(1)}, u32[]{:S(2)}, u32[]{:S(2)}) collective-permute-start(bf16[80,512]{1,0:T(8,128)(2,1)S(1)} %join_core.1.refs_2_), channel_id=1, source_target_pairs={{0,12},{2,14},{4,8},{6,10},{8,4},{10,6},{12,0},{14,2},{16,28},{18,... | collective-permute-start | bytes 245768 | tf_op jit(solution)/shard_map/ppermute | solution.py:422
  23.3 7.6 %collective-permute-start.12 = (bf16[80,512]{1,0:T(8,128)(2,1)S(1)}, bf16[80,512]{1,0:T(8,128)(2,1)S(1)}, u32[]{:S(2)}, u32[]{:S(2)}) collective-permute-start(bf16[80,512]{1,0:T(8,128)(2,1)S(1)} %join_core.1.refs_2_), channel_id=1, source_target_pairs={{0,8},{2,10},{4,12},{6,14},{8,0},{10,2},{12,4},{14,6},{16,24},{18,... | collective-permute-start | bytes 245768 | tf_op jit(solution)/shard_map/ppermute | solution.py:422
  25.6 5.4 %collective-permute-start.11 = (bf16[80,512]{1,0:T(8,128)(2,1)S(1)}, bf16[80,512]{1,0:T(8,128)(2,1)S(1)}, u32[]{:S(2)}, u32[]{:S(2)}) collective-permute-start(bf16[80,512]{1,0:T(8,128)(2,1)S(1)} %join_core.1.refs_2_), channel_id=1, source_target_pairs={{0,4},{2,6},{4,0},{6,2},{8,12},{10,14},{12,8},{14,10},{16,20},{18,... | collective-permute-start | bytes 245768 | tf_op jit(solution)/shard_map/ppermute | solution.py:422
  25.9 6.4 %collective-permute-start.9 = (bf16[32,1152]{1,0:T(8,128)(2,1)S(1)}, bf16[32,1152]{1,0:T(8,128)(2,1)S(1)}, u32[]{:S(2)}, u32[]{:S(2)}) collective-permute-start(bf16[32,1152]{1,0:T(8,128)(2,1)S(1)} %prefill_partials.2), channel_id=1, source_target_pairs={{0,16},{2,18},{4,20},{6,22},{8,24},{10,26},{12,28},{14,30},{16,0},... | collective-permute-start | bytes 221192 | tf_op jit(solution)/shard_map/ppermute | solution.py:422
  31.0 3.3 %collective-permute-start.15 = (bf16[128,512]{1,0:T(8,128)(2,1)S(1)}, bf16[128,512]{1,0:T(8,128)(2,1)S(1)}, u32[]{:S(2)}, u32[]{:S(2)}) collective-permute-start(bf16[128,512]{1,0:T(8,128)(2,1)S(1)} %pad_maximum_fusion.1.near_ref), channel_id=1, source_target_pairs={{0,2},{2,0},{4,6},{6,4},{8,10},{10,8},{12,14},{14,12},{16,18},{18,... | collective-permute-start | bytes 393224 | tf_op jit(solution)/shard_map/ppermute | solution.py:422
  32.6 5.1 %collective-permute-start.14 = (bf16[48,1024]{1,0:T(8,128)(2,1)S(1)}, bf16[48,1024]{1,0:T(8,128)(2,1)S(1)}, u32[]{:S(2)}, u32[]{:S(2)}) collective-permute-start(bf16[48,1024]{1,0:T(8,128)(2,1)S(1)} %join_parts.1.refs_0_), channel_id=1, source_target_pairs={{0,1},{1,0},{2,3},{3,2},{4,5},{5,4},{6,7},{7,6},{8,9},{9,8},{10,11... | collective-permute-start | bytes 294920 | tf_op jit(solution)/shard_map/ppermute | solution.py:462

commit v18 on v17

--- a/solution.py
+++ b/solution.py
@@ -448,12 +448,14 @@
     tables = [t for lane in lanes for t in (lane, swap(lane, 1))]
     beside = swap(part, 1)
 
+    part = join_step([part, beside], far, slots, "join_core")
+    offset = after(offset, part)
     sent = prefill_partials(offset, packs, tables, ctx, [k // KEY_SET for k in others])
     arrived = [swap(p, k) for k, p in zip(others, sent)]
+    part = after(part, sent[0])
+    around = [part] + [swap(part, k) for k in range(2, KEY_SET, 2)]
     queries = after(queries, sent[0])
     kept = prefill_partials(offset, [queries], tables, ctx, [0])
-    part = join_step([part, after(beside, sent[0])], far, slots, "join_core")
-    around = [part] + [swap(part, k) for k in range(2, KEY_SET, 2)]
     attended = join_parts([*kept] + arrived, around, slots)
     news = jnp.concatenate([a[PART_ROWS * slots :] for a in around], axis=0)
     prefill_cache_out = update_cache(offset, prefill_cache, news, swap(news, 1), tables, tokens, len(others))

time: 38.6 us -> 38.6 us (level)
  starting transfers between devices: 15.6 us -> 15.2 us
  waiting for transfers between devices: 12.1 us -> 12.5 us
    ppermute x15, waiting for transfers between devices: 10.4 us -> 10.9 us  [swap(): return lax.ppermute(array, BLK, [(i, i ^ distance) for i in range(blk)])]
    ppermute x15, starting transfers between devices: 13.9 us -> 13.5 us  [swap(): return lax.ppermute(array, BLK, [(i, i ^ distance) for i in range(blk)])]
  transfers between devices with their start and end apart: 16 -> 16, of which waited for: 7 -> 7; matrix products, arithmetic and copies ran while one was open for 0% -> 0% of each run, Pallas kernels for 19% -> 17%
where the time goes in v18:
time: 38.6 us; the launch traced here: 38.5 us
  starting transfers between devices  15.2 us (39%)
  waiting for transfers between devices  12.5 us (32%)
  Pallas kernels  8.3 us (22%)
  between operations  1.43 us (4%)
  other arithmetic  0.98 us (3%)
    ppermute x15, starting transfers between devices, swap(): return lax.ppermute(array, BLK, [(i, i ^ distance) for i in range(blk)])  13.5 us
    ppermute x15, waiting for transfers between devices, swap(): return lax.ppermute(array, BLK, [(i, i ^ distance) for i in range(blk)])  10.9 us
    pallas_call x1, Pallas kernels, decode_partials(): pl.pallas_call(decode_kernel, in_specs=[HBM] * len(inputs), out_specs=[HB...  2.82 us
    pallas_call x2, Pallas kernels, prefill_partials(): pl.pallas_call(functools.partial(prefill_kernel, sets, ctx), in_specs=[VM...  2.13 us
    pallas_call x1, Pallas kernels, update_cache(): pl.pallas_call(functools.partial(update_kernel, tokens, sets), in_specs=[...  1.71 us
    ppermute x1, starting transfers between devices, per_device(): held = [attended, lax.ppermute(attended, 'req', [(0, 1), (1, 0)])]  1.68 us
    ppermute x1, waiting for transfers between devices, per_device(): held = [attended, lax.ppermute(attended, 'req', [(0, 1), (1, 0)])]  1.61 us
    concatenate x1, other arithmetic, per_device(): table = jnp.concatenate([prefill_cache[0], new_prefill[0]], axis=0)  0.97 us
  transfers between devices with their start and end apart: 16, of which 7 were waited for; matrix products, arithmetic and copies ran while one was open for 0% of the time, Pallas kernels for 17%

profile of v18, /device:TPU:0, one launch (start us, length us, event | category | flops | bytes accessed | tf_op | source)
XLA Modules:
  0.0 38.5 jit_solution(13759990931491712531)
XLA Ops:
  0.6 0.0 copy-start
  0.6 1.0 %pad_maximum_fusion.refs_1_.refs_0_ = bf16[160,512]{1,0:T(8,128)(2,1)S(1)} fusion(bf16[32,512]{1,0:T(8,128)(2,1)} %bitcast.6, bf16[128,512]{1,0:T(8,128)(2,1)} %bitcast.5), kind=kLoop, calls=%fused_computation | loop fusion | flops 327680 | bytes 327680 | tf_op jit(solution)/shard_map/concatenate | solution.py:428
  1.6 3.1 %collective-permute-start = (bf16[160,512]{1,0:T(8,128)(2,1)S(1)}, bf16[160,512]{1,0:T(8,128)(2,1)S(1)}, u32[]{:S(2)}, u32[]{:S(2)}) collective-permute-start(bf16[160,512]{1,0:T(8,128)(2,1)S(1)} %pad_maximum_fusion.refs_1_.refs_0_), channel_id=1, source_target_pairs={{0,8},{2,10},{4,12},{6,14},{8,0},{10,2},{12,4},{14,6},{16,24},{18,... | collective-permute-start | bytes 491528 | tf_op jit(solution)/shard_map/ppermute | solution.py:422
  4.7 1.4 %collective-permute-start.1 = (bf16[160,512]{1,0:T(8,128)(2,1)S(1)}, bf16[160,512]{1,0:T(8,128)(2,1)S(1)}, u32[]{:S(2)}, u32[]{:S(2)}) collective-permute-start(bf16[160,512]{1,0:T(8,128)(2,1)S(1)} %pad_maximum_fusion.refs_1_.refs_0_), channel_id=1, source_target_pairs={{0,12},{2,14},{4,8},{6,10},{8,4},{10,6},{12,0},{14,2},{16,28},{18,... | collective-permute-start | bytes 491528 | tf_op jit(solution)/shard_map/ppermute | solution.py:422
  6.1 0.2 collective-permute-start.4
  6.2 2.8 %decode_partials.1 = (bf16[16,128,512]{2,1,0:T(8,128)(2,1)}, bf16[80,512]{1,0:T(8,128)(2,1)S(1)}, bf16[32,1024]{1,0:T(8,128)(2,1)S(1)}, f32[2,24,128]{2,1,0:T(8,128)S(1)}) custom-call(s32[16]{0:T(128)} %len_hbm.1, s32[34]{0:T(128)} %deal_hbm.1, bf16[16,1024]{1,0:T(8,128)(2,1)} %q_hbm.1, bf16[16,512]{1,0:T(8,128)(2,1)} %new_hbm.1, ...), custom_call_target="tpu_custom_call" | custom-call | flops 8388608 | bytes 4194304 | tf_op jit(solution)/shard_map/decode_partials/pallas_call | solution.py:198
  9.1 3.0 %collective-permute-start.2 = (bf16[80,512]{1,0:T(8,128)(2,1)S(1)}, bf16[80,512]{1,0:T(8,128)(2,1)S(1)}, u32[]{:S(2)}, u32[]{:S(2)}) collective-permute-start(bf16[80,512]{1,0:T(8,128)(2,1)S(1)} %get-tuple-element.22.refs_0_), channel_id=1, source_target_pairs={{0,16},{2,18},{4,20},{6,22},{8,24},{10,26},{12,28},{14,30},{16,0},... | collective-permute-start | bytes 245768 | tf_op jit(solution)/shard_map/ppermute | solution.py:422
  12.1 0.1 collective-permute-start.5
  12.8 0.0 collective-permute-done.refs_5_.refs_4_
  12.8 0.1 collective-permute-start.6
  12.9 4.5 %collective-permute-done.2.refs_1_.refs_2_ = bf16[80,512]{1,0:T(8,128)(2,1)S(1)} collective-permute-done((bf16[80,512]{1,0:T(8,128)(2,1)S(1)}, bf16[80,512]{1,0:T(8,128)(2,1)S(1)}, u32[]{:S(2)}, u32[]{:S(2)}) %collective-permute-start.2) | collective-permute-done | bytes 81952 | tf_op jit(solution)/shard_map/ppermute | solution.py:422
  17.4 1.6 %collective-permute-done.5.refs_0_ = bf16[32,1024]{1,0:T(8,128)(2,1)S(1)} collective-permute-done((bf16[32,1024]{1,0:T(8,128)(2,1)S(1)}, bf16[32,1024]{1,0:T(8,128)(2,1)S(1)}, u32[]{:S(2)}, u32[]{:S(2)}) %collective-permute-start.5) | collective-permute-done | bytes 65568 | tf_op jit(solution)/shard_map/ppermute | solution.py:422
  19.0 0.5 %collective-permute-start.9 = (bf16[160,512]{1,0:T(8,128)(2,1)S(1)}, bf16[160,512]{1,0:T(8,128)(2,1)S(1)}, u32[]{:S(2)}, u32[]{:S(2)}) collective-permute-start(bf16[160,512]{1,0:T(8,128)(2,1)S(1)} %collective-permute-done.1.refs_7_.refs_6_), channel_id=1, source_target_pairs={{0,2},{2,0},{4,6},{6,4},{8,10},{10,8},{12,14},{14,12},{16,18},{18,... | collective-permute-start | bytes 491528 | tf_op jit(solution)/shard_map/ppermute | solution.py:422
  19.5 0.3 join_far.1.refs_0_
  19.8 0.1 collective-permute-start.3
  19.9 1.2 %collective-permute-done.3.refs_1_ = bf16[48,512]{1,0:T(8,128)(2,1)S(1)} collective-permute-done((bf16[48,512]{1,0:T(8,128)(2,1)S(1)}, bf16[48,512]{1,0:T(8,128)(2,1)S(1)}, u32[]{:S(2)}, u32[]{:S(2)}) %collective-permute-start.3) | collective-permute-done | bytes 49184 | tf_op jit(solution)/shard_map/ppermute | solution.py:422
  21.1 0.3 join_core.1.refs_2_
  21.4 1.1 %prefill_partials.2 = bf16[32,1152]{1,0:T(8,128)(2,1)S(1)} custom-call(s32[8,128]{1,0:T(8,128)S(1)} %broadcast_in_dim.3.off_ref, bf16[32,1024]{1,0:T(8,128)(2,1)S(1)} %collective-permute-done.5.refs_0_, bf16[160,512]{1,0:T(8,128)(2,1)S(1)} %pad_maximum_fusion.refs_1_.refs_0_, bf16[160,512]{1,0:T(8,128)(2,1)S(1)} %collective-permute-done.6.refs_2_.refs_1_, ...), custom_call_target="tpu_custom_call" | custom-call | flops 167772160 | bytes 4194304 | tf_op jit(solution)/shard_map/prefill_partials/pallas_call | solution.py:308
  22.5 1.0 %collective-permute-start.13 = (bf16[80,512]{1,0:T(8,128)(2,1)S(1)}, bf16[80,512]{1,0:T(8,128)(2,1)S(1)}, u32[]{:S(2)}, u32[]{:S(2)}) collective-permute-start(bf16[80,512]{1,0:T(8,128)(2,1)S(1)} %join_core.1.refs_2_), channel_id=1, source_target_pairs={{0,12},{2,14},{4,8},{6,10},{8,4},{10,6},{12,0},{14,2},{16,28},{18,... | collective-permute-start | bytes 245768 | tf_op jit(solution)/shard_map/ppermute | solution.py:422
  23.5 2.2 %collective-permute-start.12 = (bf16[80,512]{1,0:T(8,128)(2,1)S(1)}, bf16[80,512]{1,0:T(8,128)(2,1)S(1)}, u32[]{:S(2)}, u32[]{:S(2)}) collective-permute-start(bf16[80,512]{1,0:T(8,128)(2,1)S(1)} %join_core.1.refs_2_), channel_id=1, source_target_pairs={{0,8},{2,10},{4,12},{6,14},{8,0},{10,2},{12,4},{14,6},{16,24},{18,... | collective-permute-start | bytes 245768 | tf_op jit(solution)/shard_map/ppermute | solution.py:422
  25.7 0.4 collective-permute-start.11
  26.1 1.5 %collective-permute-start.10 = (bf16[32,1152]{1,0:T(8,128)(2,1)S(1)}, bf16[32,1152]{1,0:T(8,128)(2,1)S(1)}, u32[]{:S(2)}, u32[]{:S(2)}) collective-permute-start(bf16[32,1152]{1,0:T(8,128)(2,1)S(1)} %prefill_partials.2), channel_id=1, source_target_pairs={{0,16},{2,18},{4,20},{6,22},{8,24},{10,26},{12,28},{14,30},{16,0},... | collective-permute-start | bytes 221192 | tf_op jit(solution)/shard_map/ppermute | solution.py:422
  27.6 1.2 %collective-permute-done.13.refs_5_ = bf16[80,512]{1,0:T(8,128)(2,1)S(1)} collective-permute-done((bf16[80,512]{1,0:T(8,128)(2,1)S(1)}, bf16[80,512]{1,0:T(8,128)(2,1)S(1)}, u32[]{:S(2)}, u32[]{:S(2)}) %collective-permute-start.13) | collective-permute-done | bytes 81952 | tf_op jit(solution)/shard_map/ppermute | solution.py:422
  28.8 2.2 %collective-permute-done.12.refs_4_ = bf16[80,512]{1,0:T(8,128)(2,1)S(1)} collective-permute-done((bf16[80,512]{1,0:T(8,128)(2,1)S(1)}, bf16[80,512]{1,0:T(8,128)(2,1)S(1)}, u32[]{:S(2)}, u32[]{:S(2)}) %collective-permute-start.12) | collective-permute-done | bytes 81952 | tf_op jit(solution)/shard_map/ppermute | solution.py:422
  31.0 0.1 collective-permute-start.15
  31.0 1.1 %prefill_partials.3.refs_0_ = bf16[32,1152]{1,0:T(8,128)(2,1)S(1)} custom-call(s32[8,128]{1,0:T(8,128)S(1)} %broadcast_in_dim.3.off_ref, bf16[32,1024]{1,0:T(8,128)(2,1)S(1)} %get-tuple-element.31.refs_0_, bf16[160,512]{1,0:T(8,128)(2,1)S(1)} %pad_maximum_fusion.refs_1_.refs_0_, bf16[160,512]{1,0:T(8,128)(2,1)S(1)} %collective-permute-done.6.refs_2_.refs_1_, ...), custom_call_target="tpu_custom_call" | custom-call | flops 167772160 | bytes 4194304 | tf_op jit(solution)/shard_map/prefill_partials/pallas_call | solution.py:308
  32.1 0.3 collective-permute-done.10.refs_1_
  32.4 0.3 join_parts.1.refs_0_
  32.7 1.7 %collective-permute-start.14 = (bf16[48,1024]{1,0:T(8,128)(2,1)S(1)}, bf16[48,1024]{1,0:T(8,128)(2,1)S(1)}, u32[]{:S(2)}, u32[]{:S(2)}) collective-permute-start(bf16[48,1024]{1,0:T(8,128)(2,1)S(1)} %join_parts.1.refs_0_), channel_id=1, source_target_pairs={{0,1},{1,0},{2,3},{3,2},{4,5},{5,4},{6,7},{7,6},{8,9},{9,8},{10,11... | collective-permute-start | bytes 294920 | tf_op jit(solution)/shard_map/ppermute | solution.py:464
  34.4 1.7 %update_cache.1 = bf16[1,128,512]{2,1,0:T(8,128)(2,1)} custom-call(s32[8,128]{1,0:T(8,128)S(1)} %broadcast_in_dim.3.off_ref, bf16[1,128,512]{2,1,0:T(8,128)(2,1)} %cache_hbm.3, bf16[128,512]{1,0:T(8,128)(2,1)S(1)} %pad_maximum_fusion.1.near_ref, bf16[128,512]{1,0:T(8,128)(2,1)S(1)} %collective-permute-done.15.beside_ref, ...), custom_call_target="tpu_custom_call" | custom-call | tf_op jit(solution)/shard_map/update_cache/pallas_call | solution.py:363
  36.1 1.6 %collective-permute-done.14.refs_1_ = bf16[48,1024]{1,0:T(8,128)(2,1)S(1)} collective-permute-done((bf16[48,1024]{1,0:T(8,128)(2,1)S(1)}, bf16[48,1024]{1,0:T(8,128)(2,1)S(1)}, u32[]{:S(2)}, u32[]{:S(2)}) %collective-permute-start.14) | collective-permute-done | bytes 98336 | tf_op jit(solution)/shard_map/ppermute | solution.py:464
  37.7 0.8 %route_outputs.1 = (bf16[1,32,1024]{2,1,0:T(8,128)(2,1)}, bf16[16,1024]{1,0:T(8,128)(2,1)}) custom-call(f32[2,24,128]{2,1,0:T(8,128)S(1)} %get-tuple-element.21.route_ref, bf16[48,1024]{1,0:T(8,128)(2,1)S(1)} %join_parts.1.refs_0_, bf16[48,1024]{1,0:T(8,128)(2,1)S(1)} %collective-permute-done.14.refs_1_), custom_call_target="tpu_custom_call" | custom-call | tf_op jit(solution)/shard_map/route_outputs/pallas_call | solution.py:391
  (17 shorter events, 0.1 us)
Async XLA Ops:
  0.6 11.4 %copy-start = (bf16[1,32,1024]{2,1,0:T(8,128)(2,1)S(1)}, bf16[1,32,1024]{2,1,0:T(8,128)(2,1)}, u32[]{:S(2)}) copy-start(bf16[1,32,1024]{2,1,0:T(8,128)(2,1)} %pre_q_hbm.1) | copy-start | bytes 196612
  1.6 11.2 %collective-permute-start = (bf16[160,512]{1,0:T(8,128)(2,1)S(1)}, bf16[160,512]{1,0:T(8,128)(2,1)S(1)}, u32[]{:S(2)}, u32[]{:S(2)}) collective-permute-start(bf16[160,512]{1,0:T(8,128)(2,1)S(1)} %pad_maximum_fusion.refs_1_.refs_0_), channel_id=1, source_target_pairs={{0,8},{2,10},{4,12},{6,14},{8,0},{10,2},{12,4},{14,6},{16,24},{18,... | collective-permute-start | bytes 491528 | tf_op jit(solution)/shard_map/ppermute | solution.py:422
  4.7 12.7 %collective-permute-start.1 = (bf16[160,512]{1,0:T(8,128)(2,1)S(1)}, bf16[160,512]{1,0:T(8,128)(2,1)S(1)}, u32[]{:S(2)}, u32[]{:S(2)}) collective-permute-start(bf16[160,512]{1,0:T(8,128)(2,1)S(1)} %pad_maximum_fusion.refs_1_.refs_0_), channel_id=1, source_target_pairs={{0,12},{2,14},{4,8},{6,10},{8,4},{10,6},{12,0},{14,2},{16,28},{18,... | collective-permute-start | bytes 491528 | tf_op jit(solution)/shard_map/ppermute | solution.py:422
  6.1 12.9 %collective-permute-start.4 = (bf16[160,512]{1,0:T(8,128)(2,1)S(1)}, bf16[160,512]{1,0:T(8,128)(2,1)S(1)}, u32[]{:S(2)}, u32[]{:S(2)}) collective-permute-start(bf16[160,512]{1,0:T(8,128)(2,1)S(1)} %pad_maximum_fusion.refs_1_.refs_0_), channel_id=1, source_target_pairs={{0,4},{2,6},{4,0},{6,2},{8,12},{10,14},{12,8},{14,10},{16,20},{18,... | collective-permute-start | bytes 491528 | tf_op jit(solution)/shard_map/ppermute | solution.py:422
  9.1 8.4 %collective-permute-start.2 = (bf16[80,512]{1,0:T(8,128)(2,1)S(1)}, bf16[80,512]{1,0:T(8,128)(2,1)S(1)}, u32[]{:S(2)}, u32[]{:S(2)}) collective-permute-start(bf16[80,512]{1,0:T(8,128)(2,1)S(1)} %get-tuple-element.22.refs_0_), channel_id=1, source_target_pairs={{0,16},{2,18},{4,20},{6,22},{8,24},{10,26},{12,28},{14,30},{16,0},... | collective-permute-start | bytes 245768 | tf_op jit(solution)/shard_map/ppermute | solution.py:422
  12.1 6.9 %collective-permute-start.5 = (bf16[32,1024]{1,0:T(8,128)(2,1)S(1)}, bf16[32,1024]{1,0:T(8,128)(2,1)S(1)}, u32[]{:S(2)}, u32[]{:S(2)}) collective-permute-start(bf16[32,1024]{1,0:T(8,128)(2,1)S(1)} %bitcast.7), channel_id=1, source_target_pairs={{0,16},{2,18},{4,20},{6,22},{8,24},{10,26},{12,28},{14,30},{16,0},... | collective-permute-start | bytes 196616 | tf_op jit(solution)/shard_map/ppermute | solution.py:422
  12.8 8.6 %collective-permute-start.6 = (bf16[160,512]{1,0:T(8,128)(2,1)S(1)}, bf16[160,512]{1,0:T(8,128)(2,1)S(1)}, u32[]{:S(2)}, u32[]{:S(2)}) collective-permute-start(bf16[160,512]{1,0:T(8,128)(2,1)S(1)} %pad_maximum_fusion.refs_1_.refs_0_), channel_id=1, source_target_pairs={{0,2},{2,0},{4,6},{6,4},{8,10},{10,8},{12,14},{14,12},{16,18},{18,... | collective-permute-start | bytes 491528 | tf_op jit(solution)/shard_map/ppermute | solution.py:422
  17.4 4.0 %collective-permute-start.8 = (bf16[160,512]{1,0:T(8,128)(2,1)S(1)}, bf16[160,512]{1,0:T(8,128)(2,1)S(1)}, u32[]{:S(2)}, u32[]{:S(2)}) collective-permute-start(bf16[160,512]{1,0:T(8,128)(2,1)S(1)} %collective-permute-done.refs_5_.refs_4_), channel_id=1, source_target_pairs={{0,2},{2,0},{4,6},{6,4},{8,10},{10,8},{12,14},{14,12},{16,18},{18,... | collective-permute-start | bytes 491528 | tf_op jit(solution)/shard_map/ppermute | solution.py:422
  19.0 2.4 %collective-permute-start.7 = (bf16[160,512]{1,0:T(8,128)(2,1)S(1)}, bf16[160,512]{1,0:T(8,128)(2,1)S(1)}, u32[]{:S(2)}, u32[]{:S(2)}) collective-permute-start(bf16[160,512]{1,0:T(8,128)(2,1)S(1)} %collective-permute-done.4.refs_3_.refs_2_), channel_id=1, source_target_pairs={{0,2},{2,0},{4,6},{6,4},{8,10},{10,8},{12,14},{14,12},{16,18},{18,... | collective-permute-start | bytes 491528 | tf_op jit(solution)/shard_map/ppermute | solution.py:422
  19.0 2.4 %collective-permute-start.9 = (bf16[160,512]{1,0:T(8,128)(2,1)S(1)}, bf16[160,512]{1,0:T(8,128)(2,1)S(1)}, u32[]{:S(2)}, u32[]{:S(2)}) collective-permute-start(bf16[160,512]{1,0:T(8,128)(2,1)S(1)} %collective-permute-done.1.refs_7_.refs_6_), channel_id=1, source_target_pairs={{0,2},{2,0},{4,6},{6,4},{8,10},{10,8},{12,14},{14,12},{16,18},{18,... | collective-permute-start | bytes 491528 | tf_op jit(solution)/shard_map/ppermute | solution.py:422
  19.8 1.3 %collective-permute-start.3 = (bf16[48,512]{1,0:T(8,128)(2,1)S(1)}, bf16[48,512]{1,0:T(8,128)(2,1)S(1)}, u32[]{:S(2)}, u32[]{:S(2)}) collective-permute-start(bf16[48,512]{1,0:T(8,128)(2,1)S(1)} %join_far.1.refs_0_), channel_id=1, source_target_pairs={{0,2},{2,0},{4,6},{6,4},{8,10},{10,8},{12,14},{14,12},{16,18},{18,... | collective-permute-start | bytes 147464 | tf_op jit(solution)/shard_map/ppermute | solution.py:422
  22.5 6.3 %collective-permute-start.13 = (bf16[80,512]{1,0:T(8,128)(2,1)S(1)}, bf16[80,512]{1,0:T(8,128)(2,1)S(1)}, u32[]{:S(2)}, u32[]{:S(2)}) collective-permute-start(bf16[80,512]{1,0:T(8,128)(2,1)S(1)} %join_core.1.refs_2_), channel_id=1, source_target_pairs={{0,12},{2,14},{4,8},{6,10},{8,4},{10,6},{12,0},{14,2},{16,28},{18,... | collective-permute-start | bytes 245768 | tf_op jit(solution)/shard_map/ppermute | solution.py:422
  23.5 7.4 %collective-permute-start.12 = (bf16[80,512]{1,0:T(8,128)(2,1)S(1)}, bf16[80,512]{1,0:T(8,128)(2,1)S(1)}, u32[]{:S(2)}, u32[]{:S(2)}) collective-permute-start(bf16[80,512]{1,0:T(8,128)(2,1)S(1)} %join_core.1.refs_2_), channel_id=1, source_target_pairs={{0,8},{2,10},{4,12},{6,14},{8,0},{10,2},{12,4},{14,6},{16,24},{18,... | collective-permute-start | bytes 245768 | tf_op jit(solution)/shard_map/ppermute | solution.py:422
  25.7 5.2 %collective-permute-start.11 = (bf16[80,512]{1,0:T(8,128)(2,1)S(1)}, bf16[80,512]{1,0:T(8,128)(2,1)S(1)}, u32[]{:S(2)}, u32[]{:S(2)}) collective-permute-start(bf16[80,512]{1,0:T(8,128)(2,1)S(1)} %join_core.1.refs_2_), channel_id=1, source_target_pairs={{0,4},{2,6},{4,0},{6,2},{8,12},{10,14},{12,8},{14,10},{16,20},{18,... | collective-permute-start | bytes 245768 | tf_op jit(solution)/shard_map/ppermute | solution.py:422
  26.1 6.3 %collective-permute-start.10 = (bf16[32,1152]{1,0:T(8,128)(2,1)S(1)}, bf16[32,1152]{1,0:T(8,128)(2,1)S(1)}, u32[]{:S(2)}, u32[]{:S(2)}) collective-permute-start(bf16[32,1152]{1,0:T(8,128)(2,1)S(1)} %prefill_partials.2), channel_id=1, source_target_pairs={{0,16},{2,18},{4,20},{6,22},{8,24},{10,26},{12,28},{14,30},{16,0},... | collective-permute-start | bytes 221192 | tf_op jit(solution)/shard_map/ppermute | solution.py:422
  31.0 3.4 %collective-permute-start.15 = (bf16[128,512]{1,0:T(8,128)(2,1)S(1)}, bf16[128,512]{1,0:T(8,128)(2,1)S(1)}, u32[]{:S(2)}, u32[]{:S(2)}) collective-permute-start(bf16[128,512]{1,0:T(8,128)(2,1)S(1)} %pad_maximum_fusion.1.near_ref), channel_id=1, source_target_pairs={{0,2},{2,0},{4,6},{6,4},{8,10},{10,8},{12,14},{14,12},{16,18},{18,... | collective-permute-start | bytes 393224 | tf_op jit(solution)/shard_map/ppermute | solution.py:422
  32.7 5.0 %collective-permute-start.14 = (bf16[48,1024]{1,0:T(8,128)(2,1)S(1)}, bf16[48,1024]{1,0:T(8,128)(2,1)S(1)}, u32[]{:S(2)}, u32[]{:S(2)}) collective-permute-start(bf16[48,1024]{1,0:T(8,128)(2,1)S(1)} %join_parts.1.refs_0_), channel_id=1, source_target_pairs={{0,1},{1,0},{2,3},{3,2},{4,5},{5,4},{6,7},{7,6},{8,9},{9,8},{10,11... | collective-permute-start | bytes 294920 | tf_op jit(solution)/shard_map/ppermute | solution.py:464

commit v19 on v18

--- a/solution.py
+++ b/solution.py
@@ -456,6 +456,7 @@
     around = [part] + [swap(part, k) for k in range(2, KEY_SET, 2)]
     queries = after(queries, sent[0])
     kept = prefill_partials(offset, [queries], tables, ctx, [0])
+    around = [part] + [after(a, *kept) for a in around[1:]]
     attended = join_parts([*kept] + arrived, around, slots)
     news = jnp.concatenate([a[PART_ROWS * slots :] for a in around], axis=0)
     prefill_cache_out = update_cache(offset, prefill_cache, news, swap(news, 1), tables, tokens, len(others))

time: 38.6 us -> 37.8 us (0.979)
  waiting for transfers between devices: 12.5 us -> 11.8 us
    ppermute x15, waiting for transfers between devices: 10.9 us -> 10.5 us  [swap(): return lax.ppermute(array, BLK, [(i, i ^ distance) for i in range(blk)])]
where the time goes in v19:
time: 37.8 us; the launch traced here: 37.6 us
  starting transfers between devices  15.1 us (40%)
  waiting for transfers between devices  11.8 us (31%)
  Pallas kernels  8.28 us (22%)
  between operations  1.44 us (4%)
  other arithmetic  0.98 us (3%)
    ppermute x15, starting transfers between devices, swap(): return lax.ppermute(array, BLK, [(i, i ^ distance) for i in range(blk)])  13.4 us
    ppermute x15, waiting for transfers between devices, swap(): return lax.ppermute(array, BLK, [(i, i ^ distance) for i in range(blk)])  10.5 us
    pallas_call x1, Pallas kernels, decode_partials(): pl.pallas_call(decode_kernel, in_specs=[HBM] * len(inputs), out_specs=[HB...  2.8 us
    pallas_call x2, Pallas kernels, prefill_partials(): pl.pallas_call(functools.partial(prefill_kernel, sets, ctx), in_specs=[VM...  2.13 us
    pallas_call x1, Pallas kernels, update_cache(): pl.pallas_call(functools.partial(update_kernel, tokens, sets), in_specs=[...  1.71 us
    ppermute x1, starting transfers between devices, per_device(): held = [attended, lax.ppermute(attended, 'req', [(0, 1), (1, 0)])]  1.69 us
    ppermute x1, waiting for transfers between devices, per_device(): held = [attended, lax.ppermute(attended, 'req', [(0, 1), (1, 0)])]  1.27 us
    concatenate x1, other arithmetic, per_device(): table = jnp.concatenate([prefill_cache[0], new_prefill[0]], axis=0)  0.97 us
  transfers between devices with their start and end apart: 16, of which 7 were waited for; matrix products, arithmetic and copies ran while one was open for 0% of the time, Pallas kernels for 17%

profile of v19, /device:TPU:0, one launch (start us, length us, event | category | flops | bytes accessed | tf_op | source)
XLA Modules:
  0.0 37.6 jit_solution(14729013605288985340)
XLA Ops:
  0.6 0.0 copy-start
  0.6 1.0 %pad_maximum_fusion.refs_1_.refs_0_ = bf16[160,512]{1,0:T(8,128)(2,1)S(1)} fusion(bf16[32,512]{1,0:T(8,128)(2,1)} %bitcast.6, bf16[128,512]{1,0:T(8,128)(2,1)} %bitcast.5), kind=kLoop, calls=%fused_computation | loop fusion | flops 327680 | bytes 327680 | tf_op jit(solution)/shard_map/concatenate | solution.py:428
  1.6 3.1 %collective-permute-start = (bf16[160,512]{1,0:T(8,128)(2,1)S(1)}, bf16[160,512]{1,0:T(8,128)(2,1)S(1)}, u32[]{:S(2)}, u32[]{:S(2)}) collective-permute-start(bf16[160,512]{1,0:T(8,128)(2,1)S(1)} %pad_maximum_fusion.refs_1_.refs_0_), channel_id=1, source_target_pairs={{0,8},{2,10},{4,12},{6,14},{8,0},{10,2},{12,4},{14,6},{16,24},{18,... | collective-permute-start | bytes 491528 | tf_op jit(solution)/shard_map/ppermute | solution.py:422
  4.7 1.4 %collective-permute-start.1 = (bf16[160,512]{1,0:T(8,128)(2,1)S(1)}, bf16[160,512]{1,0:T(8,128)(2,1)S(1)}, u32[]{:S(2)}, u32[]{:S(2)}) collective-permute-start(bf16[160,512]{1,0:T(8,128)(2,1)S(1)} %pad_maximum_fusion.refs_1_.refs_0_), channel_id=1, source_target_pairs={{0,12},{2,14},{4,8},{6,10},{8,4},{10,6},{12,0},{14,2},{16,28},{18,... | collective-permute-start | bytes 491528 | tf_op jit(solution)/shard_map/ppermute | solution.py:422
  6.1 0.2 collective-permute-start.4
  6.2 2.8 %decode_partials.1 = (bf16[16,128,512]{2,1,0:T(8,128)(2,1)}, bf16[80,512]{1,0:T(8,128)(2,1)S(1)}, bf16[32,1024]{1,0:T(8,128)(2,1)S(1)}, f32[2,24,128]{2,1,0:T(8,128)S(1)}) custom-call(s32[16]{0:T(128)} %len_hbm.1, s32[34]{0:T(128)} %deal_hbm.1, bf16[16,1024]{1,0:T(8,128)(2,1)} %q_hbm.1, bf16[16,512]{1,0:T(8,128)(2,1)} %new_hbm.1, ...), custom_call_target="tpu_custom_call" | custom-call | flops 8388608 | bytes 4194304 | tf_op jit(solution)/shard_map/decode_partials/pallas_call | solution.py:198
  9.1 3.0 %collective-permute-start.2 = (bf16[80,512]{1,0:T(8,128)(2,1)S(1)}, bf16[80,512]{1,0:T(8,128)(2,1)S(1)}, u32[]{:S(2)}, u32[]{:S(2)}) collective-permute-start(bf16[80,512]{1,0:T(8,128)(2,1)S(1)} %get-tuple-element.25.refs_0_), channel_id=1, source_target_pairs={{0,16},{2,18},{4,20},{6,22},{8,24},{10,26},{12,28},{14,30},{16,0},... | collective-permute-start | bytes 245768 | tf_op jit(solution)/shard_map/ppermute | solution.py:422
  12.1 0.1 collective-permute-start.5
  12.8 0.1 collective-permute-start.6
  12.9 4.5 %collective-permute-done.2.refs_1_.refs_2_ = bf16[80,512]{1,0:T(8,128)(2,1)S(1)} collective-permute-done((bf16[80,512]{1,0:T(8,128)(2,1)S(1)}, bf16[80,512]{1,0:T(8,128)(2,1)S(1)}, u32[]{:S(2)}, u32[]{:S(2)}) %collective-permute-start.2) | collective-permute-done | bytes 81952 | tf_op jit(solution)/shard_map/ppermute | solution.py:422
  17.4 0.0 collective-permute-start.8
  17.4 0.0 collective-permute-done.1.refs_7_.refs_6_
  17.4 1.6 %collective-permute-done.5.refs_0_ = bf16[32,1024]{1,0:T(8,128)(2,1)S(1)} collective-permute-done((bf16[32,1024]{1,0:T(8,128)(2,1)S(1)}, bf16[32,1024]{1,0:T(8,128)(2,1)S(1)}, u32[]{:S(2)}, u32[]{:S(2)}) %collective-permute-start.5) | collective-permute-done | bytes 65568 | tf_op jit(solution)/shard_map/ppermute | solution.py:422
  19.0 0.5 %collective-permute-start.9 = (bf16[160,512]{1,0:T(8,128)(2,1)S(1)}, bf16[160,512]{1,0:T(8,128)(2,1)S(1)}, u32[]{:S(2)}, u32[]{:S(2)}) collective-permute-start(bf16[160,512]{1,0:T(8,128)(2,1)S(1)} %collective-permute-done.1.refs_7_.refs_6_), channel_id=1, source_target_pairs={{0,2},{2,0},{4,6},{6,4},{8,10},{10,8},{12,14},{14,12},{16,18},{18,... | collective-permute-start | bytes 491528 | tf_op jit(solution)/shard_map/ppermute | solution.py:422
  19.5 0.3 join_far.1.refs_0_
  19.8 0.1 collective-permute-start.3
  19.9 1.2 %collective-permute-done.3.refs_1_ = bf16[48,512]{1,0:T(8,128)(2,1)S(1)} collective-permute-done((bf16[48,512]{1,0:T(8,128)(2,1)S(1)}, bf16[48,512]{1,0:T(8,128)(2,1)S(1)}, u32[]{:S(2)}, u32[]{:S(2)}) %collective-permute-start.3) | collective-permute-done | bytes 49184 | tf_op jit(solution)/shard_map/ppermute | solution.py:422
  21.1 0.3 join_core.1.refs_2_
  21.4 1.1 %prefill_partials.2 = bf16[32,1152]{1,0:T(8,128)(2,1)S(1)} custom-call(s32[8,128]{1,0:T(8,128)S(1)} %broadcast_in_dim.3.off_ref, bf16[32,1024]{1,0:T(8,128)(2,1)S(1)} %collective-permute-done.5.refs_0_, bf16[160,512]{1,0:T(8,128)(2,1)S(1)} %pad_maximum_fusion.refs_1_.refs_0_, bf16[160,512]{1,0:T(8,128)(2,1)S(1)} %collective-permute-done.6.refs_2_.refs_1_, ...), custom_call_target="tpu_custom_call" | custom-call | flops 167772160 | bytes 4194304 | tf_op jit(solution)/shard_map/prefill_partials/pallas_call | solution.py:308
  22.5 1.7 %collective-permute-start.11 = (bf16[80,512]{1,0:T(8,128)(2,1)S(1)}, bf16[80,512]{1,0:T(8,128)(2,1)S(1)}, u32[]{:S(2)}, u32[]{:S(2)}) collective-permute-start(bf16[80,512]{1,0:T(8,128)(2,1)S(1)} %join_core.1.refs_2_), channel_id=1, source_target_pairs={{0,4},{2,6},{4,0},{6,2},{8,12},{10,14},{12,8},{14,10},{16,20},{18,... | collective-permute-start | bytes 245768 | tf_op jit(solution)/shard_map/ppermute | solution.py:422
  24.3 1.8 %collective-permute-start.13 = (bf16[80,512]{1,0:T(8,128)(2,1)S(1)}, bf16[80,512]{1,0:T(8,128)(2,1)S(1)}, u32[]{:S(2)}, u32[]{:S(2)}) collective-permute-start(bf16[80,512]{1,0:T(8,128)(2,1)S(1)} %join_core.1.refs_2_), channel_id=1, source_target_pairs={{0,12},{2,14},{4,8},{6,10},{8,4},{10,6},{12,0},{14,2},{16,28},{18,... | collective-permute-start | bytes 245768 | tf_op jit(solution)/shard_map/ppermute | solution.py:422
  26.1 1.4 %collective-permute-start.10 = (bf16[32,1152]{1,0:T(8,128)(2,1)S(1)}, bf16[32,1152]{1,0:T(8,128)(2,1)S(1)}, u32[]{:S(2)}, u32[]{:S(2)}) collective-permute-start(bf16[32,1152]{1,0:T(8,128)(2,1)S(1)} %prefill_partials.2), channel_id=1, source_target_pairs={{0,16},{2,18},{4,20},{6,22},{8,24},{10,26},{12,28},{14,30},{16,0},... | collective-permute-start | bytes 221192 | tf_op jit(solution)/shard_map/ppermute | solution.py:422
  27.5 1.1 %prefill_partials.3.refs_0_ = bf16[32,1152]{1,0:T(8,128)(2,1)S(1)} custom-call(s32[8,128]{1,0:T(8,128)S(1)} %broadcast_in_dim.3.off_ref, bf16[32,1024]{1,0:T(8,128)(2,1)S(1)} %get-tuple-element.34.refs_0_, bf16[160,512]{1,0:T(8,128)(2,1)S(1)} %pad_maximum_fusion.refs_1_.refs_0_, bf16[160,512]{1,0:T(8,128)(2,1)S(1)} %collective-permute-done.6.refs_2_.refs_1_, ...), custom_call_target="tpu_custom_call" | custom-call | flops 167772160 | bytes 4194304 | tf_op jit(solution)/shard_map/prefill_partials/pallas_call | solution.py:308
  28.6 1.6 %collective-permute-done.12.refs_4_ = bf16[80,512]{1,0:T(8,128)(2,1)S(1)} collective-permute-done((bf16[80,512]{1,0:T(8,128)(2,1)S(1)}, bf16[80,512]{1,0:T(8,128)(2,1)S(1)}, u32[]{:S(2)}, u32[]{:S(2)}) %collective-permute-start.12) | collective-permute-done | bytes 81952 | tf_op jit(solution)/shard_map/ppermute | solution.py:422
  30.1 0.9 %collective-permute-done.13.refs_5_ = bf16[80,512]{1,0:T(8,128)(2,1)S(1)} collective-permute-done((bf16[80,512]{1,0:T(8,128)(2,1)S(1)}, bf16[80,512]{1,0:T(8,128)(2,1)S(1)}, u32[]{:S(2)}, u32[]{:S(2)}) %collective-permute-start.13) | collective-permute-done | bytes 81952 | tf_op jit(solution)/shard_map/ppermute | solution.py:422
  31.1 0.1 collective-permute-start.15
  31.1 0.7 %collective-permute-done.10.refs_1_ = bf16[32,1152]{1,0:T(8,128)(2,1)S(1)} collective-permute-done((bf16[32,1152]{1,0:T(8,128)(2,1)S(1)}, bf16[32,1152]{1,0:T(8,128)(2,1)S(1)}, u32[]{:S(2)}, u32[]{:S(2)}) %collective-permute-start.10) | collective-permute-done | bytes 73760 | tf_op jit(solution)/shard_map/ppermute | solution.py:422
  31.9 0.3 join_parts.1.refs_0_
  32.2 1.7 %collective-permute-start.14 = (bf16[48,1024]{1,0:T(8,128)(2,1)S(1)}, bf16[48,1024]{1,0:T(8,128)(2,1)S(1)}, u32[]{:S(2)}, u32[]{:S(2)}) collective-permute-start(bf16[48,1024]{1,0:T(8,128)(2,1)S(1)} %join_parts.1.refs_0_), channel_id=1, source_target_pairs={{0,1},{1,0},{2,3},{3,2},{4,5},{5,4},{6,7},{7,6},{8,9},{9,8},{10,11... | collective-permute-start | bytes 294920 | tf_op jit(solution)/shard_map/ppermute | solution.py:465
  33.9 1.7 %update_cache.1 = bf16[1,128,512]{2,1,0:T(8,128)(2,1)} custom-call(s32[8,128]{1,0:T(8,128)S(1)} %broadcast_in_dim.3.off_ref, bf16[1,128,512]{2,1,0:T(8,128)(2,1)} %cache_hbm.3, bf16[128,512]{1,0:T(8,128)(2,1)S(1)} %pad_maximum_fusion.1.near_ref, bf16[128,512]{1,0:T(8,128)(2,1)S(1)} %collective-permute-done.15.beside_ref, ...), custom_call_target="tpu_custom_call" | custom-call | tf_op jit(solution)/shard_map/update_cache/pallas_call | solution.py:363
  35.6 1.3 %collective-permute-done.14.refs_1_ = bf16[48,1024]{1,0:T(8,128)(2,1)S(1)} collective-permute-done((bf16[48,1024]{1,0:T(8,128)(2,1)S(1)}, bf16[48,1024]{1,0:T(8,128)(2,1)S(1)}, u32[]{:S(2)}, u32[]{:S(2)}) %collective-permute-start.14) | collective-permute-done | bytes 98336 | tf_op jit(solution)/shard_map/ppermute | solution.py:465
  36.9 0.8 %route_outputs.1 = (bf16[1,32,1024]{2,1,0:T(8,128)(2,1)}, bf16[16,1024]{1,0:T(8,128)(2,1)}) custom-call(f32[2,24,128]{2,1,0:T(8,128)S(1)} %get-tuple-element.24.route_ref, bf16[48,1024]{1,0:T(8,128)(2,1)S(1)} %join_parts.1.refs_0_, bf16[48,1024]{1,0:T(8,128)(2,1)S(1)} %collective-permute-done.14.refs_1_), custom_call_target="tpu_custom_call" | custom-call | tf_op jit(solution)/shard_map/route_outputs/pallas_call | solution.py:391
  (17 shorter events, 0.1 us)
Async XLA Ops:
  0.6 11.4 %copy-start = (bf16[1,32,1024]{2,1,0:T(8,128)(2,1)S(1)}, bf16[1,32,1024]{2,1,0:T(8,128)(2,1)}, u32[]{:S(2)}) copy-start(bf16[1,32,1024]{2,1,0:T(8,128)(2,1)} %pre_q_hbm.1) | copy-start | bytes 196612
  1.6 11.2 %collective-permute-start = (bf16[160,512]{1,0:T(8,128)(2,1)S(1)}, bf16[160,512]{1,0:T(8,128)(2,1)S(1)}, u32[]{:S(2)}, u32[]{:S(2)}) collective-permute-start(bf16[160,512]{1,0:T(8,128)(2,1)S(1)} %pad_maximum_fusion.refs_1_.refs_0_), channel_id=1, source_target_pairs={{0,8},{2,10},{4,12},{6,14},{8,0},{10,2},{12,4},{14,6},{16,24},{18,... | collective-permute-start | bytes 491528 | tf_op jit(solution)/shard_map/ppermute | solution.py:422
  4.7 12.7 %collective-permute-start.1 = (bf16[160,512]{1,0:T(8,128)(2,1)S(1)}, bf16[160,512]{1,0:T(8,128)(2,1)S(1)}, u32[]{:S(2)}, u32[]{:S(2)}) collective-permute-start(bf16[160,512]{1,0:T(8,128)(2,1)S(1)} %pad_maximum_fusion.refs_1_.refs_0_), channel_id=1, source_target_pairs={{0,12},{2,14},{4,8},{6,10},{8,4},{10,6},{12,0},{14,2},{16,28},{18,... | collective-permute-start | bytes 491528 | tf_op jit(solution)/shard_map/ppermute | solution.py:422
  6.1 12.9 %collective-permute-start.4 = (bf16[160,512]{1,0:T(8,128)(2,1)S(1)}, bf16[160,512]{1,0:T(8,128)(2,1)S(1)}, u32[]{:S(2)}, u32[]{:S(2)}) collective-permute-start(bf16[160,512]{1,0:T(8,128)(2,1)S(1)} %pad_maximum_fusion.refs_1_.refs_0_), channel_id=1, source_target_pairs={{0,4},{2,6},{4,0},{6,2},{8,12},{10,14},{12,8},{14,10},{16,20},{18,... | collective-permute-start | bytes 491528 | tf_op jit(solution)/shard_map/ppermute | solution.py:422
  9.1 8.4 %collective-permute-start.2 = (bf16[80,512]{1,0:T(8,128)(2,1)S(1)}, bf16[80,512]{1,0:T(8,128)(2,1)S(1)}, u32[]{:S(2)}, u32[]{:S(2)}) collective-permute-start(bf16[80,512]{1,0:T(8,128)(2,1)S(1)} %get-tuple-element.25.refs_0_), channel_id=1, source_target_pairs={{0,16},{2,18},{4,20},{6,22},{8,24},{10,26},{12,28},{14,30},{16,0},... | collective-permute-start | bytes 245768 | tf_op jit(solution)/shard_map/ppermute | solution.py:422
  12.1 6.9 %collective-permute-start.5 = (bf16[32,1024]{1,0:T(8,128)(2,1)S(1)}, bf16[32,1024]{1,0:T(8,128)(2,1)S(1)}, u32[]{:S(2)}, u32[]{:S(2)}) collective-permute-start(bf16[32,1024]{1,0:T(8,128)(2,1)S(1)} %bitcast.7), channel_id=1, source_target_pairs={{0,16},{2,18},{4,20},{6,22},{8,24},{10,26},{12,28},{14,30},{16,0},... | collective-permute-start | bytes 196616 | tf_op jit(solution)/shard_map/ppermute | solution.py:422
  12.8 8.6 %collective-permute-start.6 = (bf16[160,512]{1,0:T(8,128)(2,1)S(1)}, bf16[160,512]{1,0:T(8,128)(2,1)S(1)}, u32[]{:S(2)}, u32[]{:S(2)}) collective-permute-start(bf16[160,512]{1,0:T(8,128)(2,1)S(1)} %pad_maximum_fusion.refs_1_.refs_0_), channel_id=1, source_target_pairs={{0,2},{2,0},{4,6},{6,4},{8,10},{10,8},{12,14},{14,12},{16,18},{18,... | collective-permute-start | bytes 491528 | tf_op jit(solution)/shard_map/ppermute | solution.py:422
  17.4 4.0 %collective-permute-start.8 = (bf16[160,512]{1,0:T(8,128)(2,1)S(1)}, bf16[160,512]{1,0:T(8,128)(2,1)S(1)}, u32[]{:S(2)}, u32[]{:S(2)}) collective-permute-start(bf16[160,512]{1,0:T(8,128)(2,1)S(1)} %collective-permute-done.refs_5_.refs_4_), channel_id=1, source_target_pairs={{0,2},{2,0},{4,6},{6,4},{8,10},{10,8},{12,14},{14,12},{16,18},{18,... | collective-permute-start | bytes 491528 | tf_op jit(solution)/shard_map/ppermute | solution.py:422
  19.0 2.4 %collective-permute-start.7 = (bf16[160,512]{1,0:T(8,128)(2,1)S(1)}, bf16[160,512]{1,0:T(8,128)(2,1)S(1)}, u32[]{:S(2)}, u32[]{:S(2)}) collective-permute-start(bf16[160,512]{1,0:T(8,128)(2,1)S(1)} %collective-permute-done.4.refs_3_.refs_2_), channel_id=1, source_target_pairs={{0,2},{2,0},{4,6},{6,4},{8,10},{10,8},{12,14},{14,12},{16,18},{18,... | collective-permute-start | bytes 491528 | tf_op jit(solution)/shard_map/ppermute | solution.py:422
  19.0 2.4 %collective-permute-start.9 = (bf16[160,512]{1,0:T(8,128)(2,1)S(1)}, bf16[160,512]{1,0:T(8,128)(2,1)S(1)}, u32[]{:S(2)}, u32[]{:S(2)}) collective-permute-start(bf16[160,512]{1,0:T(8,128)(2,1)S(1)} %collective-permute-done.1.refs_7_.refs_6_), channel_id=1, source_target_pairs={{0,2},{2,0},{4,6},{6,4},{8,10},{10,8},{12,14},{14,12},{16,18},{18,... | collective-permute-start | bytes 491528 | tf_op jit(solution)/shard_map/ppermute | solution.py:422
  19.8 1.3 %collective-permute-start.3 = (bf16[48,512]{1,0:T(8,128)(2,1)S(1)}, bf16[48,512]{1,0:T(8,128)(2,1)S(1)}, u32[]{:S(2)}, u32[]{:S(2)}) collective-permute-start(bf16[48,512]{1,0:T(8,128)(2,1)S(1)} %join_far.1.refs_0_), channel_id=1, source_target_pairs={{0,2},{2,0},{4,6},{6,4},{8,10},{10,8},{12,14},{14,12},{16,18},{18,... | collective-permute-start | bytes 147464 | tf_op jit(solution)/shard_map/ppermute | solution.py:422
  22.5 6.1 %collective-permute-start.11 = (bf16[80,512]{1,0:T(8,128)(2,1)S(1)}, bf16[80,512]{1,0:T(8,128)(2,1)S(1)}, u32[]{:S(2)}, u32[]{:S(2)}) collective-permute-start(bf16[80,512]{1,0:T(8,128)(2,1)S(1)} %join_core.1.refs_2_), channel_id=1, source_target_pairs={{0,4},{2,6},{4,0},{6,2},{8,12},{10,14},{12,8},{14,10},{16,20},{18,... | collective-permute-start | bytes 245768 | tf_op jit(solution)/shard_map/ppermute | solution.py:422
  24.2 5.9 %collective-permute-start.12 = (bf16[80,512]{1,0:T(8,128)(2,1)S(1)}, bf16[80,512]{1,0:T(8,128)(2,1)S(1)}, u32[]{:S(2)}, u32[]{:S(2)}) collective-permute-start(bf16[80,512]{1,0:T(8,128)(2,1)S(1)} %join_core.1.refs_2_), channel_id=1, source_target_pairs={{0,8},{2,10},{4,12},{6,14},{8,0},{10,2},{12,4},{14,6},{16,24},{18,... | collective-permute-start | bytes 245768 | tf_op jit(solution)/shard_map/ppermute | solution.py:422
  24.3 6.8 %collective-permute-start.13 = (bf16[80,512]{1,0:T(8,128)(2,1)S(1)}, bf16[80,512]{1,0:T(8,128)(2,1)S(1)}, u32[]{:S(2)}, u32[]{:S(2)}) collective-permute-start(bf16[80,512]{1,0:T(8,128)(2,1)S(1)} %join_core.1.refs_2_), channel_id=1, source_target_pairs={{0,12},{2,14},{4,8},{6,10},{8,4},{10,6},{12,0},{14,2},{16,28},{18,... | collective-permute-start | bytes 245768 | tf_op jit(solution)/shard_map/ppermute | solution.py:422
  26.1 5.8 %collective-permute-start.10 = (bf16[32,1152]{1,0:T(8,128)(2,1)S(1)}, bf16[32,1152]{1,0:T(8,128)(2,1)S(1)}, u32[]{:S(2)}, u32[]{:S(2)}) collective-permute-start(bf16[32,1152]{1,0:T(8,128)(2,1)S(1)} %prefill_partials.2), channel_id=1, source_target_pairs={{0,16},{2,18},{4,20},{6,22},{8,24},{10,26},{12,28},{14,30},{16,0},... | collective-permute-start | bytes 221192 | tf_op jit(solution)/shard_map/ppermute | solution.py:422
  31.1 2.8 %collective-permute-start.15 = (bf16[128,512]{1,0:T(8,128)(2,1)S(1)}, bf16[128,512]{1,0:T(8,128)(2,1)S(1)}, u32[]{:S(2)}, u32[]{:S(2)}) collective-permute-start(bf16[128,512]{1,0:T(8,128)(2,1)S(1)} %pad_maximum_fusion.1.near_ref), channel_id=1, source_target_pairs={{0,2},{2,0},{4,6},{6,4},{8,10},{10,8},{12,14},{14,12},{16,18},{18,... | collective-permute-start | bytes 393224 | tf_op jit(solution)/shard_map/ppermute | solution.py:422
  32.2 4.7 %collective-permute-start.14 = (bf16[48,1024]{1,0:T(8,128)(2,1)S(1)}, bf16[48,1024]{1,0:T(8,128)(2,1)S(1)}, u32[]{:S(2)}, u32[]{:S(2)}) collective-permute-start(bf16[48,1024]{1,0:T(8,128)(2,1)S(1)} %join_parts.1.refs_0_), channel_id=1, source_target_pairs={{0,1},{1,0},{2,3},{3,2},{4,5},{5,4},{6,7},{7,6},{8,9},{9,8},{10,11... | collective-permute-start | bytes 294920 | tf_op jit(solution)/shard_map/ppermute | solution.py:465

commit v20 on v19

--- a/solution.py
+++ b/solution.py
@@ -25,7 +25,7 @@
 
 KVW = 2 * KW
 BLK = ("hi", "quad")
-CHUNKS = 4
+CHUNKS = 2
 TILE = 16
 
 HBM = pl.BlockSpec(memory_space=pltpu.HBM)

time: 37.8 us -> 37.8 us (level)
  no operation moved by 1% of the time
where the time goes in v20:
time: 37.8 us; the launch traced here: 37.6 us
  starting transfers between devices  15.1 us (40%)
  waiting for transfers between devices  11.8 us (31%)
  Pallas kernels  8.27 us (22%)
  between operations  1.44 us (4%)
  other arithmetic  0.98 us (3%)
    ppermute x15, starting transfers between devices, swap(): return lax.ppermute(array, BLK, [(i, i ^ distance) for i in range(blk)])  13.4 us
    ppermute x15, waiting for transfers between devices, swap(): return lax.ppermute(array, BLK, [(i, i ^ distance) for i in range(blk)])  10.5 us
    pallas_call x1, Pallas kernels, decode_partials(): pl.pallas_call(decode_kernel, in_specs=[HBM] * len(inputs), out_specs=[HB...  2.79 us
    pallas_call x2, Pallas kernels, prefill_partials(): pl.pallas_call(functools.partial(prefill_kernel, sets, ctx), in_specs=[VM...  2.13 us
    pallas_call x1, Pallas kernels, update_cache(): pl.pallas_call(functools.partial(update_kernel, tokens, sets), in_specs=[...  1.71 us
    ppermute x1, starting transfers between devices, per_device(): held = [attended, lax.ppermute(attended, 'req', [(0, 1), (1, 0)])]  1.68 us
    ppermute x1, waiting for transfers between devices, per_device(): held = [attended, lax.ppermute(attended, 'req', [(0, 1), (1, 0)])]  1.27 us
    concatenate x1, other arithmetic, per_device(): table = jnp.concatenate([prefill_cache[0], new_prefill[0]], axis=0)  0.97 us
  transfers between devices with their start and end apart: 16, of which 7 were waited for; matrix products, arithmetic and copies ran while one was open for 0% of the time, Pallas kernels for 17%

profile of v20, /device:TPU:0, one launch (start us, length us, event | category | flops | bytes accessed | tf_op | source)
XLA Modules:
  0.0 37.6 jit_solution(14781633995427050337)
XLA Ops:
  0.6 0.0 copy-start
  0.6 1.0 %pad_maximum_fusion.refs_1_.refs_0_ = bf16[160,512]{1,0:T(8,128)(2,1)S(1)} fusion(bf16[32,512]{1,0:T(8,128)(2,1)} %bitcast.6, bf16[128,512]{1,0:T(8,128)(2,1)} %bitcast.5), kind=kLoop, calls=%fused_computation | loop fusion | flops 327680 | bytes 327680 | tf_op jit(solution)/shard_map/concatenate | solution.py:428
  1.6 3.1 %collective-permute-start = (bf16[160,512]{1,0:T(8,128)(2,1)S(1)}, bf16[160,512]{1,0:T(8,128)(2,1)S(1)}, u32[]{:S(2)}, u32[]{:S(2)}) collective-permute-start(bf16[160,512]{1,0:T(8,128)(2,1)S(1)} %pad_maximum_fusion.refs_1_.refs_0_), channel_id=1, source_target_pairs={{0,8},{2,10},{4,12},{6,14},{8,0},{10,2},{12,4},{14,6},{16,24},{18,... | collective-permute-start | bytes 491528 | tf_op jit(solution)/shard_map/ppermute | solution.py:422
  4.7 1.4 %collective-permute-start.1 = (bf16[160,512]{1,0:T(8,128)(2,1)S(1)}, bf16[160,512]{1,0:T(8,128)(2,1)S(1)}, u32[]{:S(2)}, u32[]{:S(2)}) collective-permute-start(bf16[160,512]{1,0:T(8,128)(2,1)S(1)} %pad_maximum_fusion.refs_1_.refs_0_), channel_id=1, source_target_pairs={{0,12},{2,14},{4,8},{6,10},{8,4},{10,6},{12,0},{14,2},{16,28},{18,... | collective-permute-start | bytes 491528 | tf_op jit(solution)/shard_map/ppermute | solution.py:422
  6.1 0.2 collective-permute-start.4
  6.2 2.8 %decode_partials.1 = (bf16[16,128,512]{2,1,0:T(8,128)(2,1)}, bf16[80,512]{1,0:T(8,128)(2,1)S(1)}, bf16[32,1024]{1,0:T(8,128)(2,1)S(1)}, f32[2,24,128]{2,1,0:T(8,128)S(1)}) custom-call(s32[16]{0:T(128)} %len_hbm.1, s32[34]{0:T(128)} %deal_hbm.1, bf16[16,1024]{1,0:T(8,128)(2,1)} %q_hbm.1, bf16[16,512]{1,0:T(8,128)(2,1)} %new_hbm.1, ...), custom_call_target="tpu_custom_call" | custom-call | flops 8388608 | bytes 4194304 | tf_op jit(solution)/shard_map/decode_partials/pallas_call | solution.py:198
  9.0 3.0 %collective-permute-start.2 = (bf16[80,512]{1,0:T(8,128)(2,1)S(1)}, bf16[80,512]{1,0:T(8,128)(2,1)S(1)}, u32[]{:S(2)}, u32[]{:S(2)}) collective-permute-start(bf16[80,512]{1,0:T(8,128)(2,1)S(1)} %get-tuple-element.25.refs_0_), channel_id=1, source_target_pairs={{0,16},{2,18},{4,20},{6,22},{8,24},{10,26},{12,28},{14,30},{16,0},... | collective-permute-start | bytes 245768 | tf_op jit(solution)/shard_map/ppermute | solution.py:422
  12.1 0.1 collective-permute-start.5
  12.8 0.0 collective-permute-done.refs_5_.refs_4_
  12.8 0.1 collective-permute-start.6
  12.9 4.5 %collective-permute-done.2.refs_1_.refs_2_ = bf16[80,512]{1,0:T(8,128)(2,1)S(1)} collective-permute-done((bf16[80,512]{1,0:T(8,128)(2,1)S(1)}, bf16[80,512]{1,0:T(8,128)(2,1)S(1)}, u32[]{:S(2)}, u32[]{:S(2)}) %collective-permute-start.2) | collective-permute-done | bytes 81952 | tf_op jit(solution)/shard_map/ppermute | solution.py:422
  17.4 0.0 collective-permute-start.8
  17.4 1.6 %collective-permute-done.5.refs_0_ = bf16[32,1024]{1,0:T(8,128)(2,1)S(1)} collective-permute-done((bf16[32,1024]{1,0:T(8,128)(2,1)S(1)}, bf16[32,1024]{1,0:T(8,128)(2,1)S(1)}, u32[]{:S(2)}, u32[]{:S(2)}) %collective-permute-start.5) | collective-permute-done | bytes 65568 | tf_op jit(solution)/shard_map/ppermute | solution.py:422
  19.0 0.5 %collective-permute-start.9 = (bf16[160,512]{1,0:T(8,128)(2,1)S(1)}, bf16[160,512]{1,0:T(8,128)(2,1)S(1)}, u32[]{:S(2)}, u32[]{:S(2)}) collective-permute-start(bf16[160,512]{1,0:T(8,128)(2,1)S(1)} %collective-permute-done.1.refs_7_.refs_6_), channel_id=1, source_target_pairs={{0,2},{2,0},{4,6},{6,4},{8,10},{10,8},{12,14},{14,12},{16,18},{18,... | collective-permute-start | bytes 491528 | tf_op jit(solution)/shard_map/ppermute | solution.py:422
  19.5 0.3 join_far.1.refs_0_
  19.8 0.1 collective-permute-start.3
  19.9 1.2 %collective-permute-done.3.refs_1_ = bf16[48,512]{1,0:T(8,128)(2,1)S(1)} collective-permute-done((bf16[48,512]{1,0:T(8,128)(2,1)S(1)}, bf16[48,512]{1,0:T(8,128)(2,1)S(1)}, u32[]{:S(2)}, u32[]{:S(2)}) %collective-permute-start.3) | collective-permute-done | bytes 49184 | tf_op jit(solution)/shard_map/ppermute | solution.py:422
  21.1 0.3 join_core.1.refs_2_
  21.4 1.1 %prefill_partials.2 = bf16[32,1152]{1,0:T(8,128)(2,1)S(1)} custom-call(s32[8,128]{1,0:T(8,128)S(1)} %broadcast_in_dim.3.off_ref, bf16[32,1024]{1,0:T(8,128)(2,1)S(1)} %collective-permute-done.5.refs_0_, bf16[160,512]{1,0:T(8,128)(2,1)S(1)} %pad_maximum_fusion.refs_1_.refs_0_, bf16[160,512]{1,0:T(8,128)(2,1)S(1)} %collective-permute-done.6.refs_2_.refs_1_, ...), custom_call_target="tpu_custom_call" | custom-call | flops 167772160 | bytes 4194304 | tf_op jit(solution)/shard_map/prefill_partials/pallas_call | solution.py:308
  22.5 1.7 %collective-permute-start.11 = (bf16[80,512]{1,0:T(8,128)(2,1)S(1)}, bf16[80,512]{1,0:T(8,128)(2,1)S(1)}, u32[]{:S(2)}, u32[]{:S(2)}) collective-permute-start(bf16[80,512]{1,0:T(8,128)(2,1)S(1)} %join_core.1.refs_2_), channel_id=1, source_target_pairs={{0,4},{2,6},{4,0},{6,2},{8,12},{10,14},{12,8},{14,10},{16,20},{18,... | collective-permute-start | bytes 245768 | tf_op jit(solution)/shard_map/ppermute | solution.py:422
  24.2 1.8 %collective-permute-start.13 = (bf16[80,512]{1,0:T(8,128)(2,1)S(1)}, bf16[80,512]{1,0:T(8,128)(2,1)S(1)}, u32[]{:S(2)}, u32[]{:S(2)}) collective-permute-start(bf16[80,512]{1,0:T(8,128)(2,1)S(1)} %join_core.1.refs_2_), channel_id=1, source_target_pairs={{0,12},{2,14},{4,8},{6,10},{8,4},{10,6},{12,0},{14,2},{16,28},{18,... | collective-permute-start | bytes 245768 | tf_op jit(solution)/shard_map/ppermute | solution.py:422
  26.1 1.4 %collective-permute-start.10 = (bf16[32,1152]{1,0:T(8,128)(2,1)S(1)}, bf16[32,1152]{1,0:T(8,128)(2,1)S(1)}, u32[]{:S(2)}, u32[]{:S(2)}) collective-permute-start(bf16[32,1152]{1,0:T(8,128)(2,1)S(1)} %prefill_partials.2), channel_id=1, source_target_pairs={{0,16},{2,18},{4,20},{6,22},{8,24},{10,26},{12,28},{14,30},{16,0},... | collective-permute-start | bytes 221192 | tf_op jit(solution)/shard_map/ppermute | solution.py:422
  27.5 1.1 %prefill_partials.3.refs_0_ = bf16[32,1152]{1,0:T(8,128)(2,1)S(1)} custom-call(s32[8,128]{1,0:T(8,128)S(1)} %broadcast_in_dim.3.off_ref, bf16[32,1024]{1,0:T(8,128)(2,1)S(1)} %get-tuple-element.34.refs_0_, bf16[160,512]{1,0:T(8,128)(2,1)S(1)} %pad_maximum_fusion.refs_1_.refs_0_, bf16[160,512]{1,0:T(8,128)(2,1)S(1)} %collective-permute-done.6.refs_2_.refs_1_, ...), custom_call_target="tpu_custom_call" | custom-call | flops 167772160 | bytes 4194304 | tf_op jit(solution)/shard_map/prefill_partials/pallas_call | solution.py:308
  28.6 1.5 %collective-permute-done.12.refs_4_ = bf16[80,512]{1,0:T(8,128)(2,1)S(1)} collective-permute-done((bf16[80,512]{1,0:T(8,128)(2,1)S(1)}, bf16[80,512]{1,0:T(8,128)(2,1)S(1)}, u32[]{:S(2)}, u32[]{:S(2)}) %collective-permute-start.12) | collective-permute-done | bytes 81952 | tf_op jit(solution)/shard_map/ppermute | solution.py:422
  30.1 0.9 %collective-permute-done.13.refs_5_ = bf16[80,512]{1,0:T(8,128)(2,1)S(1)} collective-permute-done((bf16[80,512]{1,0:T(8,128)(2,1)S(1)}, bf16[80,512]{1,0:T(8,128)(2,1)S(1)}, u32[]{:S(2)}, u32[]{:S(2)}) %collective-permute-start.13) | collective-permute-done | bytes 81952 | tf_op jit(solution)/shard_map/ppermute | solution.py:422
  31.0 0.1 collective-permute-start.15
  31.1 0.8 %collective-permute-done.10.refs_1_ = bf16[32,1152]{1,0:T(8,128)(2,1)S(1)} collective-permute-done((bf16[32,1152]{1,0:T(8,128)(2,1)S(1)}, bf16[32,1152]{1,0:T(8,128)(2,1)S(1)}, u32[]{:S(2)}, u32[]{:S(2)}) %collective-permute-start.10) | collective-permute-done | bytes 73760 | tf_op jit(solution)/shard_map/ppermute | solution.py:422
  31.9 0.3 join_parts.1.refs_0_
  32.2 1.7 %collective-permute-start.14 = (bf16[48,1024]{1,0:T(8,128)(2,1)S(1)}, bf16[48,1024]{1,0:T(8,128)(2,1)S(1)}, u32[]{:S(2)}, u32[]{:S(2)}) collective-permute-start(bf16[48,1024]{1,0:T(8,128)(2,1)S(1)} %join_parts.1.refs_0_), channel_id=1, source_target_pairs={{0,1},{1,0},{2,3},{3,2},{4,5},{5,4},{6,7},{7,6},{8,9},{9,8},{10,11... | collective-permute-start | bytes 294920 | tf_op jit(solution)/shard_map/ppermute | solution.py:465
  33.9 1.7 %update_cache.1 = bf16[1,128,512]{2,1,0:T(8,128)(2,1)} custom-call(s32[8,128]{1,0:T(8,128)S(1)} %broadcast_in_dim.3.off_ref, bf16[1,128,512]{2,1,0:T(8,128)(2,1)} %cache_hbm.3, bf16[128,512]{1,0:T(8,128)(2,1)S(1)} %pad_maximum_fusion.1.near_ref, bf16[128,512]{1,0:T(8,128)(2,1)S(1)} %collective-permute-done.15.beside_ref, ...), custom_call_target="tpu_custom_call" | custom-call | tf_op jit(solution)/shard_map/update_cache/pallas_call | solution.py:363
  35.6 1.3 %collective-permute-done.14.refs_1_ = bf16[48,1024]{1,0:T(8,128)(2,1)S(1)} collective-permute-done((bf16[48,1024]{1,0:T(8,128)(2,1)S(1)}, bf16[48,1024]{1,0:T(8,128)(2,1)S(1)}, u32[]{:S(2)}, u32[]{:S(2)}) %collective-permute-start.14) | collective-permute-done | bytes 98336 | tf_op jit(solution)/shard_map/ppermute | solution.py:465
  36.9 0.8 %route_outputs.1 = (bf16[1,32,1024]{2,1,0:T(8,128)(2,1)}, bf16[16,1024]{1,0:T(8,128)(2,1)}) custom-call(f32[2,24,128]{2,1,0:T(8,128)S(1)} %get-tuple-element.24.route_ref, bf16[48,1024]{1,0:T(8,128)(2,1)S(1)} %join_parts.1.refs_0_, bf16[48,1024]{1,0:T(8,128)(2,1)S(1)} %collective-permute-done.14.refs_1_), custom_call_target="tpu_custom_call" | custom-call | tf_op jit(solution)/shard_map/route_outputs/pallas_call | solution.py:391
  (17 shorter events, 0.1 us)
Async XLA Ops:
  0.6 11.4 %copy-start = (bf16[1,32,1024]{2,1,0:T(8,128)(2,1)S(1)}, bf16[1,32,1024]{2,1,0:T(8,128)(2,1)}, u32[]{:S(2)}) copy-start(bf16[1,32,1024]{2,1,0:T(8,128)(2,1)} %pre_q_hbm.1) | copy-start | bytes 196612
  1.6 11.2 %collective-permute-start = (bf16[160,512]{1,0:T(8,128)(2,1)S(1)}, bf16[160,512]{1,0:T(8,128)(2,1)S(1)}, u32[]{:S(2)}, u32[]{:S(2)}) collective-permute-start(bf16[160,512]{1,0:T(8,128)(2,1)S(1)} %pad_maximum_fusion.refs_1_.refs_0_), channel_id=1, source_target_pairs={{0,8},{2,10},{4,12},{6,14},{8,0},{10,2},{12,4},{14,6},{16,24},{18,... | collective-permute-start | bytes 491528 | tf_op jit(solution)/shard_map/ppermute | solution.py:422
  4.7 12.7 %collective-permute-start.1 = (bf16[160,512]{1,0:T(8,128)(2,1)S(1)}, bf16[160,512]{1,0:T(8,128)(2,1)S(1)}, u32[]{:S(2)}, u32[]{:S(2)}) collective-permute-start(bf16[160,512]{1,0:T(8,128)(2,1)S(1)} %pad_maximum_fusion.refs_1_.refs_0_), channel_id=1, source_target_pairs={{0,12},{2,14},{4,8},{6,10},{8,4},{10,6},{12,0},{14,2},{16,28},{18,... | collective-permute-start | bytes 491528 | tf_op jit(solution)/shard_map/ppermute | solution.py:422
  6.1 12.9 %collective-permute-start.4 = (bf16[160,512]{1,0:T(8,128)(2,1)S(1)}, bf16[160,512]{1,0:T(8,128)(2,1)S(1)}, u32[]{:S(2)}, u32[]{:S(2)}) collective-permute-start(bf16[160,512]{1,0:T(8,128)(2,1)S(1)} %pad_maximum_fusion.refs_1_.refs_0_), channel_id=1, source_target_pairs={{0,4},{2,6},{4,0},{6,2},{8,12},{10,14},{12,8},{14,10},{16,20},{18,... | collective-permute-start | bytes 491528 | tf_op jit(solution)/shard_map/ppermute | solution.py:422
  9.0 8.4 %collective-permute-start.2 = (bf16[80,512]{1,0:T(8,128)(2,1)S(1)}, bf16[80,512]{1,0:T(8,128)(2,1)S(1)}, u32[]{:S(2)}, u32[]{:S(2)}) collective-permute-start(bf16[80,512]{1,0:T(8,128)(2,1)S(1)} %get-tuple-element.25.refs_0_), channel_id=1, source_target_pairs={{0,16},{2,18},{4,20},{6,22},{8,24},{10,26},{12,28},{14,30},{16,0},... | collective-permute-start | bytes 245768 | tf_op jit(solution)/shard_map/ppermute | solution.py:422
  12.1 6.9 %collective-permute-start.5 = (bf16[32,1024]{1,0:T(8,128)(2,1)S(1)}, bf16[32,1024]{1,0:T(8,128)(2,1)S(1)}, u32[]{:S(2)}, u32[]{:S(2)}) collective-permute-start(bf16[32,1024]{1,0:T(8,128)(2,1)S(1)} %bitcast.7), channel_id=1, source_target_pairs={{0,16},{2,18},{4,20},{6,22},{8,24},{10,26},{12,28},{14,30},{16,0},... | collective-permute-start | bytes 196616 | tf_op jit(solution)/shard_map/ppermute | solution.py:422
  12.8 8.6 %collective-permute-start.6 = (bf16[160,512]{1,0:T(8,128)(2,1)S(1)}, bf16[160,512]{1,0:T(8,128)(2,1)S(1)}, u32[]{:S(2)}, u32[]{:S(2)}) collective-permute-start(bf16[160,512]{1,0:T(8,128)(2,1)S(1)} %pad_maximum_fusion.refs_1_.refs_0_), channel_id=1, source_target_pairs={{0,2},{2,0},{4,6},{6,4},{8,10},{10,8},{12,14},{14,12},{16,18},{18,... | collective-permute-start | bytes 491528 | tf_op jit(solution)/shard_map/ppermute | solution.py:422
  17.4 4.0 %collective-permute-start.8 = (bf16[160,512]{1,0:T(8,128)(2,1)S(1)}, bf16[160,512]{1,0:T(8,128)(2,1)S(1)}, u32[]{:S(2)}, u32[]{:S(2)}) collective-permute-start(bf16[160,512]{1,0:T(8,128)(2,1)S(1)} %collective-permute-done.refs_5_.refs_4_), channel_id=1, source_target_pairs={{0,2},{2,0},{4,6},{6,4},{8,10},{10,8},{12,14},{14,12},{16,18},{18,... | collective-permute-start | bytes 491528 | tf_op jit(solution)/shard_map/ppermute | solution.py:422
  19.0 2.4 %collective-permute-start.7 = (bf16[160,512]{1,0:T(8,128)(2,1)S(1)}, bf16[160,512]{1,0:T(8,128)(2,1)S(1)}, u32[]{:S(2)}, u32[]{:S(2)}) collective-permute-start(bf16[160,512]{1,0:T(8,128)(2,1)S(1)} %collective-permute-done.4.refs_3_.refs_2_), channel_id=1, source_target_pairs={{0,2},{2,0},{4,6},{6,4},{8,10},{10,8},{12,14},{14,12},{16,18},{18,... | collective-permute-start | bytes 491528 | tf_op jit(solution)/shard_map/ppermute | solution.py:422
  19.0 2.4 %collective-permute-start.9 = (bf16[160,512]{1,0:T(8,128)(2,1)S(1)}, bf16[160,512]{1,0:T(8,128)(2,1)S(1)}, u32[]{:S(2)}, u32[]{:S(2)}) collective-permute-start(bf16[160,512]{1,0:T(8,128)(2,1)S(1)} %collective-permute-done.1.refs_7_.refs_6_), channel_id=1, source_target_pairs={{0,2},{2,0},{4,6},{6,4},{8,10},{10,8},{12,14},{14,12},{16,18},{18,... | collective-permute-start | bytes 491528 | tf_op jit(solution)/shard_map/ppermute | solution.py:422
  19.8 1.3 %collective-permute-start.3 = (bf16[48,512]{1,0:T(8,128)(2,1)S(1)}, bf16[48,512]{1,0:T(8,128)(2,1)S(1)}, u32[]{:S(2)}, u32[]{:S(2)}) collective-permute-start(bf16[48,512]{1,0:T(8,128)(2,1)S(1)} %join_far.1.refs_0_), channel_id=1, source_target_pairs={{0,2},{2,0},{4,6},{6,4},{8,10},{10,8},{12,14},{14,12},{16,18},{18,... | collective-permute-start | bytes 147464 | tf_op jit(solution)/shard_map/ppermute | solution.py:422
  22.5 6.1 %collective-permute-start.11 = (bf16[80,512]{1,0:T(8,128)(2,1)S(1)}, bf16[80,512]{1,0:T(8,128)(2,1)S(1)}, u32[]{:S(2)}, u32[]{:S(2)}) collective-permute-start(bf16[80,512]{1,0:T(8,128)(2,1)S(1)} %join_core.1.refs_2_), channel_id=1, source_target_pairs={{0,4},{2,6},{4,0},{6,2},{8,12},{10,14},{12,8},{14,10},{16,20},{18,... | collective-permute-start | bytes 245768 | tf_op jit(solution)/shard_map/ppermute | solution.py:422
  24.2 5.9 %collective-permute-start.12 = (bf16[80,512]{1,0:T(8,128)(2,1)S(1)}, bf16[80,512]{1,0:T(8,128)(2,1)S(1)}, u32[]{:S(2)}, u32[]{:S(2)}) collective-permute-start(bf16[80,512]{1,0:T(8,128)(2,1)S(1)} %join_core.1.refs_2_), channel_id=1, source_target_pairs={{0,8},{2,10},{4,12},{6,14},{8,0},{10,2},{12,4},{14,6},{16,24},{18,... | collective-permute-start | bytes 245768 | tf_op jit(solution)/shard_map/ppermute | solution.py:422
  24.2 6.8 %collective-permute-start.13 = (bf16[80,512]{1,0:T(8,128)(2,1)S(1)}, bf16[80,512]{1,0:T(8,128)(2,1)S(1)}, u32[]{:S(2)}, u32[]{:S(2)}) collective-permute-start(bf16[80,512]{1,0:T(8,128)(2,1)S(1)} %join_core.1.refs_2_), channel_id=1, source_target_pairs={{0,12},{2,14},{4,8},{6,10},{8,4},{10,6},{12,0},{14,2},{16,28},{18,... | collective-permute-start | bytes 245768 | tf_op jit(solution)/shard_map/ppermute | solution.py:422
  26.1 5.8 %collective-permute-start.10 = (bf16[32,1152]{1,0:T(8,128)(2,1)S(1)}, bf16[32,1152]{1,0:T(8,128)(2,1)S(1)}, u32[]{:S(2)}, u32[]{:S(2)}) collective-permute-start(bf16[32,1152]{1,0:T(8,128)(2,1)S(1)} %prefill_partials.2), channel_id=1, source_target_pairs={{0,16},{2,18},{4,20},{6,22},{8,24},{10,26},{12,28},{14,30},{16,0},... | collective-permute-start | bytes 221192 | tf_op jit(solution)/shard_map/ppermute | solution.py:422
  31.0 2.8 %collective-permute-start.15 = (bf16[128,512]{1,0:T(8,128)(2,1)S(1)}, bf16[128,512]{1,0:T(8,128)(2,1)S(1)}, u32[]{:S(2)}, u32[]{:S(2)}) collective-permute-start(bf16[128,512]{1,0:T(8,128)(2,1)S(1)} %pad_maximum_fusion.1.near_ref), channel_id=1, source_target_pairs={{0,2},{2,0},{4,6},{6,4},{8,10},{10,8},{12,14},{14,12},{16,18},{18,... | collective-permute-start | bytes 393224 | tf_op jit(solution)/shard_map/ppermute | solution.py:422
  32.2 4.7 %collective-permute-start.14 = (bf16[48,1024]{1,0:T(8,128)(2,1)S(1)}, bf16[48,1024]{1,0:T(8,128)(2,1)S(1)}, u32[]{:S(2)}, u32[]{:S(2)}) collective-permute-start(bf16[48,1024]{1,0:T(8,128)(2,1)S(1)} %join_parts.1.refs_0_), channel_id=1, source_target_pairs={{0,1},{1,0},{2,3},{3,2},{4,5},{5,4},{6,7},{7,6},{8,9},{9,8},{10,11... | collective-permute-start | bytes 294920 | tf_op jit(solution)/shard_map/ppermute | solution.py:465
